TPU v7x, 128 devices: a whole 4x4x4 slice. The times are simulated.
128 devices in a mesh: roll: 16 (over y_hi, z, core), tp: 8 (over y_lo, x).
Axes of the slice: x: 4, y: 4 (y_hi: 2, y_lo: 2; y = y_hi * 2 + y_lo), z: 4, core: 2. Of those that a mesh axis runs over, the one named last changes fastest.
Arguments:
- tokens: bfloat16 [64, 16, 4, 8192], P(None, 'roll', None, 'tp'), may hold values from -6 to 6
- query_weight: bfloat16 [8192, 8192], P('tp'), may hold values from -0.0625 to 0.0625
- query_bias: bfloat16 [8192], P('tp'), may hold values from -4 to 4
- pair_weight: bfloat16 [8192, 2048], P('tp'), may hold values from -0.0625 to 0.0625
- pair_bias: bfloat16 [2048], P('tp'), may hold values from -4 to 4
- cache_pairs: bfloat16 [64, 16, 64, 8, 256], P(None, 'roll', None, 'tp'), may hold values from -6 to 6
- prefix_pairs: bfloat16 [64, 512, 8, 256], P('roll', None, 'tp'), may hold values from -256 to 256
- owner_slot: int32 [64], replicated, may hold values from 0 to 63, each once
- prefix_blocks: int32 [64], replicated, may hold values from 1 to 4, as said below
- positions: int32 [64, 16], P(None, 'roll'), may hold values from 0 to 64, as said below
Outputs:
- attended: bfloat16 [64, 16, 4, 8192], P(None, 'roll', None, 'tp')
- new_pairs: bfloat16 [64, 16, 4, 8, 256], P(None, 'roll', None, 'tp')
Inputs may be any that keep to these rules, and one draw needn't show every extreme that they name: owner_slot is a permutation of the prompts. `prefix_blocks`: some prompt has 4 blocks. The first positions[p, g] rows of cache_pairs[p, g] are filled; some sample has 64.
All inputs are finite; a program needn't handle non-finite values.
Results may differ from a plain program's by a relative error of at most 0.02.
Values may be sent and summed in bfloat16 or wider, within the bound.
No kernel may reach another device: no remote copies, remote signals or barrier semaphores. Data moves between devices by JAX's collectives and lax.ppermute only.
A program may use at most 128 MiB of HBM per device.

v0:
```python
import math

import jax
import jax.numpy as jnp
from jax import lax
from jax.sharding import PartitionSpec as P

BLOCK = 128


rope_base = 1000000.0
neg_fill = -1e30


def rotate(values, where_at):
    half_dim = values.shape[-1] // 2
    frequency = jnp.exp(
        jnp.arange(half_dim, dtype=jnp.float32) * (-2.0 * math.log(rope_base) / values.shape[-1])
    )
    angles = where_at.astype(jnp.float32)[..., None] * frequency
    cosine = jnp.cos(angles)
    sine_part = jnp.sin(angles)
    leading = values[..., :half_dim]
    trailing = values[..., half_dim:]
    return jnp.concatenate(
        [leading * cosine - trailing * sine_part, trailing * cosine + leading * sine_part], axis=-1
    )


def projection_terms(weight_local, flat_rows):
    return lax.dot_general(
        weight_local, flat_rows, (((0,), (1,)), ((), ())), preferred_element_type=jnp.float32
    )


def merge_state(first_top, first_total, first_values, second_top, second_total, second_values):
    joined_top = jnp.maximum(first_top, second_top)
    first_keep = jnp.exp(first_top - joined_top)
    second_keep = jnp.exp(second_top - joined_top)
    merged_total = first_total * first_keep + second_total * second_keep
    merged_values = first_values * first_keep[..., None] + second_values * second_keep[..., None]
    return (joined_top, merged_total, merged_values)


def prefix_partial(query_block, prefix_block, limit_block):
    head_dim = query_block.shape[-1]
    key_span = prefix_block.shape[1]
    scores = jnp.einsum(
        "bkqd,bckd->bkqc",
        query_block,
        prefix_block[..., :head_dim],
        preferred_element_type=jnp.float32,
    ) * head_dim ** (-0.5)
    valid = (jnp.arange(key_span, dtype=jnp.int32)[None, :] < limit_block[:, None])[
        :, None, None, :
    ]
    scores = jnp.where(valid, scores, neg_fill)
    block_top = jnp.max(scores, -1)
    weights = jnp.where(valid, jnp.exp(scores - block_top[..., None]), 0.0)
    block_total = jnp.sum(weights, -1)
    block_values = jnp.einsum(
        "bkqc,bckd->bkqd",
        weights.astype(jnp.bfloat16),
        prefix_block[..., head_dim:],
        preferred_element_type=jnp.float32,
    )
    return (block_top, block_total, block_values)


def on_device(
    tokens,
    query_weight,
    query_bias,
    pair_weight,
    pair_bias,
    cache_pairs,
    prefix_pairs,
    owner_slot,
    prefix_blocks,
    positions,
):
    prompt_count, sample_count, new_count, local_width = tokens.shape
    head_dim = cache_pairs.shape[-1] // 2
    flat_rows = tokens.reshape(-1, local_width)
    tp_count = lax.axis_size("tp")
    query_share = query_weight.shape[1] // tp_count
    pair_share = pair_weight.shape[1] // tp_count
    heads_here = pair_share // (2 * head_dim)
    per_group = query_share // (heads_here * head_dim)
    query_sum = lax.psum_scatter(
        projection_terms(query_weight, flat_rows), "tp", scatter_dimension=0, tiled=True
    )
    pair_sum = lax.psum_scatter(
        projection_terms(pair_weight, flat_rows).astype(jnp.bfloat16),
        "tp",
        scatter_dimension=0,
        tiled=True,
    ).astype(jnp.float32)
    query_full = query_sum + query_bias.astype(jnp.float32)[:, None]
    pair_full = pair_sum + pair_bias.astype(jnp.float32)[:, None]
    new_index = jnp.arange(new_count, dtype=jnp.int32)
    where_at = (
        BLOCK * prefix_blocks[:, None, None] + positions[:, :, None] + new_index[None, None, :]
    )
    queries = rotate(
        query_full.T.reshape(
            prompt_count, sample_count, new_count, heads_here, per_group, head_dim
        ),
        where_at[..., None, None],
    ).astype(jnp.bfloat16)
    pair_parts = pair_full.T.reshape(prompt_count, sample_count, new_count, heads_here, 2, head_dim)
    new_keys = rotate(pair_parts[..., 0, :], where_at[..., None])
    new_pairs = jnp.concatenate([new_keys, pair_parts[..., 1, :]], axis=-1).astype(jnp.bfloat16)
    scale_factor = head_dim ** (-0.5)
    cache_length = cache_pairs.shape[2]
    cache_scores = (
        jnp.einsum(
            "pgnkhd,pgckd->pgnkhc",
            queries,
            cache_pairs[..., :head_dim],
            preferred_element_type=jnp.float32,
        )
        * scale_factor
    )
    fresh_scores = (
        jnp.einsum(
            "pgnkhd,pgmkd->pgnkhm",
            queries,
            new_pairs[..., :head_dim],
            preferred_element_type=jnp.float32,
        )
        * scale_factor
    )
    cache_valid = (
        jnp.arange(cache_length, dtype=jnp.int32)[None, None, :] < positions[:, :, None]
    )[:, :, None, None, None, :]
    fresh_valid = (new_index[:, None] >= new_index[None, :])[None, None, :, None, None, :]
    cache_scores = jnp.where(cache_valid, cache_scores, neg_fill)
    fresh_scores = jnp.where(fresh_valid, fresh_scores, neg_fill)
    local_top = jnp.maximum(jnp.max(cache_scores, -1), jnp.max(fresh_scores, -1))
    cache_weights = jnp.where(cache_valid, jnp.exp(cache_scores - local_top[..., None]), 0.0)
    fresh_weights = jnp.where(fresh_valid, jnp.exp(fresh_scores - local_top[..., None]), 0.0)
    local_total = jnp.sum(cache_weights, -1) + jnp.sum(fresh_weights, -1)
    local_values = jnp.einsum(
        "pgnkhc,pgckd->pgnkhd",
        cache_weights.astype(jnp.bfloat16),
        cache_pairs[..., head_dim:],
        preferred_element_type=jnp.float32,
    )
    local_values = local_values + jnp.einsum(
        "pgnkhm,pgmkd->pgnkhd",
        fresh_weights.astype(jnp.bfloat16),
        new_pairs[..., head_dim:],
        preferred_element_type=jnp.float32,
    )
    slot_prompt = (
        jnp.zeros((prompt_count,), jnp.int32)
        .at[owner_slot]
        .set(jnp.arange(prompt_count, dtype=jnp.int32))
    )
    query_count = sample_count * new_count * per_group
    query_rows = queries.transpose(0, 3, 1, 2, 4, 5).reshape(
        prompt_count, heads_here, query_count, head_dim
    )
    sorted_queries = jnp.take(query_rows, slot_prompt, axis=0)
    sorted_limit = BLOCK * jnp.take(prefix_blocks, slot_prompt, axis=0)
    run_top = jnp.full((prompt_count, heads_here, query_count), neg_fill, jnp.float32)
    run_total = jnp.zeros((prompt_count, heads_here, query_count), jnp.float32)
    run_values = jnp.zeros((prompt_count, heads_here, query_count, head_dim), jnp.float32)
    block_top, block_total, block_values = prefix_partial(
        sorted_queries, lax.all_gather(prefix_pairs, "roll", axis=0, tiled=True), sorted_limit
    )
    old_top = run_top
    old_total = run_total
    old_values = run_values
    joined_top, joined_total, joined_values = merge_state(
        old_top, old_total, old_values, block_top, block_total, block_values
    )
    run_top = joined_top
    run_total = joined_total
    run_values = joined_values
    prefix_top = (
        jnp.take(run_top, owner_slot, axis=0)
        .reshape(prompt_count, heads_here, sample_count, new_count, per_group)
        .transpose(0, 2, 3, 1, 4)
    )
    prefix_total = (
        jnp.take(run_total, owner_slot, axis=0)
        .reshape(prompt_count, heads_here, sample_count, new_count, per_group)
        .transpose(0, 2, 3, 1, 4)
    )
    prefix_values = (
        jnp.take(run_values, owner_slot, axis=0)
        .reshape(prompt_count, heads_here, sample_count, new_count, per_group, head_dim)
        .transpose(0, 2, 3, 1, 4, 5)
    )
    joined_top, joined_total, joined_values = merge_state(
        local_top, local_total, local_values, prefix_top, prefix_total, prefix_values
    )
    attended = (
        (joined_values / joined_total[..., None])
        .astype(jnp.bfloat16)
        .reshape(prompt_count, sample_count, new_count, heads_here * per_group * head_dim)
    )
    return (attended, new_pairs)


def solution(mesh):
    return jax.shard_map(
        on_device,
        mesh=mesh,
        in_specs=(
            P(None, "roll", None, "tp"),
            P("tp", None),
            P("tp"),
            P("tp", None),
            P("tp"),
            P(None, "roll", None, "tp", None),
            P("roll", None, "tp", None),
            P(),
            P(),
            P(None, "roll"),
        ),
        out_specs=(P(None, "roll", None, "tp"), P(None, "roll", None, "tp", None)),
        check_vma=False,
    )
```

profile of v0, /device:TPU:0, one launch (start us, length us, event | category | flops | bytes accessed | tf_op | source)
XLA Modules:
  0.0 240.9 jit_solution(10915389297680373847)
XLA Ops:
  8.0 1.2 reshape.546
  9.2 4.5 %convolution_convert_fusion = bf16[2048,256]{1,0:T(8,128)(2,1)} fusion(bf16[1024,2048]{1,0:T(8,128)(2,1)} %param.15, bf16[256,1024]{1,0:T(8,128)(2,1)S(1)} %reshape.546), kind=kOutput, calls=%fused_computation.15 | convolution fusion | flops 1074266112 | bytes 5767168 | tf_op jit(solution)/shard_map/dot_general | solution.py:31
  13.8 13.7 %fusion.84 = f32[8192,256]{1,0:T(8,128)} fusion(bf16[1024,8192]{1,0:T(8,128)(2,1)} %param.13, bf16[256,1024]{1,0:T(8,128)(2,1)S(1)} %reshape.546), kind=kOutput, calls=%fused_computation.132 | convolution fusion | flops 4294967296 | bytes 25690112 | tf_op jit(solution)/shard_map/dot_general | solution.py:31
  27.6 0.5 all-gather.2.cloned.1.call-update
  28.2 0.8 scatter_custom_fusion
  29.0 0.8 gather_fusion
  29.9 0.1 iota_compare_fusion.1
  30.1 0.1 iota_compare_fusion
  30.2 1.3 multiply_cosine_fusion.1
  31.4 24.0 %reduce-scatter.5.cloned.1.call-done = bf16[256,256]{1,0:T(8,128)(2,1)} async-done(((bf16[2048,256]{1,0:T(8,128)(2,1)}), bf16[256,256]{1,0:T(8,128)(2,1)}) %reduce-scatter.5.cloned.1.call-update) | async-done | bytes 131088 | tf_op jit(solution)/shard_map/reduce_scatter | solution.py:93
  55.5 1.0 add_bitcast_fusion.1
  56.5 0.1 copy.54
  56.6 0.1 reshape.549
  56.8 0.1 slice.57
  56.9 0.1 slice.61
  57.1 1.2 fusion.51
  58.3 0.8 maximum_bitcast_fusion.1
  59.1 90.4 %reduce-scatter.3.cloned.1.call-done = f32[1024,256]{1,0:T(8,128)} async-done(((f32[8192,256]{1,0:T(8,128)}), f32[1024,256]{1,0:T(8,128)}) %reduce-scatter.3.cloned.1.call-update) | async-done | bytes 1048592 | tf_op jit(solution)/shard_map/reduce_scatter | solution.py:90
  149.5 1.4 add_bitcast_fusion
  151.0 0.3 copy.52
  151.3 0.2 copy.79
  151.5 0.5 subtract_convert_fusion
  152.0 0.3 maximum_bitcast_fusion
  152.3 0.7 gather_fusion.1
  153.0 2.6 %fusion.83 = (f32[64,4,8]{2,1,0:T(4,128)S(1)}, f32[64,1,4,1,8,4]{4,5,2,0,3,1:T(4,128)S(1)}) fusion(bf16[64,4,8,64]{3,2,1,0:T(8,128)(2,1)S(1)} %bitcast.158, bf16[64,4,8,64]{3,2,1,0:T(8,128)(2,1)S(1)} %bitcast.155, bf16[64,1,4,1,64]{4,2,0,3,1:T(4,128)(2,1)S(1)} %get-tuple-element.19, bf16[64,1,4,1,64]{4,2,0,3,1:T(4,128)(2,1)S(1)} %get-tuple-element.18, ...), kind=kOutput, calls=%fused_computation.131 | convolution fusion | flops 3299328 | bytes 630800 | tf_op jit(solution)/shard_map/pgnkhd,pgmkd->pgnkhm/dot_general | solution.py:126
  155.6 0.1 copy.57
  155.6 2.1 fusion.82
  157.7 0.1 copy.56
  157.8 0.1 copy.58
  158.0 0.5 fusion.38
  158.5 0.1 copy.68
  158.6 0.8 fusion.29
  159.3 0.1 copy.67
  159.4 2.7 %convolution_bitcast_fusion = f32[64,128,4,8]{1,3,2,0:T(8,128)} fusion(bf16[64,1,64,1,256]{4,2,0,3,1:T(8,128)(2,1)} %bitcast.165, f32[64,1,4,1,8,64]{5,4,2,0,3,1:T(8,128)S(1)} %get-tuple-element.29, f32[64,4,8]{2,1,0:T(4,128)S(1)} %copy.58, pred[64,64]{1,0:T(8,128)(4,1)S(1)} %iota_compare_fusion.1), kind=kOutput, calls=%fused_computation.25 | convolution fusion | flops 33947648 | bytes 2633728 | tf_op jit(solution)/shard_map/pgnkhc,pgckd->pgnkhd/dot_general | solution.py:144
  162.1 50.5 %all-gather.2.cloned.1.call-done = bf16[64,512,1,256]{3,1,2,0:T(8,128)(2,1)} async-done(((bf16[4,512,1,256]{3,1,2,0:T(8,128)(2,1)}), bf16[64,512,1,256]{3,1,2,0:T(8,128)(2,1)}) %all-gather.2.cloned.1.call-update) | async-done | bytes 16777232 | tf_op jit(solution)/shard_map/all_gather | solution.py:171
  212.6 5.6 %fusion.2 = (f32[64,32]{1,0:T(8,128)S(1)}, f32[64,32,512]{2,1,0:T(8,128)S(1)}) fusion(pred[64,512]{1,0:T(8,128)(4,1)S(1)} %iota_compare_fusion, bf16[64,512,1,256]{3,1,0,2:T(8,128)(2,1)} %bitcast.160, bf16[64,32,128]{2,1,0:T(8,128)(2,1)S(1)} %gather_fusion.1, pred[64]{0:T(512)(128)(4,1)S(1)} %get-tuple-element.15), kind=kOutput, calls=%fused_computation.12 | convolution fusion | flops 271841280 | bytes 13148224 | tf_op jit(solution)/shard_map/bkqd,bckd->bkqc/dot_general | solution.py:48
  218.2 1.9 copy-done.1
  220.2 1.6 fusion.3
  221.8 0.6 gather_fusion.4
  222.4 0.6 gather_fusion.3
  223.0 0.1 bitcast_select_fusion.2
  223.3 0.1 copy.64
  223.4 0.1 copy.66
  223.5 0.1 copy.70
  223.6 5.8 %fusion.16 = f32[64,32,128]{2,1,0:T(8,128)S(1)} fusion(bf16[64,512,1,256]{3,1,0,2:T(8,128)(2,1)} %bitcast.161, f32[64,32,512]{2,1,0:T(8,128)} %copy-done.1, f32[64,32]{1,0:T(8,128)S(1)} %get-tuple-element.32, pred[64,512]{1,0:T(8,128)(4,1)S(1)} %iota_compare_fusion, f32[64,32]{1,0:T(8,128)S(1)} %get-tuple-element.25, f32[64,32]{1,0:T(8,128)S(1)} %get-tuple-element.24), kind=kOutput, calls=%fused_computation.27 | convolution fusion | flops 274202624 | bytes 13688832 | tf_op jit(solution)/shard_map/bkqc,bckd->bkqd/dot_general | solution.py:61
  229.4 0.6 gather_fusion.2
  230.0 2.5 %fusion.23 = bf16[64,1,4,1,8,128]{5,4,2,0,3,1:T(8,128)(2,1)S(1)} fusion(f32[64,128,4,8]{1,3,2,0:T(8,128)} %convolution_bitcast_fusion, f32[64,32,128]{2,1,0:T(8,128)S(1)} %gather_fusion.2, f32[64,4,8]{2,1,0:T(4,128)S(1)} %copy.70, f32[64,4,8]{2,1,0:T(4,128)S(1)} %copy.66, f32[64,4,8]{2,1,0:T(4,128)S(1)} %copy.64, pred[64]{0:T(512)(128)(4,1)S(1)} %compare_and_fusion, ...), kind=kOutput, calls=%fused_computation.32 | convolution fusion | flops 3956736 | bytes 2752592 | tf_op jit(solution)/shard_map/pgnkhm,pgmkd->pgnkhd/dot_general | solution.py:150
  232.5 0.9 reshape.557
  (37 shorter events, 0.6 us)
Async XLA Ops:
  8.0 47.5 %reduce-scatter.5.cloned.1.call-start = ((), (), s32[]{:S(2)}) async-start(), calls=%async_computation.3 | async-start | bytes 1179648 | tf_op jit(solution)/shard_map/reduce_scatter | solution.py:93
  13.7 135.8 %reduce-scatter.3.cloned.1.call-start = ((), (), s32[]{:S(2)}) async-start(), calls=%async_computation.2 | async-start | bytes 9437184 | tf_op jit(solution)/shard_map/reduce_scatter | solution.py:90
  27.5 0.7 copy-start.2
  27.5 0.7 copy-start.4
  27.5 0.7 copy-start.5
  27.5 1.5 copy-start
  27.5 2.3 copy-start.3
  27.6 185.1 %all-gather.2.cloned.1.call-start = ((), (), s32[]{:S(2)}) async-start(), calls=%async_computation.4 | async-start | bytes 17825792 | tf_op jit(solution)/shard_map/all_gather | solution.py:171
  218.2 1.9 copy-start.1
Sparse Core Ops, SparseCore 0:
  13.9 41.5 reduce-scatter.4
  57.9 91.5 reduce-scatter.2
Sparse Core Ops, SparseCore 1:
  30.5 182.1 all-gather.1
where the time goes:
time: 242 us; the launch traced here: 241 us
  waiting for transfers between devices  166 us (69%)
  matrix products  39.4 us (16%)
  between operations  15.8 us (7%)
  local copies, waits for them, and re-layouts  10.1 us (4%)
  other arithmetic  9.9 us (4%)
    reduce_scatter x1, waiting for transfers between devices, on_device(): lax.psum_scatter(projection_terms(query_weight, flat_rows), 'tp', scatter...  90.4 us
    all_gather x1, waiting for transfers between devices, on_device(): lax.all_gather(prefix_pairs, 'roll', axis=0, tiled=True)  50.5 us
    reduce_scatter x1, waiting for transfers between devices, on_device(): lax.psum_scatter(projection_terms(pair_weight, flat_rows).astype(jnp.bflo...  24 us
    dot_general x2, matrix products, projection_terms(): lax.dot_general(weight_local, flat_rows, (((0,), (1,)), ((), ())), prefer...  18.2 us
    dot_general x1, matrix products, prefix_partial(): jnp.einsum('bkqc,bckd->bkqd', weights.astype(jnp.bfloat16), prefix_block[...  5.77 us
    dot_general x1, matrix products, prefix_partial(): jnp.einsum('bkqd,bckd->bkqc', query_block, prefix_block[..., :head_dim],...  5.59 us
  transfers between devices with their start and end apart: 3, of which 3 were waited for; matrix products, arithmetic and copies ran while one was open for 14% of the time, Pallas kernels for 0%

commit v1 on v0

v1 whole, which is shorter than its diff:
```python
import functools
import math

import jax
import jax.numpy as jnp
from jax import lax
from jax.experimental import pallas as pl
from jax.experimental.pallas import tpu as pltpu
from jax.sharding import PartitionSpec as P

BLOCK = 128
HD = 128
ROPE_BASE = 1000000.0
NEG = -1e30
SCALE = HD ** -0.5
F32 = jnp.float32
BF16 = jnp.bfloat16
VMEM = 48 * 1024 * 1024

X_GROUPS = [[0, 1, 2, 3], [4, 5, 6, 7]]
Y_SWAP = [(i, (i + 4) % 8) for i in range(8)]


def roll_index(y, z, c):
    return (y * 4 + z) * 2 + c


Z_GROUPS = [[roll_index(y, z, c) for z in range(4)] for y in range(2) for c in range(2)]
YH_SWAP = [(i, (i + 8) % 16) for i in range(16)]
CORE_SWAP = [(i, i ^ 1) for i in range(16)]


def dot(a, b, dims=((1,), (0,))):
    return lax.dot_general(a, b, (dims, ((), ())), preferred_element_type=F32)


def project_kernel(x_ref, wq_ref, wp_ref, o_ref):
    x = x_ref[...]
    width = wq_ref.shape[1]
    o_ref[0, :, :width] = dot(x, wq_ref[...]).astype(BF16)
    o_ref[0, :, width:] = dot(x, wp_ref[...]).astype(BF16)


def project(x, wq, wp):
    rows, depth = x.shape
    qw, pw = wq.shape[1] // 8, wp.shape[1] // 8
    dest = lambda g: (g % 2) * 4 + g // 2
    return pl.pallas_call(
        project_kernel,
        grid=(8,),
        in_specs=[
            pl.BlockSpec((rows, depth), lambda g: (0, 0)),
            pl.BlockSpec((depth, qw), lambda g: (0, dest(g))),
            pl.BlockSpec((depth, pw), lambda g: (0, dest(g))),
        ],
        out_specs=pl.BlockSpec((1, rows, qw + pw), lambda g: (g, 0, 0)),
        out_shape=jax.ShapeDtypeStruct((8, rows, qw + pw), BF16),
        compiler_params=pltpu.CompilerParams(vmem_limit_bytes=VMEM),
        cost_estimate=pl.CostEstimate(
            flops=2 * rows * depth * 8 * (qw + pw),
            bytes_accessed=2 * depth * 8 * (qw + pw),
            transcendentals=0,
        ),
        name="project",
    )(x, wq, wp)


def column_max_sum(scores):
    top = jnp.max(scores, -1, keepdims=True)
    weights = jnp.exp(scores - top)
    return top, weights, jnp.sum(weights, -1, keepdims=True)


def prefix_kernel(where_ref, limit_ref, q_ref, *refs):
    kvs, o_ref = refs[:-1], refs[-1]
    per = kvs[0].shape[0]
    slots = q_ref.shape[1]
    lane = lax.broadcasted_iota(jnp.int32, (128, 128), 1)
    stats = jnp.zeros((128, 128), F32)
    for b, kv in enumerate(kvs):

        def step(j, stats, b=b, kv=kv):
            at = where_ref[b] * per + j
            q = q_ref[:, at].reshape(128, HD)
            s = dot(q, kv[j, :, :HD], ((1,), (1,))) * SCALE
            col = lax.broadcasted_iota(jnp.int32, s.shape, 1)
            s = jnp.where(col < limit_ref[at], s, NEG)
            top, w, total = column_max_sum(s)
            o = dot(w.astype(BF16), kv[j, :, HD:]) / total
            o_ref[:, pl.ds(at, 1)] = o.astype(BF16).reshape(4, 1, 32, HD)
            rest = top + jnp.log(total)
            for part in range(3):
                piece = rest.astype(BF16).astype(F32)
                stats = jnp.where(lane == 3 * at + part, piece, stats)
                rest = rest - piece
            return stats

        stats = lax.fori_loop(0, per, step, stats, unroll=True)
    o_ref[:, slots] = stats.astype(BF16).reshape(4, 32, 128)


def prefix_attention(where, limits, q, kvs):
    slots = q.shape[1]
    return pl.pallas_call(
        prefix_kernel,
        in_specs=[pl.BlockSpec(memory_space=pltpu.SMEM)] * 2
        + [pl.BlockSpec(memory_space=pltpu.VMEM)] * (1 + len(kvs)),
        out_specs=pl.BlockSpec(memory_space=pltpu.VMEM),
        out_shape=jax.ShapeDtypeStruct((4, slots + 1, 32, 128), BF16),
        compiler_params=pltpu.CompilerParams(vmem_limit_bytes=VMEM),
        name="prefix_attention",
    )(where, limits, q, *kvs)


def cache_kernel(order_ref, pos_ref, q_ref, new_ref, c0, c1, c2, c3, o_ref, lse_ref):
    g = pl.program_id(0)
    caches = (c0, c1, c2, c3)
    q = q_ref[...].reshape(128, HD)
    keys = jnp.concatenate([c[0, :, :HD] for c in caches], 0)
    vals = jnp.concatenate([c[0, :, HD:] for c in caches], 0)
    s = dot(q, keys, ((1,), (1,))) * SCALE
    row = lax.broadcasted_iota(jnp.int32, s.shape, 0)
    col = lax.broadcasted_iota(jnp.int32, s.shape, 1)
    length = jnp.zeros(s.shape, jnp.int32)
    for i in range(4):
        length = jnp.where(row // 32 == i, pos_ref[order_ref[g * 4 + i]], length)
    s = jnp.where((row // 32 == col // 64) & (col % 64 < length), s, NEG)
    new = new_ref[...]
    f = dot(q, new[:, :HD], ((1,), (1,))) * SCALE
    row = lax.broadcasted_iota(jnp.int32, f.shape, 0)
    col = lax.broadcasted_iota(jnp.int32, f.shape, 1)
    f = jnp.where((row // 32 == col // 4) & (col % 4 <= row % 4), f, NEG)
    top = jnp.maximum(jnp.max(s, -1, keepdims=True), jnp.max(f, -1, keepdims=True))
    ws = jnp.exp(s - top)
    wf = jnp.exp(f - top)
    total = jnp.sum(ws, -1, keepdims=True) + jnp.sum(wf, -1, keepdims=True)
    o = dot(ws.astype(BF16), vals) + dot(wf.astype(BF16), new[:, HD:])
    o_ref[...] = o / total
    lse_ref[...] = jnp.broadcast_to(top + jnp.log(total), (128, HD))


def cache_attention(order, pos, q, new, cache):
    prompts = q.shape[0]
    spec = lambda i: pl.BlockSpec((1, 64, 2 * HD), lambda g, o, p, i=i: (o[g * 4 + i], 0, 0))
    flat = pl.BlockSpec((128, HD), lambda g, o, p: (g, 0))
    return pl.pallas_call(
        cache_kernel,
        grid_spec=pltpu.PrefetchScalarGridSpec(
            num_scalar_prefetch=2,
            grid=(prompts // 4,),
            in_specs=[
                pl.BlockSpec((4, 32, HD), lambda g, o, p: (g, 0, 0)),
                pl.BlockSpec((16, 2 * HD), lambda g, o, p: (g, 0)),
            ]
            + [spec(i) for i in range(4)],
            out_specs=[flat, flat],
        ),
        out_shape=[jax.ShapeDtypeStruct((prompts * 32, HD), F32)] * 2,
        compiler_params=pltpu.CompilerParams(vmem_limit_bytes=VMEM),
        name="cache_attention",
    )(order, pos, q, new, cache, cache, cache, cache)


def merge_kernel(order_ref, far_ref, o_ref, lse_ref, out_ref):
    z = pl.program_id(0)
    slots = far_ref.shape[1] - 1
    stats = far_ref[0, slots].astype(F32)
    for a in range(slots):
        far = jnp.sum(stats[:, 3 * a : 3 * a + 3], -1, keepdims=True)
        near = lse_ref[a * 32 : a * 32 + 32]
        top = jnp.maximum(far, near)
        wf, wn = jnp.exp(far - top), jnp.exp(near - top)
        o = (far_ref[0, a].astype(F32) * wf + o_ref[a * 32 : a * 32 + 32] * wn) / (wf + wn)
        o = jnp.concatenate([o[4 * h : 4 * h + 4] for h in range(8)], 1)
        out_ref[pl.ds(order_ref[z * slots + a], 1)] = o.astype(BF16)[None]


def merge(order, far, o, lse):
    slots = far.shape[1] - 1
    prompts = order.shape[0]
    flat = pl.BlockSpec((slots * 32, HD), lambda z, o: (z, 0))
    return pl.pallas_call(
        merge_kernel,
        grid_spec=pltpu.PrefetchScalarGridSpec(
            num_scalar_prefetch=1,
            grid=(4,),
            in_specs=[pl.BlockSpec((1, slots + 1, 32, HD), lambda z, o: (z, 0, 0, 0)), flat, flat],
            out_specs=pl.BlockSpec((prompts, 4, 8 * HD), lambda z, o: (0, 0, 0)),
        ),
        out_shape=jax.ShapeDtypeStruct((prompts, 4, 8 * HD), BF16),
        compiler_params=pltpu.CompilerParams(vmem_limit_bytes=VMEM),
        name="merge",
    )(order, far, o, lse)


def rotate(values, cosine, sine):
    half = values.shape[-1] // 2
    lead, trail = values[..., :half], values[..., half:]
    return jnp.concatenate([lead * cosine - trail * sine, trail * cosine + lead * sine], -1)


def on_device(
    tokens,
    query_weight,
    query_bias,
    pair_weight,
    pair_bias,
    cache_pairs,
    prefix_pairs,
    owner_slot,
    prefix_blocks,
    positions,
):
    prompts, _, new, width = tokens.shape
    rows = prompts * new
    me = lax.axis_index("roll")
    my_y, my_c = me // 8, me % 2
    my_tp_y = lax.axis_index("tp") // 4

    index = jnp.arange(prompts, dtype=jnp.int32)
    slot_prompt = jnp.sum(jnp.where(owner_slot[None, :] == index[:, None], index[None, :], 0), 1)
    order = slot_prompt.reshape(2, 4, 2, 4).transpose(1, 0, 2, 3).reshape(prompts)
    pos = positions.reshape(prompts)

    own = prefix_pairs.reshape(4, 512, 2 * HD)
    other = lax.ppermute(own, "roll", YH_SWAP)
    own_c = lax.ppermute(own, "roll", CORE_SWAP)
    other_c = lax.ppermute(other, "roll", CORE_SWAP)

    x = jnp.take(tokens.reshape(prompts, new * width), order, axis=0).reshape(rows, width)
    part = project(x, query_weight, pair_weight)
    cols = part.shape[-1]
    got = lax.all_to_all(
        part.reshape(4, 2 * rows, cols), "tp", 0, 0, tiled=True, axis_index_groups=X_GROUPS
    )
    half = jnp.sum(got.reshape(4, 2, rows, cols).astype(F32), 0)
    send = lax.dynamic_index_in_dim(half, 1 - my_tp_y, 0, keepdims=False).astype(BF16)
    keep = lax.dynamic_index_in_dim(half, my_tp_y, 0, keepdims=False)
    full = keep + lax.ppermute(send, "tp", Y_SWAP).astype(F32)

    at = (
        BLOCK * jnp.take(prefix_blocks, order)[:, None]
        + jnp.take(pos, order)[:, None]
        + jnp.arange(new, dtype=jnp.int32)[None, :]
    ).reshape(rows)
    frequency = jnp.exp(
        jnp.arange(HD // 2, dtype=F32) * (-2.0 * math.log(ROPE_BASE) / HD)
    )
    angles = at.astype(F32)[:, None] * frequency[None, :]
    cosine, sine = jnp.cos(angles), jnp.sin(angles)

    qw = 8 * HD
    q = (full[:, :qw] + query_bias.astype(F32)).reshape(rows, 8, HD)
    q = rotate(q, cosine[:, None], sine[:, None]).astype(BF16)
    q = q.reshape(prompts, new, 8, HD).transpose(0, 2, 1, 3).reshape(prompts, 32, HD)
    pair = full[:, qw:] + pair_bias.astype(F32)
    pair = jnp.concatenate([rotate(pair[:, :HD], cosine, sine), pair[:, HD:]], -1).astype(BF16)

    q_z = lax.all_to_all(
        q.reshape(4, 16, 32, HD), "roll", 0, 0, tiled=True, axis_index_groups=Z_GROUPS
    )
    where = jnp.stack(
        [(my_y ^ dy) * 2 + (my_c ^ dc) for dy, dc in ((0, 0), (1, 0), (0, 1), (1, 1))]
    ).astype(jnp.int32)
    limits = lax.dynamic_index_in_dim(
        (BLOCK * jnp.take(prefix_blocks, order)).reshape(4, 16), (me // 2) % 4, 0, keepdims=False
    )
    far = prefix_attention(where, limits, q_z, (own, other, own_c, other_c))
    far = lax.all_to_all(far, "roll", 0, 0, tiled=True, axis_index_groups=Z_GROUPS)

    near, near_lse = cache_attention(order, pos, q, pair, cache_pairs.reshape(prompts, 64, 2 * HD))
    attended = merge(order, far, near, near_lse)

    inverse = (
        owner_slot.reshape(-1) // 8 % 4 * 16
        + owner_slot // 32 * 8
        + owner_slot // 4 % 2 * 4
        + owner_slot % 4
    )
    new_pairs = jnp.take(pair.reshape(prompts, new, 2 * HD), inverse, axis=0)
    return (
        attended.reshape(prompts, 1, new, 8 * HD),
        new_pairs.reshape(prompts, 1, new, 1, 2 * HD),
    )


def solution(mesh):
    return jax.shard_map(
        on_device,
        mesh=mesh,
        in_specs=(
            P(None, "roll", None, "tp"),
            P("tp", None),
            P("tp"),
            P("tp", None),
            P("tp"),
            P(None, "roll", None, "tp", None),
            P("roll", None, "tp", None),
            P(),
            P(),
            P(None, "roll"),
        ),
        out_specs=(P(None, "roll", None, "tp"), P(None, "roll", None, "tp", None)),
        check_vma=False,
    )
```

time: 242 us -> 159 us (0.66)
  waiting for transfers between devices: 166 us -> 78.3 us
  matrix products: 39.4 us -> 0 us
  Pallas kernels: 0 us -> 36.3 us
  starting transfers between devices: 0.12 us -> 19.4 us
  between operations: 15.8 us -> 0.99 us
  local copies, waits for them, and re-layouts: 10.1 us -> 13.3 us
    reduce_scatter x2 -> x0, waiting for transfers between devices: 114 us -> none  [the longest x1 90.4 us: on_device(): lax.psum_scatter(projection_terms(query_weight, flat_rows), 'tp', scatter...]
    all_to_all x0 -> x3, waiting for transfers between devices: none -> 64.8 us  [the longest x1 56.9 us: on_device(): lax.all_to_all(part.reshape(4, 2 * rows, cols), 'tp', 0, 0, tiled=True, a...]
    all_gather x1 -> x0, waiting for transfers between devices: 50.5 us -> none  [on_device(): lax.all_gather(prefix_pairs, 'roll', axis=0, tiled=True)]
    dot_general x8 -> x0, matrix products: 39.4 us -> none  [the longest x2 18.2 us: projection_terms(): lax.dot_general(weight_local, flat_rows, (((0,), (1,)), ((), ())), prefer...]
    pallas_call x0 -> x4, Pallas kernels: none -> 36.3 us  [the longest x1 12.9 us: project(): pl.pallas_call(project_kernel, grid=(8,), in_specs=[pl.BlockSpec((rows, d...]
    all_to_all x0 -> x3, starting transfers between devices: none -> 14 us  [the longest x1 5.49 us: on_device(): lax.all_to_all(q.reshape(4, 16, 32, HD), 'roll', 0, 0, tiled=True, axis_i...]
    ppermute x0 -> x4, waiting for transfers between devices: none -> 13.5 us  [the longest x1 13.5 us: on_device(): full = keep + lax.ppermute(send, 'tp', Y_SWAP).astype(F32)]
    unnamed x15 -> x24, local copies, waits for them, and re-layouts: 2.22 us -> 8.04 us
  transfers between devices with their start and end apart: 3 -> 7, of which waited for: 3 -> 3; matrix products, arithmetic and copies ran while one was open for 14% -> 7% of each run, Pallas kernels for 0% -> 7%
where the time goes in v1:
time: 159 us; the launch traced here: 158 us
  waiting for transfers between devices  78.3 us (49%)
  Pallas kernels  36.3 us (23%)
  starting transfers between devices  19.4 us (12%)
  local copies, waits for them, and re-layouts  13.3 us (8%)
  other arithmetic  9.72 us (6%)
    all_to_all x1, waiting for transfers between devices, on_device(): lax.all_to_all(part.reshape(4, 2 * rows, cols), 'tp', 0, 0, tiled=True, a...  56.9 us
    ppermute x1, waiting for transfers between devices, on_device(): full = keep + lax.ppermute(send, 'tp', Y_SWAP).astype(F32)  13.5 us
    pallas_call x1, Pallas kernels, project(): pl.pallas_call(project_kernel, grid=(8,), in_specs=[pl.BlockSpec((rows, d...  12.9 us
    pallas_call x1, Pallas kernels, cache_attention(): pl.pallas_call(cache_kernel, grid_spec=pltpu.PrefetchScalarGridSpec(num_s...  10.6 us
    unnamed x24, local copies, waits for them, and re-layouts  8.04 us
    all_to_all x1, waiting for transfers between devices, on_device(): lax.all_to_all(q.reshape(4, 16, 32, HD), 'roll', 0, 0, tiled=True, axis_i...  7.9 us
    pallas_call x1, Pallas kernels, prefix_attention(): pl.pallas_call(prefix_kernel, in_specs=[pl.BlockSpec(memory_space=pltpu.S...  7.58 us
    all_to_all x1, starting transfers between devices, on_device(): lax.all_to_all(q.reshape(4, 16, 32, HD), 'roll', 0, 0, tiled=True, axis_i...  5.49 us
  transfers between devices with their start and end apart: 7, of which 3 were waited for; matrix products, arithmetic and copies ran while one was open for 7% of the time, Pallas kernels for 7%

profile of v1, /device:TPU:0, one launch (start us, length us, event | category | flops | bytes accessed | tf_op | source)
XLA Modules:
  0.0 157.9 jit_solution(12838523808137601953)
XLA Ops:
  0.6 0.8 select_reduce_fusion
  1.4 0.1 reshape.182
  1.5 0.1 reshape.183.order_ref
  1.6 0.1 reshape.186
  1.8 1.4 gather_fusion.3
  3.2 0.8 gather_fusion.2
  4.0 1.2 copy.27
  5.2 0.9 gather_fusion
  6.1 0.3 gather.16
  6.4 0.1 broadcast_in_dim.58
  6.5 0.1 broadcast_in_dim.59
  6.6 0.1 broadcast_select_fusion.x_ref
  6.8 2.2 %copy-done.3 = bf16[1024,2048]{1,0:T(8,128)(2,1)S(1)} copy-done((bf16[1024,2048]{1,0:T(8,128)(2,1)S(1)}, bf16[1024,2048]{1,0:T(8,128)(2,1)}, u32[]{:S(2)}) %copy-start.3) | copy-done | bytes 4194328
  8.9 12.9 %project.1 = bf16[8,256,1280]{2,1,0:T(8,128)(2,1)} custom-call(bf16[256,1024]{1,0:T(8,128)(2,1)S(1)} %broadcast_select_fusion.x_ref, bf16[1024,8192]{1,0:T(8,128)(2,1)} %wq_ref.1, bf16[1024,2048]{1,0:T(8,128)(2,1)S(1)} %copy-done.3), custom_call_target="tpu_custom_call" | custom-call | flops 5368709120 | bytes 20971520 | tf_op jit(solution)/shard_map/project/pallas_call | solution.py:48
  21.8 5.1 %all-to-all-start = ((bf16[4,512,1280]{2,1,0:T(8,128)(2,1)}), bf16[4,512,1280]{2,1,0:T(8,128)(2,1)}, u32[]{:S(2)}, u32[]{:S(2)}) async-start(bf16[4,512,1280]{2,1,0:T(8,128)(2,1)} %bitcast.46), calls=%async_computation | async-start | bytes 10485760 | tf_op jit(solution)/shard_map/all_to_all | solution.py:233
  26.9 3.4 %collective-permute-start.1 = (bf16[4,512,256]{2,1,0:T(8,128)(2,1)}, bf16[4,512,256]{2,1,0:T(8,128)(2,1)}, u32[]{:S(2)}, u32[]{:S(2)}) collective-permute-start(bf16[4,512,256]{2,1,0:T(8,128)(2,1)} %bitcast.16.refs_0_), channel_id=1, source_target_pairs={{0,64},{8,72},{16,80},{24,88},{32,96},{40,104},{48,112},{56,120},{... | collective-permute-start | bytes 3145736 | tf_op jit(solution)/shard_map/ppermute | solution.py:226
  30.2 56.9 %all-to-all-done = bf16[4,512,1280]{2,1,0:T(8,128)(2,1)} async-done(((bf16[4,512,1280]{2,1,0:T(8,128)(2,1)}), bf16[4,512,1280]{2,1,0:T(8,128)(2,1)}, u32[]{:S(2)}, u32[]{:S(2)}) %all-to-all-start) | async-done | bytes 5242912 | tf_op jit(solution)/shard_map/all_to_all | solution.py:233
  87.1 3.6 %convert_reduce_fusion = f32[512,1280]{1,0:T(8,128)S(1)} fusion(bf16[4,512,1280]{2,1,0:T(8,128)(2,1)} %all-to-all-done), kind=kLoop, calls=%fused_computation.4 | loop fusion | flops 4587520 | bytes 7864320 | tf_op jit(solution)/shard_map/reduce_sum | solution.py:236
  90.7 0.1 fusion.1
  90.7 1.9 %collective-permute-start = (bf16[256,1280]{1,0:T(8,128)(2,1)S(1)}, bf16[256,1280]{1,0:T(8,128)(2,1)}, u32[]{:S(2)}, u32[]{:S(2)}) collective-permute-start(bf16[256,1280]{1,0:T(8,128)(2,1)S(1)} %fusion.1), channel_id=1, source_target_pairs={{0,4},{1,5},{2,6},{3,7},{4,0},{5,1},{6,2},{7,3},{8,12},{9,13},{10,... | collective-permute-start | bytes 1966088 | tf_op jit(solution)/shard_map/ppermute | solution.py:239
  92.7 0.1 reshape.184
  92.8 0.1 add_convert_fusion.2
  92.8 0.1 convert_element_type.38
  93.0 0.1 collective-permute-start.3
  93.1 13.5 %collective-permute-done = bf16[256,1280]{1,0:T(8,128)(2,1)} collective-permute-done((bf16[256,1280]{1,0:T(8,128)(2,1)S(1)}, bf16[256,1280]{1,0:T(8,128)(2,1)}, u32[]{:S(2)}, u32[]{:S(2)}) %collective-permute-start) | collective-permute-done | bytes 655392 | tf_op jit(solution)/shard_map/ppermute | solution.py:239
  106.6 1.2 bitcast_add_fusion
  107.8 0.1 fusion
  108.0 0.2 copy.28
  108.2 0.6 subtract_convert_fusion.1
  108.8 0.5 subtract_convert_fusion
  109.3 0.2 copy.25
  109.5 0.2 copy.24
  109.8 1.5 pad_maximum_fusion
  111.3 5.5 %all-to-all-start.1 = ((bf16[4,16,32,128]{3,2,1,0:T(8,128)(2,1)}), bf16[4,16,32,128]{3,2,1,0:T(8,128)(2,1)S(1)}, u32[]{:S(2)}, u32[]{:S(2)}) async-start(bf16[4,16,32,128]{3,2,1,0:T(8,128)(2,1)} %bitcast.15), calls=%async_computation.1 | async-start | bytes 1048576 | tf_op jit(solution)/shard_map/all_to_all | solution.py:259
  116.8 0.1 pad_add_fusion.where_ref
  116.9 7.9 %all-to-all-done.1.q_ref = bf16[4,16,32,128]{3,2,1,0:T(8,128)(2,1)S(1)} async-done(((bf16[4,16,32,128]{3,2,1,0:T(8,128)(2,1)}), bf16[4,16,32,128]{3,2,1,0:T(8,128)(2,1)S(1)}, u32[]{:S(2)}, u32[]{:S(2)}) %all-to-all-start.1) | async-done | bytes 524320 | tf_op jit(solution)/shard_map/all_to_all | solution.py:259
  124.8 7.6 %prefix_attention.1 = bf16[4,17,32,128]{3,2,1,0:T(8,128)(2,1)} custom-call(s32[4]{0:T(128)S(1)} %pad_add_fusion.where_ref, s32[16]{0:T(128)S(1)} %fusion.3.limit_ref, bf16[4,16,32,128]{3,2,1,0:T(8,128)(2,1)S(1)} %all-to-all-done.1.q_ref, bf16[4,512,256]{2,1,0:T(8,128)(2,1)} %bitcast.16.refs_0_, bf16[4,512,256]{2,1,0:T(8,128)(2,1)} %collective-permute-done.1.refs_1_, ...), custom_call_target="tpu_custom_call" | custom-call | tf_op jit(solution)/shard_map/prefix_attention/pallas_call | solution.py:104
  132.4 3.5 %all-to-all-start.2 = ((bf16[4,17,32,128]{3,2,1,0:T(8,128)(2,1)}), bf16[4,17,32,128]{3,2,1,0:T(8,128)(2,1)S(1)}, u32[]{:S(2)}, u32[]{:S(2)}) async-start(bf16[4,17,32,128]{3,2,1,0:T(8,128)(2,1)} %prefix_attention.1), calls=%async_computation.2 | async-start | bytes 1114112 | tf_op jit(solution)/shard_map/all_to_all | solution.py:269
  135.9 0.1 pad_maximum_fusion.2
  136.1 0.7 gather_fusion.1
  136.8 0.1 pad_maximum_fusion.1.new_ref
  136.9 10.6 %cache_attention.1 = (f32[2048,128]{1,0:T(8,128)S(1)}, f32[2048,128]{1,0:T(8,128)S(1)}) custom-call(s32[64]{0:T(128)S(1)} %reshape.183.order_ref, s32[64]{0:T(128)S(1)} %bitcast.40, bf16[64,32,128]{2,1,0:T(8,128)(2,1)} %bitcast.17.q_ref, bf16[256,256]{1,0:T(8,128)(2,1)S(1)} %pad_maximum_fusion.1.new_ref, bf16[64,64,256]{2,1,0:T(8,128)(2,1)S(1)} %bitcast.41, ...), custom_call_target="tpu_custom_call" | custom-call | tf_op jit(solution)/shard_map/cache_attention/pallas_call | solution.py:146
  147.5 1.0 copy-done.4
  148.5 1.0 copy-done.6
  149.4 0.8 bitcast_select_fusion
  150.3 1.2 copy-done.5
  151.5 1.2 copy-done.7
  152.7 5.2 %merge.1 = bf16[64,4,1024]{2,1,0:T(4,128)(2,1)} custom-call(s32[64]{0:T(128)S(1)} %reshape.183.order_ref, bf16[4,17,32,128]{3,2,1,0:T(8,128)(2,1)S(1)} %all-to-all-done.2.far_ref, f32[2048,128]{1,0:T(8,128)S(1)} %copy-done.5, f32[2048,128]{1,0:T(8,128)S(1)} %copy-done.7), custom_call_target="tpu_custom_call" | custom-call | tf_op jit(solution)/shard_map/merge/pallas_call | solution.py:182
  (37 shorter events, 0.2 us)
Async XLA Ops:
  0.6 2.6 %copy-start = (s32[64]{0:T(128)S(1)}, s32[64]{0:T(128)}, u32[]{:S(2)}) copy-start(s32[64]{0:T(128)} %param.20) | copy-start | bytes 772
  6.7 2.2 %copy-start.3 = (bf16[1024,2048]{1,0:T(8,128)(2,1)S(1)}, bf16[1024,2048]{1,0:T(8,128)(2,1)}, u32[]{:S(2)}) copy-start(bf16[1024,2048]{1,0:T(8,128)(2,1)} %wp_ref.1) | copy-start | bytes 12582916
  21.8 65.3 %all-to-all-start = ((bf16[4,512,1280]{2,1,0:T(8,128)(2,1)}), bf16[4,512,1280]{2,1,0:T(8,128)(2,1)}, u32[]{:S(2)}, u32[]{:S(2)}) async-start(bf16[4,512,1280]{2,1,0:T(8,128)(2,1)} %bitcast.46), calls=%async_computation | async-start | bytes 10485760 | tf_op jit(solution)/shard_map/all_to_all | solution.py:233
  26.9 66.1 %collective-permute-start.1 = (bf16[4,512,256]{2,1,0:T(8,128)(2,1)}, bf16[4,512,256]{2,1,0:T(8,128)(2,1)}, u32[]{:S(2)}, u32[]{:S(2)}) collective-permute-start(bf16[4,512,256]{2,1,0:T(8,128)(2,1)} %bitcast.16.refs_0_), channel_id=1, source_target_pairs={{0,64},{8,72},{16,80},{24,88},{32,96},{40,104},{48,112},{56,120},{... | collective-permute-start | bytes 3145736 | tf_op jit(solution)/shard_map/ppermute | solution.py:226
  30.2 86.7 %collective-permute-start.2 = (bf16[4,512,256]{2,1,0:T(8,128)(2,1)}, bf16[4,512,256]{2,1,0:T(8,128)(2,1)}, u32[]{:S(2)}, u32[]{:S(2)}) collective-permute-start(bf16[4,512,256]{2,1,0:T(8,128)(2,1)} %bitcast.16.refs_0_), channel_id=1, source_target_pairs={{0,8},{8,0},{16,24},{24,16},{32,40},{40,32},{48,56},{56,48},{64,72... | collective-permute-start | bytes 3145736 | tf_op jit(solution)/shard_map/ppermute | solution.py:227
  30.2 62.5 %copy-start.8 = (bf16[1024]{0:T(1024)(128)(2,1)S(1)}, bf16[1024]{0:T(1024)(128)(2,1)}, u32[]{:S(2)}) copy-start(bf16[1024]{0:T(1024)(128)(2,1)} %param.14) | copy-start | bytes 6148
  30.2 62.5 %copy-start.9 = (bf16[256]{0:T(256)(128)(2,1)S(1)}, bf16[256]{0:T(256)(128)(2,1)}, u32[]{:S(2)}) copy-start(bf16[256]{0:T(256)(128)(2,1)} %param.16) | copy-start | bytes 1540
  90.7 15.9 %collective-permute-start = (bf16[256,1280]{1,0:T(8,128)(2,1)S(1)}, bf16[256,1280]{1,0:T(8,128)(2,1)}, u32[]{:S(2)}, u32[]{:S(2)}) collective-permute-start(bf16[256,1280]{1,0:T(8,128)(2,1)S(1)} %fusion.1), channel_id=1, source_target_pairs={{0,4},{1,5},{2,6},{3,7},{4,0},{5,1},{6,2},{7,3},{8,12},{9,13},{10,... | collective-permute-start | bytes 1966088 | tf_op jit(solution)/shard_map/ppermute | solution.py:239
  93.0 23.9 %collective-permute-start.3 = (bf16[4,512,256]{2,1,0:T(8,128)(2,1)}, bf16[4,512,256]{2,1,0:T(8,128)(2,1)}, u32[]{:S(2)}, u32[]{:S(2)}) collective-permute-start(bf16[4,512,256]{2,1,0:T(8,128)(2,1)} %collective-permute-done.1.refs_1_), channel_id=1, source_target_pairs={{0,8},{8,0},{16,24},{24,16},{32,40},{40,32},{48,56},{56,48},{64,72... | collective-permute-start | bytes 3145736 | tf_op jit(solution)/shard_map/ppermute | solution.py:228
  109.3 7.5 %copy-start.10 = (s32[64]{0:T(128)S(1)}, s32[64]{0:T(128)}, u32[]{:S(2)}) copy-start(s32[64]{0:T(128)} %param.19) | copy-start | bytes 772
  111.3 13.6 %all-to-all-start.1 = ((bf16[4,16,32,128]{3,2,1,0:T(8,128)(2,1)}), bf16[4,16,32,128]{3,2,1,0:T(8,128)(2,1)S(1)}, u32[]{:S(2)}, u32[]{:S(2)}) async-start(bf16[4,16,32,128]{3,2,1,0:T(8,128)(2,1)} %bitcast.15), calls=%async_computation.1 | async-start | bytes 1048576 | tf_op jit(solution)/shard_map/all_to_all | solution.py:259
  116.9 20.0 %copy-start.1 = (s32[64,1]{0,1:T(1,128)S(1)}, s32[64,1]{0,1:T(1,128)}, u32[]{:S(2)}) copy-start(s32[64,1]{0,1:T(1,128)} %param.21) | copy-start | bytes 772
  116.9 20.0 %copy-start.2 = (bf16[64,1,64,1,256]{4,2,3,1,0:T(8,128)(2,1)S(1)}, bf16[64,1,64,1,256]{4,2,3,1,0:T(8,128)(2,1)}, u32[]{:S(2)}) copy-start(bf16[64,1,64,1,256]{4,2,3,1,0:T(8,128)(2,1)} %param.17) | copy-start | bytes 6291460
  132.4 17.8 %all-to-all-start.2 = ((bf16[4,17,32,128]{3,2,1,0:T(8,128)(2,1)}), bf16[4,17,32,128]{3,2,1,0:T(8,128)(2,1)S(1)}, u32[]{:S(2)}, u32[]{:S(2)}) async-start(bf16[4,17,32,128]{3,2,1,0:T(8,128)(2,1)} %prefix_attention.1), calls=%async_computation.2 | async-start | bytes 1114112 | tf_op jit(solution)/shard_map/all_to_all | solution.py:269
  147.5 1.0 copy-start.4
  148.5 1.0 copy-start.6
  150.3 1.2 copy-start.5
  151.5 1.2 copy-start.7

commit v2 on v1

v2 whole, which is shorter than its diff:
```python
import math

import jax
import jax.numpy as jnp
from jax import lax
from jax.experimental import pallas as pl
from jax.experimental.pallas import tpu as pltpu
from jax.sharding import PartitionSpec as P

BLOCK = 128
HD = 128
HEADS = 8
QW = HEADS * HD
PW = 2 * HD
COLS = QW + PW
ROWS = 128
ROPE_BASE = 1000000.0
NEG = -1e30
SCALE = HD ** -0.5
F32 = jnp.float32
BF16 = jnp.bfloat16
VMEM = 50 * 1024 * 1024


def tp_shift(dy, dx):
    return [(y * 4 + x, (y + dy) % 2 * 4 + (x + dx) % 4) for y in range(2) for x in range(4)]


def roll_shift(dy, dz, dc):
    return [
        ((y * 4 + z) * 2 + c, ((y + dy) % 2 * 4 + (z + dz) % 4) * 2 + (c + dc) % 2)
        for y in range(2)
        for z in range(4)
        for c in range(2)
    ]


def over_tp(a, dy, dx):
    return lax.ppermute(a, "tp", tp_shift(dy, dx))


def over_roll(a, dy, dz, dc):
    return lax.ppermute(a, "roll", roll_shift(dy, dz, dc))


def dot(a, b, dims=((1,), (0,))):
    return lax.dot_general(a, b, (dims, ((), ())), preferred_element_type=F32)


ANY = pl.BlockSpec(memory_space=pl.ANY)
IN_VMEM = pl.BlockSpec(memory_space=pltpu.VMEM)
IN_SMEM = pl.BlockSpec(memory_space=pltpu.SMEM)


def project(heads, xs, wq, wp, groups):
    count = sum(len(g) for g in groups)
    depth = wq.shape[0]

    def kernel(heads_ref, *refs):
        x_refs, (wq_ref, wp_ref), rest = refs[: len(xs)], refs[len(xs) : len(xs) + 2], refs[len(xs) + 2 :]
        outs, (q_buf, p_buf, q_sem, p_sem) = rest[:-4], rest[-4:]
        copies = []
        for d in range(count):
            k = heads_ref[d]
            copies.append(
                (
                    pltpu.make_async_copy(
                        wq_ref.at[:, pl.ds(pl.multiple_of(k * QW, QW), QW)], q_buf.at[d], q_sem.at[d]
                    ),
                    pltpu.make_async_copy(
                        wp_ref.at[:, pl.ds(pl.multiple_of(k * PW, PW), PW)], p_buf.at[d], p_sem.at[d]
                    ),
                )
            )
        for pair in copies:
            for c in pair:
                c.start()
        x = jnp.concatenate([r[...] for r in x_refs], 0) if len(xs) > 1 else x_refs[0][...]
        d = 0
        for g, group in enumerate(groups):
            for i in range(len(group)):
                for c in copies[d]:
                    c.wait()
                for buf, low, high in ((q_buf, 0, QW), (p_buf, QW, COLS)):
                    y = dot(x, buf[d]).astype(BF16)
                    for b in range(len(xs)):
                        outs[b * len(groups) + g][i, :, low:high] = y[b * ROWS : (b + 1) * ROWS]
                d += 1

    return pl.pallas_call(
        kernel,
        in_specs=[IN_SMEM] + [IN_VMEM] * len(xs) + [ANY, ANY],
        out_specs=[IN_VMEM] * (len(xs) * len(groups)),
        out_shape=[jax.ShapeDtypeStruct((len(g), ROWS, COLS), BF16) for _ in xs for g in groups],
        scratch_shapes=[
            pltpu.VMEM((count, depth, QW), BF16),
            pltpu.VMEM((count, depth, PW), BF16),
            pltpu.SemaphoreType.DMA((count,)),
            pltpu.SemaphoreType.DMA((count,)),
        ],
        compiler_params=pltpu.CompilerParams(vmem_limit_bytes=VMEM),
        cost_estimate=pl.CostEstimate(
            flops=2 * len(xs) * ROWS * depth * count * COLS,
            bytes_accessed=2 * depth * count * COLS,
            transcendentals=0,
        ),
        name="project",
    )(heads, *xs, wq, wp)


def attend(limits, lengths, q, new, cache, kvs):
    flat = [a for group in kvs for a in group]

    def kernel(limit_ref, length_ref, q_ref, new_ref, cache_ref, *refs):
        kv_refs = refs[: len(flat)]
        o_ref, buf, cbuf, sem, csem = refs[len(flat) :]
        copies, at = [], 0
        for g, group in enumerate(kvs):
            mine, slot = [], 4 * g
            for a in group:
                n = a.shape[0]
                mine.append(pltpu.make_async_copy(kv_refs[at], buf.at[pl.ds(slot, n)], sem.at[at]))
                slot, at = slot + n, at + 1
            mine.append(
                pltpu.make_async_copy(cache_ref.at[pl.ds(4 * g, 4)], cbuf.at[pl.ds(4 * g, 4)], csem.at[g])
            )
            copies.append(mine)
        for mine in copies:
            for c in mine:
                c.start()
        for g in range(8):
            for c in copies[g]:
                c.wait()
            q = q_ref[4 * g : 4 * g + 4].reshape(128, HD)
            sp = []
            for i in range(4):
                p = 4 * g + i
                s = dot(q[32 * i : 32 * i + 32], buf[p, :, :HD], ((1,), (1,))) * SCALE
                col = lax.broadcasted_iota(jnp.int32, s.shape, 1)
                sp.append(jnp.where(col < limit_ref[p], s, NEG))
            sp = jnp.concatenate(sp, 0)
            sc = dot(q, cbuf[4 * g : 4 * g + 4, :, :HD].reshape(256, HD), ((1,), (1,))) * SCALE
            row = lax.broadcasted_iota(jnp.int32, sc.shape, 0)
            col = lax.broadcasted_iota(jnp.int32, sc.shape, 1)
            length = jnp.zeros(sc.shape, jnp.int32)
            for i in range(4):
                length = jnp.where(row // 32 == i, length_ref[4 * g + i], length)
            sc = jnp.where((row // 32 == col // 64) & (col % 64 < length), sc, NEG)
            new = new_ref[16 * g : 16 * g + 16]
            sn = dot(q, new[:, :HD], ((1,), (1,))) * SCALE
            row = lax.broadcasted_iota(jnp.int32, sn.shape, 0)
            col = lax.broadcasted_iota(jnp.int32, sn.shape, 1)
            sn = jnp.where((row // 32 == col // 4) & (col % 4 <= row % 4), sn, NEG)
            top = jnp.maximum(
                jnp.maximum(jnp.max(sp, -1, keepdims=True), jnp.max(sc, -1, keepdims=True)),
                jnp.max(sn, -1, keepdims=True),
            )
            wp, wc, wn = jnp.exp(sp - top), jnp.exp(sc - top), jnp.exp(sn - top)
            total = (
                jnp.sum(wp, -1, keepdims=True)
                + jnp.sum(wc, -1, keepdims=True)
                + jnp.sum(wn, -1, keepdims=True)
            )
            wp = wp.astype(BF16)
            o = jnp.concatenate(
                [dot(wp[32 * i : 32 * i + 32], buf[4 * g + i, :, HD:]) for i in range(4)], 0
            )
            o = o + dot(wc.astype(BF16), cbuf[4 * g : 4 * g + 4, :, HD:].reshape(256, HD))
            o = o + dot(wn.astype(BF16), new[:, HD:])
            o = o / total
            for i in range(4):
                o_ref[4 * g + i] = jnp.concatenate(
                    [o[32 * i + 4 * h : 32 * i + 4 * h + 4] for h in range(HEADS)], 1
                ).astype(BF16)

    return pl.pallas_call(
        kernel,
        in_specs=[IN_SMEM, IN_SMEM, IN_VMEM, IN_VMEM, ANY] + [ANY] * len(flat),
        out_specs=IN_VMEM,
        out_shape=jax.ShapeDtypeStruct((32, 4, QW), BF16),
        scratch_shapes=[
            pltpu.VMEM((32, 512, 2 * HD), BF16),
            pltpu.VMEM((32, 64, 2 * HD), BF16),
            pltpu.SemaphoreType.DMA((len(flat),)),
            pltpu.SemaphoreType.DMA((8,)),
        ],
        compiler_params=pltpu.CompilerParams(vmem_limit_bytes=VMEM),
        cost_estimate=pl.CostEstimate(
            flops=32 * 32 * 600 * 512, bytes_accessed=10 * 2**20, transcendentals=32 * 32 * 600
        ),
        name="attend",
    )(limits, lengths, q, new, cache, *flat)


def rotate(values, cosine, sine):
    half = values.shape[-1] // 2
    lead, trail = values[..., :half], values[..., half:]
    return jnp.concatenate([lead * cosine - trail * sine, trail * cosine + lead * sine], -1)


def finish(own, from_left, from_right):
    total = own.astype(F32) + from_left.astype(F32) + from_right.astype(F32)
    return total[0], total[1].astype(BF16)


def on_device(
    tokens,
    query_weight,
    query_bias,
    pair_weight,
    pair_bias,
    cache_pairs,
    prefix_pairs,
    owner_slot,
    prefix_blocks,
    positions,
):
    prompts, _, new, width = tokens.shape
    me = lax.axis_index("roll")
    my_y, my_z, my_c = me // 8, me // 2 % 4, me % 2
    tp = lax.axis_index("tp")
    tp_y, tp_x = tp // 4, tp % 4

    index = jnp.arange(prompts, dtype=jnp.int32)
    steps = jnp.array([0, 3, 1, 2], jnp.int32)
    half = jnp.arange(2, dtype=jnp.int32)
    y_of = (1 - half + my_y) % 2
    c_of = (half + my_c) % 2
    z_of = (steps + my_z) % 4
    slot = (
        ((y_of[:, None, None, None] * 4 + z_of[None, None, :, None]) * 2 + c_of[None, :, None, None]) * 4
        + jnp.arange(4, dtype=jnp.int32)[None, None, None, :]
    ).reshape(prompts)
    order = jnp.sum(jnp.where(owner_slot[None, :] == slot[:, None], index[None, :], 0), 1)
    inverse = jnp.sum(jnp.where(slot[None, :] == owner_slot[:, None], index[None, :], 0), 1)
    pos = positions.reshape(prompts)

    x = jnp.take(tokens.reshape(prompts, new * width), order, axis=0)
    pos_sorted = jnp.take(pos, order)
    blocks = jnp.take(prefix_blocks, order[32:])
    head_row = jnp.zeros((16, width), BF16).at[0, :32].set(pos_sorted[:32].astype(BF16))
    swapped = over_roll(
        jnp.concatenate([x[:32].reshape(ROWS, width), head_row], 0), 1, 0, 0
    )
    x_t, pos_t = swapped[:ROWS], swapped[ROWS, :32].astype(jnp.int32)
    x_g, pos_g = x[32:].reshape(ROWS, width), pos_sorted[32:]
    cache = cache_pairs.reshape(prompts, 64, 2 * HD)
    cache_t = over_roll(jnp.take(cache, order[:32], axis=0), 1, 0, 0)
    cache_g = jnp.take(cache, order[32:], axis=0)

    def heads(*pairs):
        return jnp.stack([(tp_y + dy) % 2 * 4 + (tp_x + dx) % 4 for dy, dx in pairs]).astype(jnp.int32)

    far = heads((0, 2), (1, 2))
    up_g, down_g = project(far, [x_g], query_weight, pair_weight, [[0], [1]])
    up_t, down_t = project(far, [x_t], query_weight, pair_weight, [[0], [1]])
    right_t, left_t, right_g, left_g = project(
        heads((0, 1), (1, 1), (0, 3), (1, 3)), [x_t, x_g], query_weight, pair_weight, [[0, 1], [2, 3]]
    )
    own_t, own_g = project(heads((0, 0), (1, 0)), [x_t, x_g], query_weight, pair_weight, [[0, 1]])

    def reduce(up, down, right, left, own):
        up, down = over_tp(up, 0, 1), over_tp(down, 0, 3)
        right = right.at[0].add(up[0])
        left = left.at[1].add(down[0])
        keep, send = finish(own, over_tp(right, 0, 1), over_tp(left, 0, 3))
        return keep + over_tp(send, 1, 0).astype(F32)

    full_t = reduce(up_t, down_t, right_t, left_t, own_t)
    full_g = reduce(up_g, down_g, right_g, left_g, own_g)

    own = prefix_pairs.reshape(4, 512, 2 * HD)
    below, above = over_roll(own, 0, 1, 0), over_roll(own, 0, 3, 0)
    far_a, far_b = over_roll(below[:2], 0, 1, 0), over_roll(above[2:], 0, 3, 0)
    kvs = [[own], [below], [above], [far_a, far_b]]
    kvs = kvs + [[over_roll(a, 0, 0, 1) for a in group] for group in kvs]

    frequency = jnp.exp(jnp.arange(HD // 2, dtype=F32) * (-2.0 * math.log(ROPE_BASE) / HD))
    limits = BLOCK * blocks

    def rows(full, where, cache):
        at = (limits[:, None] + where[:, None] + jnp.arange(new, dtype=jnp.int32)).reshape(ROWS)
        angles = at.astype(F32)[:, None] * frequency[None, :]
        cosine, sine = jnp.cos(angles), jnp.sin(angles)
        q = (full[:, :QW] + query_bias.astype(F32)).reshape(ROWS, HEADS, HD)
        q = rotate(q, cosine[:, None], sine[:, None]).astype(BF16)
        q = q.reshape(32, new, HEADS, HD).transpose(0, 2, 1, 3).reshape(32, 32, HD)
        pair = full[:, QW:] + pair_bias.astype(F32)
        pair = jnp.concatenate([rotate(pair[:, :HD], cosine, sine), pair[:, HD:]], -1).astype(BF16)
        return attend(limits, where, q, pair, cache, kvs), pair.reshape(32, new, PW)

    done_t, pair_t = rows(full_t, pos_t, cache_t)
    back = over_roll(jnp.concatenate([done_t, pair_t], -1), 1, 0, 0)
    done_g, pair_g = rows(full_g, pos_g, cache_g)

    attended = jnp.take(jnp.concatenate([back[..., :QW], done_g], 0), inverse, axis=0)
    new_pairs = jnp.take(jnp.concatenate([back[..., QW:], pair_g], 0), inverse, axis=0)
    return (
        attended.reshape(prompts, 1, new, QW),
        new_pairs.reshape(prompts, 1, new, 1, PW),
    )


def solution(mesh):
    return jax.shard_map(
        on_device,
        mesh=mesh,
        in_specs=(
            P(None, "roll", None, "tp"),
            P("tp", None),
            P("tp"),
            P("tp", None),
            P("tp"),
            P(None, "roll", None, "tp", None),
            P("roll", None, "tp", None),
            P(),
            P(),
            P(None, "roll"),
        ),
        out_specs=(P(None, "roll", None, "tp"), P(None, "roll", None, "tp", None)),
        check_vma=False,
    )
```

time: 159 us -> 155 us (0.975)
  waiting for transfers between devices: 78.3 us -> 44.5 us
  other arithmetic: 9.72 us -> 22.7 us
  starting transfers between devices: 19.4 us -> 29.4 us
  local copies, waits for them, and re-layouts: 13.3 us -> 22.6 us
  Pallas kernels: 36.3 us -> 32.9 us
    all_to_all x3 -> x0, waiting for transfers between devices: 64.8 us -> none  [the longest x1 56.9 us: on_device(): lax.all_to_all(part.reshape(4, 2 * rows, cols), 'tp', 0, 0, tiled=True, a...]
    ppermute x4 -> x22, waiting for transfers between devices: 13.5 us -> 44.5 us  [the longest x10 43.3 us: over_tp(): return lax.ppermute(a, 'tp', tp_shift(dy, dx))]
    ppermute x4 -> x22, starting transfers between devices: 5.35 us -> 29.4 us  [the longest x10 16 us: over_tp(): return lax.ppermute(a, 'tp', tp_shift(dy, dx))]
    all_to_all x3 -> x0, starting transfers between devices: 14 us -> none  [the longest x1 5.49 us: on_device(): lax.all_to_all(q.reshape(4, 16, 32, HD), 'roll', 0, 0, tiled=True, axis_i...]
    select_n x4 -> x7, other arithmetic: 0.93 us -> 6.2 us  [the longest x1 2.38 us: on_device(): cache_g = jnp.take(cache, order[32:], axis=0)]
    slice x1 -> x8, local copies, waits for them, and re-layouts: 0.01 us -> 5.08 us  [the longest x1 1.08 us: on_device(): below[:2]]
    scatter-add x0 -> x4, other arithmetic: none -> 3.54 us  [the longest x2 2.3 us: reduce(): right = right.at[0].add(up[0])]
    pallas_call x4 -> x6, Pallas kernels: 36.3 us -> 32.9 us  [the longest x4 17.9 us: project(): pl.pallas_call(kernel, in_specs=[IN_SMEM] + [IN_VMEM] * len(xs) + [ANY, A...]
  transfers between devices with their start and end apart: 7 -> 22, of which waited for: 3 -> 9; matrix products, arithmetic and copies ran while one was open for 7% -> 22% of each run, Pallas kernels for 7% -> 17%
where the time goes in v2:
time: 155 us; the launch traced here: 153 us
  waiting for transfers between devices  44.5 us (29%)
  Pallas kernels  32.9 us (21%)
  starting transfers between devices  29.4 us (19%)
  other arithmetic  22.7 us (15%)
  local copies, waits for them, and re-layouts  22.6 us (15%)
    ppermute x10, waiting for transfers between devices, over_tp(): return lax.ppermute(a, 'tp', tp_shift(dy, dx))  43.3 us
    pallas_call x4, Pallas kernels, project(): pl.pallas_call(kernel, in_specs=[IN_SMEM] + [IN_VMEM] * len(xs) + [ANY, A...  17.9 us
    ppermute x10, starting transfers between devices, over_tp(): return lax.ppermute(a, 'tp', tp_shift(dy, dx))  16 us
    pallas_call x2, Pallas kernels, attend(): pl.pallas_call(kernel, in_specs=[IN_SMEM, IN_SMEM, IN_VMEM, IN_VMEM, ANY]...  15 us
    ppermute x12, starting transfers between devices, over_roll(): return lax.ppermute(a, 'roll', roll_shift(dy, dz, dc))  13.5 us
    unnamed x55, local copies, waits for them, and re-layouts  5.71 us
    another operation x4, other arithmetic  3.52 us
  transfers between devices with their start and end apart: 22, of which 9 were waited for; matrix products, arithmetic and copies ran while one was open for 22% of the time, Pallas kernels for 17%

profile of v2, /device:TPU:0, one launch (start us, length us, event | category | flops | bytes accessed | tf_op | source)
XLA Modules:
  0.0 153.2 jit_solution(5401759822587475622)
XLA Ops:
  0.6 2.1 %collective-permute-start.7 = (bf16[4,512,256]{2,1,0:T(8,128)(2,1)}, bf16[4,512,256]{2,1,0:T(8,128)(2,1)}, u32[]{:S(2)}, u32[]{:S(2)}) collective-permute-start(bf16[4,512,256]{2,1,0:T(8,128)(2,1)} %bitcast.85), channel_id=1, source_target_pairs={{0,16},{8,24},{16,32},{24,40},{32,48},{40,56},{48,0},{56,8},{64,80... | collective-permute-start | bytes 3145736 | tf_op jit(solution)/shard_map/ppermute | solution.py:43
  2.7 2.2 %collective-permute-start.8 = (bf16[4,512,256]{2,1,0:T(8,128)(2,1)}, bf16[4,512,256]{2,1,0:T(8,128)(2,1)}, u32[]{:S(2)}, u32[]{:S(2)}) collective-permute-start(bf16[4,512,256]{2,1,0:T(8,128)(2,1)} %bitcast.86), channel_id=1, source_target_pairs={{0,48},{8,56},{16,0},{24,8},{32,16},{40,24},{48,32},{56,40},{64,11... | collective-permute-start | bytes 3145736 | tf_op jit(solution)/shard_map/ppermute | solution.py:43
  5.9 1.4 select_reduce_fusion.1
  7.4 1.2 copy.31
  8.6 0.9 gather_fusion.1
  11.2 3.6 %project.7 = (bf16[1,128,1280]{2,1,0:T(8,128)(2,1)S(1)}, bf16[1,128,1280]{2,1,0:T(8,128)(2,1)S(1)}) custom-call(s32[2]{0:T(128)S(1)} %get-tuple-element.129.heads_ref, bf16[128,1024]{1,0:T(8,128)(2,1)S(1)} %reshape.515.refs_1_.refs_0_, bf16[1024,8192]{1,0:T(8,128)(2,1)} %refs_1_.3, bf16[1024,2048]{1,0:T(8,128)(2,1)} %refs_2_.7), custom_call_target="tpu_custom_call" | custom-call | flops 671088640 | bytes 5242880 | tf_op jit(solution)/shard_map/project/pallas_call | solution.py:90
  14.9 1.6 %collective-permute-start.17 = (bf16[1,128,1280]{2,1,0:T(8,128)(2,1)S(1)}, bf16[1,128,1280]{2,1,0:T(8,128)(2,1)}, u32[]{:S(2)}, u32[]{:S(2)}) collective-permute-start(bf16[1,128,1280]{2,1,0:T(8,128)(2,1)S(1)} %get-tuple-element.80), channel_id=1, source_target_pairs={{0,1},{1,2},{2,3},{3,0},{4,5},{5,6},{6,7},{7,4},{8,9},{9,10},{10,1... | collective-permute-start | bytes 983048 | tf_op jit(solution)/shard_map/ppermute | solution.py:39
  18.0 3.2 %collective-permute-start = (bf16[144,1024]{1,0:T(8,128)(2,1)}, bf16[144,1024]{1,0:T(8,128)(2,1)}, u32[]{:S(2)}, u32[]{:S(2)}) collective-permute-start(bf16[144,1024]{1,0:T(8,128)(2,1)} %fusion.8), channel_id=1, source_target_pairs={{0,64},{8,72},{16,80},{24,88},{32,96},{40,104},{48,112},{56,120},{... | collective-permute-start | bytes 884744 | tf_op jit(solution)/shard_map/ppermute | solution.py:43
  21.2 1.7 %collective-permute-start.19 = (bf16[1,128,1280]{2,1,0:T(8,128)(2,1)S(1)}, bf16[1,128,1280]{2,1,0:T(8,128)(2,1)}, u32[]{:S(2)}, u32[]{:S(2)}) collective-permute-start(bf16[1,128,1280]{2,1,0:T(8,128)(2,1)S(1)} %get-tuple-element.82), channel_id=1, source_target_pairs={{0,3},{1,0},{2,1},{3,2},{4,7},{5,4},{6,5},{7,6},{8,11},{9,8},{10,9... | collective-permute-start | bytes 983048 | tf_op jit(solution)/shard_map/ppermute | solution.py:39
  24.9 1.6 %gather_fusion.5 = bf16[32,64,256]{2,1,0:T(8,128)(2,1)} fusion(bf16[64,64,256]{2,1,0:T(8,128)(2,1)S(1)} %bitcast.77, s32[1024]{0:T(1024)S(1)} %pad_clamp_fusion.1), kind=kCustom, calls=%fused_computation.clone | custom fusion | bytes 2097280 | tf_op jit(solution)/shard_map/jit(_take)/gather | solution.py:248
  26.5 2.4 %broadcast_select_fusion.1 = bf16[32,64,256]{2,1,0:T(8,128)(2,1)} fusion(bf16[32,64,256]{2,1,0:T(8,128)(2,1)} %gather_fusion.5, pred[32]{0:T(512)(128)(4,1)S(1)} %get-tuple-element.91), kind=kLoop, calls=%fused_computation.10 | loop fusion | flops 524288 | bytes 2097184 | tf_op jit(solution)/shard_map/jit(_take)/select_n | solution.py:248
  29.0 1.6 %gather_fusion.6 = bf16[32,64,256]{2,1,0:T(8,128)(2,1)} fusion(bf16[64,64,256]{2,1,0:T(8,128)(2,1)S(1)} %bitcast.78, s32[1024]{0:T(1024)S(1)} %pad_clamp_fusion.3), kind=kCustom, calls=%fused_computation.1.clone | custom fusion | bytes 2097280 | tf_op jit(solution)/shard_map/jit(_take)/gather | solution.py:249
  31.3 2.4 %broadcast_select_fusion.cache_ref = bf16[32,64,256]{2,1,0:T(8,128)(2,1)} fusion(bf16[32,64,256]{2,1,0:T(8,128)(2,1)} %gather_fusion.6, pred[32]{0:T(512)(128)(4,1)S(1)} %get-tuple-element.118), kind=kLoop, calls=%fused_computation.9 | loop fusion | flops 524288 | bytes 2097184 | tf_op jit(solution)/shard_map/jit(_take)/select_n | solution.py:249
  33.7 1.0 slice.254.refs_0_
  34.6 3.8 %project.6 = (bf16[1,128,1280]{2,1,0:T(8,128)(2,1)}, bf16[1,128,1280]{2,1,0:T(8,128)(2,1)S(1)}) custom-call(s32[2]{0:T(128)S(1)} %get-tuple-element.129.heads_ref, bf16[128,1024]{1,0:T(8,128)(2,1)S(1)} %slice.254.refs_0_, bf16[1024,8192]{1,0:T(8,128)(2,1)} %refs_1_.3, bf16[1024,2048]{1,0:T(8,128)(2,1)} %refs_2_.7), custom_call_target="tpu_custom_call" | custom-call | flops 671088640 | bytes 5242880 | tf_op jit(solution)/shard_map/project/pallas_call | solution.py:90
  42.3 4.2 %project.4 = (bf16[2,128,1280]{2,1,0:T(8,128)(2,1)S(1)}, bf16[2,128,1280]{2,1,0:T(8,128)(2,1)S(1)}) custom-call(s32[2]{0:T(128)S(1)} %get-tuple-element.128.heads_ref, bf16[128,1024]{1,0:T(8,128)(2,1)S(1)} %slice.254.refs_0_, bf16[128,1024]{1,0:T(8,128)(2,1)S(1)} %reshape.515.refs_1_.refs_0_, bf16[1024,8192]{1,0:T(8,128)(2,1)} %refs_1_.3, ...), custom_call_target="tpu_custom_call" | custom-call | flops 1342177280 | bytes 5242880 | tf_op jit(solution)/shard_map/project/pallas_call | solution.py:90
  46.5 6.2 %project.5 = (bf16[2,128,1280]{2,1,0:T(8,128)(2,1)S(1)}, bf16[2,128,1280]{2,1,0:T(8,128)(2,1)S(1)}, bf16[2,128,1280]{2,1,0:T(8,128)(2,1)S(1)}, bf16[2,128,1280]{2,1,0:T(8,128)(2,1)S(1)}) custom-call(s32[4]{0:T(128)S(1)} %pad_add_fusion.1.heads_ref, bf16[128,1024]{1,0:T(8,128)(2,1)S(1)} %slice.254.refs_0_, bf16[128,1024]{1,0:T(8,128)(2,1)S(1)} %reshape.515.refs_1_.refs_0_, ...), custom_call_target="tpu_custom_call" | custom-call | flops 2684354560 | bytes 10485760 | tf_op jit(solution)/shard_map/project/pallas_call | solution.py:90
  52.8 3.0 %collective-permute-start.3 = (bf16[1,128,1280]{2,1,0:T(8,128)(2,1)S(1)}, bf16[1,128,1280]{2,1,0:T(8,128)(2,1)S(1)}, u32[]{:S(2)}, u32[]{:S(2)}) collective-permute-start(bf16[1,128,1280]{2,1,0:T(8,128)(2,1)S(1)} %copy-done.7), channel_id=1, source_target_pairs={{0,3},{1,0},{2,1},{3,2},{4,7},{5,4},{6,5},{7,6},{8,11},{9,8},{10,9... | collective-permute-start | bytes 983048 | tf_op jit(solution)/shard_map/ppermute | solution.py:39
  55.8 1.2 add_dynamic-update-slice_fusion.1
  57.1 1.1 add_dynamic-update-slice_fusion
  58.2 3.5 %collective-permute-start.20 = (bf16[2,128,1280]{2,1,0:T(8,128)(2,1)S(1)}, bf16[2,128,1280]{2,1,0:T(8,128)(2,1)S(1)}, u32[]{:S(2)}, u32[]{:S(2)}) collective-permute-start(bf16[2,128,1280]{2,1,0:T(8,128)(2,1)S(1)} %add_dynamic-update-slice_fusion), channel_id=1, source_target_pairs={{0,3},{1,0},{2,1},{3,2},{4,7},{5,4},{6,5},{7,6},{8,11},{9,8},{10,9... | collective-permute-start | bytes 1966088 | tf_op jit(solution)/shard_map/ppermute | solution.py:39
  61.7 1.1 add_dynamic-update-slice_fusion.3
  63.2 9.9 %collective-permute-done.18 = bf16[2,128,1280]{2,1,0:T(8,128)(2,1)S(1)} collective-permute-done((bf16[2,128,1280]{2,1,0:T(8,128)(2,1)S(1)}, bf16[2,128,1280]{2,1,0:T(8,128)(2,1)S(1)}, u32[]{:S(2)}, u32[]{:S(2)}) %collective-permute-start.18) | collective-permute-done | bytes 655392 | tf_op jit(solution)/shard_map/ppermute | solution.py:39
  73.1 2.3 %collective-permute-done.20 = bf16[2,128,1280]{2,1,0:T(8,128)(2,1)S(1)} collective-permute-done((bf16[2,128,1280]{2,1,0:T(8,128)(2,1)S(1)}, bf16[2,128,1280]{2,1,0:T(8,128)(2,1)S(1)}, u32[]{:S(2)}, u32[]{:S(2)}) %collective-permute-start.20) | collective-permute-done | bytes 655392 | tf_op jit(solution)/shard_map/ppermute | solution.py:39
  75.4 3.7 %collective-permute-start.4 = (bf16[2,128,1280]{2,1,0:T(8,128)(2,1)S(1)}, bf16[2,128,1280]{2,1,0:T(8,128)(2,1)S(1)}, u32[]{:S(2)}, u32[]{:S(2)}) collective-permute-start(bf16[2,128,1280]{2,1,0:T(8,128)(2,1)S(1)} %add_dynamic-update-slice_fusion.2), channel_id=1, source_target_pairs={{0,3},{1,0},{2,1},{3,2},{4,7},{5,4},{6,5},{7,6},{8,11},{9,8},{10,9... | collective-permute-start | bytes 1966088 | tf_op jit(solution)/shard_map/ppermute | solution.py:39
  79.4 1.0 copy-done.14
  80.7 1.1 slice.265
  81.8 1.7 %collective-permute-start.21 = (bf16[128,1280]{1,0:T(8,128)(2,1)S(1)}, bf16[128,1280]{1,0:T(8,128)(2,1)S(1)}, u32[]{:S(2)}, u32[]{:S(2)}) collective-permute-start(bf16[128,1280]{1,0:T(8,128)(2,1)S(1)} %fusion.7), channel_id=1, source_target_pairs={{0,4},{1,5},{2,6},{3,7},{4,0},{5,1},{6,2},{7,3},{8,12},{9,13},{10,... | collective-permute-start | bytes 983048 | tf_op jit(solution)/shard_map/ppermute | solution.py:39
  83.4 1.1 slice.266
  84.5 3.7 %collective-permute-done.2 = bf16[2,128,1280]{2,1,0:T(8,128)(2,1)S(1)} collective-permute-done((bf16[2,128,1280]{2,1,0:T(8,128)(2,1)S(1)}, bf16[2,128,1280]{2,1,0:T(8,128)(2,1)S(1)}, u32[]{:S(2)}, u32[]{:S(2)}) %collective-permute-start.2) | collective-permute-done | bytes 655392 | tf_op jit(solution)/shard_map/ppermute | solution.py:39
  88.2 3.6 %collective-permute-done.4 = bf16[2,128,1280]{2,1,0:T(8,128)(2,1)S(1)} collective-permute-done((bf16[2,128,1280]{2,1,0:T(8,128)(2,1)S(1)}, bf16[2,128,1280]{2,1,0:T(8,128)(2,1)S(1)}, u32[]{:S(2)}, u32[]{:S(2)}) %collective-permute-start.4) | collective-permute-done | bytes 655392 | tf_op jit(solution)/shard_map/ppermute | solution.py:39
  91.8 1.6 %collective-permute-start.10 = (bf16[2,512,256]{2,1,0:T(8,128)(2,1)S(1)}, bf16[2,512,256]{2,1,0:T(8,128)(2,1)S(1)}, u32[]{:S(2)}, u32[]{:S(2)}) collective-permute-start(bf16[2,512,256]{2,1,0:T(8,128)(2,1)S(1)} %slice.266), channel_id=1, source_target_pairs={{0,48},{8,56},{16,0},{24,8},{32,16},{40,24},{48,32},{56,40},{64,11... | collective-permute-start | bytes 1572872 | tf_op jit(solution)/shard_map/ppermute | solution.py:43
  93.6 17.0 %collective-permute-done.21 = bf16[128,1280]{1,0:T(8,128)(2,1)S(1)} collective-permute-done((bf16[128,1280]{1,0:T(8,128)(2,1)S(1)}, bf16[128,1280]{1,0:T(8,128)(2,1)S(1)}, u32[]{:S(2)}, u32[]{:S(2)}) %collective-permute-start.21) | collective-permute-done | bytes 327712 | tf_op jit(solution)/shard_map/ppermute | solution.py:39
  111.1 6.6 %collective-permute-done.5 = bf16[128,1280]{1,0:T(8,128)(2,1)S(1)} collective-permute-done((bf16[128,1280]{1,0:T(8,128)(2,1)S(1)}, bf16[128,1280]{1,0:T(8,128)(2,1)S(1)}, u32[]{:S(2)}, u32[]{:S(2)}) %collective-permute-start.5) | collective-permute-done | bytes 327712 | tf_op jit(solution)/shard_map/ppermute | solution.py:39
  119.1 1.2 subtract_convert_fusion.3
  121.0 0.9 copy.33
  122.4 1.0 collective-permute-done.15.refs_9_
  123.5 0.8 copy-done.12
  124.7 7.5 %attend.2 = bf16[32,4,1024]{2,1,0:T(4,128)(2,1)S(1)} custom-call(s32[32]{0:T(128)S(1)} %get-tuple-element.94.limit_ref, s32[32]{0:T(128)S(1)} %fusion.16.length_ref, bf16[32,32,128]{2,1,0:T(8,128)(2,1)S(1)} %bitcast.79, bf16[128,256]{1,0:T(8,128)(2,1)S(1)} %pad_maximum_fusion.3.new_ref, bf16[32,64,256]{2,1,0:T(8,128)(2,1)S(1)} %collective-permute-done.6.cache_ref, ...), custom_call_target="tpu_custom_call" | custom-call | flops 314572800 | bytes 10485760 | tf_op jit(solution)/shard_map/attend/pallas_call | solution.py:176
  132.2 1.7 %concatenate.75 = bf16[32,4,1280]{2,1,0:T(4,128)(2,1)} concatenate(bf16[32,4,1024]{2,1,0:T(4,128)(2,1)S(1)} %attend.2, bf16[32,4,64]{2,1,0:T(4,128)(2,1)} %bitcast.98, bf16[32,4,64]{2,1,0:T(4,128)(2,1)} %bitcast.99, bf16[32,4,128]{2,1,0:T(4,128)(2,1)} %bitcast.100), dimensions={2} | concatenate | bytes 655360 | tf_op jit(solution)/shard_map/concatenate | solution.py:293
  133.9 2.9 %collective-permute-start.16 = (bf16[32,4,1280]{2,1,0:T(4,128)(2,1)}, bf16[32,4,1280]{2,1,0:T(4,128)(2,1)}, u32[]{:S(2)}, u32[]{:S(2)}) collective-permute-start(bf16[32,4,1280]{2,1,0:T(4,128)(2,1)} %concatenate.75), channel_id=1, source_target_pairs={{0,64},{8,72},{16,80},{24,88},{32,96},{40,104},{48,112},{56,120},{... | collective-permute-start | bytes 983048 | tf_op jit(solution)/shard_map/ppermute | solution.py:43
  136.8 1.5 subtract_convert_fusion
  139.7 7.5 %attend.3 = bf16[32,4,1024]{2,1,0:T(4,128)(2,1)S(1)} custom-call(s32[32]{0:T(128)S(1)} %get-tuple-element.94.limit_ref, s32[32]{0:T(128)S(1)} %get-tuple-element.125.length_ref, bf16[32,32,128]{2,1,0:T(8,128)(2,1)S(1)} %bitcast.80, bf16[128,256]{1,0:T(8,128)(2,1)S(1)} %pad_maximum_fusion.4.new_ref, bf16[32,64,256]{2,1,0:T(8,128)(2,1)S(1)} %copy-done.1, ...), custom_call_target="tpu_custom_call" | custom-call | flops 314572800 | bytes 10485760 | tf_op jit(solution)/shard_map/attend/pallas_call | solution.py:176
  147.2 0.9 slice.277
  148.9 1.0 slice.267
  150.3 1.0 gather_fusion.3
  151.3 0.8 fusion.9
  152.1 1.1 fusion.5
  (135 shorter events, 18.2 us)
Async XLA Ops:
  0.6 24.3 %copy-start = (bf16[64,1,64,1,256]{4,2,3,1,0:T(8,128)(2,1)S(1)}, bf16[64,1,64,1,256]{4,2,3,1,0:T(8,128)(2,1)}, u32[]{:S(2)}) copy-start(bf16[64,1,64,1,256]{4,2,3,1,0:T(8,128)(2,1)} %param.28) | copy-start | bytes 6291460
  0.6 78.8 %collective-permute-start.7 = (bf16[4,512,256]{2,1,0:T(8,128)(2,1)}, bf16[4,512,256]{2,1,0:T(8,128)(2,1)}, u32[]{:S(2)}, u32[]{:S(2)}) collective-permute-start(bf16[4,512,256]{2,1,0:T(8,128)(2,1)} %bitcast.85), channel_id=1, source_target_pairs={{0,16},{8,24},{16,32},{24,40},{32,48},{40,56},{48,0},{56,8},{64,80... | collective-permute-start | bytes 3145736 | tf_op jit(solution)/shard_map/ppermute | solution.py:43
  2.7 79.1 %collective-permute-start.8 = (bf16[4,512,256]{2,1,0:T(8,128)(2,1)}, bf16[4,512,256]{2,1,0:T(8,128)(2,1)}, u32[]{:S(2)}, u32[]{:S(2)}) collective-permute-start(bf16[4,512,256]{2,1,0:T(8,128)(2,1)} %bitcast.86), channel_id=1, source_target_pairs={{0,48},{8,56},{16,0},{24,8},{32,16},{40,24},{48,32},{56,40},{64,11... | collective-permute-start | bytes 3145736 | tf_op jit(solution)/shard_map/ppermute | solution.py:43
  8.6 0.9 copy-start.8
  14.9 37.9 %collective-permute-start.17 = (bf16[1,128,1280]{2,1,0:T(8,128)(2,1)S(1)}, bf16[1,128,1280]{2,1,0:T(8,128)(2,1)}, u32[]{:S(2)}, u32[]{:S(2)}) collective-permute-start(bf16[1,128,1280]{2,1,0:T(8,128)(2,1)S(1)} %get-tuple-element.80), channel_id=1, source_target_pairs={{0,1},{1,2},{2,3},{3,0},{4,5},{5,6},{6,7},{7,4},{8,9},{9,10},{10,1... | collective-permute-start | bytes 983048 | tf_op jit(solution)/shard_map/ppermute | solution.py:39
  18.0 15.7 %collective-permute-start = (bf16[144,1024]{1,0:T(8,128)(2,1)}, bf16[144,1024]{1,0:T(8,128)(2,1)}, u32[]{:S(2)}, u32[]{:S(2)}) collective-permute-start(bf16[144,1024]{1,0:T(8,128)(2,1)} %fusion.8), channel_id=1, source_target_pairs={{0,64},{8,72},{16,80},{24,88},{32,96},{40,104},{48,112},{56,120},{... | collective-permute-start | bytes 884744 | tf_op jit(solution)/shard_map/ppermute | solution.py:43
  21.2 35.9 %collective-permute-start.19 = (bf16[1,128,1280]{2,1,0:T(8,128)(2,1)S(1)}, bf16[1,128,1280]{2,1,0:T(8,128)(2,1)}, u32[]{:S(2)}, u32[]{:S(2)}) collective-permute-start(bf16[1,128,1280]{2,1,0:T(8,128)(2,1)S(1)} %get-tuple-element.82), channel_id=1, source_target_pairs={{0,3},{1,0},{2,1},{3,2},{4,7},{5,4},{6,5},{7,6},{8,11},{9,8},{10,9... | collective-permute-start | bytes 983048 | tf_op jit(solution)/shard_map/ppermute | solution.py:39
  26.5 2.5 %copy-start.25 = (bf16[256]{0:T(256)(128)(2,1)S(1)}, bf16[256]{0:T(256)(128)(2,1)}, u32[]{:S(2)}) copy-start(bf16[256]{0:T(256)(128)(2,1)} %param.27) | copy-start | bytes 1540
  28.9 1.7 %copy-start.9 = (s32[64]{0:T(128)S(1)}, s32[64]{0:T(128)}, u32[]{:S(2)}) copy-start(s32[64]{0:T(128)} %param.31) | copy-start | bytes 772
  29.0 2.3 %copy-start.20 = (bf16[1024]{0:T(1024)(128)(2,1)S(1)}, bf16[1024]{0:T(1024)(128)(2,1)}, u32[]{:S(2)}) copy-start(bf16[1024]{0:T(1024)(128)(2,1)} %param.25) | copy-start | bytes 6148
  34.6 5.5 %copy-start.21 = (s32[64]{0:T(128)S(1)}, s32[64]{0:T(128)}, u32[]{:S(2)}) copy-start(s32[64]{0:T(128)} %get-tuple-element.98) | copy-start | bytes 772
  38.4 0.7 copy-start.6
  39.2 19.1 %collective-permute-start.1 = (bf16[1,128,1280]{2,1,0:T(8,128)(2,1)}, bf16[1,128,1280]{2,1,0:T(8,128)(2,1)}, u32[]{:S(2)}, u32[]{:S(2)}) collective-permute-start(bf16[1,128,1280]{2,1,0:T(8,128)(2,1)} %get-tuple-element.75), channel_id=1, source_target_pairs={{0,1},{1,2},{2,3},{3,0},{4,5},{5,6},{6,7},{7,4},{8,9},{9,10},{10,1... | collective-permute-start | bytes 983048 | tf_op jit(solution)/shard_map/ppermute | solution.py:39
  46.5 6.3 %copy-start.7 = (bf16[1,128,1280]{2,1,0:T(8,128)(2,1)S(1)}, bf16[1,128,1280]{2,1,0:T(8,128)(2,1)}, u32[]{:S(2)}) copy-start(bf16[1,128,1280]{2,1,0:T(8,128)(2,1)} %copy-done.6) | copy-start | bytes 983044
  52.8 10.2 %collective-permute-start.3 = (bf16[1,128,1280]{2,1,0:T(8,128)(2,1)S(1)}, bf16[1,128,1280]{2,1,0:T(8,128)(2,1)S(1)}, u32[]{:S(2)}, u32[]{:S(2)}) collective-permute-start(bf16[1,128,1280]{2,1,0:T(8,128)(2,1)S(1)} %copy-done.7), channel_id=1, source_target_pairs={{0,3},{1,0},{2,1},{3,2},{4,7},{5,4},{6,5},{7,6},{8,11},{9,8},{10,9... | collective-permute-start | bytes 983048 | tf_op jit(solution)/shard_map/ppermute | solution.py:39
  55.8 7.2 %copy-start.10 = (bf16[4,512,1,256]{3,1,2,0:T(8,128)(2,1)S(1)}, bf16[4,512,1,256]{3,1,2,0:T(8,128)(2,1)}, u32[]{:S(2)}) copy-start(bf16[4,512,1,256]{3,1,2,0:T(8,128)(2,1)} %param.29) | copy-start | bytes 3145732
  57.0 16.1 %collective-permute-start.18 = (bf16[2,128,1280]{2,1,0:T(8,128)(2,1)S(1)}, bf16[2,128,1280]{2,1,0:T(8,128)(2,1)S(1)}, u32[]{:S(2)}, u32[]{:S(2)}) collective-permute-start(bf16[2,128,1280]{2,1,0:T(8,128)(2,1)S(1)} %add_dynamic-update-slice_fusion.1), channel_id=1, source_target_pairs={{0,1},{1,2},{2,3},{3,0},{4,5},{5,6},{6,7},{7,4},{8,9},{9,10},{10,1... | collective-permute-start | bytes 1966088 | tf_op jit(solution)/shard_map/ppermute | solution.py:39
  58.2 17.2 %collective-permute-start.20 = (bf16[2,128,1280]{2,1,0:T(8,128)(2,1)S(1)}, bf16[2,128,1280]{2,1,0:T(8,128)(2,1)S(1)}, u32[]{:S(2)}, u32[]{:S(2)}) collective-permute-start(bf16[2,128,1280]{2,1,0:T(8,128)(2,1)S(1)} %add_dynamic-update-slice_fusion), channel_id=1, source_target_pairs={{0,3},{1,0},{2,1},{3,2},{4,7},{5,4},{6,5},{7,6},{8,11},{9,8},{10,9... | collective-permute-start | bytes 1966088 | tf_op jit(solution)/shard_map/ppermute | solution.py:39
  63.0 59.3 %collective-permute-start.11 = (bf16[4,512,256]{2,1,0:T(8,128)(2,1)S(1)}, bf16[4,512,256]{2,1,0:T(8,128)(2,1)S(1)}, u32[]{:S(2)}, u32[]{:S(2)}) collective-permute-start(bf16[4,512,256]{2,1,0:T(8,128)(2,1)S(1)} %bitcast.89), channel_id=1, source_target_pairs={{0,8},{8,0},{16,24},{24,16},{32,40},{40,32},{48,56},{56,48},{64,72... | collective-permute-start | bytes 3145736 | tf_op jit(solution)/shard_map/ppermute | solution.py:43
  73.1 15.1 %collective-permute-start.2 = (bf16[2,128,1280]{2,1,0:T(8,128)(2,1)S(1)}, bf16[2,128,1280]{2,1,0:T(8,128)(2,1)S(1)}, u32[]{:S(2)}, u32[]{:S(2)}) collective-permute-start(bf16[2,128,1280]{2,1,0:T(8,128)(2,1)S(1)} %add_dynamic-update-slice_fusion.3), channel_id=1, source_target_pairs={{0,1},{1,2},{2,3},{3,0},{4,5},{5,6},{6,7},{7,4},{8,9},{9,10},{10,1... | collective-permute-start | bytes 1966088 | tf_op jit(solution)/shard_map/ppermute | solution.py:39
  75.4 16.3 %collective-permute-start.4 = (bf16[2,128,1280]{2,1,0:T(8,128)(2,1)S(1)}, bf16[2,128,1280]{2,1,0:T(8,128)(2,1)S(1)}, u32[]{:S(2)}, u32[]{:S(2)}) collective-permute-start(bf16[2,128,1280]{2,1,0:T(8,128)(2,1)S(1)} %add_dynamic-update-slice_fusion.2), channel_id=1, source_target_pairs={{0,3},{1,0},{2,1},{3,2},{4,7},{5,4},{6,5},{7,6},{8,11},{9,8},{10,9... | collective-permute-start | bytes 1966088 | tf_op jit(solution)/shard_map/ppermute | solution.py:39
  79.1 1.2 copy-start.14
  80.4 37.4 %collective-permute-start.6 = (bf16[32,64,256]{2,1,0:T(8,128)(2,1)S(1)}, bf16[32,64,256]{2,1,0:T(8,128)(2,1)S(1)}, u32[]{:S(2)}, u32[]{:S(2)}) collective-permute-start(bf16[32,64,256]{2,1,0:T(8,128)(2,1)S(1)} %copy-done.14), channel_id=1, source_target_pairs={{0,64},{8,72},{16,80},{24,88},{32,96},{40,104},{48,112},{56,120},{... | collective-permute-start | bytes 3145736 | tf_op jit(solution)/shard_map/ppermute | solution.py:43
  81.8 28.8 %collective-permute-start.21 = (bf16[128,1280]{1,0:T(8,128)(2,1)S(1)}, bf16[128,1280]{1,0:T(8,128)(2,1)S(1)}, u32[]{:S(2)}, u32[]{:S(2)}) collective-permute-start(bf16[128,1280]{1,0:T(8,128)(2,1)S(1)} %fusion.7), channel_id=1, source_target_pairs={{0,4},{1,5},{2,6},{3,7},{4,0},{5,1},{6,2},{7,3},{8,12},{9,13},{10,... | collective-permute-start | bytes 983048 | tf_op jit(solution)/shard_map/ppermute | solution.py:39
  88.2 30.3 %collective-permute-start.9 = (bf16[2,512,256]{2,1,0:T(8,128)(2,1)S(1)}, bf16[2,512,256]{2,1,0:T(8,128)(2,1)S(1)}, u32[]{:S(2)}, u32[]{:S(2)}) collective-permute-start(bf16[2,512,256]{2,1,0:T(8,128)(2,1)S(1)} %slice.265), channel_id=1, source_target_pairs={{0,16},{8,24},{16,32},{24,40},{32,48},{40,56},{48,0},{56,8},{64,80... | collective-permute-start | bytes 1572872 | tf_op jit(solution)/shard_map/ppermute | solution.py:43
  91.8 26.9 %collective-permute-start.10 = (bf16[2,512,256]{2,1,0:T(8,128)(2,1)S(1)}, bf16[2,512,256]{2,1,0:T(8,128)(2,1)S(1)}, u32[]{:S(2)}, u32[]{:S(2)}) collective-permute-start(bf16[2,512,256]{2,1,0:T(8,128)(2,1)S(1)} %slice.266), channel_id=1, source_target_pairs={{0,48},{8,56},{16,0},{24,8},{32,16},{40,24},{48,32},{56,40},{64,11... | collective-permute-start | bytes 1572872 | tf_op jit(solution)/shard_map/ppermute | solution.py:43
  110.6 7.1 %collective-permute-start.5 = (bf16[128,1280]{1,0:T(8,128)(2,1)S(1)}, bf16[128,1280]{1,0:T(8,128)(2,1)S(1)}, u32[]{:S(2)}, u32[]{:S(2)}) collective-permute-start(bf16[128,1280]{1,0:T(8,128)(2,1)S(1)} %fusion.6), channel_id=1, source_target_pairs={{0,4},{1,5},{2,6},{3,7},{4,0},{5,1},{6,2},{7,3},{8,12},{9,13},{10,... | collective-permute-start | bytes 983048 | tf_op jit(solution)/shard_map/ppermute | solution.py:39
  117.7 5.7 %collective-permute-start.12 = (bf16[4,512,256]{2,1,0:T(8,128)(2,1)}, bf16[4,512,256]{2,1,0:T(8,128)(2,1)S(1)}, u32[]{:S(2)}, u32[]{:S(2)}) collective-permute-start(bf16[4,512,256]{2,1,0:T(8,128)(2,1)} %collective-permute-done.7.refs_1_), channel_id=1, source_target_pairs={{0,8},{8,0},{16,24},{24,16},{32,40},{40,32},{48,56},{56,48},{64,72... | collective-permute-start | bytes 3145736 | tf_op jit(solution)/shard_map/ppermute | solution.py:43
  117.7 1.4 copy-start.22
  117.7 1.4 copy-start.23
  117.8 1.4 copy-start.24
  117.8 5.8 %collective-permute-start.13 = (bf16[4,512,256]{2,1,0:T(8,128)(2,1)}, bf16[4,512,256]{2,1,0:T(8,128)(2,1)S(1)}, u32[]{:S(2)}, u32[]{:S(2)}) collective-permute-start(bf16[4,512,256]{2,1,0:T(8,128)(2,1)} %collective-permute-done.8.refs_2_), channel_id=1, source_target_pairs={{0,8},{8,0},{16,24},{24,16},{32,40},{40,32},{48,56},{56,48},{64,72... | collective-permute-start | bytes 3145736 | tf_op jit(solution)/shard_map/ppermute | solution.py:43
  118.5 3.8 %collective-permute-start.14 = (bf16[2,512,256]{2,1,0:T(8,128)(2,1)S(1)}, bf16[2,512,256]{2,1,0:T(8,128)(2,1)S(1)}, u32[]{:S(2)}, u32[]{:S(2)}) collective-permute-start(bf16[2,512,256]{2,1,0:T(8,128)(2,1)S(1)} %collective-permute-done.9.refs_3_), channel_id=1, source_target_pairs={{0,8},{8,0},{16,24},{24,16},{32,40},{40,32},{48,56},{56,48},{64,72... | collective-permute-start | bytes 1572872 | tf_op jit(solution)/shard_map/ppermute | solution.py:43
  118.6 4.7 %collective-permute-start.15 = (bf16[2,512,256]{2,1,0:T(8,128)(2,1)S(1)}, bf16[2,512,256]{2,1,0:T(8,128)(2,1)S(1)}, u32[]{:S(2)}, u32[]{:S(2)}) collective-permute-start(bf16[2,512,256]{2,1,0:T(8,128)(2,1)S(1)} %collective-permute-done.10.refs_4_), channel_id=1, source_target_pairs={{0,8},{8,0},{16,24},{24,16},{32,40},{40,32},{48,56},{56,48},{64,72... | collective-permute-start | bytes 1572872 | tf_op jit(solution)/shard_map/ppermute | solution.py:43
  120.3 1.6 %copy-start.17 = (bf16[128,64]{1,0:T(8,128)(2,1)}, bf16[128,64]{1,0:T(8,128)(2,1)S(1)}, u32[]{:S(2)}) copy-start(bf16[128,64]{1,0:T(8,128)(2,1)S(1)} %get-tuple-element.106) | copy-start | bytes 49156
  120.3 1.6 %copy-start.18 = (bf16[128,64]{1,0:T(8,128)(2,1)}, bf16[128,64]{1,0:T(8,128)(2,1)S(1)}, u32[]{:S(2)}) copy-start(bf16[128,64]{1,0:T(8,128)(2,1)S(1)} %get-tuple-element.107) | copy-start | bytes 49156
  120.3 1.5 %copy-start.19 = (bf16[128,128]{1,0:T(8,128)(2,1)}, bf16[128,128]{1,0:T(8,128)(2,1)S(1)}, u32[]{:S(2)}) copy-start(bf16[128,128]{1,0:T(8,128)(2,1)S(1)} %slice.330) | copy-start | bytes 98308
  122.3 1.2 copy-start.11
  122.3 9.8 %copy-start.2 = (bf16[2,512,256]{2,1,0:T(8,128)(2,1)}, bf16[2,512,256]{2,1,0:T(8,128)(2,1)S(1)}, u32[]{:S(2)}) copy-start(bf16[2,512,256]{2,1,0:T(8,128)(2,1)S(1)} %collective-permute-done.14.refs_8_) | copy-start | bytes 1572868
  123.3 8.9 %copy-start.4 = (bf16[2,512,256]{2,1,0:T(8,128)(2,1)}, bf16[2,512,256]{2,1,0:T(8,128)(2,1)S(1)}, u32[]{:S(2)}) copy-start(bf16[2,512,256]{2,1,0:T(8,128)(2,1)S(1)} %collective-permute-done.15.refs_9_) | copy-start | bytes 1572868
  123.3 1.0 copy-start.12
  123.5 1.2 copy-start.13
  133.9 13.3 %collective-permute-start.16 = (bf16[32,4,1280]{2,1,0:T(4,128)(2,1)}, bf16[32,4,1280]{2,1,0:T(4,128)(2,1)}, u32[]{:S(2)}, u32[]{:S(2)}) collective-permute-start(bf16[32,4,1280]{2,1,0:T(4,128)(2,1)} %concatenate.75), channel_id=1, source_target_pairs={{0,64},{8,72},{16,80},{24,88},{32,96},{40,104},{48,112},{56,120},{... | collective-permute-start | bytes 983048 | tf_op jit(solution)/shard_map/ppermute | solution.py:43
  136.8 1.8 %copy-start.15 = (bf16[128,64]{1,0:T(8,128)(2,1)S(1)}, bf16[128,64]{1,0:T(8,128)(2,1)}, u32[]{:S(2)}) copy-start(bf16[128,64]{1,0:T(8,128)(2,1)} %get-tuple-element.122) | copy-start | bytes 49156
  136.8 1.8 %copy-start.16 = (bf16[128,64]{1,0:T(8,128)(2,1)S(1)}, bf16[128,64]{1,0:T(8,128)(2,1)}, u32[]{:S(2)}) copy-start(bf16[128,64]{1,0:T(8,128)(2,1)} %get-tuple-element.123) | copy-start | bytes 49156
  136.8 2.3 %copy-start.5 = (bf16[2,512,256]{2,1,0:T(8,128)(2,1)S(1)}, bf16[2,512,256]{2,1,0:T(8,128)(2,1)}, u32[]{:S(2)}) copy-start(bf16[2,512,256]{2,1,0:T(8,128)(2,1)} %copy-done.4) | copy-start | bytes 1572868
  138.4 1.2 copy-start.1
  138.4 1.3 copy-start.3

commit v3 on v2

--- a/solution.py
+++ b/solution.py
@@ -75,7 +75,7 @@
         for pair in copies:
             for c in pair:
                 c.start()
-        x = jnp.concatenate([r[...] for r in x_refs], 0) if len(xs) > 1 else x_refs[0][...]
+        x = jnp.concatenate([r[:, :depth] for r in x_refs], 0)
         d = 0
         for g, group in enumerate(groups):
             for i in range(len(group)):
@@ -108,30 +108,107 @@
     )(heads, *xs, wq, wp)
 
 
-def attend(limits, lengths, q, new, cache, kvs):
-    flat = [a for group in kvs for a in group]
-
-    def kernel(limit_ref, length_ref, q_ref, new_ref, cache_ref, *refs):
-        kv_refs = refs[: len(flat)]
-        o_ref, buf, cbuf, sem, csem = refs[len(flat) :]
-        copies, at = [], 0
-        for g, group in enumerate(kvs):
-            mine, slot = [], 4 * g
-            for a in group:
-                n = a.shape[0]
-                mine.append(pltpu.make_async_copy(kv_refs[at], buf.at[pl.ds(slot, n)], sem.at[at]))
-                slot, at = slot + n, at + 1
-            mine.append(
-                pltpu.make_async_copy(cache_ref.at[pl.ds(4 * g, 4)], cbuf.at[pl.ds(4 * g, 4)], csem.at[g])
-            )
+def sort_rows(place, owner, pos, tokens):
+    rows, width = tokens.shape
+
+    def kernel(place_ref, owner_ref, pos_ref, x_ref, *outs):
+        x = x_ref[...]
+        for b, out in enumerate(outs):
+            row = lax.broadcasted_iota(jnp.int32, (ROWS, rows), 0)
+            col = lax.broadcasted_iota(jnp.int32, (ROWS, rows), 1)
+            i = row // 4
+            y, c, step, j = (1 - b + place_ref[0]) % 2, i // 16, i // 4 % 4, i % 4
+            c = jnp.where(c == 0, place_ref[2], 1 - place_ref[2])
+            z = (step + place_ref[1]) % 4
+            slot = ((y * 4 + z) * 2 + c) * 4 + j
+            hit = (owner_ref[...] == slot) & (col % 4 == row % 4)
+            at = jnp.sum(jnp.where(hit, pos_ref[...], 0.0), -1, keepdims=True)
+            hit = jnp.where(hit, 1.0, 0.0).astype(BF16)
+            out[:, :width] = dot(hit, x).astype(BF16)
+            out[:, width:] = jnp.broadcast_to(at, (ROWS, 128)).astype(BF16)
+
+    return pl.pallas_call(
+        kernel,
+        in_specs=[IN_SMEM, IN_VMEM, IN_VMEM, IN_VMEM],
+        out_specs=[IN_VMEM] * 2,
+        out_shape=[jax.ShapeDtypeStruct((ROWS, width + 128), BF16)] * 2,
+        compiler_params=pltpu.CompilerParams(vmem_limit_bytes=VMEM),
+        name="sort_rows",
+    )(place, owner, pos, tokens)
+
+
+def place_rows(order, first, second):
+    def kernel(order_ref, a_ref, b_ref, o_ref, p_ref):
+        for half, ref in enumerate((a_ref, b_ref)):
+
+            def step(i, carry, half=half, ref=ref):
+                at = order_ref[32 * half + i]
+                o_ref[at] = ref[i, :, :QW]
+                p_ref[at] = ref[i, :, QW:]
+                return carry
+
+            lax.fori_loop(0, 32, step, 0, unroll=8)
+
+    return pl.pallas_call(
+        kernel,
+        in_specs=[IN_SMEM, IN_VMEM, IN_VMEM],
+        out_specs=[IN_VMEM] * 2,
+        out_shape=[jax.ShapeDtypeStruct((64, 4, QW), BF16), jax.ShapeDtypeStruct((64, 4, PW), BF16)],
+        compiler_params=pltpu.CompilerParams(vmem_limit_bytes=VMEM),
+        name="place_rows",
+    )(order, first, second)
+
+
+def sum_x(own, from_left, from_right):
+    def kernel(a, b, c, keep, send):
+        for i, out in enumerate((keep, send)):
+            out[...] = (a[i].astype(F32) + b[i].astype(F32) + c[i].astype(F32)).astype(out.dtype)
+
+    return pl.pallas_call(
+        kernel,
+        in_specs=[IN_VMEM] * 3,
+        out_specs=[IN_VMEM] * 2,
+        out_shape=[jax.ShapeDtypeStruct((ROWS, COLS), F32), jax.ShapeDtypeStruct((ROWS, COLS), BF16)],
+        compiler_params=pltpu.CompilerParams(vmem_limit_bytes=VMEM),
+        name="sum_x",
+    )(own, from_left, from_right)
+
+
+def attend(limits, lengths, cache_at, keep, more, bias, cosine, sine, cache, kvs):
+    def kernel(
+        limit_ref, length_ref, at_ref, keep_ref, more_ref, bias_ref, cos_ref, sin_ref, cache_ref, kv_a, kv_b,
+        o_ref, buf, cbuf, qbuf, sem, csem,
+    ):
+        copies = []
+        for g in range(8):
+            kv = (kv_a, kv_b)[g // 4]
+            mine = [pltpu.make_async_copy(kv.at[limit_ref[32 + g % 4]], buf.at[pl.ds(4 * g, 4)], sem.at[g])]
+            for p in range(4 * g, 4 * g + 4):
+                mine.append(pltpu.make_async_copy(cache_ref.at[at_ref[p]], cbuf.at[p], csem.at[p]))
             copies.append(mine)
         for mine in copies:
             for c in mine:
                 c.start()
+        cos, sin = cos_ref[...], sin_ref[...]
+
+        def turn(v):
+            return v * cos + pltpu.roll(v, HD // 2, 1) * sin
+
+        for h in range(HEADS):
+            low, high = h * HD, h * HD + HD
+            v = keep_ref[:, low:high] + more_ref[:, low:high].astype(F32) + bias_ref[:, low:high]
+            v = turn(v)
+            for p in range(32):
+                qbuf[32 * p + 4 * h : 32 * p + 4 * h + 4, :] = v[4 * p : 4 * p + 4]
+        u = keep_ref[:, QW:] + more_ref[:, QW:].astype(F32) + bias_ref[:, QW:]
+        new_all = jnp.concatenate([turn(u[:, :HD]), u[:, HD:]], 1)
+        for p in range(32):
+            o_ref[p, :, QW:] = new_all[4 * p : 4 * p + 4].astype(BF16)
+        new_all = new_all.astype(BF16)
         for g in range(8):
             for c in copies[g]:
                 c.wait()
-            q = q_ref[4 * g : 4 * g + 4].reshape(128, HD)
+            q = qbuf[128 * g : 128 * g + 128, :].astype(BF16)
             sp = []
             for i in range(4):
                 p = 4 * g + i
@@ -146,7 +223,7 @@
             for i in range(4):
                 length = jnp.where(row // 32 == i, length_ref[4 * g + i], length)
             sc = jnp.where((row // 32 == col // 64) & (col % 64 < length), sc, NEG)
-            new = new_ref[16 * g : 16 * g + 16]
+            new = new_all[16 * g : 16 * g + 16]
             sn = dot(q, new[:, :HD], ((1,), (1,))) * SCALE
             row = lax.broadcasted_iota(jnp.int32, sn.shape, 0)
             col = lax.broadcasted_iota(jnp.int32, sn.shape, 1)
@@ -169,38 +246,29 @@
             o = o + dot(wn.astype(BF16), new[:, HD:])
             o = o / total
             for i in range(4):
-                o_ref[4 * g + i] = jnp.concatenate(
-                    [o[32 * i + 4 * h : 32 * i + 4 * h + 4] for h in range(HEADS)], 1
-                ).astype(BF16)
-
-    return pl.pallas_call(
-        kernel,
-        in_specs=[IN_SMEM, IN_SMEM, IN_VMEM, IN_VMEM, ANY] + [ANY] * len(flat),
+                for h in range(HEADS):
+                    o_ref[4 * g + i, :, h * HD : h * HD + HD] = o[
+                        32 * i + 4 * h : 32 * i + 4 * h + 4
+                    ].astype(BF16)
+
+    return pl.pallas_call(
+        kernel,
+        in_specs=[IN_SMEM] * 3 + [IN_VMEM] * 5 + [ANY] * 3,
         out_specs=IN_VMEM,
-        out_shape=jax.ShapeDtypeStruct((32, 4, QW), BF16),
+        out_shape=jax.ShapeDtypeStruct((32, 4, COLS), BF16),
         scratch_shapes=[
             pltpu.VMEM((32, 512, 2 * HD), BF16),
             pltpu.VMEM((32, 64, 2 * HD), BF16),
-            pltpu.SemaphoreType.DMA((len(flat),)),
+            pltpu.VMEM((1024, HD), F32),
             pltpu.SemaphoreType.DMA((8,)),
+            pltpu.SemaphoreType.DMA((32,)),
         ],
         compiler_params=pltpu.CompilerParams(vmem_limit_bytes=VMEM),
         cost_estimate=pl.CostEstimate(
             flops=32 * 32 * 600 * 512, bytes_accessed=10 * 2**20, transcendentals=32 * 32 * 600
         ),
         name="attend",
-    )(limits, lengths, q, new, cache, *flat)
-
-
-def rotate(values, cosine, sine):
-    half = values.shape[-1] // 2
-    lead, trail = values[..., :half], values[..., half:]
-    return jnp.concatenate([lead * cosine - trail * sine, trail * cosine + lead * sine], -1)
-
-
-def finish(own, from_left, from_right):
-    total = own.astype(F32) + from_left.astype(F32) + from_right.astype(F32)
-    return total[0], total[1].astype(BF16)
+    )(limits, lengths, cache_at, keep, more, bias, cosine, sine, cache, *kvs)
 
 
 def on_device(
@@ -220,81 +288,76 @@
     my_y, my_z, my_c = me // 8, me // 2 % 4, me % 2
     tp = lax.axis_index("tp")
     tp_y, tp_x = tp // 4, tp % 4
+    pos = positions.reshape(prompts)
+
+    z_groups = [[(y * 4 + z) * 2 + c for z in range(4)] for y in range(2) for c in range(2)]
+    own_core = lax.all_gather(
+        prefix_pairs.reshape(4, 512, 2 * HD), "roll", axis=0, axis_index_groups=z_groups
+    )
+    other_core = over_roll(own_core, 0, 0, 1)
+
+    sorted_t, sorted_g = sort_rows(
+        jnp.stack([my_y, my_z, my_c]).astype(jnp.int32),
+        jnp.repeat(owner_slot, new)[None],
+        jnp.repeat(pos, new)[None].astype(F32),
+        tokens.reshape(prompts * new, width),
+    )
+    swapped = over_roll(sorted_t, 1, 0, 0)
 
     index = jnp.arange(prompts, dtype=jnp.int32)
-    steps = jnp.array([0, 3, 1, 2], jnp.int32)
-    half = jnp.arange(2, dtype=jnp.int32)
-    y_of = (1 - half + my_y) % 2
-    c_of = (half + my_c) % 2
-    z_of = (steps + my_z) % 4
+    half, quarter = jnp.arange(2, dtype=jnp.int32), jnp.arange(4, dtype=jnp.int32)
+    y_of, c_of, z_of = (1 - half + my_y) % 2, (half + my_c) % 2, (quarter + my_z) % 4
     slot = (
         ((y_of[:, None, None, None] * 4 + z_of[None, None, :, None]) * 2 + c_of[None, :, None, None]) * 4
-        + jnp.arange(4, dtype=jnp.int32)[None, None, None, :]
+        + quarter[None, None, None, :]
     ).reshape(prompts)
-    order = jnp.sum(jnp.where(owner_slot[None, :] == slot[:, None], index[None, :], 0), 1)
-    inverse = jnp.sum(jnp.where(slot[None, :] == owner_slot[:, None], index[None, :], 0), 1)
-    pos = positions.reshape(prompts)
-
-    x = jnp.take(tokens.reshape(prompts, new * width), order, axis=0)
-    pos_sorted = jnp.take(pos, order)
-    blocks = jnp.take(prefix_blocks, order[32:])
-    head_row = jnp.zeros((16, width), BF16).at[0, :32].set(pos_sorted[:32].astype(BF16))
-    swapped = over_roll(
-        jnp.concatenate([x[:32].reshape(ROWS, width), head_row], 0), 1, 0, 0
-    )
-    x_t, pos_t = swapped[:ROWS], swapped[ROWS, :32].astype(jnp.int32)
-    x_g, pos_g = x[32:].reshape(ROWS, width), pos_sorted[32:]
+    hit = owner_slot[None, :] == slot[:, None]
+    order = jnp.sum(jnp.where(hit, index[None, :], 0), 1)
+    limits = BLOCK * jnp.sum(jnp.where(hit[32:], prefix_blocks[None, :], 0), 1)
+    limits = jnp.concatenate([limits, z_of])
+    pos_g = jnp.sum(jnp.where(hit[32:], pos[None, :], 0), 1)
+    pos_t = swapped[::4, width].astype(jnp.int32)
+
     cache = cache_pairs.reshape(prompts, 64, 2 * HD)
-    cache_t = over_roll(jnp.take(cache, order[:32], axis=0), 1, 0, 0)
-    cache_g = jnp.take(cache, order[32:], axis=0)
+    cache_t = over_roll(cache.at[order[:32]].get(mode="promise_in_bounds"), 1, 0, 0)
 
     def heads(*pairs):
         return jnp.stack([(tp_y + dy) % 2 * 4 + (tp_x + dx) % 4 for dy, dx in pairs]).astype(jnp.int32)
 
     far = heads((0, 2), (1, 2))
-    up_g, down_g = project(far, [x_g], query_weight, pair_weight, [[0], [1]])
-    up_t, down_t = project(far, [x_t], query_weight, pair_weight, [[0], [1]])
+    up_g, down_g = project(far, [sorted_g], query_weight, pair_weight, [[0], [1]])
+    up_t, down_t = project(far, [swapped], query_weight, pair_weight, [[0], [1]])
     right_t, left_t, right_g, left_g = project(
-        heads((0, 1), (1, 1), (0, 3), (1, 3)), [x_t, x_g], query_weight, pair_weight, [[0, 1], [2, 3]]
-    )
-    own_t, own_g = project(heads((0, 0), (1, 0)), [x_t, x_g], query_weight, pair_weight, [[0, 1]])
+        heads((0, 1), (1, 1), (0, 3), (1, 3)), [swapped, sorted_g], query_weight, pair_weight, [[0, 1], [2, 3]]
+    )
+    own_t, own_g = project(heads((0, 0), (1, 0)), [swapped, sorted_g], query_weight, pair_weight, [[0, 1]])
 
     def reduce(up, down, right, left, own):
         up, down = over_tp(up, 0, 1), over_tp(down, 0, 3)
         right = right.at[0].add(up[0])
         left = left.at[1].add(down[0])
-        keep, send = finish(own, over_tp(right, 0, 1), over_tp(left, 0, 3))
-        return keep + over_tp(send, 1, 0).astype(F32)
+        keep, send = sum_x(own, over_tp(right, 0, 1), over_tp(left, 0, 3))
+        return keep, over_tp(send, 1, 0)
 
     full_t = reduce(up_t, down_t, right_t, left_t, own_t)
     full_g = reduce(up_g, down_g, right_g, left_g, own_g)
 
-    own = prefix_pairs.reshape(4, 512, 2 * HD)
-    below, above = over_roll(own, 0, 1, 0), over_roll(own, 0, 3, 0)
-    far_a, far_b = over_roll(below[:2], 0, 1, 0), over_roll(above[2:], 0, 3, 0)
-    kvs = [[own], [below], [above], [far_a, far_b]]
-    kvs = kvs + [[over_roll(a, 0, 0, 1) for a in group] for group in kvs]
-
     frequency = jnp.exp(jnp.arange(HD // 2, dtype=F32) * (-2.0 * math.log(ROPE_BASE) / HD))
-    limits = BLOCK * blocks
-
-    def rows(full, where, cache):
-        at = (limits[:, None] + where[:, None] + jnp.arange(new, dtype=jnp.int32)).reshape(ROWS)
+    bias = jnp.concatenate([query_bias, pair_bias]).astype(F32)[None]
+
+    def rows(full, where, cache_at, cache):
+        at = (limits[:32, None] + where[:, None] + jnp.arange(new, dtype=jnp.int32)).reshape(ROWS)
         angles = at.astype(F32)[:, None] * frequency[None, :]
         cosine, sine = jnp.cos(angles), jnp.sin(angles)
-        q = (full[:, :QW] + query_bias.astype(F32)).reshape(ROWS, HEADS, HD)
-        q = rotate(q, cosine[:, None], sine[:, None]).astype(BF16)
-        q = q.reshape(32, new, HEADS, HD).transpose(0, 2, 1, 3).reshape(32, 32, HD)
-        pair = full[:, QW:] + pair_bias.astype(F32)
-        pair = jnp.concatenate([rotate(pair[:, :HD], cosine, sine), pair[:, HD:]], -1).astype(BF16)
-        return attend(limits, where, q, pair, cache, kvs), pair.reshape(32, new, PW)
-
-    done_t, pair_t = rows(full_t, pos_t, cache_t)
-    back = over_roll(jnp.concatenate([done_t, pair_t], -1), 1, 0, 0)
-    done_g, pair_g = rows(full_g, pos_g, cache_g)
-
-    attended = jnp.take(jnp.concatenate([back[..., :QW], done_g], 0), inverse, axis=0)
-    new_pairs = jnp.take(jnp.concatenate([back[..., QW:], pair_g], 0), inverse, axis=0)
+        cosine = jnp.concatenate([cosine, cosine], 1)
+        sine = jnp.concatenate([-sine, sine], 1)
+        return attend(
+            limits, where, cache_at, *full, bias, cosine, sine, cache, (own_core, other_core)
+        )
+
+    back = over_roll(rows(full_t, pos_t, index[:32], cache_t), 1, 0, 0)
+    done = rows(full_g, pos_g, order[32:], cache)
+    attended, new_pairs = place_rows(order, back, done)
     return (
         attended.reshape(prompts, 1, new, QW),
         new_pairs.reshape(prompts, 1, new, 1, PW),

time: 155 us -> 164 us (1.058)
  waiting for transfers between devices: 44.5 us -> 72.4 us
  local copies, waits for them, and re-layouts: 22.6 us -> 5.88 us
  other arithmetic: 22.7 us -> 8.58 us
  between operations: 1.22 us -> 14.4 us
  starting transfers between devices: 29.4 us -> 22.2 us
  Pallas kernels: 32.9 us -> 40 us
    all_gather x0 -> x1, waiting for transfers between devices: none -> 35.4 us  [on_device(): lax.all_gather(prefix_pairs.reshape(4, 512, 2 * HD), 'roll', axis=0, axis...]
    ppermute x12 -> x4, starting transfers between devices: 13.5 us -> 6.41 us  [over_roll(): return lax.ppermute(a, 'roll', roll_shift(dy, dz, dc))]
    ppermute x10, waiting for transfers between devices: 43.3 us -> 36.4 us  [over_tp(): return lax.ppermute(a, 'tp', tp_shift(dy, dx))]
    select_n x7 -> x2, other arithmetic: 6.2 us -> 0.02 us  [the longest x1 0.01 us: on_device(): (half + my_c) % 2]
    pallas_call x2 -> x6, Pallas kernels: 15 us -> 20.9 us  [the longest x2 15.9 us: attend(): pl.pallas_call(kernel, in_specs=[IN_SMEM] * 3 + [IN_VMEM] * 5 + [ANY] * 3...]
    gather x7 -> x1, local copies, waits for them, and re-layouts: 7.22 us -> 1.69 us  [on_device(): cache.at[order[:32]].get(mode='promise_in_bounds')]
    slice x8 -> x1, local copies, waits for them, and re-layouts: 5.08 us -> 0.03 us  [on_device(): pos_t = swapped[::4, width].astype(jnp.int32)]
    unnamed x55 -> x20, local copies, waits for them, and re-layouts: 5.71 us -> 1.57 us
  transfers between devices with their start and end apart: 22 -> 15, of which waited for: 9 -> 4; matrix products, arithmetic and copies ran while one was open for 22% -> 8% of each run, Pallas kernels for 17% -> 24%
where the time goes in v3:
time: 164 us
  waiting for transfers between devices  72.4 us (44%)
  Pallas kernels  40 us (24%)
  starting transfers between devices  22.2 us (14%)
  between operations  14.4 us (9%)
  other arithmetic  8.58 us (5%)
  local copies, waits for them, and re-layouts  5.88 us (4%)
    ppermute x10, waiting for transfers between devices, over_tp(): return lax.ppermute(a, 'tp', tp_shift(dy, dx))  36.4 us
    all_gather x1, waiting for transfers between devices, on_device(): lax.all_gather(prefix_pairs.reshape(4, 512, 2 * HD), 'roll', axis=0, axis...  35.4 us
    pallas_call x4, Pallas kernels, project(): pl.pallas_call(kernel, in_specs=[IN_SMEM] + [IN_VMEM] * len(xs) + [ANY, A...  19.1 us
    pallas_call x2, Pallas kernels, attend(): pl.pallas_call(kernel, in_specs=[IN_SMEM] * 3 + [IN_VMEM] * 5 + [ANY] * 3...  15.9 us
    ppermute x10, starting transfers between devices, over_tp(): return lax.ppermute(a, 'tp', tp_shift(dy, dx))  15.8 us
    ppermute x4, starting transfers between devices, over_roll(): return lax.ppermute(a, 'roll', roll_shift(dy, dz, dc))  6.41 us
    scatter-add x2, other arithmetic, reduce(): right = right.at[0].add(up[0])  3.75 us
  transfers between devices with their start and end apart: 15, of which 4 were waited for; matrix products, arithmetic and copies ran while one was open for 8% of the time, Pallas kernels for 24%

profile of v3, /device:TPU:0, one launch (start us, length us, event | category | flops | bytes accessed | tf_op | source)
XLA Modules:
  0.0 163.5 jit_solution(2194971986570703619)
XLA Ops:
  7.2 0.7 all-gather.3.cloned.1.call-update
  7.9 0.7 bitcast_convert_fusion
  8.7 0.1 convert_element_type.43.pos_ref
  8.8 0.7 broadcast_in_dim.61
  9.5 0.1 broadcast_in_dim_reshape.2.owner_ref
  9.6 1.2 reshape.335.x_ref
  10.9 0.9 sort_rows.1
  11.8 3.4 %collective-permute-start = (bf16[128,1152]{1,0:T(8,128)(2,1)S(1)}, bf16[128,1152]{1,0:T(8,128)(2,1)S(1)}, u32[]{:S(2)}, u32[]{:S(2)}) collective-permute-start(bf16[128,1152]{1,0:T(8,128)(2,1)S(1)} %get-tuple-element.68), channel_id=1, source_target_pairs={{0,64},{8,72},{16,80},{24,88},{32,96},{40,104},{48,112},{56,120},{... | collective-permute-start | bytes 884744 | tf_op jit(solution)/shard_map/ppermute | solution.py:43
  15.3 3.9 %project.7 = (bf16[1,128,1280]{2,1,0:T(8,128)(2,1)}, bf16[1,128,1280]{2,1,0:T(8,128)(2,1)S(1)}) custom-call(s32[2]{0:T(128)S(1)} %get-tuple-element.115.heads_ref, bf16[128,1152]{1,0:T(8,128)(2,1)S(1)} %get-tuple-element.69.refs_1_.refs_0_, bf16[1024,8192]{1,0:T(8,128)(2,1)} %refs_1_.3, bf16[1024,2048]{1,0:T(8,128)(2,1)} %refs_2_.7), custom_call_target="tpu_custom_call" | custom-call | flops 671088640 | bytes 5242880 | tf_op jit(solution)/shard_map/project/pallas_call | solution.py:90
  19.2 1.6 collective-permute-start.9
  20.8 1.7 %collective-permute-start.11 = (bf16[1,128,1280]{2,1,0:T(8,128)(2,1)S(1)}, bf16[1,128,1280]{2,1,0:T(8,128)(2,1)}, u32[]{:S(2)}, u32[]{:S(2)}) collective-permute-start(bf16[1,128,1280]{2,1,0:T(8,128)(2,1)S(1)} %get-tuple-element.81), channel_id=1, source_target_pairs={{0,3},{1,0},{2,1},{3,2},{4,7},{5,4},{6,5},{7,6},{8,11},{9,8},{10,9... | collective-permute-start | bytes 983048 | tf_op jit(solution)/shard_map/ppermute | solution.py:39
  22.8 0.1 add.304
  22.9 0.2 select_reduce_fusion.order_ref
  23.1 1.7 %gather_fusion = bf16[32,64,256]{2,1,0:T(8,128)(2,1)} fusion(bf16[64,64,256]{2,1,0:T(8,128)(2,1)S(1)} %bitcast.24, s32[1024]{0:T(1024)S(1)} %pad_clamp_fusion), kind=kCustom, calls=%fused_computation | custom fusion | bytes 2097280 | tf_op jit(solution)/shard_map/gather | solution.py:322
  24.8 0.3 collective-permute-start.6
  25.2 0.1 select_reduce_fusion.1
  25.3 35.4 %all-gather.3.cloned.1.call-done = bf16[16,512,1,256]{3,1,2,0:T(8,128)(2,1)} async-done(((bf16[4,512,1,256]{3,1,2,0:T(8,128)(2,1)}), bf16[16,512,1,256]{3,1,2,0:T(8,128)(2,1)}) %all-gather.3.cloned.1.call-update) | async-done | bytes 4194320 | tf_op jit(solution)/shard_map/all_gather | solution.py:294
  60.7 0.1 convert_element_type.51
  60.9 0.1 copy.21
  61.1 3.8 %project.6 = (bf16[1,128,1280]{2,1,0:T(8,128)(2,1)}, bf16[1,128,1280]{2,1,0:T(8,128)(2,1)S(1)}) custom-call(s32[2]{0:T(128)S(1)} %get-tuple-element.115.heads_ref, bf16[128,1152]{1,0:T(8,128)(2,1)S(1)} %collective-permute-done.refs_0_, bf16[1024,8192]{1,0:T(8,128)(2,1)} %refs_1_.3, bf16[1024,2048]{1,0:T(8,128)(2,1)} %refs_2_.7), custom_call_target="tpu_custom_call" | custom-call | flops 671088640 | bytes 5242880 | tf_op jit(solution)/shard_map/project/pallas_call | solution.py:90
  64.9 0.7 copy-done.3
  65.6 1.5 collective-permute-start.1
  67.1 0.1 fusion.2
  67.3 7.1 %project.5 = (bf16[2,128,1280]{2,1,0:T(8,128)(2,1)}, bf16[2,128,1280]{2,1,0:T(8,128)(2,1)S(1)}, bf16[2,128,1280]{2,1,0:T(8,128)(2,1)}, bf16[2,128,1280]{2,1,0:T(8,128)(2,1)}) custom-call(s32[4]{0:T(128)S(1)} %pad_add_fusion.3.heads_ref, bf16[128,1152]{1,0:T(8,128)(2,1)S(1)} %collective-permute-done.refs_0_, ...), custom_call_target="tpu_custom_call" | custom-call | flops 2684354560 | bytes 10485760 | tf_op jit(solution)/shard_map/project/pallas_call | solution.py:90
  74.4 1.9 %collective-permute-start.3 = (bf16[1,128,1280]{2,1,0:T(8,128)(2,1)S(1)}, bf16[1,128,1280]{2,1,0:T(8,128)(2,1)S(1)}, u32[]{:S(2)}, u32[]{:S(2)}) collective-permute-start(bf16[1,128,1280]{2,1,0:T(8,128)(2,1)S(1)} %copy-done.4), channel_id=1, source_target_pairs={{0,3},{1,0},{2,1},{3,2},{4,7},{5,4},{6,5},{7,6},{8,11},{9,8},{10,9... | collective-permute-start | bytes 983048 | tf_op jit(solution)/shard_map/ppermute | solution.py:39
  76.3 1.9 %add_dynamic-update-slice_fusion = bf16[2,128,1280]{2,1,0:T(8,128)(2,1)} fusion(bf16[2,128,1280]{2,1,0:T(8,128)(2,1)} %get-tuple-element.80, bf16[1,128,1280]{2,1,0:T(8,128)(2,1)} %collective-permute-done.11), kind=kLoop, calls=%fused_computation.1 | loop fusion | flops 655360 | bytes 983040 | tf_op jit(solution)/shard_map/scatter-add | solution.py:338
  78.2 6.2 %collective-permute-done.3 = bf16[1,128,1280]{2,1,0:T(8,128)(2,1)S(1)} collective-permute-done((bf16[1,128,1280]{2,1,0:T(8,128)(2,1)S(1)}, bf16[1,128,1280]{2,1,0:T(8,128)(2,1)S(1)}, u32[]{:S(2)}, u32[]{:S(2)}) %collective-permute-start.3) | collective-permute-done | bytes 327712 | tf_op jit(solution)/shard_map/ppermute | solution.py:39
  84.3 3.0 %collective-permute-start.12 = (bf16[2,128,1280]{2,1,0:T(8,128)(2,1)}, bf16[2,128,1280]{2,1,0:T(8,128)(2,1)S(1)}, u32[]{:S(2)}, u32[]{:S(2)}) collective-permute-start(bf16[2,128,1280]{2,1,0:T(8,128)(2,1)} %add_dynamic-update-slice_fusion), channel_id=1, source_target_pairs={{0,3},{1,0},{2,1},{3,2},{4,7},{5,4},{6,5},{7,6},{8,11},{9,8},{10,9... | collective-permute-start | bytes 1966088 | tf_op jit(solution)/shard_map/ppermute | solution.py:39
  87.3 0.1 add_dynamic-update-slice_fusion.2
  87.5 0.3 collective-permute-start.4
  87.8 1.9 %add_dynamic-update-slice_fusion.3 = bf16[2,128,1280]{2,1,0:T(8,128)(2,1)} fusion(bf16[2,128,1280]{2,1,0:T(8,128)(2,1)} %get-tuple-element.71, bf16[1,128,1280]{2,1,0:T(8,128)(2,1)} %collective-permute-done.1), kind=kLoop, calls=%fused_computation.4 | loop fusion | flops 655360 | bytes 983040 | tf_op jit(solution)/shard_map/scatter-add | solution.py:337
  89.7 1.8 %collective-permute-start.2 = (bf16[2,128,1280]{2,1,0:T(8,128)(2,1)}, bf16[2,128,1280]{2,1,0:T(8,128)(2,1)}, u32[]{:S(2)}, u32[]{:S(2)}) collective-permute-start(bf16[2,128,1280]{2,1,0:T(8,128)(2,1)} %add_dynamic-update-slice_fusion.3), channel_id=1, source_target_pairs={{0,1},{1,2},{2,3},{3,0},{4,5},{5,6},{6,7},{7,4},{8,9},{9,10},{10,1... | collective-permute-start | bytes 1966088 | tf_op jit(solution)/shard_map/ppermute | solution.py:39
  91.5 1.9 %add_dynamic-update-slice_fusion.1 = bf16[2,128,1280]{2,1,0:T(8,128)(2,1)} fusion(bf16[2,128,1280]{2,1,0:T(8,128)(2,1)} %get-tuple-element.78, bf16[1,128,1280]{2,1,0:T(8,128)(2,1)} %collective-permute-done.9), kind=kLoop, calls=%fused_computation.2 | loop fusion | flops 655360 | bytes 983040 | tf_op jit(solution)/shard_map/scatter-add | solution.py:337
  93.3 21.8 %collective-permute-done.4.c = bf16[2,128,1280]{2,1,0:T(8,128)(2,1)S(1)} collective-permute-done((bf16[2,128,1280]{2,1,0:T(8,128)(2,1)S(1)}, bf16[2,128,1280]{2,1,0:T(8,128)(2,1)S(1)}, u32[]{:S(2)}, u32[]{:S(2)}) %collective-permute-start.4) | collective-permute-done | bytes 655392 | tf_op jit(solution)/shard_map/ppermute | solution.py:39
  115.2 0.8 copy-done.1
  116.0 1.0 collective-permute-start.10
  117.0 0.1 convert_element_type.49
  117.1 4.2 %project.4 = (bf16[2,128,1280]{2,1,0:T(8,128)(2,1)S(1)}, bf16[2,128,1280]{2,1,0:T(8,128)(2,1)S(1)}) custom-call(s32[2]{0:T(128)S(1)} %get-tuple-element.114.heads_ref, bf16[128,1152]{1,0:T(8,128)(2,1)S(1)} %collective-permute-done.refs_0_, bf16[128,1152]{1,0:T(8,128)(2,1)S(1)} %get-tuple-element.69.refs_1_.refs_0_, bf16[1024,8192]{1,0:T(8,128)(2,1)} %refs_1_.3, ...), custom_call_target="tpu_custom_call" | custom-call | flops 1342177280 | bytes 5242880 | tf_op jit(solution)/shard_map/project/pallas_call | solution.py:90
  121.4 1.3 sum_x.2
  122.7 1.6 collective-permute-start.5
  124.3 0.5 fusion.1
  125.0 8.4 %collective-permute-done.10.b = bf16[2,128,1280]{2,1,0:T(8,128)(2,1)} collective-permute-done((bf16[2,128,1280]{2,1,0:T(8,128)(2,1)}, bf16[2,128,1280]{2,1,0:T(8,128)(2,1)}, u32[]{:S(2)}, u32[]{:S(2)}) %collective-permute-start.10) | collective-permute-done | bytes 655392 | tf_op jit(solution)/shard_map/ppermute | solution.py:39
  133.4 1.3 sum_x.3
  134.7 1.6 collective-permute-start.13
  136.3 7.9 %attend.2 = bf16[32,4,1280]{2,1,0:T(4,128)(2,1)S(1)} custom-call(s32[36]{0:T(128)S(1)} %pad_add_fusion.limit_ref, s32[32]{0:T(128)S(1)} %get-tuple-element.97.length_ref, s32[32]{0:T(128)S(1)} %bitcast.26, f32[128,1280]{1,0:T(8,128)S(1)} %get-tuple-element.75.keep_ref, bf16[128,1280]{1,0:T(8,128)(2,1)S(1)} %collective-permute-done.5.more_ref, ...), custom_call_target="tpu_custom_call" | custom-call | flops 314572800 | bytes 10485760 | tf_op jit(solution)/shard_map/attend/pallas_call | solution.py:254
  144.2 2.8 %collective-permute-start.8 = (bf16[32,4,1280]{2,1,0:T(4,128)(2,1)S(1)}, bf16[32,4,1280]{2,1,0:T(4,128)(2,1)S(1)}, u32[]{:S(2)}, u32[]{:S(2)}) collective-permute-start(bf16[32,4,1280]{2,1,0:T(4,128)(2,1)S(1)} %attend.2), channel_id=1, source_target_pairs={{0,64},{8,72},{16,80},{24,88},{32,96},{40,104},{48,112},{56,120},{... | collective-permute-start | bytes 983048 | tf_op jit(solution)/shard_map/ppermute | solution.py:43
  147.2 7.9 %attend.3.b_ref = bf16[32,4,1280]{2,1,0:T(4,128)(2,1)S(1)} custom-call(s32[36]{0:T(128)S(1)} %pad_add_fusion.limit_ref, s32[32]{0:T(128)S(1)} %get-tuple-element.94.length_ref, s32[32]{0:T(128)S(1)} %get-tuple-element.110.at_ref, f32[128,1280]{1,0:T(8,128)S(1)} %get-tuple-element.82.keep_ref, bf16[128,1280]{1,0:T(8,128)(2,1)S(1)} %collective-permute-done.13.more_ref, ...), custom_call_target="tpu_custom_call" | custom-call | flops 314572800 | bytes 10485760 | tf_op jit(solution)/shard_map/attend/pallas_call | solution.py:254
  155.2 1.5 place_rows.1
  (57 shorter events, 1.4 us)
Async XLA Ops:
  7.2 53.5 %all-gather.3.cloned.1.call-start = ((), (), s32[]{:S(2)}) async-start(), calls=%async_computation | async-start | bytes 5242880 | tf_op jit(solution)/shard_map/all_gather | solution.py:294
  11.8 49.3 %collective-permute-start = (bf16[128,1152]{1,0:T(8,128)(2,1)S(1)}, bf16[128,1152]{1,0:T(8,128)(2,1)S(1)}, u32[]{:S(2)}, u32[]{:S(2)}) collective-permute-start(bf16[128,1152]{1,0:T(8,128)(2,1)S(1)} %get-tuple-element.68), channel_id=1, source_target_pairs={{0,64},{8,72},{16,80},{24,88},{32,96},{40,104},{48,112},{56,120},{... | collective-permute-start | bytes 884744 | tf_op jit(solution)/shard_map/ppermute | solution.py:43
  15.2 7.6 %copy-start.5 = (s32[64]{0:T(128)S(1)}, s32[64]{0:T(128)}, u32[]{:S(2)}) copy-start(s32[64]{0:T(128)} %param.25) | copy-start | bytes 772
  15.2 7.9 %copy-start = (bf16[64,1,64,1,256]{4,2,3,1,0:T(8,128)(2,1)S(1)}, bf16[64,1,64,1,256]{4,2,3,1,0:T(8,128)(2,1)}, u32[]{:S(2)}) copy-start(bf16[64,1,64,1,256]{4,2,3,1,0:T(8,128)(2,1)} %param.23) | copy-start | bytes 6291460
  15.2 9.8 %copy-start.9 = (bf16[256]{0:T(256)(128)(2,1)S(1)}, bf16[256]{0:T(256)(128)(2,1)}, u32[]{:S(2)}) copy-start(bf16[256]{0:T(256)(128)(2,1)} %param.22) | copy-start | bytes 1540
  15.2 9.8 %copy-start.6 = (bf16[1024]{0:T(1024)(128)(2,1)S(1)}, bf16[1024]{0:T(1024)(128)(2,1)}, u32[]{:S(2)}) copy-start(bf16[1024]{0:T(1024)(128)(2,1)} %param.20) | copy-start | bytes 6148
  15.2 9.9 %copy-start.7 = (s32[64,1]{0,1:T(1,128)S(1)}, s32[64,1]{0,1:T(1,128)}, u32[]{:S(2)}) copy-start(s32[64,1]{0,1:T(1,128)} %param.27) | copy-start | bytes 772
  15.2 9.9 %copy-start.8 = (s32[64]{0:T(128)S(1)}, s32[64]{0:T(128)}, u32[]{:S(2)}) copy-start(s32[64]{0:T(128)} %param.26) | copy-start | bytes 772
  19.2 70.5 %collective-permute-start.9 = (bf16[1,128,1280]{2,1,0:T(8,128)(2,1)}, bf16[1,128,1280]{2,1,0:T(8,128)(2,1)}, u32[]{:S(2)}, u32[]{:S(2)}) collective-permute-start(bf16[1,128,1280]{2,1,0:T(8,128)(2,1)} %get-tuple-element.79), channel_id=1, source_target_pairs={{0,1},{1,2},{2,3},{3,0},{4,5},{5,6},{6,7},{7,4},{8,9},{9,10},{10,1... | collective-permute-start | bytes 983048 | tf_op jit(solution)/shard_map/ppermute | solution.py:39
  20.8 53.6 %collective-permute-start.11 = (bf16[1,128,1280]{2,1,0:T(8,128)(2,1)S(1)}, bf16[1,128,1280]{2,1,0:T(8,128)(2,1)}, u32[]{:S(2)}, u32[]{:S(2)}) collective-permute-start(bf16[1,128,1280]{2,1,0:T(8,128)(2,1)S(1)} %get-tuple-element.81), channel_id=1, source_target_pairs={{0,3},{1,0},{2,1},{3,2},{4,7},{5,4},{6,5},{7,6},{8,11},{9,8},{10,9... | collective-permute-start | bytes 983048 | tf_op jit(solution)/shard_map/ppermute | solution.py:39
  24.8 111.4 %collective-permute-start.6 = (bf16[32,64,256]{2,1,0:T(8,128)(2,1)}, bf16[32,64,256]{2,1,0:T(8,128)(2,1)}, u32[]{:S(2)}, u32[]{:S(2)}) collective-permute-start(bf16[32,64,256]{2,1,0:T(8,128)(2,1)} %gather_fusion), channel_id=1, source_target_pairs={{0,64},{8,72},{16,80},{24,88},{32,96},{40,104},{48,112},{56,120},{... | collective-permute-start | bytes 3145736 | tf_op jit(solution)/shard_map/ppermute | solution.py:43
  60.7 75.6 %collective-permute-start.7 = (bf16[4,4,512,256]{3,2,1,0:T(8,128)(2,1)}, bf16[4,4,512,256]{3,2,1,0:T(8,128)(2,1)}, u32[]{:S(2)}, u32[]{:S(2)}) collective-permute-start(bf16[4,4,512,256]{3,2,1,0:T(8,128)(2,1)} %bitcast.27), channel_id=1, source_target_pairs={{0,8},{8,0},{16,24},{24,16},{32,40},{40,32},{48,56},{56,48},{64,72... | collective-permute-start | bytes 12582920 | tf_op jit(solution)/shard_map/ppermute | solution.py:43
  64.9 0.7 copy-start.3
  65.6 21.8 %collective-permute-start.1 = (bf16[1,128,1280]{2,1,0:T(8,128)(2,1)}, bf16[1,128,1280]{2,1,0:T(8,128)(2,1)}, u32[]{:S(2)}, u32[]{:S(2)}) collective-permute-start(bf16[1,128,1280]{2,1,0:T(8,128)(2,1)} %get-tuple-element.72), channel_id=1, source_target_pairs={{0,1},{1,2},{2,3},{3,0},{4,5},{5,6},{6,7},{7,4},{8,9},{9,10},{10,1... | collective-permute-start | bytes 983048 | tf_op jit(solution)/shard_map/ppermute | solution.py:39
  67.3 7.2 %copy-start.4 = (bf16[1,128,1280]{2,1,0:T(8,128)(2,1)S(1)}, bf16[1,128,1280]{2,1,0:T(8,128)(2,1)}, u32[]{:S(2)}) copy-start(bf16[1,128,1280]{2,1,0:T(8,128)(2,1)} %copy-done.3) | copy-start | bytes 983044
  74.4 9.9 %collective-permute-start.3 = (bf16[1,128,1280]{2,1,0:T(8,128)(2,1)S(1)}, bf16[1,128,1280]{2,1,0:T(8,128)(2,1)S(1)}, u32[]{:S(2)}, u32[]{:S(2)}) collective-permute-start(bf16[1,128,1280]{2,1,0:T(8,128)(2,1)S(1)} %copy-done.4), channel_id=1, source_target_pairs={{0,3},{1,0},{2,1},{3,2},{4,7},{5,4},{6,5},{7,6},{8,11},{9,8},{10,9... | collective-permute-start | bytes 983048 | tf_op jit(solution)/shard_map/ppermute | solution.py:39
  84.3 40.7 %collective-permute-start.12 = (bf16[2,128,1280]{2,1,0:T(8,128)(2,1)}, bf16[2,128,1280]{2,1,0:T(8,128)(2,1)S(1)}, u32[]{:S(2)}, u32[]{:S(2)}) collective-permute-start(bf16[2,128,1280]{2,1,0:T(8,128)(2,1)} %add_dynamic-update-slice_fusion), channel_id=1, source_target_pairs={{0,3},{1,0},{2,1},{3,2},{4,7},{5,4},{6,5},{7,6},{8,11},{9,8},{10,9... | collective-permute-start | bytes 1966088 | tf_op jit(solution)/shard_map/ppermute | solution.py:39
  87.5 27.7 %collective-permute-start.4 = (bf16[2,128,1280]{2,1,0:T(8,128)(2,1)S(1)}, bf16[2,128,1280]{2,1,0:T(8,128)(2,1)S(1)}, u32[]{:S(2)}, u32[]{:S(2)}) collective-permute-start(bf16[2,128,1280]{2,1,0:T(8,128)(2,1)S(1)} %add_dynamic-update-slice_fusion.2), channel_id=1, source_target_pairs={{0,3},{1,0},{2,1},{3,2},{4,7},{5,4},{6,5},{7,6},{8,11},{9,8},{10,9... | collective-permute-start | bytes 1966088 | tf_op jit(solution)/shard_map/ppermute | solution.py:39
  89.7 31.7 %collective-permute-start.2 = (bf16[2,128,1280]{2,1,0:T(8,128)(2,1)}, bf16[2,128,1280]{2,1,0:T(8,128)(2,1)}, u32[]{:S(2)}, u32[]{:S(2)}) collective-permute-start(bf16[2,128,1280]{2,1,0:T(8,128)(2,1)} %add_dynamic-update-slice_fusion.3), channel_id=1, source_target_pairs={{0,1},{1,2},{2,3},{3,0},{4,5},{5,6},{6,7},{7,4},{8,9},{9,10},{10,1... | collective-permute-start | bytes 1966088 | tf_op jit(solution)/shard_map/ppermute | solution.py:39
  115.2 0.8 copy-start.1
  116.0 17.4 %collective-permute-start.10 = (bf16[2,128,1280]{2,1,0:T(8,128)(2,1)}, bf16[2,128,1280]{2,1,0:T(8,128)(2,1)}, u32[]{:S(2)}, u32[]{:S(2)}) collective-permute-start(bf16[2,128,1280]{2,1,0:T(8,128)(2,1)} %add_dynamic-update-slice_fusion.1), channel_id=1, source_target_pairs={{0,1},{1,2},{2,3},{3,0},{4,5},{5,6},{6,7},{7,4},{8,9},{9,10},{10,1... | collective-permute-start | bytes 1966088 | tf_op jit(solution)/shard_map/ppermute | solution.py:39
  117.1 4.3 %copy-start.2 = (bf16[2,128,1280]{2,1,0:T(8,128)(2,1)S(1)}, bf16[2,128,1280]{2,1,0:T(8,128)(2,1)}, u32[]{:S(2)}) copy-start(bf16[2,128,1280]{2,1,0:T(8,128)(2,1)} %copy-done.1) | copy-start | bytes 1966084
  122.7 13.5 %collective-permute-start.5 = (bf16[128,1280]{1,0:T(8,128)(2,1)S(1)}, bf16[128,1280]{1,0:T(8,128)(2,1)S(1)}, u32[]{:S(2)}, u32[]{:S(2)}) collective-permute-start(bf16[128,1280]{1,0:T(8,128)(2,1)S(1)} %get-tuple-element.76), channel_id=1, source_target_pairs={{0,4},{1,5},{2,6},{3,7},{4,0},{5,1},{6,2},{7,3},{8,12},{9,13},{10,... | collective-permute-start | bytes 983048 | tf_op jit(solution)/shard_map/ppermute | solution.py:39
  134.7 12.5 %collective-permute-start.13 = (bf16[128,1280]{1,0:T(8,128)(2,1)S(1)}, bf16[128,1280]{1,0:T(8,128)(2,1)S(1)}, u32[]{:S(2)}, u32[]{:S(2)}) collective-permute-start(bf16[128,1280]{1,0:T(8,128)(2,1)S(1)} %get-tuple-element.83), channel_id=1, source_target_pairs={{0,4},{1,5},{2,6},{3,7},{4,0},{5,1},{6,2},{7,3},{8,12},{9,13},{10,... | collective-permute-start | bytes 983048 | tf_op jit(solution)/shard_map/ppermute | solution.py:39
  144.2 10.9 %collective-permute-start.8 = (bf16[32,4,1280]{2,1,0:T(4,128)(2,1)S(1)}, bf16[32,4,1280]{2,1,0:T(4,128)(2,1)S(1)}, u32[]{:S(2)}, u32[]{:S(2)}) collective-permute-start(bf16[32,4,1280]{2,1,0:T(4,128)(2,1)S(1)} %attend.2), channel_id=1, source_target_pairs={{0,64},{8,72},{16,80},{24,88},{32,96},{40,104},{48,112},{56,120},{... | collective-permute-start | bytes 983048 | tf_op jit(solution)/shard_map/ppermute | solution.py:43
Sparse Core Ops, SparseCore 0:
  9.7 50.9 all-gather.2

commit v4 on v3

--- a/solution.py
+++ b/solution.py
@@ -49,6 +49,7 @@
 
 ANY = pl.BlockSpec(memory_space=pl.ANY)
 IN_VMEM = pl.BlockSpec(memory_space=pltpu.VMEM)
+SMALL = pl.CostEstimate(flops=10**6, bytes_accessed=10**5, transcendentals=0)
 IN_SMEM = pl.BlockSpec(memory_space=pltpu.SMEM)
 
 
@@ -99,11 +100,7 @@
             pltpu.SemaphoreType.DMA((count,)),
         ],
         compiler_params=pltpu.CompilerParams(vmem_limit_bytes=VMEM),
-        cost_estimate=pl.CostEstimate(
-            flops=2 * len(xs) * ROWS * depth * count * COLS,
-            bytes_accessed=2 * depth * count * COLS,
-            transcendentals=0,
-        ),
+        cost_estimate=SMALL,
         name="project",
     )(heads, *xs, wq, wp)
 
@@ -119,7 +116,7 @@
             i = row // 4
             y, c, step, j = (1 - b + place_ref[0]) % 2, i // 16, i // 4 % 4, i % 4
             c = jnp.where(c == 0, place_ref[2], 1 - place_ref[2])
-            z = (step + place_ref[1]) % 4
+            z = (jnp.where(step == 1, 3, jnp.where(step == 0, 0, step - 1)) + place_ref[1]) % 4
             slot = ((y * 4 + z) * 2 + c) * 4 + j
             hit = (owner_ref[...] == slot) & (col % 4 == row % 4)
             at = jnp.sum(jnp.where(hit, pos_ref[...], 0.0), -1, keepdims=True)
@@ -133,6 +130,7 @@
         out_specs=[IN_VMEM] * 2,
         out_shape=[jax.ShapeDtypeStruct((ROWS, width + 128), BF16)] * 2,
         compiler_params=pltpu.CompilerParams(vmem_limit_bytes=VMEM),
+        cost_estimate=SMALL,
         name="sort_rows",
     )(place, owner, pos, tokens)
 
@@ -155,8 +153,48 @@
         out_specs=[IN_VMEM] * 2,
         out_shape=[jax.ShapeDtypeStruct((64, 4, QW), BF16), jax.ShapeDtypeStruct((64, 4, PW), BF16)],
         compiler_params=pltpu.CompilerParams(vmem_limit_bytes=VMEM),
+        cost_estimate=SMALL,
         name="place_rows",
     )(order, first, second)
+
+
+def add_far(right, left, up, down):
+    def kernel(r, l, u, d, r_out, l_out):
+        r_out[...] = (r[...].astype(F32) + u[...].astype(F32)).astype(BF16)
+        l_out[...] = (l[...].astype(F32) + d[...].astype(F32)).astype(BF16)
+
+    block = [pl.BlockSpec((1, ROWS, COLS), lambda i, h=h: (h, 0, 0)) for h in (0, 1)]
+    return pl.pallas_call(
+        kernel,
+        grid=(1,),
+        in_specs=block + [block[0]] * 2,
+        out_specs=block,
+        out_shape=[jax.ShapeDtypeStruct(right.shape, BF16)] * 2,
+        input_output_aliases={0: 0, 1: 1},
+        compiler_params=pltpu.CompilerParams(vmem_limit_bytes=VMEM),
+        cost_estimate=SMALL,
+        name="add_far",
+    )(right, left, up, down)
+
+
+def pick_cache(order, cache, after):
+    def kernel(order_ref, cache_ref, *refs):
+        out, sem = refs[-2:]
+        copies = [pltpu.make_async_copy(cache_ref.at[order_ref[i]], out.at[i], sem.at[i]) for i in range(32)]
+        for c in copies:
+            c.start()
+        for c in copies:
+            c.wait()
+
+    return pl.pallas_call(
+        kernel,
+        in_specs=[IN_SMEM] + [ANY] * (1 + len(after)),
+        out_specs=ANY,
+        out_shape=jax.ShapeDtypeStruct((32,) + cache.shape[1:], BF16),
+        scratch_shapes=[pltpu.SemaphoreType.DMA((32,))],
+        cost_estimate=SMALL,
+        name="pick_cache",
+    )(order, cache, *after)
 
 
 def sum_x(own, from_left, from_right):
@@ -170,19 +208,25 @@
         out_specs=[IN_VMEM] * 2,
         out_shape=[jax.ShapeDtypeStruct((ROWS, COLS), F32), jax.ShapeDtypeStruct((ROWS, COLS), BF16)],
         compiler_params=pltpu.CompilerParams(vmem_limit_bytes=VMEM),
+        cost_estimate=SMALL,
         name="sum_x",
     )(own, from_left, from_right)
 
 
 def attend(limits, lengths, cache_at, keep, more, bias, cosine, sine, cache, kvs):
+    flat = [a for group in kvs for a in group]
+
     def kernel(
-        limit_ref, length_ref, at_ref, keep_ref, more_ref, bias_ref, cos_ref, sin_ref, cache_ref, kv_a, kv_b,
-        o_ref, buf, cbuf, qbuf, sem, csem,
+        limit_ref, length_ref, at_ref, keep_ref, more_ref, bias_ref, cos_ref, sin_ref, cache_ref, *refs
     ):
-        copies = []
-        for g in range(8):
-            kv = (kv_a, kv_b)[g // 4]
-            mine = [pltpu.make_async_copy(kv.at[limit_ref[32 + g % 4]], buf.at[pl.ds(4 * g, 4)], sem.at[g])]
+        o_ref, buf, cbuf, qbuf, sem, csem = refs[len(flat) :]
+        copies, k = [], 0
+        for g, group in enumerate(kvs):
+            mine, slot = [], 4 * g
+            for a in group:
+                n = a.shape[0]
+                mine.append(pltpu.make_async_copy(refs[k], buf.at[pl.ds(slot, n)], sem.at[k]))
+                slot, k = slot + n, k + 1
             for p in range(4 * g, 4 * g + 4):
                 mine.append(pltpu.make_async_copy(cache_ref.at[at_ref[p]], cbuf.at[p], csem.at[p]))
             copies.append(mine)
@@ -253,22 +297,20 @@
 
     return pl.pallas_call(
         kernel,
-        in_specs=[IN_SMEM] * 3 + [IN_VMEM] * 5 + [ANY] * 3,
+        in_specs=[IN_SMEM] * 3 + [IN_VMEM] * 5 + [ANY] * (1 + len(flat)),
         out_specs=IN_VMEM,
         out_shape=jax.ShapeDtypeStruct((32, 4, COLS), BF16),
         scratch_shapes=[
             pltpu.VMEM((32, 512, 2 * HD), BF16),
             pltpu.VMEM((32, 64, 2 * HD), BF16),
             pltpu.VMEM((1024, HD), F32),
-            pltpu.SemaphoreType.DMA((8,)),
+            pltpu.SemaphoreType.DMA((len(flat),)),
             pltpu.SemaphoreType.DMA((32,)),
         ],
         compiler_params=pltpu.CompilerParams(vmem_limit_bytes=VMEM),
-        cost_estimate=pl.CostEstimate(
-            flops=32 * 32 * 600 * 512, bytes_accessed=10 * 2**20, transcendentals=32 * 32 * 600
-        ),
+        cost_estimate=SMALL,
         name="attend",
-    )(limits, lengths, cache_at, keep, more, bias, cosine, sine, cache, *kvs)
+    )(limits, lengths, cache_at, keep, more, bias, cosine, sine, cache, *flat)
 
 
 def on_device(
@@ -290,11 +332,11 @@
     tp_y, tp_x = tp // 4, tp % 4
     pos = positions.reshape(prompts)
 
-    z_groups = [[(y * 4 + z) * 2 + c for z in range(4)] for y in range(2) for c in range(2)]
-    own_core = lax.all_gather(
-        prefix_pairs.reshape(4, 512, 2 * HD), "roll", axis=0, axis_index_groups=z_groups
-    )
-    other_core = over_roll(own_core, 0, 0, 1)
+    own = prefix_pairs.reshape(4, 512, 2 * HD)
+    below, above = over_roll(own, 0, 1, 0), over_roll(own, 0, 3, 0)
+    far_a, far_b = over_roll(below[:2], 0, 1, 0), over_roll(above[2:], 0, 3, 0)
+    kvs = [[own], [below], [above], [far_a, far_b]]
+    kvs = kvs + [[over_roll(a, 0, 0, 1) for a in group] for group in kvs]
 
     sorted_t, sorted_g = sort_rows(
         jnp.stack([my_y, my_z, my_c]).astype(jnp.int32),
@@ -306,7 +348,7 @@
 
     index = jnp.arange(prompts, dtype=jnp.int32)
     half, quarter = jnp.arange(2, dtype=jnp.int32), jnp.arange(4, dtype=jnp.int32)
-    y_of, c_of, z_of = (1 - half + my_y) % 2, (half + my_c) % 2, (quarter + my_z) % 4
+    y_of, c_of, z_of = (1 - half + my_y) % 2, (half + my_c) % 2, (jnp.array([0, 3, 1, 2], jnp.int32) + my_z) % 4
     slot = (
         ((y_of[:, None, None, None] * 4 + z_of[None, None, :, None]) * 2 + c_of[None, :, None, None]) * 4
         + quarter[None, None, None, :]
@@ -314,12 +356,11 @@
     hit = owner_slot[None, :] == slot[:, None]
     order = jnp.sum(jnp.where(hit, index[None, :], 0), 1)
     limits = BLOCK * jnp.sum(jnp.where(hit[32:], prefix_blocks[None, :], 0), 1)
-    limits = jnp.concatenate([limits, z_of])
     pos_g = jnp.sum(jnp.where(hit[32:], pos[None, :], 0), 1)
     pos_t = swapped[::4, width].astype(jnp.int32)
 
     cache = cache_pairs.reshape(prompts, 64, 2 * HD)
-    cache_t = over_roll(cache.at[order[:32]].get(mode="promise_in_bounds"), 1, 0, 0)
+    cache_t = over_roll(pick_cache(order, cache, (below, above)), 1, 0, 0)
 
     def heads(*pairs):
         return jnp.stack([(tp_y + dy) % 2 * 4 + (tp_x + dx) % 4 for dy, dx in pairs]).astype(jnp.int32)
@@ -334,8 +375,7 @@
 
     def reduce(up, down, right, left, own):
         up, down = over_tp(up, 0, 1), over_tp(down, 0, 3)
-        right = right.at[0].add(up[0])
-        left = left.at[1].add(down[0])
+        right, left = add_far(right, left, up, down)
         keep, send = sum_x(own, over_tp(right, 0, 1), over_tp(left, 0, 3))
         return keep, over_tp(send, 1, 0)
 
@@ -346,13 +386,13 @@
     bias = jnp.concatenate([query_bias, pair_bias]).astype(F32)[None]
 
     def rows(full, where, cache_at, cache):
-        at = (limits[:32, None] + where[:, None] + jnp.arange(new, dtype=jnp.int32)).reshape(ROWS)
+        at = (limits[:, None] + where[:, None] + jnp.arange(new, dtype=jnp.int32)).reshape(ROWS)
         angles = at.astype(F32)[:, None] * frequency[None, :]
         cosine, sine = jnp.cos(angles), jnp.sin(angles)
         cosine = jnp.concatenate([cosine, cosine], 1)
         sine = jnp.concatenate([-sine, sine], 1)
         return attend(
-            limits, where, cache_at, *full, bias, cosine, sine, cache, (own_core, other_core)
+            limits, where, cache_at, *full, bias, cosine, sine, cache, kvs
         )
 
     back = over_roll(rows(full_t, pos_t, index[:32], cache_t), 1, 0, 0)

time: 164 us -> 164 us (level)
  Pallas kernels: 40 us -> 76.6 us
  waiting for transfers between devices: 72.4 us -> 36.7 us
  between operations: 14.4 us -> 1.01 us
  local copies, waits for them, and re-layouts: 5.88 us -> 15.3 us
  starting transfers between devices: 22.2 us -> 30.7 us
  other arithmetic: 8.58 us -> 3.13 us
    pallas_call x2 -> x5, Pallas kernels: 15.9 us -> 52.7 us  [the longest x1 33.8 us: pick_cache(): pl.pallas_call(kernel, in_specs=[IN_SMEM] + [ANY] * (1 + len(after)), out...]
    all_gather x1 -> x0, waiting for transfers between devices: 35.4 us -> none  [on_device(): lax.all_gather(prefix_pairs.reshape(4, 512, 2 * HD), 'roll', axis=0, axis...]
    ppermute x4 -> x12, waiting for transfers between devices: 0.01 us -> 9.07 us  [over_roll(): return lax.ppermute(a, 'roll', roll_shift(dy, dz, dc))]
    ppermute x4 -> x12, starting transfers between devices: 6.41 us -> 15.4 us  [over_roll(): return lax.ppermute(a, 'roll', roll_shift(dy, dz, dc))]
    ppermute x10, waiting for transfers between devices: 36.4 us -> 27.6 us  [over_tp(): return lax.ppermute(a, 'tp', tp_shift(dy, dx))]
    unnamed x20 -> x38, local copies, waits for them, and re-layouts: 1.57 us -> 8.83 us
    scatter-add x4 -> x0, other arithmetic: 5.78 us -> none  [the longest x2 3.75 us: reduce(): right = right.at[0].add(up[0])]
    slice x0 -> x3, local copies, waits for them, and re-layouts: none -> 3.83 us  [the longest x1 1.89 us: on_device(): above[2:]]
  transfers between devices with their start and end apart: 15 -> 22, of which waited for: 4 -> 5; matrix products, arithmetic and copies ran while one was open for 8% -> 6% of each run, Pallas kernels for 24% -> 46%
where the time goes in v4:
time: 164 us; the launch traced here: 163 us
  Pallas kernels  76.6 us (47%)
  waiting for transfers between devices  36.7 us (22%)
  starting transfers between devices  30.7 us (19%)
  local copies, waits for them, and re-layouts  15.3 us (9%)
  other arithmetic  3.13 us (2%)
    pallas_call x1, Pallas kernels, pick_cache(): pl.pallas_call(kernel, in_specs=[IN_SMEM] + [ANY] * (1 + len(after)), out...  33.8 us
    ppermute x10, waiting for transfers between devices, over_tp(): return lax.ppermute(a, 'tp', tp_shift(dy, dx))  27.6 us
    pallas_call x4, Pallas kernels, project(): pl.pallas_call(kernel, in_specs=[IN_SMEM] + [IN_VMEM] * len(xs) + [ANY, A...  19.3 us
    ppermute x12, starting transfers between devices, over_roll(): return lax.ppermute(a, 'roll', roll_shift(dy, dz, dc))  15.4 us
    ppermute x10, starting transfers between devices, over_tp(): return lax.ppermute(a, 'tp', tp_shift(dy, dx))  15.3 us
    pallas_call x2, Pallas kernels, attend(): pl.pallas_call(kernel, in_specs=[IN_SMEM] * 3 + [IN_VMEM] * 5 + [ANY] * (...  15.3 us
    ppermute x12, waiting for transfers between devices, over_roll(): return lax.ppermute(a, 'roll', roll_shift(dy, dz, dc))  9.07 us
    unnamed x38, local copies, waits for them, and re-layouts  8.83 us
  transfers between devices with their start and end apart: 22, of which 5 were waited for; matrix products, arithmetic and copies ran while one was open for 6% of the time, Pallas kernels for 46%

profile of v4, /device:TPU:0, one launch (start us, length us, event | category | flops | bytes accessed | tf_op | source)
XLA Modules:
  0.0 163.4 jit_solution(1293600789046513446)
XLA Ops:
  0.6 2.1 %collective-permute-start.6 = (bf16[4,512,256]{2,1,0:T(8,128)(2,1)}, bf16[4,512,256]{2,1,0:T(8,128)(2,1)}, u32[]{:S(2)}, u32[]{:S(2)}) collective-permute-start(bf16[4,512,256]{2,1,0:T(8,128)(2,1)} %bitcast.14.refs_0_), channel_id=1, source_target_pairs={{0,16},{8,24},{16,32},{24,40},{32,48},{40,56},{48,0},{56,8},{64,80... | collective-permute-start | bytes 3145736 | tf_op jit(solution)/shard_map/ppermute | solution.py:43
  2.7 2.2 %collective-permute-start.7 = (bf16[4,512,256]{2,1,0:T(8,128)(2,1)}, bf16[4,512,256]{2,1,0:T(8,128)(2,1)}, u32[]{:S(2)}, u32[]{:S(2)}) collective-permute-start(bf16[4,512,256]{2,1,0:T(8,128)(2,1)} %bitcast.14.refs_0_), channel_id=1, source_target_pairs={{0,48},{8,56},{16,0},{24,8},{32,16},{40,24},{48,32},{56,40},{64,11... | collective-permute-start | bytes 3145736 | tf_op jit(solution)/shard_map/ppermute | solution.py:43
  4.9 1.2 reshape.210.x_ref
  6.1 0.7 bitcast_convert_fusion
  6.9 0.7 broadcast_in_dim.58
  7.9 0.9 sort_rows.1
  8.8 3.6 %project.7 = (bf16[1,128,1280]{2,1,0:T(8,128)(2,1)S(1)}, bf16[1,128,1280]{2,1,0:T(8,128)(2,1)S(1)}) custom-call(s32[2]{0:T(128)S(1)} %pad_add_fusion.3.heads_ref, bf16[128,1152]{1,0:T(8,128)(2,1)S(1)} %get-tuple-element.25.refs_1_.refs_0_, bf16[1024,8192]{1,0:T(8,128)(2,1)} %refs_1_.3, bf16[1024,2048]{1,0:T(8,128)(2,1)} %refs_2_.7), custom_call_target="tpu_custom_call" | custom-call | flops 1000000 | bytes 100000 | tf_op jit(solution)/shard_map/project/pallas_call | solution.py:91
  12.5 1.6 collective-permute-start.17
  14.1 1.7 %collective-permute-start.18 = (bf16[1,128,1280]{2,1,0:T(8,128)(2,1)S(1)}, bf16[1,128,1280]{2,1,0:T(8,128)(2,1)S(1)}, u32[]{:S(2)}, u32[]{:S(2)}) collective-permute-start(bf16[1,128,1280]{2,1,0:T(8,128)(2,1)S(1)} %get-tuple-element.39), channel_id=1, source_target_pairs={{0,3},{1,0},{2,1},{3,2},{4,7},{5,4},{6,5},{7,6},{8,11},{9,8},{10,9... | collective-permute-start | bytes 983048 | tf_op jit(solution)/shard_map/ppermute | solution.py:39
  15.8 3.2 %collective-permute-start = (bf16[128,1152]{1,0:T(8,128)(2,1)S(1)}, bf16[128,1152]{1,0:T(8,128)(2,1)S(1)}, u32[]{:S(2)}, u32[]{:S(2)}) collective-permute-start(bf16[128,1152]{1,0:T(8,128)(2,1)S(1)} %get-tuple-element.24), channel_id=1, source_target_pairs={{0,64},{8,72},{16,80},{24,88},{32,96},{40,104},{48,112},{56,120},{... | collective-permute-start | bytes 884744 | tf_op jit(solution)/shard_map/ppermute | solution.py:43
  19.2 6.1 %collective-permute-done.refs_0_ = bf16[128,1152]{1,0:T(8,128)(2,1)S(1)} collective-permute-done((bf16[128,1152]{1,0:T(8,128)(2,1)S(1)}, bf16[128,1152]{1,0:T(8,128)(2,1)S(1)}, u32[]{:S(2)}, u32[]{:S(2)}) %collective-permute-start) | collective-permute-done | bytes 294944 | tf_op jit(solution)/shard_map/ppermute | solution.py:43
  25.2 4.4 %project.6 = (bf16[1,128,1280]{2,1,0:T(8,128)(2,1)S(1)}, bf16[1,128,1280]{2,1,0:T(8,128)(2,1)}) custom-call(s32[2]{0:T(128)S(1)} %pad_add_fusion.3.heads_ref, bf16[128,1152]{1,0:T(8,128)(2,1)S(1)} %collective-permute-done.refs_0_, bf16[1024,8192]{1,0:T(8,128)(2,1)} %refs_1_.3, bf16[1024,2048]{1,0:T(8,128)(2,1)} %refs_2_.7), custom_call_target="tpu_custom_call" | custom-call | flops 1000000 | bytes 100000 | tf_op jit(solution)/shard_map/project/pallas_call | solution.py:91
  30.0 7.0 %project.5 = (bf16[2,128,1280]{2,1,0:T(8,128)(2,1)S(1)}, bf16[2,128,1280]{2,1,0:T(8,128)(2,1)}, bf16[2,128,1280]{2,1,0:T(8,128)(2,1)}, bf16[2,128,1280]{2,1,0:T(8,128)(2,1)S(1)}) custom-call(s32[4]{0:T(128)S(1)} %pad_add_fusion.2.heads_ref, bf16[128,1152]{1,0:T(8,128)(2,1)S(1)} %collective-permute-done.refs_0_, ...), custom_call_target="tpu_custom_call" | custom-call | flops 1000000 | bytes 100000 | tf_op jit(solution)/shard_map/project/pallas_call | solution.py:91
  37.2 1.8 %add_far.3 = (bf16[2,128,1280]{2,1,0:T(8,128)(2,1)}, bf16[2,128,1280]{2,1,0:T(8,128)(2,1)S(1)}) custom-call(bf16[2,128,1280]{2,1,0:T(8,128)(2,1)} %get-tuple-element.36.r, bf16[2,128,1280]{2,1,0:T(8,128)(2,1)S(1)} %get-tuple-element.37.l, bf16[1,128,1280]{2,1,0:T(8,128)(2,1)S(1)} %collective-permute-done.17.u, ...), custom_call_target="tpu_custom_call", output_to_operand_aliasing={{0}: (0, {}), {1}: (1, {})} | custom-call | flops 1000000 | bytes 100000 | tf_op jit(solution)/shard_map/add_far/pallas_call | solution.py:167
  39.0 1.5 collective-permute-start.19
  40.6 0.7 copy-done.10
  41.3 1.7 %collective-permute-start.2 = (bf16[1,128,1280]{2,1,0:T(8,128)(2,1)}, bf16[1,128,1280]{2,1,0:T(8,128)(2,1)S(1)}, u32[]{:S(2)}, u32[]{:S(2)}) collective-permute-start(bf16[1,128,1280]{2,1,0:T(8,128)(2,1)} %get-tuple-element.30), channel_id=1, source_target_pairs={{0,3},{1,0},{2,1},{3,2},{4,7},{5,4},{6,5},{7,6},{8,11},{9,8},{10,9... | collective-permute-start | bytes 983048 | tf_op jit(solution)/shard_map/ppermute | solution.py:39
  43.3 8.0 %collective-permute-done.2.d = bf16[1,128,1280]{2,1,0:T(8,128)(2,1)S(1)} collective-permute-done((bf16[1,128,1280]{2,1,0:T(8,128)(2,1)}, bf16[1,128,1280]{2,1,0:T(8,128)(2,1)S(1)}, u32[]{:S(2)}, u32[]{:S(2)}) %collective-permute-start.2) | collective-permute-done | bytes 327712 | tf_op jit(solution)/shard_map/ppermute | solution.py:39
  51.3 3.0 %collective-permute-start.20 = (bf16[2,128,1280]{2,1,0:T(8,128)(2,1)}, bf16[2,128,1280]{2,1,0:T(8,128)(2,1)S(1)}, u32[]{:S(2)}, u32[]{:S(2)}) collective-permute-start(bf16[2,128,1280]{2,1,0:T(8,128)(2,1)} %copy-done.7), channel_id=1, source_target_pairs={{0,3},{1,0},{2,1},{3,2},{4,7},{5,4},{6,5},{7,6},{8,11},{9,8},{10,9... | collective-permute-start | bytes 1966088 | tf_op jit(solution)/shard_map/ppermute | solution.py:39
  54.4 1.0 copy-done.11
  55.3 1.8 %add_far.2 = (bf16[2,128,1280]{2,1,0:T(8,128)(2,1)S(1)}, bf16[2,128,1280]{2,1,0:T(8,128)(2,1)}) custom-call(bf16[2,128,1280]{2,1,0:T(8,128)(2,1)S(1)} %get-tuple-element.27.r, bf16[2,128,1280]{2,1,0:T(8,128)(2,1)} %get-tuple-element.28.l, bf16[1,128,1280]{2,1,0:T(8,128)(2,1)S(1)} %copy-done.11, ...), custom_call_target="tpu_custom_call", output_to_operand_aliasing={{0}: (0, {}), {1}: (1, {})} | custom-call | flops 1000000 | bytes 100000 | tf_op jit(solution)/shard_map/add_far/pallas_call | solution.py:167
  57.5 0.4 copy-done.6
  58.0 3.2 %collective-permute-start.4 = (bf16[2,128,1280]{2,1,0:T(8,128)(2,1)}, bf16[2,128,1280]{2,1,0:T(8,128)(2,1)}, u32[]{:S(2)}, u32[]{:S(2)}) collective-permute-start(bf16[2,128,1280]{2,1,0:T(8,128)(2,1)} %get-tuple-element.32), channel_id=1, source_target_pairs={{0,3},{1,0},{2,1},{3,2},{4,7},{5,4},{6,5},{7,6},{8,11},{9,8},{10,9... | collective-permute-start | bytes 1966088 | tf_op jit(solution)/shard_map/ppermute | solution.py:39
  61.3 1.9 %slice.26 = bf16[2,512,256]{2,1,0:T(8,128)(2,1)} slice(bf16[4,512,256]{2,1,0:T(8,128)(2,1)} %collective-permute-done.6.refs_0_.refs_1_), slice={[0:2], [0:512], [0:256]} | slice | bytes 1048576 | tf_op jit(solution)/shard_map/slice | solution.py:337
  63.2 0.7 select_reduce_fusion.order_ref
  64.0 1.9 %slice.27 = bf16[2,512,256]{2,1,0:T(8,128)(2,1)} slice(bf16[4,512,256]{2,1,0:T(8,128)(2,1)} %collective-permute-done.7.refs_1_.refs_2_), slice={[2:4], [0:512], [0:256]} | slice | bytes 1048576 | tf_op jit(solution)/shard_map/slice | solution.py:337
  65.9 33.8 %pick_cache.1 = bf16[32,64,256]{2,1,0:T(8,128)(2,1)} custom-call(s32[64]{0:T(128)} %select_reduce_fusion.order_ref, bf16[64,64,256]{2,1,0:T(8,128)(2,1)} %bitcast.25, bf16[4,512,256]{2,1,0:T(8,128)(2,1)} %collective-permute-done.6.refs_0_.refs_1_, bf16[4,512,256]{2,1,0:T(8,128)(2,1)} %collective-permute-done.7.refs_1_.refs_2_), custom_call_target="tpu_custom_call" | custom-call | flops 1000000 | bytes 100000 | tf_op jit(solution)/shard_map/pick_cache/pallas_call | solution.py:189
  99.7 0.9 copy-done
  100.6 3.2 %collective-permute-start.10 = (bf16[2,512,256]{2,1,0:T(8,128)(2,1)}, bf16[2,512,256]{2,1,0:T(8,128)(2,1)S(1)}, u32[]{:S(2)}, u32[]{:S(2)}) collective-permute-start(bf16[2,512,256]{2,1,0:T(8,128)(2,1)} %slice.27), channel_id=1, source_target_pairs={{0,48},{8,56},{16,0},{24,8},{32,16},{40,24},{48,32},{56,40},{64,11... | collective-permute-start | bytes 1572872 | tf_op jit(solution)/shard_map/ppermute | solution.py:43
  103.8 3.2 %collective-permute-start.8 = (bf16[32,64,256]{2,1,0:T(8,128)(2,1)}, bf16[32,64,256]{2,1,0:T(8,128)(2,1)}, u32[]{:S(2)}, u32[]{:S(2)}) collective-permute-start(bf16[32,64,256]{2,1,0:T(8,128)(2,1)} %pick_cache.1), channel_id=1, source_target_pairs={{0,64},{8,72},{16,80},{24,88},{32,96},{40,104},{48,112},{56,120},{... | collective-permute-start | bytes 3145736 | tf_op jit(solution)/shard_map/ppermute | solution.py:43
  107.1 0.5 collective-permute-start.13
  107.9 4.2 %project.4 = (bf16[2,128,1280]{2,1,0:T(8,128)(2,1)S(1)}, bf16[2,128,1280]{2,1,0:T(8,128)(2,1)S(1)}) custom-call(s32[2]{0:T(128)S(1)} %pad_add_fusion.1.heads_ref, bf16[128,1152]{1,0:T(8,128)(2,1)S(1)} %collective-permute-done.refs_0_, bf16[128,1152]{1,0:T(8,128)(2,1)S(1)} %get-tuple-element.25.refs_1_.refs_0_, bf16[1024,8192]{1,0:T(8,128)(2,1)} %refs_1_.3, ...), custom_call_target="tpu_custom_call" | custom-call | flops 1000000 | bytes 100000 | tf_op jit(solution)/shard_map/project/pallas_call | solution.py:91
  112.1 0.8 copy-done.4
  113.0 1.1 copy-done.3
  114.1 2.0 %sum_x.2 = (f32[128,1280]{1,0:T(8,128)S(1)}, bf16[128,1280]{1,0:T(8,128)(2,1)}) custom-call(bf16[2,128,1280]{2,1,0:T(8,128)(2,1)S(1)} %get-tuple-element.26.a, bf16[2,128,1280]{2,1,0:T(8,128)(2,1)S(1)} %copy-done.3, bf16[2,128,1280]{2,1,0:T(8,128)(2,1)} %collective-permute-done.4.c), custom_call_target="tpu_custom_call" | custom-call | flops 1000000 | bytes 100000 | tf_op jit(solution)/shard_map/sum_x/pallas_call | solution.py:205
  116.0 0.7 collective-permute-start.5
  117.0 19.2 %collective-permute-done.5.more_ref = bf16[128,1280]{1,0:T(8,128)(2,1)S(1)} collective-permute-done((bf16[128,1280]{1,0:T(8,128)(2,1)}, bf16[128,1280]{1,0:T(8,128)(2,1)S(1)}, u32[]{:S(2)}, u32[]{:S(2)}) %collective-permute-start.5) | collective-permute-done | bytes 327712 | tf_op jit(solution)/shard_map/ppermute | solution.py:39
  136.2 0.7 copy-done.8
  137.1 0.5 fusion.1
  137.7 1.1 copy-done.1
  138.8 1.1 copy-done.5
  140.1 1.4 collective-permute-start.21
  141.6 1.0 copy-done.9
  142.6 7.6 %attend.2 = bf16[32,4,1280]{2,1,0:T(4,128)(2,1)S(1)} custom-call(s32[32]{0:T(128)S(1)} %get-tuple-element.67.limit_ref, s32[32]{0:T(128)S(1)} %get-tuple-element.55.length_ref, s32[32]{0:T(128)S(1)} %bitcast.24, f32[128,1280]{1,0:T(8,128)S(1)} %get-tuple-element.33.keep_ref, bf16[128,1280]{1,0:T(8,128)(2,1)S(1)} %copy-done.9, ...), custom_call_target="tpu_custom_call" | custom-call | flops 1000000 | bytes 100000 | tf_op jit(solution)/shard_map/attend/pallas_call | solution.py:298
  150.2 0.8 collective-permute-start.16
  151.2 7.6 %attend.3.b_ref = bf16[32,4,1280]{2,1,0:T(4,128)(2,1)S(1)} custom-call(s32[32]{0:T(128)S(1)} %get-tuple-element.67.limit_ref, s32[32]{0:T(128)S(1)} %get-tuple-element.52.length_ref, s32[32]{0:T(128)S(1)} %slice.24.at_ref, f32[128,1280]{1,0:T(8,128)S(1)} %get-tuple-element.42.keep_ref, bf16[128,1280]{1,0:T(8,128)(2,1)S(1)} %collective-permute-done.21.more_ref, ...), custom_call_target="tpu_custom_call" | custom-call | flops 1000000 | bytes 100000 | tf_op jit(solution)/shard_map/attend/pallas_call | solution.py:298
  158.9 3.0 %collective-permute-done.16.a_ref = bf16[32,4,1280]{2,1,0:T(4,128)(2,1)S(1)} collective-permute-done((bf16[32,4,1280]{2,1,0:T(4,128)(2,1)S(1)}, bf16[32,4,1280]{2,1,0:T(4,128)(2,1)S(1)}, u32[]{:S(2)}, u32[]{:S(2)}) %collective-permute-start.16) | collective-permute-done | bytes 327712 | tf_op jit(solution)/shard_map/ppermute | solution.py:43
  161.9 1.5 place_rows.1
  (86 shorter events, 3.3 us)
Async XLA Ops:
  0.6 57.3 %collective-permute-start.6 = (bf16[4,512,256]{2,1,0:T(8,128)(2,1)}, bf16[4,512,256]{2,1,0:T(8,128)(2,1)}, u32[]{:S(2)}, u32[]{:S(2)}) collective-permute-start(bf16[4,512,256]{2,1,0:T(8,128)(2,1)} %bitcast.14.refs_0_), channel_id=1, source_target_pairs={{0,16},{8,24},{16,32},{24,40},{32,48},{40,56},{48,0},{56,8},{64,80... | collective-permute-start | bytes 3145736 | tf_op jit(solution)/shard_map/ppermute | solution.py:43
  2.7 60.5 %collective-permute-start.7 = (bf16[4,512,256]{2,1,0:T(8,128)(2,1)}, bf16[4,512,256]{2,1,0:T(8,128)(2,1)}, u32[]{:S(2)}, u32[]{:S(2)}) collective-permute-start(bf16[4,512,256]{2,1,0:T(8,128)(2,1)} %bitcast.14.refs_0_), channel_id=1, source_target_pairs={{0,48},{8,56},{16,0},{24,8},{32,16},{40,24},{48,32},{56,40},{64,11... | collective-permute-start | bytes 3145736 | tf_op jit(solution)/shard_map/ppermute | solution.py:43
  8.8 10.2 %copy-start.18 = (s32[4]{0:T(128)S(1)}, s32[4]{0:T(128)}, u32[]{:S(2)}) copy-start(s32[4]{0:T(128)} %constant.143.clone) | copy-start | bytes 52
  12.5 24.6 %collective-permute-start.17 = (bf16[1,128,1280]{2,1,0:T(8,128)(2,1)S(1)}, bf16[1,128,1280]{2,1,0:T(8,128)(2,1)S(1)}, u32[]{:S(2)}, u32[]{:S(2)}) collective-permute-start(bf16[1,128,1280]{2,1,0:T(8,128)(2,1)S(1)} %get-tuple-element.38), channel_id=1, source_target_pairs={{0,1},{1,2},{2,3},{3,0},{4,5},{5,6},{6,7},{7,4},{8,9},{9,10},{10,1... | collective-permute-start | bytes 983048 | tf_op jit(solution)/shard_map/ppermute | solution.py:39
  14.1 23.1 %collective-permute-start.18 = (bf16[1,128,1280]{2,1,0:T(8,128)(2,1)S(1)}, bf16[1,128,1280]{2,1,0:T(8,128)(2,1)S(1)}, u32[]{:S(2)}, u32[]{:S(2)}) collective-permute-start(bf16[1,128,1280]{2,1,0:T(8,128)(2,1)S(1)} %get-tuple-element.39), channel_id=1, source_target_pairs={{0,3},{1,0},{2,1},{3,2},{4,7},{5,4},{6,5},{7,6},{8,11},{9,8},{10,9... | collective-permute-start | bytes 983048 | tf_op jit(solution)/shard_map/ppermute | solution.py:39
  15.8 9.4 %collective-permute-start = (bf16[128,1152]{1,0:T(8,128)(2,1)S(1)}, bf16[128,1152]{1,0:T(8,128)(2,1)S(1)}, u32[]{:S(2)}, u32[]{:S(2)}) collective-permute-start(bf16[128,1152]{1,0:T(8,128)(2,1)S(1)} %get-tuple-element.24), channel_id=1, source_target_pairs={{0,64},{8,72},{16,80},{24,88},{32,96},{40,104},{48,112},{56,120},{... | collective-permute-start | bytes 884744 | tf_op jit(solution)/shard_map/ppermute | solution.py:43
  29.6 10.9 %collective-permute-start.1 = (bf16[1,128,1280]{2,1,0:T(8,128)(2,1)S(1)}, bf16[1,128,1280]{2,1,0:T(8,128)(2,1)S(1)}, u32[]{:S(2)}, u32[]{:S(2)}) collective-permute-start(bf16[1,128,1280]{2,1,0:T(8,128)(2,1)S(1)} %get-tuple-element.29), channel_id=1, source_target_pairs={{0,1},{1,2},{2,3},{3,0},{4,5},{5,6},{6,7},{7,4},{8,9},{9,10},{10,1... | collective-permute-start | bytes 983048 | tf_op jit(solution)/shard_map/ppermute | solution.py:39
  30.0 13.2 %copy-start.13 = (s32[64]{0:T(128)S(1)}, s32[64]{0:T(128)}, u32[]{:S(2)}) copy-start(s32[64]{0:T(128)} %param.18) | copy-start | bytes 772
  30.0 31.2 %copy-start.15 = (s32[64,1]{0,1:T(1,128)S(1)}, s32[64,1]{0,1:T(1,128)}, u32[]{:S(2)}) copy-start(s32[64,1]{0,1:T(1,128)} %param.20) | copy-start | bytes 772
  30.0 31.2 %copy-start.16 = (s32[64]{0:T(128)S(1)}, s32[64]{0:T(128)}, u32[]{:S(2)}) copy-start(s32[64]{0:T(128)} %param.19) | copy-start | bytes 772
  37.1 66.8 %collective-permute-start.11 = (bf16[4,512,256]{2,1,0:T(8,128)(2,1)}, bf16[4,512,256]{2,1,0:T(8,128)(2,1)}, u32[]{:S(2)}, u32[]{:S(2)}) collective-permute-start(bf16[4,512,256]{2,1,0:T(8,128)(2,1)} %bitcast.14.refs_0_), channel_id=1, source_target_pairs={{0,8},{8,0},{16,24},{24,16},{32,40},{40,32},{48,56},{56,48},{64,72... | collective-permute-start | bytes 3145736 | tf_op jit(solution)/shard_map/ppermute | solution.py:43
  39.0 12.3 %copy-start.7 = (bf16[2,128,1280]{2,1,0:T(8,128)(2,1)}, bf16[2,128,1280]{2,1,0:T(8,128)(2,1)S(1)}, u32[]{:S(2)}) copy-start(bf16[2,128,1280]{2,1,0:T(8,128)(2,1)S(1)} %get-tuple-element.41) | copy-start | bytes 1966084
  39.0 18.5 %collective-permute-start.19 = (bf16[2,128,1280]{2,1,0:T(8,128)(2,1)}, bf16[2,128,1280]{2,1,0:T(8,128)(2,1)S(1)}, u32[]{:S(2)}, u32[]{:S(2)}) collective-permute-start(bf16[2,128,1280]{2,1,0:T(8,128)(2,1)} %get-tuple-element.40), channel_id=1, source_target_pairs={{0,1},{1,2},{2,3},{3,0},{4,5},{5,6},{6,7},{7,4},{8,9},{9,10},{10,1... | collective-permute-start | bytes 1966088 | tf_op jit(solution)/shard_map/ppermute | solution.py:39
  40.6 0.7 copy-start.10
  41.3 10.0 %collective-permute-start.2 = (bf16[1,128,1280]{2,1,0:T(8,128)(2,1)}, bf16[1,128,1280]{2,1,0:T(8,128)(2,1)S(1)}, u32[]{:S(2)}, u32[]{:S(2)}) collective-permute-start(bf16[1,128,1280]{2,1,0:T(8,128)(2,1)} %get-tuple-element.30), channel_id=1, source_target_pairs={{0,3},{1,0},{2,1},{3,2},{4,7},{5,4},{6,5},{7,6},{8,11},{9,8},{10,9... | collective-permute-start | bytes 983048 | tf_op jit(solution)/shard_map/ppermute | solution.py:39
  51.3 48.4 %collective-permute-start.20 = (bf16[2,128,1280]{2,1,0:T(8,128)(2,1)}, bf16[2,128,1280]{2,1,0:T(8,128)(2,1)S(1)}, u32[]{:S(2)}, u32[]{:S(2)}) collective-permute-start(bf16[2,128,1280]{2,1,0:T(8,128)(2,1)} %copy-done.7), channel_id=1, source_target_pairs={{0,3},{1,0},{2,1},{3,2},{4,7},{5,4},{6,5},{7,6},{8,11},{9,8},{10,9... | collective-permute-start | bytes 1966088 | tf_op jit(solution)/shard_map/ppermute | solution.py:39
  54.4 1.0 copy-start.11
  57.1 0.8 copy-start.6
  57.1 50.6 %copy-start.14 = (bf16[1024]{0:T(1024)(128)(2,1)S(1)}, bf16[1024]{0:T(1024)(128)(2,1)}, u32[]{:S(2)}) copy-start(bf16[1024]{0:T(1024)(128)(2,1)} %param.13) | copy-start | bytes 6148
  57.1 50.7 %copy-start.17 = (bf16[256]{0:T(256)(128)(2,1)S(1)}, bf16[256]{0:T(256)(128)(2,1)}, u32[]{:S(2)}) copy-start(bf16[256]{0:T(256)(128)(2,1)} %param.15) | copy-start | bytes 1540
  58.0 49.1 %collective-permute-start.3 = (bf16[2,128,1280]{2,1,0:T(8,128)(2,1)}, bf16[2,128,1280]{2,1,0:T(8,128)(2,1)S(1)}, u32[]{:S(2)}, u32[]{:S(2)}) collective-permute-start(bf16[2,128,1280]{2,1,0:T(8,128)(2,1)} %copy-done.6), channel_id=1, source_target_pairs={{0,1},{1,2},{2,3},{3,0},{4,5},{5,6},{6,7},{7,4},{8,9},{9,10},{10,1... | collective-permute-start | bytes 1966088 | tf_op jit(solution)/shard_map/ppermute | solution.py:39
  58.0 49.1 %collective-permute-start.4 = (bf16[2,128,1280]{2,1,0:T(8,128)(2,1)}, bf16[2,128,1280]{2,1,0:T(8,128)(2,1)}, u32[]{:S(2)}, u32[]{:S(2)}) collective-permute-start(bf16[2,128,1280]{2,1,0:T(8,128)(2,1)} %get-tuple-element.32), channel_id=1, source_target_pairs={{0,3},{1,0},{2,1},{3,2},{4,7},{5,4},{6,5},{7,6},{8,11},{9,8},{10,9... | collective-permute-start | bytes 1966088 | tf_op jit(solution)/shard_map/ppermute | solution.py:39
  63.2 52.9 %collective-permute-start.9 = (bf16[2,512,256]{2,1,0:T(8,128)(2,1)}, bf16[2,512,256]{2,1,0:T(8,128)(2,1)S(1)}, u32[]{:S(2)}, u32[]{:S(2)}) collective-permute-start(bf16[2,512,256]{2,1,0:T(8,128)(2,1)} %slice.26), channel_id=1, source_target_pairs={{0,16},{8,24},{16,32},{24,40},{32,48},{40,56},{48,0},{56,8},{64,80... | collective-permute-start | bytes 1572872 | tf_op jit(solution)/shard_map/ppermute | solution.py:43
  99.7 0.9 copy-start
  100.6 16.3 %collective-permute-start.10 = (bf16[2,512,256]{2,1,0:T(8,128)(2,1)}, bf16[2,512,256]{2,1,0:T(8,128)(2,1)S(1)}, u32[]{:S(2)}, u32[]{:S(2)}) collective-permute-start(bf16[2,512,256]{2,1,0:T(8,128)(2,1)} %slice.27), channel_id=1, source_target_pairs={{0,48},{8,56},{16,0},{24,8},{32,16},{40,24},{48,32},{56,40},{64,11... | collective-permute-start | bytes 1572872 | tf_op jit(solution)/shard_map/ppermute | solution.py:43
  103.8 37.7 %collective-permute-start.8 = (bf16[32,64,256]{2,1,0:T(8,128)(2,1)}, bf16[32,64,256]{2,1,0:T(8,128)(2,1)}, u32[]{:S(2)}, u32[]{:S(2)}) collective-permute-start(bf16[32,64,256]{2,1,0:T(8,128)(2,1)} %pick_cache.1), channel_id=1, source_target_pairs={{0,64},{8,72},{16,80},{24,88},{32,96},{40,104},{48,112},{56,120},{... | collective-permute-start | bytes 3145736 | tf_op jit(solution)/shard_map/ppermute | solution.py:43
  107.0 5.1 %copy-start.2 = (bf16[2,128,1280]{2,1,0:T(8,128)(2,1)}, bf16[2,128,1280]{2,1,0:T(8,128)(2,1)S(1)}, u32[]{:S(2)}) copy-start(bf16[2,128,1280]{2,1,0:T(8,128)(2,1)S(1)} %collective-permute-done.3.b) | copy-start | bytes 1966084
  107.0 34.5 %collective-permute-start.12 = (bf16[4,512,256]{2,1,0:T(8,128)(2,1)}, bf16[4,512,256]{2,1,0:T(8,128)(2,1)}, u32[]{:S(2)}, u32[]{:S(2)}) collective-permute-start(bf16[4,512,256]{2,1,0:T(8,128)(2,1)} %collective-permute-done.6.refs_0_.refs_1_), channel_id=1, source_target_pairs={{0,8},{8,0},{16,24},{24,16},{32,40},{40,32},{48,56},{56,48},{64,72... | collective-permute-start | bytes 3145736 | tf_op jit(solution)/shard_map/ppermute | solution.py:43
  107.1 34.5 %collective-permute-start.13 = (bf16[4,512,256]{2,1,0:T(8,128)(2,1)}, bf16[4,512,256]{2,1,0:T(8,128)(2,1)}, u32[]{:S(2)}, u32[]{:S(2)}) collective-permute-start(bf16[4,512,256]{2,1,0:T(8,128)(2,1)} %collective-permute-done.7.refs_1_.refs_2_), channel_id=1, source_target_pairs={{0,8},{8,0},{16,24},{24,16},{32,40},{40,32},{48,56},{56,48},{64,72... | collective-permute-start | bytes 3145736 | tf_op jit(solution)/shard_map/ppermute | solution.py:43
  112.1 0.8 copy-start.4
  113.0 1.1 copy-start.3
  116.0 20.1 %collective-permute-start.5 = (bf16[128,1280]{1,0:T(8,128)(2,1)}, bf16[128,1280]{1,0:T(8,128)(2,1)S(1)}, u32[]{:S(2)}, u32[]{:S(2)}) collective-permute-start(bf16[128,1280]{1,0:T(8,128)(2,1)} %get-tuple-element.34), channel_id=1, source_target_pairs={{0,4},{1,5},{2,6},{3,7},{4,0},{5,1},{6,2},{7,3},{8,12},{9,13},{10,... | collective-permute-start | bytes 983048 | tf_op jit(solution)/shard_map/ppermute | solution.py:39
  116.9 23.2 %collective-permute-start.14 = (bf16[2,512,256]{2,1,0:T(8,128)(2,1)S(1)}, bf16[2,512,256]{2,1,0:T(8,128)(2,1)S(1)}, u32[]{:S(2)}, u32[]{:S(2)}) collective-permute-start(bf16[2,512,256]{2,1,0:T(8,128)(2,1)S(1)} %collective-permute-done.9.refs_3_), channel_id=1, source_target_pairs={{0,8},{8,0},{16,24},{24,16},{32,40},{40,32},{48,56},{56,48},{64,72... | collective-permute-start | bytes 1572872 | tf_op jit(solution)/shard_map/ppermute | solution.py:43
  136.2 0.7 copy-start.8
  136.9 4.7 %collective-permute-start.15 = (bf16[2,512,256]{2,1,0:T(8,128)(2,1)S(1)}, bf16[2,512,256]{2,1,0:T(8,128)(2,1)S(1)}, u32[]{:S(2)}, u32[]{:S(2)}) collective-permute-start(bf16[2,512,256]{2,1,0:T(8,128)(2,1)S(1)} %collective-permute-done.10.refs_4_), channel_id=1, source_target_pairs={{0,8},{8,0},{16,24},{24,16},{32,40},{40,32},{48,56},{56,48},{64,72... | collective-permute-start | bytes 1572872 | tf_op jit(solution)/shard_map/ppermute | solution.py:43
  137.7 1.1 copy-start.1
  138.8 1.1 copy-start.5
  140.1 11.1 %collective-permute-start.21 = (bf16[128,1280]{1,0:T(8,128)(2,1)S(1)}, bf16[128,1280]{1,0:T(8,128)(2,1)S(1)}, u32[]{:S(2)}, u32[]{:S(2)}) collective-permute-start(bf16[128,1280]{1,0:T(8,128)(2,1)S(1)} %get-tuple-element.43), channel_id=1, source_target_pairs={{0,4},{1,5},{2,6},{3,7},{4,0},{5,1},{6,2},{7,3},{8,12},{9,13},{10,... | collective-permute-start | bytes 983048 | tf_op jit(solution)/shard_map/ppermute | solution.py:39
  141.6 1.0 copy-start.9
  142.6 8.5 %copy-start.12 = (s32[64]{0:T(128)S(1)}, s32[64]{0:T(128)}, u32[]{:S(2)}) copy-start(s32[64]{0:T(128)} %select_reduce_fusion.order_ref) | copy-start | bytes 772
  150.2 11.6 %collective-permute-start.16 = (bf16[32,4,1280]{2,1,0:T(4,128)(2,1)S(1)}, bf16[32,4,1280]{2,1,0:T(4,128)(2,1)S(1)}, u32[]{:S(2)}, u32[]{:S(2)}) collective-permute-start(bf16[32,4,1280]{2,1,0:T(4,128)(2,1)S(1)} %attend.2), channel_id=1, source_target_pairs={{0,64},{8,72},{16,80},{24,88},{32,96},{40,104},{48,112},{56,120},{... | collective-permute-start | bytes 983048 | tf_op jit(solution)/shard_map/ppermute | solution.py:43

commit v5 on v4

v5 whole, which is shorter than its diff:
```python
import math

import jax
import jax.numpy as jnp
from jax import lax
from jax.experimental import pallas as pl
from jax.experimental.pallas import tpu as pltpu
from jax.sharding import PartitionSpec as P

BLOCK = 128
HD = 128
HEADS = 8
QW = HEADS * HD
PW = 2 * HD
COLS = QW + PW
ROWS = 128
ROPE_BASE = 1000000.0
NEG = -1e30
SCALE = HD ** -0.5
F32 = jnp.float32
BF16 = jnp.bfloat16
VMEM = 24 * 1024 * 1024


def tp_shift(dy, dx):
    return [(y * 4 + x, (y + dy) % 2 * 4 + (x + dx) % 4) for y in range(2) for x in range(4)]


def roll_shift(dy, dz, dc):
    return [
        ((y * 4 + z) * 2 + c, ((y + dy) % 2 * 4 + (z + dz) % 4) * 2 + (c + dc) % 2)
        for y in range(2)
        for z in range(4)
        for c in range(2)
    ]


def over_tp(a, dy, dx):
    return lax.ppermute(a, "tp", tp_shift(dy, dx))


def over_roll(a, dy, dz, dc):
    return lax.ppermute(a, "roll", roll_shift(dy, dz, dc))


def dot(a, b, dims=((1,), (0,))):
    return lax.dot_general(a, b, (dims, ((), ())), preferred_element_type=F32)


ANY = pl.BlockSpec(memory_space=pl.ANY)
IN_HBM = pl.BlockSpec(memory_space=pltpu.HBM)
IN_VMEM = pl.BlockSpec(memory_space=pltpu.VMEM)
SMALL = pl.CostEstimate(flops=10**6, bytes_accessed=10**5, transcendentals=0)
IN_SMEM = pl.BlockSpec(memory_space=pltpu.SMEM)


def project(heads, xs, wq, wp, groups):
    count = sum(len(g) for g in groups)
    depth = wq.shape[0]

    def kernel(heads_ref, *refs):
        x_refs, (wq_ref, wp_ref), rest = refs[: len(xs)], refs[len(xs) : len(xs) + 2], refs[len(xs) + 2 :]
        outs, (q_buf, p_buf, q_sem, p_sem) = rest[:-4], rest[-4:]
        copies = []
        for d in range(count):
            k = heads_ref[d]
            copies.append(
                (
                    pltpu.make_async_copy(
                        wq_ref.at[:, pl.ds(pl.multiple_of(k * QW, QW), QW)], q_buf.at[d], q_sem.at[d]
                    ),
                    pltpu.make_async_copy(
                        wp_ref.at[:, pl.ds(pl.multiple_of(k * PW, PW), PW)], p_buf.at[d], p_sem.at[d]
                    ),
                )
            )
        for pair in copies:
            for c in pair:
                c.start()
        x = jnp.concatenate([r[...] for r in x_refs], 0)
        d = 0
        for g, group in enumerate(groups):
            for i in range(len(group)):
                for c in copies[d]:
                    c.wait()
                for buf, low, high in ((q_buf, 0, QW), (p_buf, QW, COLS)):
                    y = dot(x, buf[d]).astype(BF16)
                    for b in range(len(xs)):
                        outs[b * len(groups) + g][i, :, low:high] = y[b * ROWS : (b + 1) * ROWS]
                d += 1

    return pl.pallas_call(
        kernel,
        in_specs=[IN_SMEM] + [IN_VMEM] * len(xs) + [IN_HBM, IN_HBM],
        out_specs=[IN_VMEM] * (len(xs) * len(groups)),
        out_shape=[jax.ShapeDtypeStruct((len(g), ROWS, COLS), BF16) for _ in xs for g in groups],
        scratch_shapes=[
            pltpu.VMEM((count, depth, QW), BF16),
            pltpu.VMEM((count, depth, PW), BF16),
            pltpu.SemaphoreType.DMA((count,)),
            pltpu.SemaphoreType.DMA((count,)),
        ],
        compiler_params=pltpu.CompilerParams(vmem_limit_bytes=VMEM),
        cost_estimate=SMALL,
        name="project",
    )(heads, *xs, wq, wp)


def sort_rows(place, owner, tokens):
    rows, width = tokens.shape

    def kernel(place_ref, owner_ref, x_ref, *outs):
        x = x_ref[...]
        for b, out in enumerate(outs):
            row = lax.broadcasted_iota(jnp.int32, (ROWS, rows), 0)
            col = lax.broadcasted_iota(jnp.int32, (ROWS, rows), 1)
            i = row // 4
            y, c, step, j = (1 - b + place_ref[0]) % 2, i // 16, i // 4 % 4, i % 4
            c = jnp.where(c == 0, place_ref[2], 1 - place_ref[2])
            z = (jnp.where(step == 1, 3, jnp.where(step == 0, 0, step - 1)) + place_ref[1]) % 4
            slot = ((y * 4 + z) * 2 + c) * 4 + j
            hit = (owner_ref[...] == slot) & (col % 4 == row % 4)
            out[...] = dot(jnp.where(hit, 1.0, 0.0).astype(BF16), x).astype(BF16)

    return pl.pallas_call(
        kernel,
        in_specs=[IN_SMEM, IN_VMEM, IN_VMEM],
        out_specs=[IN_VMEM] * 2,
        out_shape=[jax.ShapeDtypeStruct((ROWS, width), BF16)] * 2,
        compiler_params=pltpu.CompilerParams(vmem_limit_bytes=VMEM),
        cost_estimate=SMALL,
        name="sort_rows",
    )(place, owner, tokens)


def add_far(right, left, up, down):
    def kernel(r, l, u, d, r_out, l_out):
        r_out[...] = (r[...].astype(F32) + u[...].astype(F32)).astype(BF16)
        l_out[...] = (l[...].astype(F32) + d[...].astype(F32)).astype(BF16)

    block = [pl.BlockSpec((1, ROWS, COLS), lambda i, h=h: (h, 0, 0)) for h in (0, 1)]
    return pl.pallas_call(
        kernel,
        grid=(1,),
        in_specs=block + [block[0]] * 2,
        out_specs=block,
        out_shape=[jax.ShapeDtypeStruct(right.shape, BF16)] * 2,
        input_output_aliases={0: 0, 1: 1},
        compiler_params=pltpu.CompilerParams(vmem_limit_bytes=VMEM),
        cost_estimate=SMALL,
        name="add_far",
    )(right, left, up, down)


def sum_x(own, from_left, from_right):
    def kernel(a, b, c, keep, send):
        for i, out in enumerate((keep, send)):
            out[...] = (a[i].astype(F32) + b[i].astype(F32) + c[i].astype(F32)).astype(out.dtype)

    return pl.pallas_call(
        kernel,
        in_specs=[IN_VMEM] * 3,
        out_specs=[IN_VMEM] * 2,
        out_shape=[jax.ShapeDtypeStruct((ROWS, COLS), F32), jax.ShapeDtypeStruct((ROWS, COLS), BF16)],
        compiler_params=pltpu.CompilerParams(vmem_limit_bytes=VMEM),
        cost_estimate=SMALL,
        name="sum_x",
    )(own, from_left, from_right)


def rotated(keep_ref, more_ref, bias_ref, cos_ref, sin_ref, first, q_buf):
    cos, sin = cos_ref[first : first + ROWS, :], sin_ref[first : first + ROWS, :]

    def turn(v):
        return v * cos + pltpu.roll(v, HD // 2, 1) * sin

    for h in range(HEADS):
        low, high = h * HD, h * HD + HD
        v = turn(keep_ref[:, low:high] + more_ref[:, low:high].astype(F32) + bias_ref[:, low:high])
        for p in range(32):
            q_buf[32 * p + 4 * h : 32 * p + 4 * h + 4, :] = v[4 * p : 4 * p + 4]
    u = keep_ref[:, QW:] + more_ref[:, QW:].astype(F32) + bias_ref[:, QW:]
    return jnp.concatenate([turn(u[:, :HD]), u[:, HD:]], 1)


def prefix_scores(q, buf, limit_ref, g):
    parts = []
    for i in range(4):
        p = 4 * g + i
        s = dot(q[32 * i : 32 * i + 32], buf[p, :, :HD], ((1,), (1,))) * SCALE
        col = lax.broadcasted_iota(jnp.int32, s.shape, 1)
        parts.append(jnp.where(col < limit_ref[p], s, NEG))
    return jnp.concatenate(parts, 0)


def prefix_values(w, buf, g):
    w = w.astype(BF16)
    return jnp.concatenate([dot(w[32 * i : 32 * i + 32], buf[4 * g + i, :, HD:]) for i in range(4)], 0)


def near_scores(q, cbuf, new, length_ref, g):
    sc = dot(q, cbuf[4 * g : 4 * g + 4, :, :HD].reshape(256, HD), ((1,), (1,))) * SCALE
    row = lax.broadcasted_iota(jnp.int32, sc.shape, 0)
    col = lax.broadcasted_iota(jnp.int32, sc.shape, 1)
    length = jnp.zeros(sc.shape, jnp.int32)
    for i in range(4):
        length = jnp.where(row // 32 == i, length_ref[4 * g + i], length)
    sc = jnp.where((row // 32 == col // 64) & (col % 64 < length), sc, NEG)
    sn = dot(q, new[:, :HD], ((1,), (1,))) * SCALE
    row = lax.broadcasted_iota(jnp.int32, sn.shape, 0)
    col = lax.broadcasted_iota(jnp.int32, sn.shape, 1)
    sn = jnp.where((row // 32 == col // 4) & (col % 4 <= row % 4), sn, NEG)
    return sc, sn


def near_values(wc, wn, cbuf, new, g):
    o = dot(wc.astype(BF16), cbuf[4 * g : 4 * g + 4, :, HD:].reshape(256, HD))
    return o + dot(wn.astype(BF16), new[:, HD:])


def softmax(*scores):
    top = jnp.max(scores[0], -1, keepdims=True)
    for s in scores[1:]:
        top = jnp.maximum(top, jnp.max(s, -1, keepdims=True))
    weights = [jnp.exp(s - top) for s in scores]
    total = jnp.sum(weights[0], -1, keepdims=True)
    for w in weights[1:]:
        total = total + jnp.sum(w, -1, keepdims=True)
    return top, weights, total


def prefix_copies(kvs, refs, buf, sem):
    copies, k = [], 0
    for g, group in enumerate(kvs):
        mine, slot = [], 4 * g
        for a in group:
            n = a.shape[0]
            mine.append(pltpu.make_async_copy(refs[k], buf.at[pl.ds(slot, n)], sem.at[k]))
            slot, k = slot + n, k + 1
        copies.append(mine)
    return copies


def cache_copies(cache_ref, at_ref, first, cbuf, sem):
    return [
        pltpu.make_async_copy(cache_ref.at[at_ref[first + p]], cbuf.at[p], sem.at[p]) for p in range(32)
    ]


CACHE_SCRATCH = [pltpu.VMEM((32, 64, 2 * HD), BF16), pltpu.SemaphoreType.DMA((32,))]


def attend(limits, lengths, order, keep, more, bias, cosine, sine, cache, kvs):
    flat = [a for group in kvs for a in group]

    def kernel(limit_ref, length_ref, at_ref, keep_ref, more_ref, bias_ref, cos_ref, sin_ref, cache_ref, *refs):
        o_ref, buf, sem, qbuf, cbuf, csem = refs[len(flat) :]
        prefix = prefix_copies(kvs, refs, buf, sem)
        caches = cache_copies(cache_ref, at_ref, 32, cbuf, csem)
        for g in range(8):
            for c in prefix[g] + caches[4 * g : 4 * g + 4]:
                c.start()
        new_all = rotated(keep_ref, more_ref, bias_ref, cos_ref, sin_ref, ROWS, qbuf)
        for p in range(32):
            o_ref[p, :, QW:] = new_all[4 * p : 4 * p + 4].astype(BF16)
        new_all = new_all.astype(BF16)
        for g in range(8):
            for c in prefix[g] + caches[4 * g : 4 * g + 4]:
                c.wait()
            q = qbuf[128 * g : 128 * g + 128, :].astype(BF16)
            new = new_all[16 * g : 16 * g + 16]
            sp = prefix_scores(q, buf, limit_ref, g)
            sc, sn = near_scores(q, cbuf, new, length_ref.at[pl.ds(32, 32)], g)
            _, (wp, wc, wn), total = softmax(sp, sc, sn)
            o = (prefix_values(wp, buf, g) + near_values(wc, wn, cbuf, new, g)) / total
            for i in range(4):
                for h in range(HEADS):
                    o_ref[4 * g + i, :, h * HD : h * HD + HD] = o[
                        32 * i + 4 * h : 32 * i + 4 * h + 4
                    ].astype(BF16)

    return pl.pallas_call(
        kernel,
        in_specs=[IN_SMEM] * 3 + [IN_VMEM] * 5 + [ANY] * (1 + len(flat)),
        out_specs=IN_VMEM,
        out_shape=jax.ShapeDtypeStruct((32, 4, COLS), BF16),
        scratch_shapes=[
            pltpu.VMEM((32, 512, 2 * HD), BF16),
            pltpu.SemaphoreType.DMA((len(flat),)),
            pltpu.VMEM((1024, HD), F32),
        ]
        + CACHE_SCRATCH,
        compiler_params=pltpu.CompilerParams(vmem_limit_bytes=VMEM),
        cost_estimate=SMALL,
        name="attend",
    )(limits, lengths, order, keep, more, bias, cosine, sine, cache, *flat)


def make_queries(keep, more, bias, cosine, sine):
    def kernel(keep_ref, more_ref, bias_ref, cos_ref, sin_ref, q_ref, new_ref, qbuf):
        new_ref[...] = rotated(keep_ref, more_ref, bias_ref, cos_ref, sin_ref, 0, qbuf).astype(BF16)
        q_ref[...] = qbuf[...].astype(BF16).reshape(32, 32, HD)

    return pl.pallas_call(
        kernel,
        in_specs=[IN_VMEM] * 5,
        out_specs=[IN_VMEM] * 2,
        out_shape=[jax.ShapeDtypeStruct((32, 32, HD), BF16), jax.ShapeDtypeStruct((ROWS, PW), BF16)],
        scratch_shapes=[pltpu.VMEM((1024, HD), F32)],
        compiler_params=pltpu.CompilerParams(vmem_limit_bytes=VMEM),
        cost_estimate=SMALL,
        name="make_queries",
    )(keep, more, bias, cosine, sine)


def attend_prefix(limits, q, kvs):
    flat = [a for group in kvs for a in group]

    def kernel(limit_ref, q_ref, *refs):
        o_ref, buf, sem = refs[len(flat) :]
        prefix = prefix_copies(kvs, refs, buf, sem)
        for mine in prefix:
            for c in mine:
                c.start()
        lane = lax.broadcasted_iota(jnp.int32, (32, 128), 1)
        stats = jnp.zeros((32, 128), F32)
        for g in range(8):
            for c in prefix[g]:
                c.wait()
            q = q_ref[4 * g : 4 * g + 4].reshape(128, HD)
            top, (w,), total = softmax(prefix_scores(q, buf, limit_ref, g))
            o = prefix_values(w, buf, g) / total
            o_ref[4 * g : 4 * g + 4] = o.astype(BF16).reshape(4, 32, HD)
            rest = top + jnp.log(total)
            for part in range(3):
                piece = rest.astype(BF16).astype(F32)
                for i in range(4):
                    stats = jnp.where(lane == 3 * (4 * g + i) + part, piece[32 * i : 32 * i + 32], stats)
                rest = rest - piece
        o_ref[32] = stats.astype(BF16)

    return pl.pallas_call(
        kernel,
        in_specs=[IN_SMEM, IN_VMEM] + [ANY] * len(flat),
        out_specs=IN_VMEM,
        out_shape=jax.ShapeDtypeStruct((33, 32, HD), BF16),
        scratch_shapes=[pltpu.VMEM((32, 512, 2 * HD), BF16), pltpu.SemaphoreType.DMA((len(flat),))],
        compiler_params=pltpu.CompilerParams(vmem_limit_bytes=VMEM),
        cost_estimate=SMALL,
        name="attend_prefix",
    )(limits, q, *flat)


def attend_near(lengths, order, q, new, cache):
    def kernel(length_ref, at_ref, q_ref, new_ref, cache_ref, o_ref, l_ref, cbuf, csem):
        caches = cache_copies(cache_ref, at_ref, 0, cbuf, csem)
        for c in caches:
            c.start()
        for g in range(8):
            for c in caches[4 * g : 4 * g + 4]:
                c.wait()
            q = q_ref[4 * g : 4 * g + 4].reshape(128, HD)
            new = new_ref[16 * g : 16 * g + 16]
            top, (wc, wn), total = softmax(*near_scores(q, cbuf, new, length_ref, g))
            o_ref[128 * g : 128 * g + 128] = near_values(wc, wn, cbuf, new, g) / total
            l_ref[128 * g : 128 * g + 128] = jnp.broadcast_to(top + jnp.log(total), (128, HD))

    return pl.pallas_call(
        kernel,
        in_specs=[IN_SMEM] * 2 + [IN_VMEM] * 2 + [ANY],
        out_specs=[IN_VMEM] * 2,
        out_shape=[jax.ShapeDtypeStruct((1024, HD), F32)] * 2,
        scratch_shapes=CACHE_SCRATCH,
        compiler_params=pltpu.CompilerParams(vmem_limit_bytes=VMEM),
        cost_estimate=SMALL,
        name="attend_near",
    )(lengths, order, q, new, cache)


def merge_rows(order, far, near, near_log, new, done):
    def kernel(order_ref, far_ref, o_ref, l_ref, new_ref, done_ref, out_ref, pair_ref):
        stats = far_ref[32].astype(F32)
        for p in range(32):
            at = order_ref[p]
            theirs = jnp.sum(stats[:, 3 * p : 3 * p + 3], -1, keepdims=True)
            ours = l_ref[32 * p : 32 * p + 32]
            top = jnp.maximum(theirs, ours)
            wt, wo = jnp.exp(theirs - top), jnp.exp(ours - top)
            o = (far_ref[p].astype(F32) * wt + o_ref[32 * p : 32 * p + 32] * wo) / (wt + wo)
            for h in range(HEADS):
                out_ref[at, :, h * HD : h * HD + HD] = o[4 * h : 4 * h + 4].astype(BF16)
            pair_ref[at] = new_ref[p]
            at = order_ref[32 + p]
            out_ref[at] = done_ref[p, :, :QW]
            pair_ref[at] = done_ref[p, :, QW:]

    return pl.pallas_call(
        kernel,
        in_specs=[IN_SMEM] + [IN_VMEM] * 5,
        out_specs=[IN_VMEM] * 2,
        out_shape=[jax.ShapeDtypeStruct((64, 4, QW), BF16), jax.ShapeDtypeStruct((64, 4, PW), BF16)],
        compiler_params=pltpu.CompilerParams(vmem_limit_bytes=VMEM),
        cost_estimate=SMALL,
        name="merge_rows",
    )(order, far, near, near_log, new, done)


def on_device(
    tokens,
    query_weight,
    query_bias,
    pair_weight,
    pair_bias,
    cache_pairs,
    prefix_pairs,
    owner_slot,
    prefix_blocks,
    positions,
):
    prompts, _, new, width = tokens.shape
    me = lax.axis_index("roll")
    my_y, my_z, my_c = me // 8, me // 2 % 4, me % 2
    tp = lax.axis_index("tp")
    tp_y, tp_x = tp // 4, tp % 4
    pos = positions.reshape(prompts)

    own = prefix_pairs.reshape(4, 512, 2 * HD)
    below, above = over_roll(own, 0, 1, 0), over_roll(own, 0, 3, 0)
    far_a, far_b = over_roll(below[:2], 0, 1, 0), over_roll(above[2:], 0, 3, 0)
    kvs = [[own], [below], [above], [far_a, far_b]]
    kvs = kvs + [[over_roll(a, 0, 0, 1) for a in group] for group in kvs]

    x_o, x_m = sort_rows(
        jnp.stack([my_y, my_z, my_c]).astype(jnp.int32),
        jnp.broadcast_to(owner_slot[:, None], (prompts, new)).reshape(1, prompts * new),
        tokens.reshape(prompts * new, width),
    )

    def heads(*pairs):
        return jnp.stack([(tp_y + dy) % 2 * 4 + (tp_x + dx) % 4 for dy, dx in pairs]).astype(jnp.int32)

    weights = (query_weight, pair_weight)
    up_o, down_o, up_m, down_m = project(heads((0, 2), (1, 2)), [x_o, x_m], *weights, [[0], [1]])
    right_o, left_o, right_m, left_m = project(
        heads((0, 1), (1, 1), (0, 3), (1, 3)), [x_o, x_m], *weights, [[0, 1], [2, 3]]
    )
    own_o, own_m = project(heads((0, 0), (1, 0)), [x_o, x_m], *weights, [[0, 1]])

    def reduce(up, down, right, left, own):
        up, down = over_tp(up, 0, 1), over_tp(down, 0, 3)
        right, left = add_far(right, left, up, down)
        keep, send = sum_x(own, over_tp(right, 0, 1), over_tp(left, 0, 3))
        return keep, over_tp(send, 1, 0)

    full_o = reduce(up_o, down_o, right_o, left_o, own_o)
    full_m = reduce(up_m, down_m, right_m, left_m, own_m)

    index = jnp.arange(prompts, dtype=jnp.int32)
    half, quarter = jnp.arange(2, dtype=jnp.int32), jnp.arange(4, dtype=jnp.int32)
    y_of, c_of = (1 - half + my_y) % 2, (half + my_c) % 2
    z_of = (jnp.array([0, 3, 1, 2], jnp.int32) + my_z) % 4
    slot = (
        ((y_of[:, None, None, None] * 4 + z_of[None, None, :, None]) * 2 + c_of[None, :, None, None]) * 4
        + quarter[None, None, None, :]
    ).reshape(prompts)
    hit = owner_slot[None, :] == slot[:, None]
    order = jnp.sum(jnp.where(hit, index[None, :], 0), 1)
    limits = BLOCK * jnp.sum(jnp.where(hit, prefix_blocks[None, :], 0), 1)
    lengths = jnp.sum(jnp.where(hit, pos[None, :], 0), 1)
    my_limits = limits[32:]
    at = (limits[:, None] + lengths[:, None] + quarter[None, :]).reshape(prompts * new)
    frequency = jnp.exp(jnp.arange(HD // 2, dtype=F32) * (-2.0 * math.log(ROPE_BASE) / HD))
    angles = at.astype(F32)[:, None] * frequency[None, :]
    cosine, sine = jnp.cos(angles), jnp.sin(angles)
    tables = (
        jnp.concatenate([query_bias, pair_bias]).astype(F32)[None],
        jnp.concatenate([cosine, cosine], 1),
        jnp.concatenate([-sine, sine], 1),
    )
    cache = cache_pairs.reshape(prompts, 64, 2 * HD)

    q_o, new_o = make_queries(*full_o, *tables)
    far = over_roll(attend_prefix(my_limits, over_roll(q_o, 1, 0, 0), kvs), 1, 0, 0)
    near, near_log = attend_near(lengths, order, q_o, new_o, cache)
    done = attend(my_limits, lengths, order, *full_m, *tables, cache, kvs)
    attended, new_pairs = merge_rows(order, far, near, near_log, new_o.reshape(32, new, PW), done)
    return (
        attended.reshape(prompts, 1, new, QW),
        new_pairs.reshape(prompts, 1, new, 1, PW),
    )


def solution(mesh):
    return jax.shard_map(
        on_device,
        mesh=mesh,
        in_specs=(
            P(None, "roll", None, "tp"),
            P("tp", None),
            P("tp"),
            P("tp", None),
            P("tp"),
            P(None, "roll", None, "tp", None),
            P("roll", None, "tp", None),
            P(),
            P(),
            P(None, "roll"),
        ),
        out_specs=(P(None, "roll", None, "tp"), P(None, "roll", None, "tp", None)),
        check_vma=False,
    )
```

time: 164 us -> 150 us (0.915)
  local copies, waits for them, and re-layouts: 15.3 us -> 45.4 us
  Pallas kernels: 76.6 us -> 47.6 us
  waiting for transfers between devices: 36.7 us -> 26.3 us
  starting transfers between devices: 30.7 us -> 26 us
    unnamed x38 -> x78, local copies, waits for them, and re-layouts: 8.83 us -> 40.4 us
    pallas_call x7 -> x8, Pallas kernels: 55.5 us -> 31.5 us  [the longest x3 14.9 us: project(): pl.pallas_call(kernel, in_specs=[IN_SMEM] + [IN_VMEM] * len(xs) + [IN_HBM...]
    ppermute x10, waiting for transfers between devices: 27.6 us -> 13.4 us  [over_tp(): return lax.ppermute(a, 'tp', tp_shift(dy, dx))]
    pallas_call x2 -> x1, Pallas kernels: 15.3 us -> 8.65 us  [attend(): pl.pallas_call(kernel, in_specs=[IN_SMEM] * 3 + [IN_VMEM] * 5 + [ANY] * (...]
    ppermute x10, starting transfers between devices: 15.3 us -> 11.4 us  [over_tp(): return lax.ppermute(a, 'tp', tp_shift(dy, dx))]
    ppermute x12 -> x11, waiting for transfers between devices: 9.07 us -> 12.8 us  [over_roll(): return lax.ppermute(a, 'roll', roll_shift(dy, dz, dc))]
    ppermute x12 -> x11, starting transfers between devices: 15.4 us -> 14.6 us  [over_roll(): return lax.ppermute(a, 'roll', roll_shift(dy, dz, dc))]
  transfers between devices with their start and end apart: 22 -> 21, of which waited for: 5 -> 5; matrix products, arithmetic and copies ran while one was open for 6% -> 5% of each run, Pallas kernels for 46% -> 29%
where the time goes in v5:
time: 150 us; the launch traced here: 149 us
  Pallas kernels  47.6 us (32%)
  local copies, waits for them, and re-layouts  45.4 us (30%)
  waiting for transfers between devices  26.3 us (18%)
  starting transfers between devices  26 us (17%)
  other arithmetic  2.05 us (1%)
    unnamed x78, local copies, waits for them, and re-layouts  40.4 us
    pallas_call x3, Pallas kernels, project(): pl.pallas_call(kernel, in_specs=[IN_SMEM] + [IN_VMEM] * len(xs) + [IN_HBM...  14.9 us
    ppermute x11, starting transfers between devices, over_roll(): return lax.ppermute(a, 'roll', roll_shift(dy, dz, dc))  14.6 us
    ppermute x10, waiting for transfers between devices, over_tp(): return lax.ppermute(a, 'tp', tp_shift(dy, dx))  13.4 us
    ppermute x11, waiting for transfers between devices, over_roll(): return lax.ppermute(a, 'roll', roll_shift(dy, dz, dc))  12.8 us
    ppermute x10, starting transfers between devices, over_tp(): return lax.ppermute(a, 'tp', tp_shift(dy, dx))  11.4 us
    pallas_call x1, Pallas kernels, attend(): pl.pallas_call(kernel, in_specs=[IN_SMEM] * 3 + [IN_VMEM] * 5 + [ANY] * (...  8.65 us
    pallas_call x1, Pallas kernels, attend_prefix(): pl.pallas_call(kernel, in_specs=[IN_SMEM, IN_VMEM] + [ANY] * len(flat), o...  5.85 us
  transfers between devices with their start and end apart: 21, of which 5 were waited for; matrix products, arithmetic and copies ran while one was open for 5% of the time, Pallas kernels for 29%

profile of v5, /device:TPU:0, one launch (start us, length us, event | category | flops | bytes accessed | tf_op | source)
XLA Modules:
  0.0 148.5 jit_solution(8086233854919444187)
XLA Ops:
  0.6 2.1 %collective-permute-start.6 = (bf16[4,512,256]{2,1,0:T(8,128)(2,1)}, bf16[4,512,256]{2,1,0:T(8,128)(2,1)S(1)}, u32[]{:S(2)}, u32[]{:S(2)}) collective-permute-start(bf16[4,512,256]{2,1,0:T(8,128)(2,1)} %bitcast.22), channel_id=1, source_target_pairs={{0,16},{8,24},{16,32},{24,40},{32,48},{40,56},{48,0},{56,8},{64,80... | collective-permute-start | bytes 3145736 | tf_op jit(solution)/shard_map/ppermute | solution.py:43
  2.7 2.2 %collective-permute-start.7 = (bf16[4,512,256]{2,1,0:T(8,128)(2,1)}, bf16[4,512,256]{2,1,0:T(8,128)(2,1)}, u32[]{:S(2)}, u32[]{:S(2)}) collective-permute-start(bf16[4,512,256]{2,1,0:T(8,128)(2,1)} %bitcast.23), channel_id=1, source_target_pairs={{0,48},{8,56},{16,0},{24,8},{32,16},{40,24},{48,32},{56,40},{64,11... | collective-permute-start | bytes 3145736 | tf_op jit(solution)/shard_map/ppermute | solution.py:43
  4.9 1.2 reshape.175.x_ref
  7.1 0.9 sort_rows.1
  8.0 5.8 %copy-done = bf16[1024,8192]{1,0:T(8,128)(2,1)S(1)} copy-done((bf16[1024,8192]{1,0:T(8,128)(2,1)S(1)}, bf16[1024,8192]{1,0:T(8,128)(2,1)}, u32[]{:S(2)}) %copy-start) | copy-done | bytes 16777240
  13.8 2.2 %copy-done.3 = bf16[1024,2048]{1,0:T(8,128)(2,1)S(1)} copy-done((bf16[1024,2048]{1,0:T(8,128)(2,1)S(1)}, bf16[1024,2048]{1,0:T(8,128)(2,1)}, u32[]{:S(2)}) %copy-start.3) | copy-done | bytes 4194328
  15.9 4.3 %project.5 = (bf16[1,128,1280]{2,1,0:T(8,128)(2,1)S(1)}, bf16[1,128,1280]{2,1,0:T(8,128)(2,1)S(1)}, bf16[1,128,1280]{2,1,0:T(8,128)(2,1)}, bf16[1,128,1280]{2,1,0:T(8,128)(2,1)}) custom-call(s32[2]{0:T(128)S(1)} %pad_add_fusion.3.heads_ref, bf16[128,1024]{1,0:T(8,128)(2,1)S(1)} %get-tuple-element.28.refs_0_, ...), custom_call_target="tpu_custom_call" | custom-call | flops 1000000 | bytes 100000 | tf_op jit(solution)/shard_map/project/pallas_call | solution.py:92
  20.2 1.6 %collective-permute-start.16 = (bf16[1,128,1280]{2,1,0:T(8,128)(2,1)}, bf16[1,128,1280]{2,1,0:T(8,128)(2,1)S(1)}, u32[]{:S(2)}, u32[]{:S(2)}) collective-permute-start(bf16[1,128,1280]{2,1,0:T(8,128)(2,1)} %get-tuple-element.46), channel_id=1, source_target_pairs={{0,1},{1,2},{2,3},{3,0},{4,5},{5,6},{6,7},{7,4},{8,9},{9,10},{10,1... | collective-permute-start | bytes 983048 | tf_op jit(solution)/shard_map/ppermute | solution.py:39
  21.8 1.5 %collective-permute-start = (bf16[1,128,1280]{2,1,0:T(8,128)(2,1)S(1)}, bf16[1,128,1280]{2,1,0:T(8,128)(2,1)S(1)}, u32[]{:S(2)}, u32[]{:S(2)}) collective-permute-start(bf16[1,128,1280]{2,1,0:T(8,128)(2,1)S(1)} %get-tuple-element.33), channel_id=1, source_target_pairs={{0,1},{1,2},{2,3},{3,0},{4,5},{5,6},{6,7},{7,4},{8,9},{9,10},{10,1... | collective-permute-start | bytes 983048 | tf_op jit(solution)/shard_map/ppermute | solution.py:39
  23.3 1.7 %collective-permute-start.1 = (bf16[1,128,1280]{2,1,0:T(8,128)(2,1)S(1)}, bf16[1,128,1280]{2,1,0:T(8,128)(2,1)S(1)}, u32[]{:S(2)}, u32[]{:S(2)}) collective-permute-start(bf16[1,128,1280]{2,1,0:T(8,128)(2,1)S(1)} %get-tuple-element.34), channel_id=1, source_target_pairs={{0,3},{1,0},{2,1},{3,2},{4,7},{5,4},{6,5},{7,6},{8,11},{9,8},{10,9... | collective-permute-start | bytes 983048 | tf_op jit(solution)/shard_map/ppermute | solution.py:39
  25.1 5.8 %copy-done.1 = bf16[1024,8192]{1,0:T(8,128)(2,1)S(1)} copy-done((bf16[1024,8192]{1,0:T(8,128)(2,1)S(1)}, bf16[1024,8192]{1,0:T(8,128)(2,1)}, u32[]{:S(2)}) %copy-start.1) | copy-done | bytes 16777240
  30.9 2.2 %copy-done.4 = bf16[1024,2048]{1,0:T(8,128)(2,1)S(1)} copy-done((bf16[1024,2048]{1,0:T(8,128)(2,1)S(1)}, bf16[1024,2048]{1,0:T(8,128)(2,1)}, u32[]{:S(2)}) %copy-start.4) | copy-done | bytes 4194328
  33.1 7.3 %project.4 = (bf16[2,128,1280]{2,1,0:T(8,128)(2,1)}, bf16[2,128,1280]{2,1,0:T(8,128)(2,1)S(1)}, bf16[2,128,1280]{2,1,0:T(8,128)(2,1)}, bf16[2,128,1280]{2,1,0:T(8,128)(2,1)}) custom-call(s32[4]{0:T(128)S(1)} %pad_add_fusion.2.heads_ref, bf16[128,1024]{1,0:T(8,128)(2,1)S(1)} %get-tuple-element.28.refs_0_, bf16[128,1024]{1,0:T(8,128)(2,1)S(1)} %get-tuple-element.29.refs_1_, ...), custom_call_target="tpu_custom_call" | custom-call | flops 1000000 | bytes 100000 | tf_op jit(solution)/shard_map/project/pallas_call | solution.py:92
  41.0 1.8 %add_far.2 = (bf16[2,128,1280]{2,1,0:T(8,128)(2,1)}, bf16[2,128,1280]{2,1,0:T(8,128)(2,1)S(1)}) custom-call(bf16[2,128,1280]{2,1,0:T(8,128)(2,1)} %get-tuple-element.31.r, bf16[2,128,1280]{2,1,0:T(8,128)(2,1)S(1)} %get-tuple-element.32.l, bf16[1,128,1280]{2,1,0:T(8,128)(2,1)S(1)} %collective-permute-done.u, ...), custom_call_target="tpu_custom_call", output_to_operand_aliasing={{0}: (0, {}), {1}: (1, {})} | custom-call | flops 1000000 | bytes 100000 | tf_op jit(solution)/shard_map/add_far/pallas_call | solution.py:142
  43.7 1.5 %collective-permute-start.2 = (bf16[2,128,1280]{2,1,0:T(8,128)(2,1)}, bf16[2,128,1280]{2,1,0:T(8,128)(2,1)S(1)}, u32[]{:S(2)}, u32[]{:S(2)}) collective-permute-start(bf16[2,128,1280]{2,1,0:T(8,128)(2,1)} %get-tuple-element.35), channel_id=1, source_target_pairs={{0,1},{1,2},{2,3},{3,0},{4,5},{5,6},{6,7},{7,4},{8,9},{9,10},{10,1... | collective-permute-start | bytes 1966088 | tf_op jit(solution)/shard_map/ppermute | solution.py:39
  45.2 1.8 %collective-permute-start.3 = (bf16[2,128,1280]{2,1,0:T(8,128)(2,1)}, bf16[2,128,1280]{2,1,0:T(8,128)(2,1)}, u32[]{:S(2)}, u32[]{:S(2)}) collective-permute-start(bf16[2,128,1280]{2,1,0:T(8,128)(2,1)} %copy-done.25), channel_id=1, source_target_pairs={{0,3},{1,0},{2,1},{3,2},{4,7},{5,4},{6,5},{7,6},{8,11},{9,8},{10,9... | collective-permute-start | bytes 1966088 | tf_op jit(solution)/shard_map/ppermute | solution.py:39
  47.1 4.3 %collective-permute-done.17.d = bf16[1,128,1280]{2,1,0:T(8,128)(2,1)S(1)} collective-permute-done((bf16[1,128,1280]{2,1,0:T(8,128)(2,1)}, bf16[1,128,1280]{2,1,0:T(8,128)(2,1)S(1)}, u32[]{:S(2)}, u32[]{:S(2)}) %collective-permute-start.17) | collective-permute-done | bytes 327712 | tf_op jit(solution)/shard_map/ppermute | solution.py:39
  51.4 2.0 %add_far.3 = (bf16[2,128,1280]{2,1,0:T(8,128)(2,1)}, bf16[2,128,1280]{2,1,0:T(8,128)(2,1)}) custom-call(bf16[2,128,1280]{2,1,0:T(8,128)(2,1)} %get-tuple-element.44.r, bf16[2,128,1280]{2,1,0:T(8,128)(2,1)} %get-tuple-element.45.l, bf16[1,128,1280]{2,1,0:T(8,128)(2,1)S(1)} %collective-permute-done.16.u, ...), custom_call_target="tpu_custom_call", output_to_operand_aliasing={{0}: (0, {}), {1}: (1, {})} | custom-call | flops 1000000 | bytes 100000 | tf_op jit(solution)/shard_map/add_far/pallas_call | solution.py:142
  53.6 9.1 %collective-permute-done.2.b = bf16[2,128,1280]{2,1,0:T(8,128)(2,1)S(1)} collective-permute-done((bf16[2,128,1280]{2,1,0:T(8,128)(2,1)}, bf16[2,128,1280]{2,1,0:T(8,128)(2,1)S(1)}, u32[]{:S(2)}, u32[]{:S(2)}) %collective-permute-start.2) | collective-permute-done | bytes 655392 | tf_op jit(solution)/shard_map/ppermute | solution.py:39
  64.2 5.8 %copy-done.2 = bf16[1024,8192]{1,0:T(8,128)(2,1)S(1)} copy-done((bf16[1024,8192]{1,0:T(8,128)(2,1)S(1)}, bf16[1024,8192]{1,0:T(8,128)(2,1)}, u32[]{:S(2)}) %copy-start.2) | copy-done | bytes 16777240
  69.9 2.2 %copy-done.5 = bf16[1024,2048]{1,0:T(8,128)(2,1)S(1)} copy-done((bf16[1024,2048]{1,0:T(8,128)(2,1)S(1)}, bf16[1024,2048]{1,0:T(8,128)(2,1)}, u32[]{:S(2)}) %copy-start.5) | copy-done | bytes 4194328
  72.2 3.3 %project.3 = (bf16[2,128,1280]{2,1,0:T(8,128)(2,1)S(1)}, bf16[2,128,1280]{2,1,0:T(8,128)(2,1)S(1)}) custom-call(s32[2]{0:T(128)S(1)} %pad_add_fusion.heads_ref, bf16[128,1024]{1,0:T(8,128)(2,1)S(1)} %get-tuple-element.28.refs_0_, bf16[128,1024]{1,0:T(8,128)(2,1)S(1)} %get-tuple-element.29.refs_1_, bf16[1024,8192]{1,0:T(8,128)(2,1)S(1)} %copy-done.2, ...), custom_call_target="tpu_custom_call" | custom-call | flops 1000000 | bytes 100000 | tf_op jit(solution)/shard_map/project/pallas_call | solution.py:92
  75.5 1.5 %sum_x.2 = (f32[128,1280]{1,0:T(8,128)S(1)}, bf16[128,1280]{1,0:T(8,128)(2,1)S(1)}) custom-call(bf16[2,128,1280]{2,1,0:T(8,128)(2,1)S(1)} %get-tuple-element.30.a, bf16[2,128,1280]{2,1,0:T(8,128)(2,1)S(1)} %copy-done.24, bf16[2,128,1280]{2,1,0:T(8,128)(2,1)} %collective-permute-done.3.c), custom_call_target="tpu_custom_call" | custom-call | flops 1000000 | bytes 100000 | tf_op jit(solution)/shard_map/sum_x/pallas_call | solution.py:160
  77.1 1.7 %collective-permute-start.4 = (bf16[128,1280]{1,0:T(8,128)(2,1)S(1)}, bf16[128,1280]{1,0:T(8,128)(2,1)S(1)}, u32[]{:S(2)}, u32[]{:S(2)}) collective-permute-start(bf16[128,1280]{1,0:T(8,128)(2,1)S(1)} %get-tuple-element.38), channel_id=1, source_target_pairs={{0,4},{1,5},{2,6},{3,7},{4,0},{5,1},{6,2},{7,3},{8,12},{9,13},{10,... | collective-permute-start | bytes 983048 | tf_op jit(solution)/shard_map/ppermute | solution.py:39
  80.4 1.9 %slice.13 = bf16[2,512,256]{2,1,0:T(8,128)(2,1)} slice(bf16[4,512,256]{2,1,0:T(8,128)(2,1)} %collective-permute-done.7.refs_2_), slice={[2:4], [0:512], [0:256]} | slice | bytes 1048576 | tf_op jit(solution)/shard_map/slice | solution.py:429
  82.3 3.2 %collective-permute-start.9 = (bf16[2,512,256]{2,1,0:T(8,128)(2,1)}, bf16[2,512,256]{2,1,0:T(8,128)(2,1)}, u32[]{:S(2)}, u32[]{:S(2)}) collective-permute-start(bf16[2,512,256]{2,1,0:T(8,128)(2,1)} %slice.13), channel_id=1, source_target_pairs={{0,48},{8,56},{16,0},{24,8},{32,16},{40,24},{48,32},{56,40},{64,11... | collective-permute-start | bytes 1572872 | tf_op jit(solution)/shard_map/ppermute | solution.py:43
  87.8 8.4 %collective-permute-done.8.refs_3_ = bf16[2,512,256]{2,1,0:T(8,128)(2,1)} collective-permute-done((bf16[2,512,256]{2,1,0:T(8,128)(2,1)}, bf16[2,512,256]{2,1,0:T(8,128)(2,1)}, u32[]{:S(2)}, u32[]{:S(2)}) %collective-permute-start.8) | collective-permute-done | bytes 524320 | tf_op jit(solution)/shard_map/ppermute | solution.py:43
  96.3 1.2 collective-permute-done.9.refs_4_
  97.4 1.1 copy-done.20
  98.5 1.0 copy-done.27
  99.8 3.0 %collective-permute-start.5 = (bf16[32,32,128]{2,1,0:T(8,128)(2,1)S(1)}, bf16[32,32,128]{2,1,0:T(8,128)(2,1)S(1)}, u32[]{:S(2)}, u32[]{:S(2)}) collective-permute-start(bf16[32,32,128]{2,1,0:T(8,128)(2,1)S(1)} %get-tuple-element.39.q_ref), channel_id=1, source_target_pairs={{0,64},{8,72},{16,80},{24,88},{32,96},{40,104},{48,112},{56,120},{... | collective-permute-start | bytes 786440 | tf_op jit(solution)/shard_map/ppermute | solution.py:43
  102.8 1.1 copy-done.22
  103.9 2.1 %sum_x.3 = (f32[128,1280]{1,0:T(8,128)S(1)}, bf16[128,1280]{1,0:T(8,128)(2,1)}) custom-call(bf16[2,128,1280]{2,1,0:T(8,128)(2,1)S(1)} %copy-done.22, bf16[2,128,1280]{2,1,0:T(8,128)(2,1)} %collective-permute-done.18.b, bf16[2,128,1280]{2,1,0:T(8,128)(2,1)} %collective-permute-done.19.c), custom_call_target="tpu_custom_call" | custom-call | flops 1000000 | bytes 100000 | tf_op jit(solution)/shard_map/sum_x/pallas_call | solution.py:160
  106.0 0.9 copy-done.17
  106.9 3.2 %collective-permute-done.5.q_ref = bf16[32,32,128]{2,1,0:T(8,128)(2,1)S(1)} collective-permute-done((bf16[32,32,128]{2,1,0:T(8,128)(2,1)S(1)}, bf16[32,32,128]{2,1,0:T(8,128)(2,1)S(1)}, u32[]{:S(2)}, u32[]{:S(2)}) %collective-permute-start.5) | collective-permute-done | bytes 262176 | tf_op jit(solution)/shard_map/ppermute | solution.py:43
  110.7 1.6 %copy-done.8 = bf16[4,512,1,256]{3,1,2,0:T(8,128)(2,1)S(1)} copy-done((bf16[4,512,1,256]{3,1,2,0:T(8,128)(2,1)S(1)}, bf16[4,512,1,256]{3,1,2,0:T(8,128)(2,1)}, u32[]{:S(2)}) %copy-start.8) | copy-done | bytes 1048600
  112.3 1.2 copy-done.11
  113.6 5.9 %attend_prefix.1 = bf16[33,32,128]{2,1,0:T(8,128)(2,1)} custom-call(s32[32]{0:T(128)S(1)} %slice.9.limit_ref, bf16[32,32,128]{2,1,0:T(8,128)(2,1)S(1)} %collective-permute-done.5.q_ref, bf16[4,512,256]{2,1,0:T(8,128)(2,1)S(1)} %bitcast.25, bf16[4,512,256]{2,1,0:T(8,128)(2,1)S(1)} %collective-permute-done.6.refs_1_, ...), custom_call_target="tpu_custom_call" | custom-call | flops 1000000 | bytes 100000 | tf_op jit(solution)/shard_map/attend_prefix/pallas_call | solution.py:342
  119.5 3.5 %collective-permute-start.15 = (bf16[33,32,128]{2,1,0:T(8,128)(2,1)}, bf16[33,32,128]{2,1,0:T(8,128)(2,1)}, u32[]{:S(2)}, u32[]{:S(2)}) collective-permute-start(bf16[33,32,128]{2,1,0:T(8,128)(2,1)} %attend_prefix.1), channel_id=1, source_target_pairs={{0,64},{8,72},{16,80},{24,88},{32,96},{40,104},{48,112},{56,120},{... | collective-permute-start | bytes 811016 | tf_op jit(solution)/shard_map/ppermute | solution.py:43
  123.0 0.9 copy-done.29
  123.9 5.6 %attend_near.1 = (f32[1024,128]{1,0:T(8,128)S(1)}, f32[1024,128]{1,0:T(8,128)S(1)}) custom-call(s32[64]{0:T(128)S(1)} %get-tuple-element.60.length_ref, s32[64]{0:T(128)S(1)} %get-tuple-element.62.at_ref.order_ref, bf16[32,32,128]{2,1,0:T(8,128)(2,1)S(1)} %copy-done.29, bf16[128,256]{1,0:T(8,128)(2,1)S(1)} %get-tuple-element.40.new_ref, ...), custom_call_target="tpu_custom_call" | custom-call | flops 1000000 | bytes 100000 | tf_op jit(solution)/shard_map/attend_near/pallas_call | solution.py:368
  129.5 1.2 copy-done.9
  130.7 1.2 copy-done.12
  132.0 1.0 copy-done.14
  133.0 1.0 copy-done.16
  134.0 1.1 copy-done.18
  135.8 8.7 %attend.1.done_ref = bf16[32,4,1280]{2,1,0:T(4,128)(2,1)S(1)} custom-call(s32[32]{0:T(128)S(1)} %copy-done.31, s32[64]{0:T(128)S(1)} %get-tuple-element.60.length_ref, s32[64]{0:T(128)S(1)} %get-tuple-element.62.at_ref.order_ref, f32[128,1280]{1,0:T(8,128)S(1)} %copy-done.18, bf16[128,1280]{1,0:T(8,128)(2,1)} %collective-permute-done.20.more_ref, ...), custom_call_target="tpu_custom_call" | custom-call | flops 1000000 | bytes 100000 | tf_op jit(solution)/shard_map/attend/pallas_call | solution.py:282
  144.5 4.0 %merge_rows.1 = (bf16[64,4,1024]{2,1,0:T(4,128)(2,1)}, bf16[64,4,256]{2,1,0:T(4,128)(2,1)}) custom-call(s32[64]{0:T(128)S(1)} %get-tuple-element.62.at_ref.order_ref, bf16[33,32,128]{2,1,0:T(8,128)(2,1)} %collective-permute-done.15.far_ref, f32[1024,128]{1,0:T(8,128)S(1)} %get-tuple-element.41.o_ref, f32[1024,128]{1,0:T(8,128)S(1)} %get-tuple-element.42.l_ref, ...), custom_call_target="tpu_custom_call" | custom-call | flops 1000000 | bytes 100000 | tf_op jit(solution)/shard_map/merge_rows/pallas_call | solution.py:397
  (113 shorter events, 9.8 us)
Async XLA Ops:
  0.6 78.3 %collective-permute-start.6 = (bf16[4,512,256]{2,1,0:T(8,128)(2,1)}, bf16[4,512,256]{2,1,0:T(8,128)(2,1)S(1)}, u32[]{:S(2)}, u32[]{:S(2)}) collective-permute-start(bf16[4,512,256]{2,1,0:T(8,128)(2,1)} %bitcast.22), channel_id=1, source_target_pairs={{0,16},{8,24},{16,32},{24,40},{32,48},{40,56},{48,0},{56,8},{64,80... | collective-permute-start | bytes 3145736 | tf_op jit(solution)/shard_map/ppermute | solution.py:43
  2.7 77.7 %collective-permute-start.7 = (bf16[4,512,256]{2,1,0:T(8,128)(2,1)}, bf16[4,512,256]{2,1,0:T(8,128)(2,1)}, u32[]{:S(2)}, u32[]{:S(2)}) collective-permute-start(bf16[4,512,256]{2,1,0:T(8,128)(2,1)} %bitcast.23), channel_id=1, source_target_pairs={{0,48},{8,56},{16,0},{24,8},{32,16},{40,24},{48,32},{56,40},{64,11... | collective-permute-start | bytes 3145736 | tf_op jit(solution)/shard_map/ppermute | solution.py:43
  8.0 5.8 %copy-start = (bf16[1024,8192]{1,0:T(8,128)(2,1)S(1)}, bf16[1024,8192]{1,0:T(8,128)(2,1)}, u32[]{:S(2)}) copy-start(bf16[1024,8192]{1,0:T(8,128)(2,1)} %refs_2_.5) | copy-start | bytes 50331652
  13.8 2.2 %copy-start.3 = (bf16[1024,2048]{1,0:T(8,128)(2,1)S(1)}, bf16[1024,2048]{1,0:T(8,128)(2,1)}, u32[]{:S(2)}) copy-start(bf16[1024,2048]{1,0:T(8,128)(2,1)} %refs_3_.5) | copy-start | bytes 12582916
  20.2 25.0 %collective-permute-start.16 = (bf16[1,128,1280]{2,1,0:T(8,128)(2,1)}, bf16[1,128,1280]{2,1,0:T(8,128)(2,1)S(1)}, u32[]{:S(2)}, u32[]{:S(2)}) collective-permute-start(bf16[1,128,1280]{2,1,0:T(8,128)(2,1)} %get-tuple-element.46), channel_id=1, source_target_pairs={{0,1},{1,2},{2,3},{3,0},{4,5},{5,6},{6,7},{7,4},{8,9},{9,10},{10,1... | collective-permute-start | bytes 983048 | tf_op jit(solution)/shard_map/ppermute | solution.py:39
  21.8 18.6 %collective-permute-start = (bf16[1,128,1280]{2,1,0:T(8,128)(2,1)S(1)}, bf16[1,128,1280]{2,1,0:T(8,128)(2,1)S(1)}, u32[]{:S(2)}, u32[]{:S(2)}) collective-permute-start(bf16[1,128,1280]{2,1,0:T(8,128)(2,1)S(1)} %get-tuple-element.33), channel_id=1, source_target_pairs={{0,1},{1,2},{2,3},{3,0},{4,5},{5,6},{6,7},{7,4},{8,9},{9,10},{10,1... | collective-permute-start | bytes 983048 | tf_op jit(solution)/shard_map/ppermute | solution.py:39
  23.3 17.7 %collective-permute-start.1 = (bf16[1,128,1280]{2,1,0:T(8,128)(2,1)S(1)}, bf16[1,128,1280]{2,1,0:T(8,128)(2,1)S(1)}, u32[]{:S(2)}, u32[]{:S(2)}) collective-permute-start(bf16[1,128,1280]{2,1,0:T(8,128)(2,1)S(1)} %get-tuple-element.34), channel_id=1, source_target_pairs={{0,3},{1,0},{2,1},{3,2},{4,7},{5,4},{6,5},{7,6},{8,11},{9,8},{10,9... | collective-permute-start | bytes 983048 | tf_op jit(solution)/shard_map/ppermute | solution.py:39
  25.1 5.8 %copy-start.1 = (bf16[1024,8192]{1,0:T(8,128)(2,1)S(1)}, bf16[1024,8192]{1,0:T(8,128)(2,1)}, u32[]{:S(2)}) copy-start(bf16[1024,8192]{1,0:T(8,128)(2,1)} %refs_2_.5) | copy-start | bytes 50331652
  30.9 2.2 %copy-start.4 = (bf16[1024,2048]{1,0:T(8,128)(2,1)S(1)}, bf16[1024,2048]{1,0:T(8,128)(2,1)}, u32[]{:S(2)}) copy-start(bf16[1024,2048]{1,0:T(8,128)(2,1)} %refs_3_.5) | copy-start | bytes 12582916
  33.1 7.3 %copy-start.38 = (s32[4]{0:T(128)S(1)}, s32[4]{0:T(128)}, u32[]{:S(2)}) copy-start(s32[4]{0:T(128)} %constant.143.clone) | copy-start | bytes 52
  40.4 10.9 %collective-permute-start.17 = (bf16[1,128,1280]{2,1,0:T(8,128)(2,1)}, bf16[1,128,1280]{2,1,0:T(8,128)(2,1)S(1)}, u32[]{:S(2)}, u32[]{:S(2)}) collective-permute-start(bf16[1,128,1280]{2,1,0:T(8,128)(2,1)} %get-tuple-element.47), channel_id=1, source_target_pairs={{0,3},{1,0},{2,1},{3,2},{4,7},{5,4},{6,5},{7,6},{8,11},{9,8},{10,9... | collective-permute-start | bytes 983048 | tf_op jit(solution)/shard_map/ppermute | solution.py:39
  43.7 19.1 %collective-permute-start.2 = (bf16[2,128,1280]{2,1,0:T(8,128)(2,1)}, bf16[2,128,1280]{2,1,0:T(8,128)(2,1)S(1)}, u32[]{:S(2)}, u32[]{:S(2)}) collective-permute-start(bf16[2,128,1280]{2,1,0:T(8,128)(2,1)} %get-tuple-element.35), channel_id=1, source_target_pairs={{0,1},{1,2},{2,3},{3,0},{4,5},{5,6},{6,7},{7,4},{8,9},{9,10},{10,1... | collective-permute-start | bytes 1966088 | tf_op jit(solution)/shard_map/ppermute | solution.py:39
  45.2 30.3 %collective-permute-start.3 = (bf16[2,128,1280]{2,1,0:T(8,128)(2,1)}, bf16[2,128,1280]{2,1,0:T(8,128)(2,1)}, u32[]{:S(2)}, u32[]{:S(2)}) collective-permute-start(bf16[2,128,1280]{2,1,0:T(8,128)(2,1)} %copy-done.25), channel_id=1, source_target_pairs={{0,3},{1,0},{2,1},{3,2},{4,7},{5,4},{6,5},{7,6},{8,11},{9,8},{10,9... | collective-permute-start | bytes 1966088 | tf_op jit(solution)/shard_map/ppermute | solution.py:39
  53.3 29.0 %collective-permute-start.18 = (bf16[2,128,1280]{2,1,0:T(8,128)(2,1)}, bf16[2,128,1280]{2,1,0:T(8,128)(2,1)}, u32[]{:S(2)}, u32[]{:S(2)}) collective-permute-start(bf16[2,128,1280]{2,1,0:T(8,128)(2,1)} %get-tuple-element.48), channel_id=1, source_target_pairs={{0,1},{1,2},{2,3},{3,0},{4,5},{5,6},{6,7},{7,4},{8,9},{9,10},{10,1... | collective-permute-start | bytes 1966088 | tf_op jit(solution)/shard_map/ppermute | solution.py:39
  63.6 22.0 %collective-permute-start.19 = (bf16[2,128,1280]{2,1,0:T(8,128)(2,1)}, bf16[2,128,1280]{2,1,0:T(8,128)(2,1)}, u32[]{:S(2)}, u32[]{:S(2)}) collective-permute-start(bf16[2,128,1280]{2,1,0:T(8,128)(2,1)} %get-tuple-element.49), channel_id=1, source_target_pairs={{0,3},{1,0},{2,1},{3,2},{4,7},{5,4},{6,5},{7,6},{8,11},{9,8},{10,9... | collective-permute-start | bytes 1966088 | tf_op jit(solution)/shard_map/ppermute | solution.py:39
  64.2 5.8 %copy-start.2 = (bf16[1024,8192]{1,0:T(8,128)(2,1)S(1)}, bf16[1024,8192]{1,0:T(8,128)(2,1)}, u32[]{:S(2)}) copy-start(bf16[1024,8192]{1,0:T(8,128)(2,1)} %refs_2_.5) | copy-start | bytes 50331652
  69.9 2.2 %copy-start.5 = (bf16[1024,2048]{1,0:T(8,128)(2,1)S(1)}, bf16[1024,2048]{1,0:T(8,128)(2,1)}, u32[]{:S(2)}) copy-start(bf16[1024,2048]{1,0:T(8,128)(2,1)} %refs_3_.5) | copy-start | bytes 12582916
  72.1 3.4 %copy-start.24 = (bf16[2,128,1280]{2,1,0:T(8,128)(2,1)S(1)}, bf16[2,128,1280]{2,1,0:T(8,128)(2,1)}, u32[]{:S(2)}) copy-start(bf16[2,128,1280]{2,1,0:T(8,128)(2,1)} %copy-done.23) | copy-start | bytes 1966084
  72.1 6.6 %copy-start.32 = (s32[64]{0:T(128)S(1)}, s32[64]{0:T(128)}, u32[]{:S(2)}) copy-start(s32[64]{0:T(128)} %param.18) | copy-start | bytes 772
  72.1 6.6 %copy-start.34 = (s32[64,1]{0,1:T(1,128)S(1)}, s32[64,1]{0,1:T(1,128)}, u32[]{:S(2)}) copy-start(s32[64,1]{0,1:T(1,128)} %param.20) | copy-start | bytes 772
  72.1 6.6 %copy-start.35 = (s32[64]{0:T(128)S(1)}, s32[64]{0:T(128)}, u32[]{:S(2)}) copy-start(s32[64]{0:T(128)} %param.19) | copy-start | bytes 772
  72.1 6.8 %copy-start.7 = (bf16[4,512,1,256]{3,1,2,0:T(8,128)(2,1)S(1)}, bf16[4,512,1,256]{3,1,2,0:T(8,128)(2,1)}, u32[]{:S(2)}) copy-start(bf16[4,512,1,256]{3,1,2,0:T(8,128)(2,1)} %param.17) | copy-start | bytes 3145732
  72.2 14.9 %copy-start.33 = (bf16[1024]{0:T(1024)(128)(2,1)S(1)}, bf16[1024]{0:T(1024)(128)(2,1)}, u32[]{:S(2)}) copy-start(bf16[1024]{0:T(1024)(128)(2,1)} %param.13) | copy-start | bytes 6148
  72.2 14.9 %copy-start.37 = (bf16[256]{0:T(256)(128)(2,1)S(1)}, bf16[256]{0:T(256)(128)(2,1)}, u32[]{:S(2)}) copy-start(bf16[256]{0:T(256)(128)(2,1)} %param.15) | copy-start | bytes 1540
  75.5 10.1 %copy-start.21 = (bf16[2,128,1280]{2,1,0:T(8,128)(2,1)}, bf16[2,128,1280]{2,1,0:T(8,128)(2,1)S(1)}, u32[]{:S(2)}) copy-start(bf16[2,128,1280]{2,1,0:T(8,128)(2,1)S(1)} %get-tuple-element.43.a) | copy-start | bytes 1966084
  77.1 8.5 %copy-start.19 = (f32[128,1280]{1,0:T(8,128)}, f32[128,1280]{1,0:T(8,128)S(1)}, u32[]{:S(2)}) copy-start(f32[128,1280]{1,0:T(8,128)S(1)} %get-tuple-element.37.keep_ref) | copy-start | bytes 1966084
  77.1 8.6 %collective-permute-start.4 = (bf16[128,1280]{1,0:T(8,128)(2,1)S(1)}, bf16[128,1280]{1,0:T(8,128)(2,1)S(1)}, u32[]{:S(2)}, u32[]{:S(2)}) collective-permute-start(bf16[128,1280]{1,0:T(8,128)(2,1)S(1)} %get-tuple-element.38), channel_id=1, source_target_pairs={{0,4},{1,5},{2,6},{3,7},{4,0},{5,1},{6,2},{7,3},{8,12},{9,13},{10,... | collective-permute-start | bytes 983048 | tf_op jit(solution)/shard_map/ppermute | solution.py:39
  79.0 20.8 %collective-permute-start.10 = (bf16[4,512,256]{2,1,0:T(8,128)(2,1)S(1)}, bf16[4,512,256]{2,1,0:T(8,128)(2,1)S(1)}, u32[]{:S(2)}, u32[]{:S(2)}) collective-permute-start(bf16[4,512,256]{2,1,0:T(8,128)(2,1)S(1)} %bitcast.24), channel_id=1, source_target_pairs={{0,8},{8,0},{16,24},{24,16},{32,40},{40,32},{48,56},{56,48},{64,72... | collective-permute-start | bytes 3145736 | tf_op jit(solution)/shard_map/ppermute | solution.py:43
  80.4 15.9 %collective-permute-start.8 = (bf16[2,512,256]{2,1,0:T(8,128)(2,1)}, bf16[2,512,256]{2,1,0:T(8,128)(2,1)}, u32[]{:S(2)}, u32[]{:S(2)}) collective-permute-start(bf16[2,512,256]{2,1,0:T(8,128)(2,1)} %slice.12), channel_id=1, source_target_pairs={{0,16},{8,24},{16,32},{24,40},{32,48},{40,56},{48,0},{56,8},{64,80... | collective-permute-start | bytes 1572872 | tf_op jit(solution)/shard_map/ppermute | solution.py:43
  82.3 15.1 %collective-permute-start.9 = (bf16[2,512,256]{2,1,0:T(8,128)(2,1)}, bf16[2,512,256]{2,1,0:T(8,128)(2,1)}, u32[]{:S(2)}, u32[]{:S(2)}) collective-permute-start(bf16[2,512,256]{2,1,0:T(8,128)(2,1)} %slice.13), channel_id=1, source_target_pairs={{0,48},{8,56},{16,0},{24,8},{32,16},{40,24},{48,32},{56,40},{64,11... | collective-permute-start | bytes 1572872 | tf_op jit(solution)/shard_map/ppermute | solution.py:43
  85.5 25.1 %collective-permute-start.11 = (bf16[4,512,256]{2,1,0:T(8,128)(2,1)S(1)}, bf16[4,512,256]{2,1,0:T(8,128)(2,1)}, u32[]{:S(2)}, u32[]{:S(2)}) collective-permute-start(bf16[4,512,256]{2,1,0:T(8,128)(2,1)S(1)} %collective-permute-done.6.refs_1_), channel_id=1, source_target_pairs={{0,8},{8,0},{16,24},{24,16},{32,40},{40,32},{48,56},{56,48},{64,72... | collective-permute-start | bytes 3145736 | tf_op jit(solution)/shard_map/ppermute | solution.py:43
  86.4 24.3 %collective-permute-start.12 = (bf16[4,512,256]{2,1,0:T(8,128)(2,1)}, bf16[4,512,256]{2,1,0:T(8,128)(2,1)}, u32[]{:S(2)}, u32[]{:S(2)}) collective-permute-start(bf16[4,512,256]{2,1,0:T(8,128)(2,1)} %collective-permute-done.7.refs_2_), channel_id=1, source_target_pairs={{0,8},{8,0},{16,24},{24,16},{32,40},{40,32},{48,56},{56,48},{64,72... | collective-permute-start | bytes 3145736 | tf_op jit(solution)/shard_map/ppermute | solution.py:43
  87.1 23.5 %copy-start.36 = (s32[64]{0:T(128)S(1)}, s32[64]{0:T(128)}, u32[]{:S(2)}) copy-start(s32[64]{0:T(128)} %get-tuple-element.67) | copy-start | bytes 772
  96.3 14.4 %collective-permute-start.13 = (bf16[2,512,256]{2,1,0:T(8,128)(2,1)}, bf16[2,512,256]{2,1,0:T(8,128)(2,1)S(1)}, u32[]{:S(2)}, u32[]{:S(2)}) collective-permute-start(bf16[2,512,256]{2,1,0:T(8,128)(2,1)} %collective-permute-done.8.refs_3_), channel_id=1, source_target_pairs={{0,8},{8,0},{16,24},{24,16},{32,40},{40,32},{48,56},{56,48},{64,72... | collective-permute-start | bytes 1572872 | tf_op jit(solution)/shard_map/ppermute | solution.py:43
  97.4 13.2 %collective-permute-start.14 = (bf16[2,512,256]{2,1,0:T(8,128)(2,1)}, bf16[2,512,256]{2,1,0:T(8,128)(2,1)S(1)}, u32[]{:S(2)}, u32[]{:S(2)}) collective-permute-start(bf16[2,512,256]{2,1,0:T(8,128)(2,1)} %collective-permute-done.9.refs_4_), channel_id=1, source_target_pairs={{0,8},{8,0},{16,24},{24,16},{32,40},{40,32},{48,56},{56,48},{64,72... | collective-permute-start | bytes 1572872 | tf_op jit(solution)/shard_map/ppermute | solution.py:43
  99.8 10.9 %copy-start.28 = (bf16[32,32,128]{2,1,0:T(8,128)(2,1)}, bf16[32,32,128]{2,1,0:T(8,128)(2,1)S(1)}, u32[]{:S(2)}) copy-start(bf16[32,32,128]{2,1,0:T(8,128)(2,1)S(1)} %get-tuple-element.39.q_ref) | copy-start | bytes 786436
  99.8 10.8 %copy-start.10 = (bf16[4,512,256]{2,1,0:T(8,128)(2,1)}, bf16[4,512,256]{2,1,0:T(8,128)(2,1)S(1)}, u32[]{:S(2)}) copy-start(bf16[4,512,256]{2,1,0:T(8,128)(2,1)S(1)} %collective-permute-done.10.refs_5_) | copy-start | bytes 3145732
  99.8 10.3 %collective-permute-start.5 = (bf16[32,32,128]{2,1,0:T(8,128)(2,1)S(1)}, bf16[32,32,128]{2,1,0:T(8,128)(2,1)S(1)}, u32[]{:S(2)}, u32[]{:S(2)}) collective-permute-start(bf16[32,32,128]{2,1,0:T(8,128)(2,1)S(1)} %get-tuple-element.39.q_ref), channel_id=1, source_target_pairs={{0,64},{8,72},{16,80},{24,88},{32,96},{40,104},{48,112},{56,120},{... | collective-permute-start | bytes 786440 | tf_op jit(solution)/shard_map/ppermute | solution.py:43
  110.1 19.4 %collective-permute-start.20 = (bf16[128,1280]{1,0:T(8,128)(2,1)}, bf16[128,1280]{1,0:T(8,128)(2,1)}, u32[]{:S(2)}, u32[]{:S(2)}) collective-permute-start(bf16[128,1280]{1,0:T(8,128)(2,1)} %get-tuple-element.51), channel_id=1, source_target_pairs={{0,4},{1,5},{2,6},{3,7},{4,0},{5,1},{6,2},{7,3},{8,12},{9,13},{10,... | collective-permute-start | bytes 983048 | tf_op jit(solution)/shard_map/ppermute | solution.py:39
  110.6 8.8 %copy-start.30 = (s32[32]{0:T(128)}, s32[32]{0:T(128)S(1)}, u32[]{:S(2)}) copy-start(s32[32]{0:T(128)S(1)} %slice.9.limit_ref) | copy-start | bytes 388
  110.6 12.3 %copy-start.6 = (bf16[64,1,64,1,256]{4,2,3,1,0:T(8,128)(2,1)S(1)}, bf16[64,1,64,1,256]{4,2,3,1,0:T(8,128)(2,1)}, u32[]{:S(2)}) copy-start(bf16[64,1,64,1,256]{4,2,3,1,0:T(8,128)(2,1)} %param.16) | copy-start | bytes 6291460
  110.6 8.8 %copy-start.13 = (bf16[2,512,256]{2,1,0:T(8,128)(2,1)}, bf16[2,512,256]{2,1,0:T(8,128)(2,1)S(1)}, u32[]{:S(2)}) copy-start(bf16[2,512,256]{2,1,0:T(8,128)(2,1)S(1)} %collective-permute-done.13.refs_8_) | copy-start | bytes 1572868
  110.6 8.8 %copy-start.15 = (bf16[2,512,256]{2,1,0:T(8,128)(2,1)}, bf16[2,512,256]{2,1,0:T(8,128)(2,1)S(1)}, u32[]{:S(2)}) copy-start(bf16[2,512,256]{2,1,0:T(8,128)(2,1)S(1)} %collective-permute-done.14.refs_9_) | copy-start | bytes 1572868
  110.7 1.6 %copy-start.8 = (bf16[4,512,1,256]{3,1,2,0:T(8,128)(2,1)S(1)}, bf16[4,512,1,256]{3,1,2,0:T(8,128)(2,1)}, u32[]{:S(2)}) copy-start(bf16[4,512,1,256]{3,1,2,0:T(8,128)(2,1)} %param.17) | copy-start | bytes 3145732
  112.3 1.2 copy-start.11
  119.5 25.0 %collective-permute-start.15 = (bf16[33,32,128]{2,1,0:T(8,128)(2,1)}, bf16[33,32,128]{2,1,0:T(8,128)(2,1)}, u32[]{:S(2)}, u32[]{:S(2)}) collective-permute-start(bf16[33,32,128]{2,1,0:T(8,128)(2,1)} %attend_prefix.1), channel_id=1, source_target_pairs={{0,64},{8,72},{16,80},{24,88},{32,96},{40,104},{48,112},{56,120},{... | collective-permute-start | bytes 811016 | tf_op jit(solution)/shard_map/ppermute | solution.py:43
  129.5 1.2 copy-start.9
  130.7 1.2 copy-start.12
  (12 other events, 11.2 us)

commit v6 on v5

--- a/solution.py
+++ b/solution.py
@@ -19,7 +19,8 @@
 SCALE = HD ** -0.5
 F32 = jnp.float32
 BF16 = jnp.bfloat16
-VMEM = 24 * 1024 * 1024
+VMEM = 20 * 1024 * 1024
+VMEM_PROJECT = 50 * 1024 * 1024
 
 
 def tp_shift(dy, dx):
@@ -100,7 +101,7 @@
             pltpu.SemaphoreType.DMA((count,)),
             pltpu.SemaphoreType.DMA((count,)),
         ],
-        compiler_params=pltpu.CompilerParams(vmem_limit_bytes=VMEM),
+        compiler_params=pltpu.CompilerParams(vmem_limit_bytes=VMEM_PROJECT),
         cost_estimate=SMALL,
         name="project",
     )(heads, *xs, wq, wp)
@@ -229,16 +230,8 @@
     return top, weights, total
 
 
-def prefix_copies(kvs, refs, buf, sem):
-    copies, k = [], 0
-    for g, group in enumerate(kvs):
-        mine, slot = [], 4 * g
-        for a in group:
-            n = a.shape[0]
-            mine.append(pltpu.make_async_copy(refs[k], buf.at[pl.ds(slot, n)], sem.at[k]))
-            slot, k = slot + n, k + 1
-        copies.append(mine)
-    return copies
+def prefix_copies(refs, buf, sem):
+    return [pltpu.make_async_copy(refs[g], buf.at[pl.ds(4 * g, 4)], sem.at[g]) for g in range(8)]
 
 
 def cache_copies(cache_ref, at_ref, first, cbuf, sem):
@@ -251,21 +244,19 @@
 
 
 def attend(limits, lengths, order, keep, more, bias, cosine, sine, cache, kvs):
-    flat = [a for group in kvs for a in group]
-
     def kernel(limit_ref, length_ref, at_ref, keep_ref, more_ref, bias_ref, cos_ref, sin_ref, cache_ref, *refs):
-        o_ref, buf, sem, qbuf, cbuf, csem = refs[len(flat) :]
-        prefix = prefix_copies(kvs, refs, buf, sem)
+        o_ref, buf, sem, qbuf, cbuf, csem = refs[len(kvs) :]
+        prefix = prefix_copies(refs, buf, sem)
         caches = cache_copies(cache_ref, at_ref, 32, cbuf, csem)
         for g in range(8):
-            for c in prefix[g] + caches[4 * g : 4 * g + 4]:
+            for c in [prefix[g]] + caches[4 * g : 4 * g + 4]:
                 c.start()
         new_all = rotated(keep_ref, more_ref, bias_ref, cos_ref, sin_ref, ROWS, qbuf)
         for p in range(32):
             o_ref[p, :, QW:] = new_all[4 * p : 4 * p + 4].astype(BF16)
         new_all = new_all.astype(BF16)
         for g in range(8):
-            for c in prefix[g] + caches[4 * g : 4 * g + 4]:
+            for c in [prefix[g]] + caches[4 * g : 4 * g + 4]:
                 c.wait()
             q = qbuf[128 * g : 128 * g + 128, :].astype(BF16)
             new = new_all[16 * g : 16 * g + 16]
@@ -281,19 +272,19 @@
 
     return pl.pallas_call(
         kernel,
-        in_specs=[IN_SMEM] * 3 + [IN_VMEM] * 5 + [ANY] * (1 + len(flat)),
+        in_specs=[IN_SMEM] * 3 + [IN_VMEM] * 5 + [ANY] * (1 + len(kvs)),
         out_specs=IN_VMEM,
         out_shape=jax.ShapeDtypeStruct((32, 4, COLS), BF16),
         scratch_shapes=[
             pltpu.VMEM((32, 512, 2 * HD), BF16),
-            pltpu.SemaphoreType.DMA((len(flat),)),
+            pltpu.SemaphoreType.DMA((len(kvs),)),
             pltpu.VMEM((1024, HD), F32),
         ]
         + CACHE_SCRATCH,
         compiler_params=pltpu.CompilerParams(vmem_limit_bytes=VMEM),
         cost_estimate=SMALL,
         name="attend",
-    )(limits, lengths, order, keep, more, bias, cosine, sine, cache, *flat)
+    )(limits, lengths, order, keep, more, bias, cosine, sine, cache, *kvs)
 
 
 def make_queries(keep, more, bias, cosine, sine):
@@ -314,19 +305,15 @@
 
 
 def attend_prefix(limits, q, kvs):
-    flat = [a for group in kvs for a in group]
-
     def kernel(limit_ref, q_ref, *refs):
-        o_ref, buf, sem = refs[len(flat) :]
-        prefix = prefix_copies(kvs, refs, buf, sem)
-        for mine in prefix:
-            for c in mine:
-                c.start()
+        o_ref, buf, sem = refs[len(kvs) :]
+        prefix = prefix_copies(refs, buf, sem)
+        for c in prefix:
+            c.start()
         lane = lax.broadcasted_iota(jnp.int32, (32, 128), 1)
         stats = jnp.zeros((32, 128), F32)
         for g in range(8):
-            for c in prefix[g]:
-                c.wait()
+            prefix[g].wait()
             q = q_ref[4 * g : 4 * g + 4].reshape(128, HD)
             top, (w,), total = softmax(prefix_scores(q, buf, limit_ref, g))
             o = prefix_values(w, buf, g) / total
@@ -341,14 +328,14 @@
 
     return pl.pallas_call(
         kernel,
-        in_specs=[IN_SMEM, IN_VMEM] + [ANY] * len(flat),
+        in_specs=[IN_SMEM, IN_VMEM] + [ANY] * len(kvs),
         out_specs=IN_VMEM,
         out_shape=jax.ShapeDtypeStruct((33, 32, HD), BF16),
-        scratch_shapes=[pltpu.VMEM((32, 512, 2 * HD), BF16), pltpu.SemaphoreType.DMA((len(flat),))],
+        scratch_shapes=[pltpu.VMEM((32, 512, 2 * HD), BF16), pltpu.SemaphoreType.DMA((len(kvs),))],
         compiler_params=pltpu.CompilerParams(vmem_limit_bytes=VMEM),
         cost_estimate=SMALL,
         name="attend_prefix",
-    )(limits, q, *flat)
+    )(limits, q, *kvs)
 
 
 def attend_near(lengths, order, q, new, cache):
@@ -426,9 +413,8 @@
 
     own = prefix_pairs.reshape(4, 512, 2 * HD)
     below, above = over_roll(own, 0, 1, 0), over_roll(own, 0, 3, 0)
-    far_a, far_b = over_roll(below[:2], 0, 1, 0), over_roll(above[2:], 0, 3, 0)
-    kvs = [[own], [below], [above], [far_a, far_b]]
-    kvs = kvs + [[over_roll(a, 0, 0, 1) for a in group] for group in kvs]
+    kvs = [own, below, above, over_roll(below, 0, 1, 0)]
+    kvs = kvs + [over_roll(a, 0, 0, 1) for a in kvs]
 
     x_o, x_m = sort_rows(
         jnp.stack([my_y, my_z, my_c]).astype(jnp.int32),

time: 150 us -> 132 us (0.88)
  local copies, waits for them, and re-layouts: 45.4 us -> 13.4 us
  waiting for transfers between devices: 26.3 us -> 41.5 us
    unnamed x78 -> x44, local copies, waits for them, and re-layouts: 40.4 us -> 11.1 us
    ppermute x10, waiting for transfers between devices: 13.4 us -> 30.3 us  [over_tp(): return lax.ppermute(a, 'tp', tp_shift(dy, dx))]
    ppermute x11 -> x9, starting transfers between devices: 14.6 us -> 11.3 us  [over_roll(): return lax.ppermute(a, 'roll', roll_shift(dy, dz, dc))]
    ppermute x10, starting transfers between devices: 11.4 us -> 14.8 us  [over_tp(): return lax.ppermute(a, 'tp', tp_shift(dy, dx))]
    slice x2 -> x0, local copies, waits for them, and re-layouts: 2.72 us -> none  [the longest x1 1.9 us: on_device(): above[2:]]
    ppermute x11 -> x9, waiting for transfers between devices: 12.8 us -> 11.2 us  [over_roll(): return lax.ppermute(a, 'roll', roll_shift(dy, dz, dc))]
  transfers between devices with their start and end apart: 21 -> 19, of which waited for: 5 -> 6; matrix products, arithmetic and copies ran while one was open for 5% -> 3% of each run, Pallas kernels for 29% -> 34%
where the time goes in v6:
time: 132 us
  Pallas kernels  48.3 us (37%)
  waiting for transfers between devices  41.5 us (31%)
  starting transfers between devices  26 us (20%)
  local copies, waits for them, and re-layouts  13.4 us (10%)
  other arithmetic  1.54 us (1%)
    ppermute x10, waiting for transfers between devices, over_tp(): return lax.ppermute(a, 'tp', tp_shift(dy, dx))  30.3 us
    pallas_call x3, Pallas kernels, project(): pl.pallas_call(kernel, in_specs=[IN_SMEM] + [IN_VMEM] * len(xs) + [IN_HBM...  15.8 us
    ppermute x10, starting transfers between devices, over_tp(): return lax.ppermute(a, 'tp', tp_shift(dy, dx))  14.8 us
    ppermute x9, starting transfers between devices, over_roll(): return lax.ppermute(a, 'roll', roll_shift(dy, dz, dc))  11.3 us
    ppermute x9, waiting for transfers between devices, over_roll(): return lax.ppermute(a, 'roll', roll_shift(dy, dz, dc))  11.2 us
    unnamed x44, local copies, waits for them, and re-layouts  11.1 us
    pallas_call x1, Pallas kernels, attend(): pl.pallas_call(kernel, in_specs=[IN_SMEM] * 3 + [IN_VMEM] * 5 + [ANY] * (...  8.49 us
    pallas_call x1, Pallas kernels, attend_prefix(): pl.pallas_call(kernel, in_specs=[IN_SMEM, IN_VMEM] + [ANY] * len(kvs), ou...  6.29 us
  transfers between devices with their start and end apart: 19, of which 6 were waited for; matrix products, arithmetic and copies ran while one was open for 3% of the time, Pallas kernels for 34%

profile of v6, /device:TPU:0, one launch (start us, length us, event | category | flops | bytes accessed | tf_op | source)
XLA Modules:
  0.0 131.7 jit_solution(1974170049435645034)
XLA Ops:
  0.6 2.1 %collective-permute-start.6 = (bf16[4,512,256]{2,1,0:T(8,128)(2,1)}, bf16[4,512,256]{2,1,0:T(8,128)(2,1)}, u32[]{:S(2)}, u32[]{:S(2)}) collective-permute-start(bf16[4,512,256]{2,1,0:T(8,128)(2,1)} %bitcast.22), channel_id=1, source_target_pairs={{0,16},{8,24},{16,32},{24,40},{32,48},{40,56},{48,0},{56,8},{64,80... | collective-permute-start | bytes 3145736 | tf_op jit(solution)/shard_map/ppermute | solution.py:44
  2.7 2.2 %collective-permute-start.7 = (bf16[4,512,256]{2,1,0:T(8,128)(2,1)}, bf16[4,512,256]{2,1,0:T(8,128)(2,1)}, u32[]{:S(2)}, u32[]{:S(2)}) collective-permute-start(bf16[4,512,256]{2,1,0:T(8,128)(2,1)} %bitcast.23), channel_id=1, source_target_pairs={{0,48},{8,56},{16,0},{24,8},{32,16},{40,24},{48,32},{56,40},{64,11... | collective-permute-start | bytes 3145736 | tf_op jit(solution)/shard_map/ppermute | solution.py:44
  4.9 1.2 reshape.175.x_ref
  6.1 0.7 broadcast_in_dim.48
  7.0 0.9 sort_rows.1
  8.0 4.2 %project.5 = (bf16[1,128,1280]{2,1,0:T(8,128)(2,1)S(1)}, bf16[1,128,1280]{2,1,0:T(8,128)(2,1)S(1)}, bf16[1,128,1280]{2,1,0:T(8,128)(2,1)S(1)}, bf16[1,128,1280]{2,1,0:T(8,128)(2,1)S(1)}) custom-call(s32[2]{0:T(128)S(1)} %pad_add_fusion.3.heads_ref, bf16[128,1024]{1,0:T(8,128)(2,1)S(1)} %get-tuple-element.28.refs_0_, ...), custom_call_target="tpu_custom_call" | custom-call | flops 1000000 | bytes 100000 | tf_op jit(solution)/shard_map/project/pallas_call | solution.py:93
  12.2 1.6 %collective-permute-start.14 = (bf16[1,128,1280]{2,1,0:T(8,128)(2,1)S(1)}, bf16[1,128,1280]{2,1,0:T(8,128)(2,1)S(1)}, u32[]{:S(2)}, u32[]{:S(2)}) collective-permute-start(bf16[1,128,1280]{2,1,0:T(8,128)(2,1)S(1)} %get-tuple-element.46), channel_id=1, source_target_pairs={{0,1},{1,2},{2,3},{3,0},{4,5},{5,6},{6,7},{7,4},{8,9},{9,10},{10,1... | collective-permute-start | bytes 983048 | tf_op jit(solution)/shard_map/ppermute | solution.py:40
  13.8 1.5 %collective-permute-start = (bf16[1,128,1280]{2,1,0:T(8,128)(2,1)S(1)}, bf16[1,128,1280]{2,1,0:T(8,128)(2,1)S(1)}, u32[]{:S(2)}, u32[]{:S(2)}) collective-permute-start(bf16[1,128,1280]{2,1,0:T(8,128)(2,1)S(1)} %get-tuple-element.33), channel_id=1, source_target_pairs={{0,1},{1,2},{2,3},{3,0},{4,5},{5,6},{6,7},{7,4},{8,9},{9,10},{10,1... | collective-permute-start | bytes 983048 | tf_op jit(solution)/shard_map/ppermute | solution.py:40
  15.3 1.7 %collective-permute-start.1 = (bf16[1,128,1280]{2,1,0:T(8,128)(2,1)S(1)}, bf16[1,128,1280]{2,1,0:T(8,128)(2,1)S(1)}, u32[]{:S(2)}, u32[]{:S(2)}) collective-permute-start(bf16[1,128,1280]{2,1,0:T(8,128)(2,1)S(1)} %get-tuple-element.34), channel_id=1, source_target_pairs={{0,3},{1,0},{2,1},{3,2},{4,7},{5,4},{6,5},{7,6},{8,11},{9,8},{10,9... | collective-permute-start | bytes 983048 | tf_op jit(solution)/shard_map/ppermute | solution.py:40
  17.2 11.1 %collective-permute-done.6.refs_1_ = bf16[4,512,256]{2,1,0:T(8,128)(2,1)} collective-permute-done((bf16[4,512,256]{2,1,0:T(8,128)(2,1)}, bf16[4,512,256]{2,1,0:T(8,128)(2,1)}, u32[]{:S(2)}, u32[]{:S(2)}) %collective-permute-start.6) | collective-permute-done | bytes 1048608 | tf_op jit(solution)/shard_map/ppermute | solution.py:44
  28.4 7.3 %project.4 = (bf16[2,128,1280]{2,1,0:T(8,128)(2,1)}, bf16[2,128,1280]{2,1,0:T(8,128)(2,1)}, bf16[2,128,1280]{2,1,0:T(8,128)(2,1)}, bf16[2,128,1280]{2,1,0:T(8,128)(2,1)S(1)}) custom-call(s32[4]{0:T(128)S(1)} %pad_add_fusion.2.heads_ref, bf16[128,1024]{1,0:T(8,128)(2,1)S(1)} %get-tuple-element.28.refs_0_, bf16[128,1024]{1,0:T(8,128)(2,1)S(1)} %get-tuple-element.29.refs_1_, ...), custom_call_target="tpu_custom_call" | custom-call | flops 1000000 | bytes 100000 | tf_op jit(solution)/shard_map/project/pallas_call | solution.py:93
  35.7 2.8 %collective-permute-start.15 = (bf16[1,128,1280]{2,1,0:T(8,128)(2,1)S(1)}, bf16[1,128,1280]{2,1,0:T(8,128)(2,1)S(1)}, u32[]{:S(2)}, u32[]{:S(2)}) collective-permute-start(bf16[1,128,1280]{2,1,0:T(8,128)(2,1)S(1)} %get-tuple-element.47), channel_id=1, source_target_pairs={{0,3},{1,0},{2,1},{3,2},{4,7},{5,4},{6,5},{7,6},{8,11},{9,8},{10,9... | collective-permute-start | bytes 983048 | tf_op jit(solution)/shard_map/ppermute | solution.py:40
  38.5 2.0 %add_far.2 = (bf16[2,128,1280]{2,1,0:T(8,128)(2,1)}, bf16[2,128,1280]{2,1,0:T(8,128)(2,1)}) custom-call(bf16[2,128,1280]{2,1,0:T(8,128)(2,1)} %get-tuple-element.31.r, bf16[2,128,1280]{2,1,0:T(8,128)(2,1)} %get-tuple-element.32.l, bf16[1,128,1280]{2,1,0:T(8,128)(2,1)S(1)} %collective-permute-done.u, ...), custom_call_target="tpu_custom_call", output_to_operand_aliasing={{0}: (0, {}), {1}: (1, {})} | custom-call | flops 1000000 | bytes 100000 | tf_op jit(solution)/shard_map/add_far/pallas_call | solution.py:143
  40.5 3.2 %collective-permute-start.3 = (bf16[2,128,1280]{2,1,0:T(8,128)(2,1)}, bf16[2,128,1280]{2,1,0:T(8,128)(2,1)}, u32[]{:S(2)}, u32[]{:S(2)}) collective-permute-start(bf16[2,128,1280]{2,1,0:T(8,128)(2,1)} %get-tuple-element.36), channel_id=1, source_target_pairs={{0,3},{1,0},{2,1},{3,2},{4,7},{5,4},{6,5},{7,6},{8,11},{9,8},{10,9... | collective-permute-start | bytes 1966088 | tf_op jit(solution)/shard_map/ppermute | solution.py:40
  43.8 2.9 %collective-permute-done.15.d = bf16[1,128,1280]{2,1,0:T(8,128)(2,1)S(1)} collective-permute-done((bf16[1,128,1280]{2,1,0:T(8,128)(2,1)S(1)}, bf16[1,128,1280]{2,1,0:T(8,128)(2,1)S(1)}, u32[]{:S(2)}, u32[]{:S(2)}) %collective-permute-start.15) | collective-permute-done | bytes 327712 | tf_op jit(solution)/shard_map/ppermute | solution.py:40
  46.7 1.8 %add_far.3 = (bf16[2,128,1280]{2,1,0:T(8,128)(2,1)}, bf16[2,128,1280]{2,1,0:T(8,128)(2,1)S(1)}) custom-call(bf16[2,128,1280]{2,1,0:T(8,128)(2,1)} %get-tuple-element.44.r, bf16[2,128,1280]{2,1,0:T(8,128)(2,1)S(1)} %get-tuple-element.45.l, bf16[1,128,1280]{2,1,0:T(8,128)(2,1)S(1)} %collective-permute-done.14.u, ...), custom_call_target="tpu_custom_call", output_to_operand_aliasing={{0}: (0, {}), {1}: (1, {})} | custom-call | flops 1000000 | bytes 100000 | tf_op jit(solution)/shard_map/add_far/pallas_call | solution.py:143
  48.5 1.2 collective-permute-start.16
  50.0 4.2 %project.3 = (bf16[2,128,1280]{2,1,0:T(8,128)(2,1)S(1)}, bf16[2,128,1280]{2,1,0:T(8,128)(2,1)S(1)}) custom-call(s32[2]{0:T(128)S(1)} %pad_add_fusion.heads_ref, bf16[128,1024]{1,0:T(8,128)(2,1)S(1)} %get-tuple-element.28.refs_0_, bf16[128,1024]{1,0:T(8,128)(2,1)S(1)} %get-tuple-element.29.refs_1_, bf16[1024,8192]{1,0:T(8,128)(2,1)} %refs_2_.5, ...), custom_call_target="tpu_custom_call" | custom-call | flops 1000000 | bytes 100000 | tf_op jit(solution)/shard_map/project/pallas_call | solution.py:93
  54.2 0.9 copy-done.7
  55.1 0.2 fusion.3
  55.3 4.3 %collective-permute-done.2.b = bf16[2,128,1280]{2,1,0:T(8,128)(2,1)S(1)} collective-permute-done((bf16[2,128,1280]{2,1,0:T(8,128)(2,1)}, bf16[2,128,1280]{2,1,0:T(8,128)(2,1)S(1)}, u32[]{:S(2)}, u32[]{:S(2)}) %collective-permute-start.2) | collective-permute-done | bytes 655392 | tf_op jit(solution)/shard_map/ppermute | solution.py:40
  59.6 0.9 copy-done.9
  60.5 1.1 copy-done.10
  61.6 1.3 sum_x.2
  62.9 1.8 %collective-permute-start.4 = (bf16[128,1280]{1,0:T(8,128)(2,1)S(1)}, bf16[128,1280]{1,0:T(8,128)(2,1)S(1)}, u32[]{:S(2)}, u32[]{:S(2)}) collective-permute-start(bf16[128,1280]{1,0:T(8,128)(2,1)S(1)} %get-tuple-element.38), channel_id=1, source_target_pairs={{0,4},{1,5},{2,6},{3,7},{4,0},{5,1},{6,2},{7,3},{8,12},{9,13},{10,... | collective-permute-start | bytes 983048 | tf_op jit(solution)/shard_map/ppermute | solution.py:40
  64.7 7.0 %collective-permute-done.16.b = bf16[2,128,1280]{2,1,0:T(8,128)(2,1)} collective-permute-done((bf16[2,128,1280]{2,1,0:T(8,128)(2,1)}, bf16[2,128,1280]{2,1,0:T(8,128)(2,1)}, u32[]{:S(2)}, u32[]{:S(2)}) %collective-permute-start.16) | collective-permute-done | bytes 655392 | tf_op jit(solution)/shard_map/ppermute | solution.py:40
  71.7 0.5 collective-permute-start.11
  72.6 0.7 collective-permute-done.4.more_ref
  73.3 0.2 collective-permute-start.17
  73.4 0.5 fusion
  74.1 0.3 make_queries.1
  74.4 15.5 %collective-permute-done.17.c = bf16[2,128,1280]{2,1,0:T(8,128)(2,1)S(1)} collective-permute-done((bf16[2,128,1280]{2,1,0:T(8,128)(2,1)}, bf16[2,128,1280]{2,1,0:T(8,128)(2,1)S(1)}, u32[]{:S(2)}, u32[]{:S(2)}) %collective-permute-start.17) | collective-permute-done | bytes 655392 | tf_op jit(solution)/shard_map/ppermute | solution.py:40
  89.9 3.2 %collective-permute-start.5 = (bf16[32,32,128]{2,1,0:T(8,128)(2,1)S(1)}, bf16[32,32,128]{2,1,0:T(8,128)(2,1)S(1)}, u32[]{:S(2)}, u32[]{:S(2)}) collective-permute-start(bf16[32,32,128]{2,1,0:T(8,128)(2,1)S(1)} %get-tuple-element.39.q_ref), channel_id=1, source_target_pairs={{0,64},{8,72},{16,80},{24,88},{32,96},{40,104},{48,112},{56,120},{... | collective-permute-start | bytes 786440 | tf_op jit(solution)/shard_map/ppermute | solution.py:44
  93.1 1.1 copy-done.8
  94.2 1.9 %sum_x.3 = (f32[128,1280]{1,0:T(8,128)S(1)}, bf16[128,1280]{1,0:T(8,128)(2,1)}) custom-call(bf16[2,128,1280]{2,1,0:T(8,128)(2,1)S(1)} %copy-done.8, bf16[2,128,1280]{2,1,0:T(8,128)(2,1)} %collective-permute-done.16.b, bf16[2,128,1280]{2,1,0:T(8,128)(2,1)S(1)} %collective-permute-done.17.c), custom_call_target="tpu_custom_call" | custom-call | flops 1000000 | bytes 100000 | tf_op jit(solution)/shard_map/sum_x/pallas_call | solution.py:161
  96.1 0.9 copy-done.5
  97.0 1.0 copy-done.2
  98.0 0.7 collective-permute-start.18
  98.8 1.4 %copy-done.3 = bf16[4,512,256]{2,1,0:T(8,128)(2,1)S(1)} copy-done((bf16[4,512,256]{2,1,0:T(8,128)(2,1)S(1)}, bf16[4,512,256]{2,1,0:T(8,128)(2,1)}, u32[]{:S(2)}) %copy-start.3) | copy-done | bytes 1048600
  100.2 6.3 %attend_prefix.1 = bf16[33,32,128]{2,1,0:T(8,128)(2,1)} custom-call(s32[32]{0:T(128)S(1)} %slice.3.limit_ref, bf16[32,32,128]{2,1,0:T(8,128)(2,1)S(1)} %collective-permute-done.5.q_ref, bf16[4,512,256]{2,1,0:T(8,128)(2,1)S(1)} %bitcast.25, bf16[4,512,256]{2,1,0:T(8,128)(2,1)} %collective-permute-done.6.refs_1_, ...), custom_call_target="tpu_custom_call" | custom-call | flops 1000000 | bytes 100000 | tf_op jit(solution)/shard_map/attend_prefix/pallas_call | solution.py:329
  106.5 3.2 %collective-permute-start.13 = (bf16[33,32,128]{2,1,0:T(8,128)(2,1)}, bf16[33,32,128]{2,1,0:T(8,128)(2,1)}, u32[]{:S(2)}, u32[]{:S(2)}) collective-permute-start(bf16[33,32,128]{2,1,0:T(8,128)(2,1)} %attend_prefix.1), channel_id=1, source_target_pairs={{0,64},{8,72},{16,80},{24,88},{32,96},{40,104},{48,112},{56,120},{... | collective-permute-start | bytes 811016 | tf_op jit(solution)/shard_map/ppermute | solution.py:44
  109.7 0.9 copy-done.13
  110.6 5.6 %attend_near.1 = (f32[1024,128]{1,0:T(8,128)S(1)}, f32[1024,128]{1,0:T(8,128)S(1)}) custom-call(s32[64]{0:T(128)S(1)} %get-tuple-element.60.length_ref, s32[64]{0:T(128)S(1)} %get-tuple-element.62.at_ref.order_ref, bf16[32,32,128]{2,1,0:T(8,128)(2,1)S(1)} %copy-done.13, bf16[128,256]{1,0:T(8,128)(2,1)S(1)} %get-tuple-element.40.new_ref, ...), custom_call_target="tpu_custom_call" | custom-call | flops 1000000 | bytes 100000 | tf_op jit(solution)/shard_map/attend_near/pallas_call | solution.py:355
  116.2 1.2 copy-done.4
  117.5 1.1 copy-done.6
  118.5 0.7 copy-done.15
  119.2 8.5 %attend.1.done_ref = bf16[32,4,1280]{2,1,0:T(4,128)(2,1)S(1)} custom-call(s32[32]{0:T(128)S(1)} %copy-done.15, s32[64]{0:T(128)S(1)} %get-tuple-element.60.length_ref, s32[64]{0:T(128)S(1)} %get-tuple-element.62.at_ref.order_ref, f32[128,1280]{1,0:T(8,128)S(1)} %copy-done.6, bf16[128,1280]{1,0:T(8,128)(2,1)} %collective-permute-done.18.more_ref, ...), custom_call_target="tpu_custom_call" | custom-call | flops 1000000 | bytes 100000 | tf_op jit(solution)/shard_map/attend/pallas_call | solution.py:273
  127.7 4.0 %merge_rows.1 = (bf16[64,4,1024]{2,1,0:T(4,128)(2,1)}, bf16[64,4,256]{2,1,0:T(4,128)(2,1)}) custom-call(s32[64]{0:T(128)S(1)} %get-tuple-element.62.at_ref.order_ref, bf16[33,32,128]{2,1,0:T(8,128)(2,1)} %collective-permute-done.13.far_ref, f32[1024,128]{1,0:T(8,128)S(1)} %get-tuple-element.41.o_ref, f32[1024,128]{1,0:T(8,128)S(1)} %get-tuple-element.42.l_ref, ...), custom_call_target="tpu_custom_call" | custom-call | flops 1000000 | bytes 100000 | tf_op jit(solution)/shard_map/merge_rows/pallas_call | solution.py:384
  (73 shorter events, 1.4 us)
Async XLA Ops:
  0.6 27.7 %collective-permute-start.6 = (bf16[4,512,256]{2,1,0:T(8,128)(2,1)}, bf16[4,512,256]{2,1,0:T(8,128)(2,1)}, u32[]{:S(2)}, u32[]{:S(2)}) collective-permute-start(bf16[4,512,256]{2,1,0:T(8,128)(2,1)} %bitcast.22), channel_id=1, source_target_pairs={{0,16},{8,24},{16,32},{24,40},{32,48},{40,56},{48,0},{56,8},{64,80... | collective-permute-start | bytes 3145736 | tf_op jit(solution)/shard_map/ppermute | solution.py:44
  2.7 69.0 %collective-permute-start.7 = (bf16[4,512,256]{2,1,0:T(8,128)(2,1)}, bf16[4,512,256]{2,1,0:T(8,128)(2,1)}, u32[]{:S(2)}, u32[]{:S(2)}) collective-permute-start(bf16[4,512,256]{2,1,0:T(8,128)(2,1)} %bitcast.23), channel_id=1, source_target_pairs={{0,48},{8,56},{16,0},{24,8},{32,16},{40,24},{48,32},{56,40},{64,11... | collective-permute-start | bytes 3145736 | tf_op jit(solution)/shard_map/ppermute | solution.py:44
  8.0 9.1 %copy-start.21 = (s32[4]{0:T(128)S(1)}, s32[4]{0:T(128)}, u32[]{:S(2)}) copy-start(s32[4]{0:T(128)} %constant.143.clone) | copy-start | bytes 52
  12.2 28.3 %collective-permute-start.14 = (bf16[1,128,1280]{2,1,0:T(8,128)(2,1)S(1)}, bf16[1,128,1280]{2,1,0:T(8,128)(2,1)S(1)}, u32[]{:S(2)}, u32[]{:S(2)}) collective-permute-start(bf16[1,128,1280]{2,1,0:T(8,128)(2,1)S(1)} %get-tuple-element.46), channel_id=1, source_target_pairs={{0,1},{1,2},{2,3},{3,0},{4,5},{5,6},{6,7},{7,4},{8,9},{9,10},{10,1... | collective-permute-start | bytes 983048 | tf_op jit(solution)/shard_map/ppermute | solution.py:40
  13.8 21.9 %collective-permute-start = (bf16[1,128,1280]{2,1,0:T(8,128)(2,1)S(1)}, bf16[1,128,1280]{2,1,0:T(8,128)(2,1)S(1)}, u32[]{:S(2)}, u32[]{:S(2)}) collective-permute-start(bf16[1,128,1280]{2,1,0:T(8,128)(2,1)S(1)} %get-tuple-element.33), channel_id=1, source_target_pairs={{0,1},{1,2},{2,3},{3,0},{4,5},{5,6},{6,7},{7,4},{8,9},{9,10},{10,1... | collective-permute-start | bytes 983048 | tf_op jit(solution)/shard_map/ppermute | solution.py:40
  15.3 23.2 %collective-permute-start.1 = (bf16[1,128,1280]{2,1,0:T(8,128)(2,1)S(1)}, bf16[1,128,1280]{2,1,0:T(8,128)(2,1)S(1)}, u32[]{:S(2)}, u32[]{:S(2)}) collective-permute-start(bf16[1,128,1280]{2,1,0:T(8,128)(2,1)S(1)} %get-tuple-element.34), channel_id=1, source_target_pairs={{0,3},{1,0},{2,1},{3,2},{4,7},{5,4},{6,5},{7,6},{8,11},{9,8},{10,9... | collective-permute-start | bytes 983048 | tf_op jit(solution)/shard_map/ppermute | solution.py:40
  28.3 43.9 %collective-permute-start.8 = (bf16[4,512,256]{2,1,0:T(8,128)(2,1)}, bf16[4,512,256]{2,1,0:T(8,128)(2,1)}, u32[]{:S(2)}, u32[]{:S(2)}) collective-permute-start(bf16[4,512,256]{2,1,0:T(8,128)(2,1)} %collective-permute-done.6.refs_1_), channel_id=1, source_target_pairs={{0,16},{8,24},{16,32},{24,40},{32,48},{40,56},{48,0},{56,8},{64,80... | collective-permute-start | bytes 3145736 | tf_op jit(solution)/shard_map/ppermute | solution.py:44
  35.7 11.0 %collective-permute-start.15 = (bf16[1,128,1280]{2,1,0:T(8,128)(2,1)S(1)}, bf16[1,128,1280]{2,1,0:T(8,128)(2,1)S(1)}, u32[]{:S(2)}, u32[]{:S(2)}) collective-permute-start(bf16[1,128,1280]{2,1,0:T(8,128)(2,1)S(1)} %get-tuple-element.47), channel_id=1, source_target_pairs={{0,3},{1,0},{2,1},{3,2},{4,7},{5,4},{6,5},{7,6},{8,11},{9,8},{10,9... | collective-permute-start | bytes 983048 | tf_op jit(solution)/shard_map/ppermute | solution.py:40
  40.5 19.1 %collective-permute-start.2 = (bf16[2,128,1280]{2,1,0:T(8,128)(2,1)}, bf16[2,128,1280]{2,1,0:T(8,128)(2,1)S(1)}, u32[]{:S(2)}, u32[]{:S(2)}) collective-permute-start(bf16[2,128,1280]{2,1,0:T(8,128)(2,1)} %get-tuple-element.35), channel_id=1, source_target_pairs={{0,1},{1,2},{2,3},{3,0},{4,5},{5,6},{6,7},{7,4},{8,9},{9,10},{10,1... | collective-permute-start | bytes 1966088 | tf_op jit(solution)/shard_map/ppermute | solution.py:40
  40.5 19.9 %collective-permute-start.3 = (bf16[2,128,1280]{2,1,0:T(8,128)(2,1)}, bf16[2,128,1280]{2,1,0:T(8,128)(2,1)}, u32[]{:S(2)}, u32[]{:S(2)}) collective-permute-start(bf16[2,128,1280]{2,1,0:T(8,128)(2,1)} %get-tuple-element.36), channel_id=1, source_target_pairs={{0,3},{1,0},{2,1},{3,2},{4,7},{5,4},{6,5},{7,6},{8,11},{9,8},{10,9... | collective-permute-start | bytes 1966088 | tf_op jit(solution)/shard_map/ppermute | solution.py:40
  48.5 1.4 %copy-start.11 = (bf16[2,128,1280]{2,1,0:T(8,128)(2,1)}, bf16[2,128,1280]{2,1,0:T(8,128)(2,1)S(1)}, u32[]{:S(2)}) copy-start(bf16[2,128,1280]{2,1,0:T(8,128)(2,1)S(1)} %get-tuple-element.49) | copy-start | bytes 1966084
  48.5 23.3 %collective-permute-start.16 = (bf16[2,128,1280]{2,1,0:T(8,128)(2,1)}, bf16[2,128,1280]{2,1,0:T(8,128)(2,1)}, u32[]{:S(2)}, u32[]{:S(2)}) collective-permute-start(bf16[2,128,1280]{2,1,0:T(8,128)(2,1)} %get-tuple-element.48), channel_id=1, source_target_pairs={{0,1},{1,2},{2,3},{3,0},{4,5},{5,6},{6,7},{7,4},{8,9},{9,10},{10,1... | collective-permute-start | bytes 1966088 | tf_op jit(solution)/shard_map/ppermute | solution.py:40
  49.9 5.2 %copy-start.16 = (s32[64]{0:T(128)S(1)}, s32[64]{0:T(128)}, u32[]{:S(2)}) copy-start(s32[64]{0:T(128)} %param.18) | copy-start | bytes 772
  49.9 5.2 %copy-start.18 = (s32[64,1]{0,1:T(1,128)S(1)}, s32[64,1]{0,1:T(1,128)}, u32[]{:S(2)}) copy-start(s32[64,1]{0,1:T(1,128)} %param.20) | copy-start | bytes 772
  49.9 5.2 %copy-start.19 = (s32[64]{0:T(128)S(1)}, s32[64]{0:T(128)}, u32[]{:S(2)}) copy-start(s32[64]{0:T(128)} %param.19) | copy-start | bytes 772
  49.9 10.5 %copy-start.1 = (bf16[4,512,1,256]{3,1,2,0:T(8,128)(2,1)S(1)}, bf16[4,512,1,256]{3,1,2,0:T(8,128)(2,1)}, u32[]{:S(2)}) copy-start(bf16[4,512,1,256]{3,1,2,0:T(8,128)(2,1)} %param.17) | copy-start | bytes 3145732
  49.9 22.6 %copy-start.17 = (bf16[1024]{0:T(1024)(128)(2,1)S(1)}, bf16[1024]{0:T(1024)(128)(2,1)}, u32[]{:S(2)}) copy-start(bf16[1024]{0:T(1024)(128)(2,1)} %param.13) | copy-start | bytes 6148
  50.0 22.6 %copy-start.20 = (bf16[256]{0:T(256)(128)(2,1)S(1)}, bf16[256]{0:T(256)(128)(2,1)}, u32[]{:S(2)}) copy-start(bf16[256]{0:T(256)(128)(2,1)} %param.15) | copy-start | bytes 1540
  54.2 0.9 copy-start.7
  59.6 0.9 copy-start.9
  60.5 36.6 %collective-permute-start.9 = (bf16[4,512,256]{2,1,0:T(8,128)(2,1)S(1)}, bf16[4,512,256]{2,1,0:T(8,128)(2,1)S(1)}, u32[]{:S(2)}, u32[]{:S(2)}) collective-permute-start(bf16[4,512,256]{2,1,0:T(8,128)(2,1)S(1)} %bitcast.24), channel_id=1, source_target_pairs={{0,8},{8,0},{16,24},{24,16},{32,40},{40,32},{48,56},{56,48},{64,72... | collective-permute-start | bytes 3145736 | tf_op jit(solution)/shard_map/ppermute | solution.py:44
  60.5 1.1 copy-start.10
  62.9 10.4 %collective-permute-start.4 = (bf16[128,1280]{1,0:T(8,128)(2,1)S(1)}, bf16[128,1280]{1,0:T(8,128)(2,1)S(1)}, u32[]{:S(2)}, u32[]{:S(2)}) collective-permute-start(bf16[128,1280]{1,0:T(8,128)(2,1)S(1)} %get-tuple-element.38), channel_id=1, source_target_pairs={{0,4},{1,5},{2,6},{3,7},{4,0},{5,1},{6,2},{7,3},{8,12},{9,13},{10,... | collective-permute-start | bytes 983048 | tf_op jit(solution)/shard_map/ppermute | solution.py:40
  71.7 27.0 %collective-permute-start.10 = (bf16[4,512,256]{2,1,0:T(8,128)(2,1)}, bf16[4,512,256]{2,1,0:T(8,128)(2,1)}, u32[]{:S(2)}, u32[]{:S(2)}) collective-permute-start(bf16[4,512,256]{2,1,0:T(8,128)(2,1)} %collective-permute-done.6.refs_1_), channel_id=1, source_target_pairs={{0,8},{8,0},{16,24},{24,16},{32,40},{40,32},{48,56},{56,48},{64,72... | collective-permute-start | bytes 3145736 | tf_op jit(solution)/shard_map/ppermute | solution.py:44
  71.7 27.0 %collective-permute-start.11 = (bf16[4,512,256]{2,1,0:T(8,128)(2,1)}, bf16[4,512,256]{2,1,0:T(8,128)(2,1)}, u32[]{:S(2)}, u32[]{:S(2)}) collective-permute-start(bf16[4,512,256]{2,1,0:T(8,128)(2,1)} %collective-permute-done.7.refs_2_), channel_id=1, source_target_pairs={{0,8},{8,0},{16,24},{24,16},{32,40},{40,32},{48,56},{56,48},{64,72... | collective-permute-start | bytes 3145736 | tf_op jit(solution)/shard_map/ppermute | solution.py:44
  72.2 26.5 %collective-permute-start.12 = (bf16[4,512,256]{2,1,0:T(8,128)(2,1)}, bf16[4,512,256]{2,1,0:T(8,128)(2,1)}, u32[]{:S(2)}, u32[]{:S(2)}) collective-permute-start(bf16[4,512,256]{2,1,0:T(8,128)(2,1)} %collective-permute-done.8.refs_3_), channel_id=1, source_target_pairs={{0,8},{8,0},{16,24},{24,16},{32,40},{40,32},{48,56},{56,48},{64,72... | collective-permute-start | bytes 3145736 | tf_op jit(solution)/shard_map/ppermute | solution.py:44
  73.3 16.7 %collective-permute-start.17 = (bf16[2,128,1280]{2,1,0:T(8,128)(2,1)}, bf16[2,128,1280]{2,1,0:T(8,128)(2,1)S(1)}, u32[]{:S(2)}, u32[]{:S(2)}) collective-permute-start(bf16[2,128,1280]{2,1,0:T(8,128)(2,1)} %copy-done.11), channel_id=1, source_target_pairs={{0,3},{1,0},{2,1},{3,2},{4,7},{5,4},{6,5},{7,6},{8,11},{9,8},{10,9... | collective-permute-start | bytes 1966088 | tf_op jit(solution)/shard_map/ppermute | solution.py:40
  74.4 24.4 %copy-start.12 = (bf16[32,32,128]{2,1,0:T(8,128)(2,1)}, bf16[32,32,128]{2,1,0:T(8,128)(2,1)S(1)}, u32[]{:S(2)}) copy-start(bf16[32,32,128]{2,1,0:T(8,128)(2,1)S(1)} %get-tuple-element.39.q_ref) | copy-start | bytes 786436
  89.9 8.8 %collective-permute-start.5 = (bf16[32,32,128]{2,1,0:T(8,128)(2,1)S(1)}, bf16[32,32,128]{2,1,0:T(8,128)(2,1)S(1)}, u32[]{:S(2)}, u32[]{:S(2)}) collective-permute-start(bf16[32,32,128]{2,1,0:T(8,128)(2,1)S(1)} %get-tuple-element.39.q_ref), channel_id=1, source_target_pairs={{0,64},{8,72},{16,80},{24,88},{32,96},{40,104},{48,112},{56,120},{... | collective-permute-start | bytes 786440 | tf_op jit(solution)/shard_map/ppermute | solution.py:44
  93.1 1.1 copy-start.8
  96.1 0.9 copy-start.5
  97.0 1.0 copy-start.2
  98.0 18.2 %collective-permute-start.18 = (bf16[128,1280]{1,0:T(8,128)(2,1)}, bf16[128,1280]{1,0:T(8,128)(2,1)}, u32[]{:S(2)}, u32[]{:S(2)}) collective-permute-start(bf16[128,1280]{1,0:T(8,128)(2,1)} %get-tuple-element.51), channel_id=1, source_target_pairs={{0,4},{1,5},{2,6},{3,7},{4,0},{5,1},{6,2},{7,3},{8,12},{9,13},{10,... | collective-permute-start | bytes 983048 | tf_op jit(solution)/shard_map/ppermute | solution.py:40
  98.7 7.7 %copy-start.14 = (s32[32]{0:T(128)}, s32[32]{0:T(128)S(1)}, u32[]{:S(2)}) copy-start(s32[32]{0:T(128)S(1)} %slice.3.limit_ref) | copy-start | bytes 388
  98.7 10.9 %copy-start = (bf16[64,1,64,1,256]{4,2,3,1,0:T(8,128)(2,1)S(1)}, bf16[64,1,64,1,256]{4,2,3,1,0:T(8,128)(2,1)}, u32[]{:S(2)}) copy-start(bf16[64,1,64,1,256]{4,2,3,1,0:T(8,128)(2,1)} %param.16) | copy-start | bytes 6291460
  98.8 1.4 %copy-start.3 = (bf16[4,512,256]{2,1,0:T(8,128)(2,1)S(1)}, bf16[4,512,256]{2,1,0:T(8,128)(2,1)}, u32[]{:S(2)}) copy-start(bf16[4,512,256]{2,1,0:T(8,128)(2,1)} %copy-done.2) | copy-start | bytes 3145732
  106.5 21.2 %collective-permute-start.13 = (bf16[33,32,128]{2,1,0:T(8,128)(2,1)}, bf16[33,32,128]{2,1,0:T(8,128)(2,1)}, u32[]{:S(2)}, u32[]{:S(2)}) collective-permute-start(bf16[33,32,128]{2,1,0:T(8,128)(2,1)} %attend_prefix.1), channel_id=1, source_target_pairs={{0,64},{8,72},{16,80},{24,88},{32,96},{40,104},{48,112},{56,120},{... | collective-permute-start | bytes 811016 | tf_op jit(solution)/shard_map/ppermute | solution.py:44
  109.7 1.0 copy-start.13
  116.2 1.2 copy-start.4
  117.4 1.1 copy-start.6
  118.5 0.7 copy-start.15

commit v7 on v6

v7 whole, which is shorter than its diff:
```python
import math

import jax
import jax.numpy as jnp
from jax import lax
from jax.experimental import pallas as pl
from jax.experimental.pallas import tpu as pltpu
from jax.sharding import PartitionSpec as P

BLOCK = 128
HD = 128
HEADS = 8
QW = HEADS * HD
PW = 2 * HD
COLS = QW + PW
ROWS = 128
ROPE_BASE = 1000000.0
NEG = -1e30
LOG2_SCALE = HD ** -0.5 / math.log(2.0)
F32 = jnp.float32
BF16 = jnp.bfloat16
VMEM = 20 * 1024 * 1024
VMEM_PROJECT = 50 * 1024 * 1024


def tp_shift(dy, dx):
    return [(y * 4 + x, (y + dy) % 2 * 4 + (x + dx) % 4) for y in range(2) for x in range(4)]


def roll_shift(dy, dz, dc):
    return [
        ((y * 4 + z) * 2 + c, ((y + dy) % 2 * 4 + (z + dz) % 4) * 2 + (c + dc) % 2)
        for y in range(2)
        for z in range(4)
        for c in range(2)
    ]


def over_tp(a, dy, dx):
    return lax.ppermute(a, "tp", tp_shift(dy, dx))


def over_roll(a, dy, dz, dc):
    return lax.ppermute(a, "roll", roll_shift(dy, dz, dc))


def dot(a, b, dims=((1,), (0,))):
    return lax.dot_general(a, b, (dims, ((), ())), preferred_element_type=F32)


ANY = pl.BlockSpec(memory_space=pl.ANY)
IN_HBM = pl.BlockSpec(memory_space=pltpu.HBM)
IN_VMEM = pl.BlockSpec(memory_space=pltpu.VMEM)


def cost(us):
    return pl.CostEstimate(flops=10**6, bytes_accessed=int(us * 2_500_000), transcendentals=0)


SMALL = cost(0.04)
IN_SMEM = pl.BlockSpec(memory_space=pltpu.SMEM)


def project(heads, xs, wq, wp, groups, after=()):
    count = sum(len(g) for g in groups)
    depth = wq.shape[0]

    def kernel(heads_ref, *refs):
        x_refs, (wq_ref, wp_ref) = refs[: len(xs)], refs[len(xs) : len(xs) + 2]
        rest = refs[len(xs) + 2 + len(after) :]
        outs, (q_buf, p_buf, q_sem, p_sem) = rest[:-4], rest[-4:]
        copies = []
        for d in range(count):
            k = heads_ref[d]
            copies.append(
                (
                    pltpu.make_async_copy(
                        wq_ref.at[:, pl.ds(pl.multiple_of(k * QW, QW), QW)], q_buf.at[d], q_sem.at[d]
                    ),
                    pltpu.make_async_copy(
                        wp_ref.at[:, pl.ds(pl.multiple_of(k * PW, PW), PW)], p_buf.at[d], p_sem.at[d]
                    ),
                )
            )
        for pair in copies:
            for c in pair:
                c.start()
        x = jnp.concatenate([r[...] for r in x_refs], 0)
        d = 0
        for g, group in enumerate(groups):
            for i in range(len(group)):
                for c in copies[d]:
                    c.wait()
                for buf, low, high in ((q_buf, 0, QW), (p_buf, QW, COLS)):
                    y = dot(x, buf[d]).astype(BF16)
                    for b in range(len(xs)):
                        outs[b * len(groups) + g][i, :, low:high] = y[b * ROWS : (b + 1) * ROWS]
                d += 1

    return pl.pallas_call(
        kernel,
        in_specs=[IN_SMEM] + [IN_VMEM] * len(xs) + [IN_HBM, IN_HBM] + [ANY] * len(after),
        out_specs=[IN_VMEM] * (len(xs) * len(groups)),
        out_shape=[jax.ShapeDtypeStruct((len(g), ROWS, COLS), BF16) for _ in xs for g in groups],
        scratch_shapes=[
            pltpu.VMEM((count, depth, QW), BF16),
            pltpu.VMEM((count, depth, PW), BF16),
            pltpu.SemaphoreType.DMA((count,)),
            pltpu.SemaphoreType.DMA((count,)),
        ],
        compiler_params=pltpu.CompilerParams(vmem_limit_bytes=VMEM_PROJECT),
        cost_estimate=SMALL,
        name="project",
    )(heads, *xs, wq, wp, *after)


def sort_rows(place, owner, tokens):
    rows, width = tokens.shape

    def kernel(place_ref, owner_ref, x_ref, *outs):
        x = x_ref[...]
        for b, out in enumerate(outs):
            row = lax.broadcasted_iota(jnp.int32, (ROWS, rows), 0)
            col = lax.broadcasted_iota(jnp.int32, (ROWS, rows), 1)
            i = row // 4
            y, c, step, j = (1 - b + place_ref[0]) % 2, i // 16, i // 4 % 4, i % 4
            c = jnp.where(c == 0, place_ref[2], 1 - place_ref[2])
            z = (jnp.where(step == 1, 3, jnp.where(step == 0, 0, step - 1)) + place_ref[1]) % 4
            slot = ((y * 4 + z) * 2 + c) * 4 + j
            hit = (owner_ref[...] == slot) & (col % 4 == row % 4)
            out[...] = dot(jnp.where(hit, 1.0, 0.0).astype(BF16), x).astype(BF16)

    return pl.pallas_call(
        kernel,
        in_specs=[IN_SMEM, IN_VMEM, IN_VMEM],
        out_specs=[IN_VMEM] * 2,
        out_shape=[jax.ShapeDtypeStruct((ROWS, width), BF16)] * 2,
        compiler_params=pltpu.CompilerParams(vmem_limit_bytes=VMEM),
        cost_estimate=SMALL,
        name="sort_rows",
    )(place, owner, tokens)


def add_far(right, left, up, down, after):
    def kernel(r, l, u, d, *refs):
        r_out, l_out = refs[len(after) :]
        r_out[...] = (r[...].astype(F32) + u[...].astype(F32)).astype(BF16)
        l_out[...] = (l[...].astype(F32) + d[...].astype(F32)).astype(BF16)

    block = [pl.BlockSpec((1, ROWS, COLS), lambda i, h=h: (h, 0, 0)) for h in (0, 1)]
    return pl.pallas_call(
        kernel,
        grid=(1,),
        in_specs=block + [block[0]] * 2 + [ANY] * len(after),
        out_specs=block,
        out_shape=[jax.ShapeDtypeStruct(right.shape, BF16)] * 2,
        input_output_aliases={0: 0, 1: 1},
        compiler_params=pltpu.CompilerParams(vmem_limit_bytes=VMEM),
        cost_estimate=SMALL,
        name="add_far",
    )(right, left, up, down, *after)


def turn_far(core, below, above, after):
    count = below.shape[0]

    def kernel(core_ref, below_ref, above_ref, after_ref, o_ref, both_ref, sem):
        copies = [
            pltpu.make_async_copy(below_ref, both_ref.at[pl.ds(0, count)], sem.at[0]),
            pltpu.make_async_copy(above_ref, both_ref.at[pl.ds(count, count)], sem.at[1]),
        ]
        for c in copies:
            c.start()
        for c in copies:
            c.wait()
        o_ref[...] = both_ref[pl.ds(pl.multiple_of(core_ref[0] * count, count), count)]

    return pl.pallas_call(
        kernel,
        in_specs=[IN_SMEM, ANY, ANY, ANY],
        out_specs=[IN_VMEM] * 2,
        out_shape=[
            jax.ShapeDtypeStruct(below.shape, BF16),
            jax.ShapeDtypeStruct((2 * count,) + below.shape[1:], BF16),
        ],
        scratch_shapes=[pltpu.SemaphoreType.DMA((2,))],
        compiler_params=pltpu.CompilerParams(vmem_limit_bytes=VMEM),
        cost_estimate=SMALL,
        name="turn_far",
    )(core, below, above, after)


def hold(array, after):
    def kernel(*refs):
        pass

    return pl.pallas_call(
        kernel,
        in_specs=[ANY] * 2,
        out_specs=ANY,
        out_shape=jax.ShapeDtypeStruct(array.shape, array.dtype),
        input_output_aliases={0: 0},
        cost_estimate=SMALL,
        name="hold",
    )(array, after)


def prefix_copies(refs, buf, sem):
    sources = []
    for own, both, far in (refs[:3], refs[3:6]):
        sources += [own, both.at[pl.ds(0, 4)], both.at[pl.ds(4, 4)], far]
    return [
        pltpu.make_async_copy(sources[g], buf.at[pl.ds(4 * g, 4), pl.ds(0, 512)], sem.at[g]) for g in range(8)
    ]


def sum_x(own, from_left, from_right):
    def kernel(a, b, c, keep, send):
        for i, out in enumerate((keep, send)):
            out[...] = (a[i].astype(F32) + b[i].astype(F32) + c[i].astype(F32)).astype(out.dtype)

    return pl.pallas_call(
        kernel,
        in_specs=[IN_VMEM] * 3,
        out_specs=[IN_VMEM] * 2,
        out_shape=[jax.ShapeDtypeStruct((ROWS, COLS), F32), jax.ShapeDtypeStruct((ROWS, COLS), BF16)],
        compiler_params=pltpu.CompilerParams(vmem_limit_bytes=VMEM),
        cost_estimate=SMALL,
        name="sum_x",
    )(own, from_left, from_right)


def rotated(keep_ref, more_ref, bias_ref, cos_ref, sin_ref, first, q_buf):
    cos, sin = cos_ref[first : first + ROWS, :], sin_ref[first : first + ROWS, :]

    def turn(v):
        return v * cos + pltpu.roll(v, HD // 2, 1) * sin

    for h in range(HEADS):
        low, high = h * HD, h * HD + HD
        v = turn(keep_ref[:, low:high] + more_ref[:, low:high].astype(F32) + bias_ref[:, low:high])
        for p in range(32):
            q_buf[32 * p + 4 * h : 32 * p + 4 * h + 4, :] = v[4 * p : 4 * p + 4]
    u = keep_ref[:, QW:] + more_ref[:, QW:].astype(F32) + bias_ref[:, QW:]
    return jnp.concatenate([turn(u[:, :HD]), u[:, HD:]], 1)


def masked_scores(q, keys, valid):
    return jnp.where(valid, dot(q, keys, ((1,), (1,))) * LOG2_SCALE, NEG)


def weigh(s_buf, w_buf, top_buf, sum_buf):
    for g in range(8):
        rows = slice(128 * g, 128 * g + 128)
        s = s_buf[rows, :]
        top = jnp.max(s, -1, keepdims=True)
        w = jnp.exp2(s - top)
        w_buf[rows, :] = w.astype(BF16)
        top_buf[rows, :] = top
        sum_buf[rows, :] = jnp.sum(w, -1, keepdims=True)


def new_block(new_ref_rows):
    return jnp.concatenate([new_ref_rows, jnp.zeros((12, PW), F32)], 0).astype(BF16)


def buffers(keys):
    return [
        pltpu.VMEM((32, keys, PW), BF16),
        pltpu.VMEM((1024, keys), F32),
        pltpu.VMEM((1024, keys), BF16),
        pltpu.VMEM((1024, 1), F32),
        pltpu.VMEM((1024, 1), F32),
    ]


def pack_logs(top_buf, sum_buf):
    lane = lax.broadcasted_iota(jnp.int32, (32, 128), 1)
    packed = jnp.zeros((32, 128), F32)
    for p in range(32):
        rows = slice(32 * p, 32 * p + 32)
        packed = jnp.where(lane == 4 * p, top_buf[rows, :] + jnp.log2(sum_buf[rows, :]), packed)
    return packed


def attend(limits, lengths, order, keep, more, bias, cosine, sine, cache, kvs):
    keys = 512 + 64 + 16

    def kernel(limit_ref, length_ref, at_ref, keep_ref, more_ref, bias_ref, cos_ref, sin_ref, cache_ref, *refs):
        o_ref, buf, s_buf, w_buf, top_buf, sum_buf, qbuf, sem, csem = refs[6:]
        copies = prefix_copies(refs, buf, sem) + [
            pltpu.make_async_copy(cache_ref.at[at_ref[32 + p]], buf.at[p, pl.ds(512, 64)], csem.at[p])
            for p in range(32)
        ]
        for c in copies:
            c.start()
        new_all = rotated(keep_ref, more_ref, bias_ref, cos_ref, sin_ref, ROWS, qbuf)
        for p in range(32):
            o_ref[p, :, QW:] = new_all[4 * p : 4 * p + 4].astype(BF16)
            buf[p, 576:592, :] = new_block(new_all[4 * p : 4 * p + 4])
        row = lax.broadcasted_iota(jnp.int32, (32, keys), 0)
        col = lax.broadcasted_iota(jnp.int32, (32, keys), 1)
        fresh = (col >= 576) & (col - 576 <= row & 3)
        for c in copies:
            c.wait()
        for p in range(32):
            valid = (col < limit_ref[p]) | ((col >= 512) & (col < 512 + length_ref[32 + p])) | fresh
            rows = slice(32 * p, 32 * p + 32)
            s_buf[rows, :] = masked_scores(qbuf[rows, :].astype(BF16), buf[p, :, :HD], valid)
        weigh(s_buf, w_buf, top_buf, sum_buf)
        for p in range(32):
            rows = slice(32 * p, 32 * p + 32)
            o = dot(w_buf[rows, :], buf[p, :, HD:]) / sum_buf[rows, :]
            for h in range(HEADS):
                o_ref[p, :, h * HD : h * HD + HD] = o[4 * h : 4 * h + 4].astype(BF16)

    return pl.pallas_call(
        kernel,
        in_specs=[IN_SMEM] * 3 + [IN_VMEM] * 5 + [ANY] * 7,
        out_specs=IN_VMEM,
        out_shape=jax.ShapeDtypeStruct((32, 4, COLS), BF16),
        scratch_shapes=buffers(keys)
        + [pltpu.VMEM((1024, HD), F32), pltpu.SemaphoreType.DMA((8,)), pltpu.SemaphoreType.DMA((32,))],
        compiler_params=pltpu.CompilerParams(vmem_limit_bytes=VMEM),
        cost_estimate=SMALL,
        name="attend",
    )(limits, lengths, order, keep, more, bias, cosine, sine, cache, *kvs)


def make_queries(keep, more, bias, cosine, sine, after):
    def kernel(keep_ref, more_ref, bias_ref, cos_ref, sin_ref, after_ref, q_ref, new_ref, qbuf):
        new_ref[...] = rotated(keep_ref, more_ref, bias_ref, cos_ref, sin_ref, 0, qbuf).astype(BF16)
        q_ref[...] = qbuf[...].astype(BF16).reshape(32, 32, HD)

    return pl.pallas_call(
        kernel,
        in_specs=[IN_VMEM] * 5 + [ANY],
        out_specs=[IN_VMEM] * 2,
        out_shape=[jax.ShapeDtypeStruct((32, 32, HD), BF16), jax.ShapeDtypeStruct((ROWS, PW), BF16)],
        scratch_shapes=[pltpu.VMEM((1024, HD), F32)],
        compiler_params=pltpu.CompilerParams(vmem_limit_bytes=VMEM),
        cost_estimate=SMALL,
        name="make_queries",
    )(keep, more, bias, cosine, sine, after)


def attend_prefix(limits, q, kvs):
    keys = 512

    def kernel(limit_ref, q_ref, *refs):
        o_ref, buf, s_buf, w_buf, top_buf, sum_buf, sem = refs[6:]
        copies = prefix_copies(refs, buf, sem)
        for c in copies:
            c.start()
        col = lax.broadcasted_iota(jnp.int32, (32, keys), 1)
        for g in range(8):
            copies[g].wait()
            for p in range(4 * g, 4 * g + 4):
                s_buf[32 * p : 32 * p + 32, :] = masked_scores(q_ref[p], buf[p, :, :HD], col < limit_ref[p])
        weigh(s_buf, w_buf, top_buf, sum_buf)
        for p in range(32):
            rows = slice(32 * p, 32 * p + 32)
            o_ref[p] = (dot(w_buf[rows, :], buf[p, :, HD:]) / sum_buf[rows, :]).astype(BF16)
        rest = pack_logs(top_buf, sum_buf)
        lane = lax.broadcasted_iota(jnp.int32, (32, 128), 1)
        packed = jnp.zeros((32, 128), F32)
        for part in range(3):
            piece = rest.astype(BF16).astype(F32)
            packed = jnp.where(lane % 4 == part, pltpu.roll(piece, part, 1), packed)
            rest = rest - piece
        o_ref[32] = packed.astype(BF16)

    return pl.pallas_call(
        kernel,
        in_specs=[IN_SMEM, IN_VMEM] + [ANY] * 6,
        out_specs=IN_VMEM,
        out_shape=jax.ShapeDtypeStruct((33, 32, HD), BF16),
        scratch_shapes=buffers(keys) + [pltpu.SemaphoreType.DMA((8,))],
        compiler_params=pltpu.CompilerParams(vmem_limit_bytes=VMEM),
        cost_estimate=SMALL,
        name="attend_prefix",
    )(limits, q, *kvs)


def attend_near(lengths, order, q, new, cache, after):
    keys = 64 + 16

    def kernel(
        length_ref, at_ref, q_ref, new_ref, cache_ref, after_ref, o_ref, buf, s_buf, w_buf, top_buf, sum_buf, sem
    ):
        copies = [
            pltpu.make_async_copy(cache_ref.at[at_ref[p]], buf.at[p, pl.ds(0, 64)], sem.at[p])
            for p in range(32)
        ]
        for c in copies:
            c.start()
        for p in range(32):
            buf[p, 64:80, :] = new_block(new_ref[4 * p : 4 * p + 4].astype(F32))
        row = lax.broadcasted_iota(jnp.int32, (32, keys), 0)
        col = lax.broadcasted_iota(jnp.int32, (32, keys), 1)
        fresh = (col >= 64) & (col - 64 <= row & 3)
        for c in copies:
            c.wait()
        for p in range(32):
            valid = (col < length_ref[p]) | fresh
            s_buf[32 * p : 32 * p + 32, :] = masked_scores(q_ref[p], buf[p, :, :HD], valid)
        weigh(s_buf, w_buf, top_buf, sum_buf)
        for p in range(32):
            rows = slice(32 * p, 32 * p + 32)
            o_ref[p] = dot(w_buf[rows, :], buf[p, :, HD:]) / sum_buf[rows, :]
        o_ref[32] = pack_logs(top_buf, sum_buf)

    return pl.pallas_call(
        kernel,
        in_specs=[IN_SMEM] * 2 + [IN_VMEM] * 2 + [ANY] * 2,
        out_specs=IN_VMEM,
        out_shape=jax.ShapeDtypeStruct((33, 32, HD), F32),
        scratch_shapes=buffers(keys) + [pltpu.SemaphoreType.DMA((32,))],
        compiler_params=pltpu.CompilerParams(vmem_limit_bytes=VMEM),
        cost_estimate=SMALL,
        name="attend_near",
    )(lengths, order, q, new, cache, after)


def merge_rows(order, far, near, new, done):
    def kernel(order_ref, far_ref, near_ref, new_ref, done_ref, out_ref, pair_ref):
        parts = far_ref[32].astype(F32)
        theirs = parts + pltpu.roll(parts, 127, 1) + pltpu.roll(parts, 126, 1)
        ours = near_ref[32]
        top = jnp.maximum(theirs, ours)
        wt, wo = jnp.exp2(theirs - top), jnp.exp2(ours - top)
        share = wt / (wt + wo)
        for p in range(32):
            at = order_ref[p]
            mine = near_ref[p]
            o = mine + (far_ref[p].astype(F32) - mine) * share[:, 4 * p : 4 * p + 1]
            for h in range(HEADS):
                out_ref[at, :, h * HD : h * HD + HD] = o[4 * h : 4 * h + 4].astype(BF16)
            pair_ref[at] = new_ref[p]
            at = order_ref[32 + p]
            out_ref[at] = done_ref[p, :, :QW]
            pair_ref[at] = done_ref[p, :, QW:]

    return pl.pallas_call(
        kernel,
        in_specs=[IN_SMEM] + [IN_VMEM] * 4,
        out_specs=[IN_VMEM] * 2,
        out_shape=[jax.ShapeDtypeStruct((64, 4, QW), BF16), jax.ShapeDtypeStruct((64, 4, PW), BF16)],
        compiler_params=pltpu.CompilerParams(vmem_limit_bytes=VMEM),
        cost_estimate=SMALL,
        name="merge_rows",
    )(order, far, near, new, done)


def on_device(
    tokens,
    query_weight,
    query_bias,
    pair_weight,
    pair_bias,
    cache_pairs,
    prefix_pairs,
    owner_slot,
    prefix_blocks,
    positions,
):
    prompts, _, new, width = tokens.shape
    me = lax.axis_index("roll")
    my_y, my_z, my_c = me // 8, me // 2 % 4, me % 2
    tp = lax.axis_index("tp")
    tp_y, tp_x = tp // 4, tp % 4
    pos = positions.reshape(prompts)

    own = prefix_pairs.reshape(-1, 512, 2 * HD)
    below, above, own_c = over_roll(own, 0, 1, 0), over_roll(own, 0, 3, 0), over_roll(own, 0, 0, 1)

    x_o, x_m = sort_rows(
        jnp.stack([my_y, my_z, my_c]).astype(jnp.int32),
        jnp.broadcast_to(owner_slot[:, None], (prompts, new)).reshape(1, prompts * new),
        tokens.reshape(prompts * new, width),
    )

    def heads(*pairs):
        return jnp.stack([(tp_y + dy) % 2 * 4 + (tp_x + dx) % 4 for dy, dx in pairs]).astype(jnp.int32)

    weights = (query_weight, pair_weight)
    up_o, down_o, up_m, down_m = project(heads((0, 2), (1, 2)), [x_o, x_m], *weights, [[0], [1]])
    right_o, left_o, right_m, left_m = project(
        heads((0, 1), (1, 1), (0, 3), (1, 3)), [x_o, x_m], *weights, [[0, 1], [2, 3]], after=(own_c,)
    )
    right_o, left_o = add_far(right_o, left_o, over_tp(up_o, 0, 1), over_tp(down_o, 0, 3), ())
    right_m, left_m = add_far(right_m, left_m, over_tp(up_m, 0, 1), over_tp(down_m, 0, 3), (right_o,))
    own_o, own_m = project(heads((0, 0), (1, 0)), [x_o, x_m], *weights, [[0, 1]], after=(right_o, left_o))

    def reduce(right, left, own_part):
        keep, send = sum_x(own_part, over_tp(right, 0, 1), over_tp(left, 0, 3))
        return keep, over_tp(send, 1, 0)

    full_o = reduce(right_o, left_o, own_o)
    full_m = reduce(right_m, left_m, own_m)

    far, both = turn_far(jnp.stack([my_c]).astype(jnp.int32), below, above, full_o[0])
    far = lax.ppermute(
        far,
        "roll",
        [
            ((y * 4 + z) * 2 + c, (y * 4 + (z + 1 + 2 * c) % 4) * 2 + c)
            for y in range(2)
            for z in range(4)
            for c in range(2)
        ],
    )

    index = jnp.arange(prompts, dtype=jnp.int32)
    half, quarter = jnp.arange(2, dtype=jnp.int32), jnp.arange(4, dtype=jnp.int32)
    y_of, c_of = (1 - half + my_y) % 2, (half + my_c) % 2
    z_of = (jnp.array([0, 3, 1, 2], jnp.int32) + my_z) % 4
    slot = (
        ((y_of[:, None, None, None] * 4 + z_of[None, None, :, None]) * 2 + c_of[None, :, None, None]) * 4
        + quarter[None, None, None, :]
    ).reshape(prompts)
    hit = owner_slot[None, :] == slot[:, None]
    order = jnp.sum(jnp.where(hit, index[None, :], 0), 1)
    limits = BLOCK * jnp.sum(jnp.where(hit, prefix_blocks[None, :], 0), 1)
    lengths = jnp.sum(jnp.where(hit, pos[None, :], 0), 1)
    my_limits = limits[32:]
    at = (limits[:, None] + lengths[:, None] + quarter[None, :]).reshape(prompts * new)
    frequency = jnp.exp(jnp.arange(HD // 2, dtype=F32) * (-2.0 * math.log(ROPE_BASE) / HD))
    angles = at.astype(F32)[:, None] * frequency[None, :]
    cosine, sine = jnp.cos(angles), jnp.sin(angles)
    tables = (
        jnp.concatenate([query_bias, pair_bias]).astype(F32)[None],
        jnp.concatenate([cosine, cosine], 1),
        jnp.concatenate([-sine, sine], 1),
    )
    cache = cache_pairs.reshape(prompts, 64, 2 * HD)

    q_o, new_o = make_queries(*full_o, *tables, right_m)
    far = hold(far, q_o)
    kvs = [own, both, far, own_c, over_roll(both, 0, 0, 1), over_roll(far, 0, 0, 1)]
    values = attend_prefix(my_limits, over_roll(q_o, 1, 0, 0), kvs)
    far = over_roll(values, 1, 0, 0)
    near = attend_near(lengths, order, q_o, new_o, cache, values)
    done = attend(my_limits, lengths, order, *full_m, *tables, cache, kvs)
    attended, new_pairs = merge_rows(order, far, near, new_o.reshape(32, new, PW), done)
    return (
        attended.reshape(prompts, 1, new, QW),
        new_pairs.reshape(prompts, 1, new, 1, PW),
    )


def solution(mesh):
    return jax.shard_map(
        on_device,
        mesh=mesh,
        in_specs=(
            P(None, "roll", None, "tp"),
            P("tp", None),
            P("tp"),
            P("tp", None),
            P("tp"),
            P(None, "roll", None, "tp", None),
            P("roll", None, "tp", None),
            P(),
            P(),
            P(None, "roll"),
        ),
        out_specs=(P(None, "roll", None, "tp"), P(None, "roll", None, "tp", None)),
        check_vma=False,
    )
```

time: 132 us -> 118 us (0.89)
  waiting for transfers between devices: 41.5 us -> 32.1 us
  Pallas kernels: 48.3 us -> 44 us
  local copies, waits for them, and re-layouts: 13.4 us -> 10.7 us
    ppermute x9 -> x7, waiting for transfers between devices: 11.2 us -> 0.02 us  [over_roll(): return lax.ppermute(a, 'roll', roll_shift(dy, dz, dc))]
    pallas_call x7 -> x9, Pallas kernels: 28.4 us -> 24.4 us  [the longest x1 6.21 us: attend(): pl.pallas_call(kernel, in_specs=[IN_SMEM] * 3 + [IN_VMEM] * 5 + [ANY] * 7...]
    ppermute x0 -> x1, waiting for transfers between devices: none -> 3.33 us  [on_device(): lax.ppermute(far, 'roll', [((y * 4 + z) * 2 + c, (y * 4 + (z + 1 + 2 * c)...]
    unnamed x44 -> x52, local copies, waits for them, and re-layouts: 11.1 us -> 8.41 us
    ppermute x10, waiting for transfers between devices: 30.3 us -> 28.8 us  [over_tp(): return lax.ppermute(a, 'tp', tp_shift(dy, dx))]
    ppermute x9 -> x7, starting transfers between devices: 11.3 us -> 11.9 us  [over_roll(): return lax.ppermute(a, 'roll', roll_shift(dy, dz, dc))]
  transfers between devices with their start and end apart: 19 -> 18, of which waited for: 6 -> 5; matrix products, arithmetic and copies ran while one was open for 3% -> 4% of each run, Pallas kernels for 34% -> 36%
where the time goes in v7:
time: 118 us
  Pallas kernels  44 us (37%)
  waiting for transfers between devices  32.1 us (27%)
  starting transfers between devices  27 us (23%)
  local copies, waits for them, and re-layouts  10.7 us (9%)
  other arithmetic  2.73 us (2%)
    ppermute x10, waiting for transfers between devices, over_tp(): return lax.ppermute(a, 'tp', tp_shift(dy, dx))  28.8 us
    pallas_call x3, Pallas kernels, project(): pl.pallas_call(kernel, in_specs=[IN_SMEM] + [IN_VMEM] * len(xs) + [IN_HBM...  15.6 us
    ppermute x10, starting transfers between devices, over_tp(): return lax.ppermute(a, 'tp', tp_shift(dy, dx))  15 us
    ppermute x7, starting transfers between devices, over_roll(): return lax.ppermute(a, 'roll', roll_shift(dy, dz, dc))  11.9 us
    unnamed x52, local copies, waits for them, and re-layouts  8.41 us
    pallas_call x1, Pallas kernels, attend(): pl.pallas_call(kernel, in_specs=[IN_SMEM] * 3 + [IN_VMEM] * 5 + [ANY] * 7...  6.21 us
    pallas_call x1, Pallas kernels, attend_prefix(): pl.pallas_call(kernel, in_specs=[IN_SMEM, IN_VMEM] + [ANY] * 6, out_specs...  5.75 us
    pallas_call x1, Pallas kernels, attend_near(): pl.pallas_call(kernel, in_specs=[IN_SMEM] * 2 + [IN_VMEM] * 2 + [ANY] * 2...  3.75 us
  transfers between devices with their start and end apart: 18, of which 5 were waited for; matrix products, arithmetic and copies ran while one was open for 4% of the time, Pallas kernels for 36%

profile of v7, /device:TPU:0, one launch (start us, length us, event | category | flops | bytes accessed | tf_op | source)
XLA Modules:
  0.0 117.7 jit_solution(11599901397592422012)
XLA Ops:
  0.7 4.2 %collective-permute-start.10 = (bf16[4,512,256]{2,1,0:T(8,128)(2,1)}, bf16[4,512,256]{2,1,0:T(8,128)(2,1)}, u32[]{:S(2)}, u32[]{:S(2)}) collective-permute-start(bf16[4,512,256]{2,1,0:T(8,128)(2,1)} %bitcast.23), channel_id=1, source_target_pairs={{0,48},{8,56},{16,0},{24,8},{32,16},{40,24},{48,32},{56,40},{64,11... | collective-permute-start | bytes 3145736 | tf_op jit(solution)/shard_map/ppermute | solution.py:44
  4.9 1.2 reshape.175.x_ref
  6.1 0.7 broadcast_in_dim.48
  7.0 0.9 sort_rows.1
  8.0 5.2 %project.4 = (bf16[1,128,1280]{2,1,0:T(8,128)(2,1)}, bf16[1,128,1280]{2,1,0:T(8,128)(2,1)}, bf16[1,128,1280]{2,1,0:T(8,128)(2,1)}, bf16[1,128,1280]{2,1,0:T(8,128)(2,1)}) custom-call(s32[2]{0:T(128)S(1)} %pad_add_fusion.3.heads_ref, bf16[128,1024]{1,0:T(8,128)(2,1)S(1)} %get-tuple-element.28.refs_0_, bf16[128,1024]{1,0:T(8,128)(2,1)S(1)} %get-tuple-element.29.refs_1_, ...), custom_call_target="tpu_custom_call" | custom-call | flops 1000000 | bytes 100000 | tf_op jit(solution)/shard_map/project/pallas_call | solution.py:100
  13.2 1.6 %collective-permute-start.1 = (bf16[1,128,1280]{2,1,0:T(8,128)(2,1)}, bf16[1,128,1280]{2,1,0:T(8,128)(2,1)}, u32[]{:S(2)}, u32[]{:S(2)}) collective-permute-start(bf16[1,128,1280]{2,1,0:T(8,128)(2,1)} %get-tuple-element.32), channel_id=1, source_target_pairs={{0,1},{1,2},{2,3},{3,0},{4,5},{5,6},{6,7},{7,4},{8,9},{9,10},{10,1... | collective-permute-start | bytes 983048 | tf_op jit(solution)/shard_map/ppermute | solution.py:40
  14.8 1.7 %collective-permute-start.2 = (bf16[1,128,1280]{2,1,0:T(8,128)(2,1)}, bf16[1,128,1280]{2,1,0:T(8,128)(2,1)}, u32[]{:S(2)}, u32[]{:S(2)}) collective-permute-start(bf16[1,128,1280]{2,1,0:T(8,128)(2,1)} %get-tuple-element.33), channel_id=1, source_target_pairs={{0,3},{1,0},{2,1},{3,2},{4,7},{5,4},{6,5},{7,6},{8,11},{9,8},{10,9... | collective-permute-start | bytes 983048 | tf_op jit(solution)/shard_map/ppermute | solution.py:40
  16.8 0.3 collective-permute-start.6
  17.1 0.6 copy-done
  17.8 6.2 %project.3 = (bf16[2,128,1280]{2,1,0:T(8,128)(2,1)S(1)}, bf16[2,128,1280]{2,1,0:T(8,128)(2,1)S(1)}, bf16[2,128,1280]{2,1,0:T(8,128)(2,1)S(1)}, bf16[2,128,1280]{2,1,0:T(8,128)(2,1)S(1)}) custom-call(s32[4]{0:T(128)S(1)} %pad_add_fusion.2.heads_ref, bf16[128,1024]{1,0:T(8,128)(2,1)S(1)} %get-tuple-element.28.refs_0_, ...), custom_call_target="tpu_custom_call" | custom-call | flops 1000000 | bytes 100000 | tf_op jit(solution)/shard_map/project/pallas_call | solution.py:100
  24.0 1.3 %collective-permute-done.1.u = bf16[1,128,1280]{2,1,0:T(8,128)(2,1)} collective-permute-done((bf16[1,128,1280]{2,1,0:T(8,128)(2,1)}, bf16[1,128,1280]{2,1,0:T(8,128)(2,1)}, u32[]{:S(2)}, u32[]{:S(2)}) %collective-permute-start.1) | collective-permute-done | bytes 327712 | tf_op jit(solution)/shard_map/ppermute | solution.py:40
  25.3 1.6 %add_far.2 = (bf16[2,128,1280]{2,1,0:T(8,128)(2,1)S(1)}, bf16[2,128,1280]{2,1,0:T(8,128)(2,1)S(1)}) custom-call(bf16[2,128,1280]{2,1,0:T(8,128)(2,1)S(1)} %get-tuple-element.30.r, bf16[2,128,1280]{2,1,0:T(8,128)(2,1)S(1)} %get-tuple-element.31.l, bf16[1,128,1280]{2,1,0:T(8,128)(2,1)} %collective-permute-done.1.u, ...), custom_call_target="tpu_custom_call", output_to_operand_aliasing={{0}: (0, {}), {1}: (1, {})} | custom-call | flops 1000000 | bytes 100000 | tf_op jit(solution)/shard_map/add_far/pallas_call | solution.py:151
  26.9 0.8 collective-permute-start.3
  27.7 2.5 %collective-permute-start.4 = (bf16[2,128,1280]{2,1,0:T(8,128)(2,1)S(1)}, bf16[2,128,1280]{2,1,0:T(8,128)(2,1)}, u32[]{:S(2)}, u32[]{:S(2)}) collective-permute-start(bf16[2,128,1280]{2,1,0:T(8,128)(2,1)S(1)} %get-tuple-element.35.refs_5_), channel_id=1, source_target_pairs={{0,3},{1,0},{2,1},{3,2},{4,7},{5,4},{6,5},{7,6},{8,11},{9,8},{10,9... | collective-permute-start | bytes 1966088 | tf_op jit(solution)/shard_map/ppermute | solution.py:40
  30.5 0.9 fusion.3
  31.4 4.2 %project.5 = (bf16[2,128,1280]{2,1,0:T(8,128)(2,1)S(1)}, bf16[2,128,1280]{2,1,0:T(8,128)(2,1)S(1)}) custom-call(s32[2]{0:T(128)S(1)} %pad_add_fusion.heads_ref, bf16[128,1024]{1,0:T(8,128)(2,1)S(1)} %get-tuple-element.28.refs_0_, bf16[128,1024]{1,0:T(8,128)(2,1)S(1)} %get-tuple-element.29.refs_1_, bf16[1024,8192]{1,0:T(8,128)(2,1)} %refs_2_.5, ...), custom_call_target="tpu_custom_call" | custom-call | flops 1000000 | bytes 100000 | tf_op jit(solution)/shard_map/project/pallas_call | solution.py:100
  35.7 9.9 %collective-permute-done.3.b = bf16[2,128,1280]{2,1,0:T(8,128)(2,1)} collective-permute-done((bf16[2,128,1280]{2,1,0:T(8,128)(2,1)S(1)}, bf16[2,128,1280]{2,1,0:T(8,128)(2,1)}, u32[]{:S(2)}, u32[]{:S(2)}) %collective-permute-start.3) | collective-permute-done | bytes 655392 | tf_op jit(solution)/shard_map/ppermute | solution.py:40
  45.6 1.5 %collective-permute-start.7 = (bf16[1,128,1280]{2,1,0:T(8,128)(2,1)}, bf16[1,128,1280]{2,1,0:T(8,128)(2,1)}, u32[]{:S(2)}, u32[]{:S(2)}) collective-permute-start(bf16[1,128,1280]{2,1,0:T(8,128)(2,1)} %get-tuple-element.42), channel_id=1, source_target_pairs={{0,3},{1,0},{2,1},{3,2},{4,7},{5,4},{6,5},{7,6},{8,11},{9,8},{10,9... | collective-permute-start | bytes 983048 | tf_op jit(solution)/shard_map/ppermute | solution.py:40
  47.2 2.2 %sum_x.2 = (f32[128,1280]{1,0:T(8,128)S(1)}, bf16[128,1280]{1,0:T(8,128)(2,1)}) custom-call(bf16[2,128,1280]{2,1,0:T(8,128)(2,1)S(1)} %get-tuple-element.36.a, bf16[2,128,1280]{2,1,0:T(8,128)(2,1)} %collective-permute-done.3.b, bf16[2,128,1280]{2,1,0:T(8,128)(2,1)} %collective-permute-done.4.c), custom_call_target="tpu_custom_call" | custom-call | flops 1000000 | bytes 100000 | tf_op jit(solution)/shard_map/sum_x/pallas_call | solution.py:222
  49.4 3.2 %turn_far.1 = (bf16[4,512,256]{2,1,0:T(8,128)(2,1)}, bf16[8,512,256]{2,1,0:T(8,128)(2,1)}) custom-call(s32[1]{0:T(128)} %bitcast.4.core_ref, bf16[4,512,256]{2,1,0:T(8,128)(2,1)} %collective-permute-done.9.below_ref, bf16[4,512,256]{2,1,0:T(8,128)(2,1)} %collective-permute-done.10.above_ref, f32[128,1280]{1,0:T(8,128)S(1)} %get-tuple-element.37.keep_ref.after_ref), custom_call_target="tpu_custom_call" | custom-call | flops 1000000 | bytes 100000 | tf_op jit(solution)/shard_map/turn_far/pallas_call | solution.py:178
  52.6 1.4 %collective-permute-start.12 = (bf16[8,512,256]{2,1,0:T(8,128)(2,1)}, bf16[8,512,256]{2,1,0:T(8,128)(2,1)}, u32[]{:S(2)}, u32[]{:S(2)}) collective-permute-start(bf16[8,512,256]{2,1,0:T(8,128)(2,1)} %get-tuple-element.45.refs_1_), channel_id=1, source_target_pairs={{0,8},{8,0},{16,24},{24,16},{32,40},{40,32},{48,56},{56,48},{64,72... | collective-permute-start | bytes 6291464 | tf_op jit(solution)/shard_map/ppermute | solution.py:44
  54.0 0.5 fusion.8
  54.6 0.1 convert_element_type.22
  54.8 0.5 fusion
  55.3 1.7 %collective-permute-start.5 = (bf16[128,1280]{1,0:T(8,128)(2,1)}, bf16[128,1280]{1,0:T(8,128)(2,1)S(1)}, u32[]{:S(2)}, u32[]{:S(2)}) collective-permute-start(bf16[128,1280]{1,0:T(8,128)(2,1)} %get-tuple-element.38), channel_id=1, source_target_pairs={{0,4},{1,5},{2,6},{3,7},{4,0},{5,1},{6,2},{7,3},{8,12},{9,13},{10,... | collective-permute-start | bytes 983048 | tf_op jit(solution)/shard_map/ppermute | solution.py:40
  57.0 0.1 pad_maximum_fusion
  57.2 1.1 copy-done.15
  58.3 1.6 %add_far.3 = (bf16[2,128,1280]{2,1,0:T(8,128)(2,1)S(1)}, bf16[2,128,1280]{2,1,0:T(8,128)(2,1)S(1)}) custom-call(bf16[2,128,1280]{2,1,0:T(8,128)(2,1)S(1)} %get-tuple-element.39.r, bf16[2,128,1280]{2,1,0:T(8,128)(2,1)S(1)} %copy-done.15, bf16[1,128,1280]{2,1,0:T(8,128)(2,1)} %collective-permute-done.6.u, ...), custom_call_target="tpu_custom_call", output_to_operand_aliasing={{0}: (0, {}), {1}: (1, {})} | custom-call | flops 1000000 | bytes 100000 | tf_op jit(solution)/shard_map/add_far/pallas_call | solution.py:151
  59.8 5.4 %collective-permute-done.5.more_ref = bf16[128,1280]{1,0:T(8,128)(2,1)S(1)} collective-permute-done((bf16[128,1280]{1,0:T(8,128)(2,1)}, bf16[128,1280]{1,0:T(8,128)(2,1)S(1)}, u32[]{:S(2)}, u32[]{:S(2)}) %collective-permute-start.5) | collective-permute-done | bytes 327712 | tf_op jit(solution)/shard_map/ppermute | solution.py:40
  65.2 0.3 make_queries.1
  65.5 3.3 %collective-permute-done.11.refs_0_ = bf16[4,512,256]{2,1,0:T(8,128)(2,1)S(1)} collective-permute-done((bf16[4,512,256]{2,1,0:T(8,128)(2,1)}, bf16[4,512,256]{2,1,0:T(8,128)(2,1)S(1)}, u32[]{:S(2)}, u32[]{:S(2)}) %collective-permute-start.11) | collective-permute-done | bytes 1048608 | tf_op jit(solution)/shard_map/ppermute | solution.py:503
  68.9 1.0 copy-done.2
  70.0 0.6 collective-permute-start.15
  70.5 2.8 %collective-permute-start.16 = (bf16[2,128,1280]{2,1,0:T(8,128)(2,1)}, bf16[2,128,1280]{2,1,0:T(8,128)(2,1)S(1)}, u32[]{:S(2)}, u32[]{:S(2)}) collective-permute-start(bf16[2,128,1280]{2,1,0:T(8,128)(2,1)} %copy-done.16), channel_id=1, source_target_pairs={{0,3},{1,0},{2,1},{3,2},{4,7},{5,4},{6,5},{7,6},{8,11},{9,8},{10,9... | collective-permute-start | bytes 1966088 | tf_op jit(solution)/shard_map/ppermute | solution.py:40
  73.3 3.2 %collective-permute-start.8 = (bf16[32,32,128]{2,1,0:T(8,128)(2,1)}, bf16[32,32,128]{2,1,0:T(8,128)(2,1)S(1)}, u32[]{:S(2)}, u32[]{:S(2)}) collective-permute-start(bf16[32,32,128]{2,1,0:T(8,128)(2,1)} %copy-done.10), channel_id=1, source_target_pairs={{0,64},{8,72},{16,80},{24,88},{32,96},{40,104},{48,112},{56,120},{... | collective-permute-start | bytes 786440 | tf_op jit(solution)/shard_map/ppermute | solution.py:44
  76.5 12.1 %collective-permute-done.15.b = bf16[2,128,1280]{2,1,0:T(8,128)(2,1)S(1)} collective-permute-done((bf16[2,128,1280]{2,1,0:T(8,128)(2,1)}, bf16[2,128,1280]{2,1,0:T(8,128)(2,1)S(1)}, u32[]{:S(2)}, u32[]{:S(2)}) %collective-permute-start.15) | collective-permute-done | bytes 655392 | tf_op jit(solution)/shard_map/ppermute | solution.py:40
  88.5 1.1 copy-done.18
  89.6 0.9 sum_x.3
  90.5 0.9 copy-done.12
  91.4 1.6 %collective-permute-start.17 = (bf16[128,1280]{1,0:T(8,128)(2,1)}, bf16[128,1280]{1,0:T(8,128)(2,1)}, u32[]{:S(2)}, u32[]{:S(2)}) collective-permute-start(bf16[128,1280]{1,0:T(8,128)(2,1)} %get-tuple-element.51), channel_id=1, source_target_pairs={{0,4},{1,5},{2,6},{3,7},{4,0},{5,1},{6,2},{7,3},{8,12},{9,13},{10,... | collective-permute-start | bytes 983048 | tf_op jit(solution)/shard_map/ppermute | solution.py:40
  93.1 5.8 %attend_prefix.1.after_ref = bf16[33,32,128]{2,1,0:T(8,128)(2,1)} custom-call(s32[32]{0:T(128)S(1)} %slice.3.limit_ref, bf16[32,32,128]{2,1,0:T(8,128)(2,1)S(1)} %collective-permute-done.8.q_ref, bf16[4,512,256]{2,1,0:T(8,128)(2,1)S(1)} %bitcast.25, bf16[8,512,256]{2,1,0:T(8,128)(2,1)} %get-tuple-element.45.refs_1_, bf16[4,512,256]{2,1,0:T(8,128)(2,1)S(1)} %copy-done.3, ...), custom_call_target="tpu_custom_call" | custom-call | flops 1000000 | bytes 100000 | tf_op jit(solution)/shard_map/attend_prefix/pallas_call | solution.py:373
  98.9 3.0 %collective-permute-start.14 = (bf16[33,32,128]{2,1,0:T(8,128)(2,1)}, bf16[33,32,128]{2,1,0:T(8,128)(2,1)}, u32[]{:S(2)}, u32[]{:S(2)}) collective-permute-start(bf16[33,32,128]{2,1,0:T(8,128)(2,1)} %attend_prefix.1.after_ref), channel_id=1, source_target_pairs={{0,64},{8,72},{16,80},{24,88},{32,96},{40,104},{48,112},{56,120},{... | collective-permute-start | bytes 811016 | tf_op jit(solution)/shard_map/ppermute | solution.py:44
  101.9 1.6 %copy-done.4 = bf16[64,1,64,1,256]{4,2,3,1,0:T(8,128)(2,1)S(1)} copy-done((bf16[64,1,64,1,256]{4,2,3,1,0:T(8,128)(2,1)S(1)}, bf16[64,1,64,1,256]{4,2,3,1,0:T(8,128)(2,1)}, u32[]{:S(2)}) %copy-start.4) | copy-done | bytes 2097176
  103.5 0.9 copy-done.11
  104.5 3.7 %attend_near.1.near_ref = f32[33,32,128]{2,1,0:T(8,128)S(1)} custom-call(s32[64]{0:T(128)S(1)} %get-tuple-element.60.length_ref, s32[64]{0:T(128)S(1)} %get-tuple-element.62.at_ref.order_ref, bf16[32,32,128]{2,1,0:T(8,128)(2,1)S(1)} %copy-done.11, bf16[128,256]{1,0:T(8,128)(2,1)S(1)} %get-tuple-element.47.new_ref, bf16[64,64,256]{2,1,0:T(8,128)(2,1)S(1)} %bitcast.20, ...), custom_call_target="tpu_custom_call" | custom-call | flops 1000000 | bytes 100000 | tf_op jit(solution)/shard_map/attend_near/pallas_call | solution.py:413
  108.3 1.1 copy-done.13
  109.4 6.2 %attend.1.done_ref = bf16[32,4,1280]{2,1,0:T(4,128)(2,1)S(1)} custom-call(s32[32]{0:T(128)S(1)} %copy-done.20, s32[64]{0:T(128)S(1)} %get-tuple-element.60.length_ref, s32[64]{0:T(128)S(1)} %get-tuple-element.62.at_ref.order_ref, f32[128,1280]{1,0:T(8,128)S(1)} %copy-done.13, bf16[128,1280]{1,0:T(8,128)(2,1)} %collective-permute-done.17.more_ref, ...), custom_call_target="tpu_custom_call" | custom-call | flops 1000000 | bytes 100000 | tf_op jit(solution)/shard_map/attend/pallas_call | solution.py:317
  115.6 2.1 %merge_rows.1 = (bf16[64,4,1024]{2,1,0:T(4,128)(2,1)}, bf16[64,4,256]{2,1,0:T(4,128)(2,1)}) custom-call(s32[64]{0:T(128)S(1)} %get-tuple-element.62.at_ref.order_ref, bf16[33,32,128]{2,1,0:T(8,128)(2,1)} %collective-permute-done.14.far_ref, f32[33,32,128]{2,1,0:T(8,128)S(1)} %attend_near.1.near_ref, bf16[32,4,256]{2,1,0:T(4,128)(2,1)S(1)} %reshape.178.new_ref, ...), custom_call_target="tpu_custom_call" | custom-call | flops 1000000 | bytes 100000 | tf_op jit(solution)/shard_map/merge_rows/pallas_call | solution.py:444
  (81 shorter events, 1.3 us)
Async XLA Ops:
  0.6 16.1 %collective-permute-start = (bf16[4,512,256]{2,1,0:T(8,128)(2,1)}, bf16[4,512,256]{2,1,0:T(8,128)(2,1)S(1)}, u32[]{:S(2)}, u32[]{:S(2)}) collective-permute-start(bf16[4,512,256]{2,1,0:T(8,128)(2,1)} %bitcast.22), channel_id=1, source_target_pairs={{0,8},{8,0},{16,24},{24,16},{32,40},{40,32},{48,56},{56,48},{64,72... | collective-permute-start | bytes 3145736 | tf_op jit(solution)/shard_map/ppermute | solution.py:44
  0.7 48.6 %collective-permute-start.10 = (bf16[4,512,256]{2,1,0:T(8,128)(2,1)}, bf16[4,512,256]{2,1,0:T(8,128)(2,1)}, u32[]{:S(2)}, u32[]{:S(2)}) collective-permute-start(bf16[4,512,256]{2,1,0:T(8,128)(2,1)} %bitcast.23), channel_id=1, source_target_pairs={{0,48},{8,56},{16,0},{24,8},{32,16},{40,24},{48,32},{56,40},{64,11... | collective-permute-start | bytes 3145736 | tf_op jit(solution)/shard_map/ppermute | solution.py:44
  4.9 44.4 %collective-permute-start.9 = (bf16[4,512,256]{2,1,0:T(8,128)(2,1)}, bf16[4,512,256]{2,1,0:T(8,128)(2,1)}, u32[]{:S(2)}, u32[]{:S(2)}) collective-permute-start(bf16[4,512,256]{2,1,0:T(8,128)(2,1)} %bitcast.24), channel_id=1, source_target_pairs={{0,16},{8,24},{16,32},{24,40},{32,48},{40,56},{48,0},{56,8},{64,80... | collective-permute-start | bytes 3145736 | tf_op jit(solution)/shard_map/ppermute | solution.py:44
  8.0 8.5 %copy-start.25 = (s32[4]{0:T(128)S(1)}, s32[4]{0:T(128)}, u32[]{:S(2)}) copy-start(s32[4]{0:T(128)} %constant.143.clone) | copy-start | bytes 52
  13.2 12.1 %collective-permute-start.1 = (bf16[1,128,1280]{2,1,0:T(8,128)(2,1)}, bf16[1,128,1280]{2,1,0:T(8,128)(2,1)}, u32[]{:S(2)}, u32[]{:S(2)}) collective-permute-start(bf16[1,128,1280]{2,1,0:T(8,128)(2,1)} %get-tuple-element.32), channel_id=1, source_target_pairs={{0,1},{1,2},{2,3},{3,0},{4,5},{5,6},{6,7},{7,4},{8,9},{9,10},{10,1... | collective-permute-start | bytes 983048 | tf_op jit(solution)/shard_map/ppermute | solution.py:40
  14.8 10.6 %collective-permute-start.2 = (bf16[1,128,1280]{2,1,0:T(8,128)(2,1)}, bf16[1,128,1280]{2,1,0:T(8,128)(2,1)}, u32[]{:S(2)}, u32[]{:S(2)}) collective-permute-start(bf16[1,128,1280]{2,1,0:T(8,128)(2,1)} %get-tuple-element.33), channel_id=1, source_target_pairs={{0,3},{1,0},{2,1},{3,2},{4,7},{5,4},{6,5},{7,6},{8,11},{9,8},{10,9... | collective-permute-start | bytes 983048 | tf_op jit(solution)/shard_map/ppermute | solution.py:40
  16.8 1.0 copy-start
  16.8 13.8 %copy-start.21 = (s32[64]{0:T(128)S(1)}, s32[64]{0:T(128)}, u32[]{:S(2)}) copy-start(s32[64]{0:T(128)} %param.18) | copy-start | bytes 772
  16.8 40.4 %collective-permute-start.6 = (bf16[1,128,1280]{2,1,0:T(8,128)(2,1)}, bf16[1,128,1280]{2,1,0:T(8,128)(2,1)}, u32[]{:S(2)}, u32[]{:S(2)}) collective-permute-start(bf16[1,128,1280]{2,1,0:T(8,128)(2,1)} %get-tuple-element.41), channel_id=1, source_target_pairs={{0,1},{1,2},{2,3},{3,0},{4,5},{5,6},{6,7},{7,4},{8,9},{9,10},{10,1... | collective-permute-start | bytes 983048 | tf_op jit(solution)/shard_map/ppermute | solution.py:40
  24.0 3.7 %copy-start.14 = (bf16[2,128,1280]{2,1,0:T(8,128)(2,1)}, bf16[2,128,1280]{2,1,0:T(8,128)(2,1)S(1)}, u32[]{:S(2)}) copy-start(bf16[2,128,1280]{2,1,0:T(8,128)(2,1)S(1)} %get-tuple-element.40.l) | copy-start | bytes 1966084
  26.9 18.7 %collective-permute-start.3 = (bf16[2,128,1280]{2,1,0:T(8,128)(2,1)S(1)}, bf16[2,128,1280]{2,1,0:T(8,128)(2,1)}, u32[]{:S(2)}, u32[]{:S(2)}) collective-permute-start(bf16[2,128,1280]{2,1,0:T(8,128)(2,1)S(1)} %get-tuple-element.34.refs_4_.refs_0_), channel_id=1, source_target_pairs={{0,1},{1,2},{2,3},{3,0},{4,5},{5,6},{6,7},{7,4},{8,9},{9,10},{10,1... | collective-permute-start | bytes 1966088 | tf_op jit(solution)/shard_map/ppermute | solution.py:40
  27.7 19.5 %collective-permute-start.4 = (bf16[2,128,1280]{2,1,0:T(8,128)(2,1)S(1)}, bf16[2,128,1280]{2,1,0:T(8,128)(2,1)}, u32[]{:S(2)}, u32[]{:S(2)}) collective-permute-start(bf16[2,128,1280]{2,1,0:T(8,128)(2,1)S(1)} %get-tuple-element.35.refs_5_), channel_id=1, source_target_pairs={{0,3},{1,0},{2,1},{3,2},{4,7},{5,4},{6,5},{7,6},{8,11},{9,8},{10,9... | collective-permute-start | bytes 1966088 | tf_op jit(solution)/shard_map/ppermute | solution.py:40
  35.7 16.9 %copy-start.17 = (bf16[2,128,1280]{2,1,0:T(8,128)(2,1)}, bf16[2,128,1280]{2,1,0:T(8,128)(2,1)S(1)}, u32[]{:S(2)}) copy-start(bf16[2,128,1280]{2,1,0:T(8,128)(2,1)S(1)} %get-tuple-element.48.a) | copy-start | bytes 1966084
  45.6 11.5 %collective-permute-start.7 = (bf16[1,128,1280]{2,1,0:T(8,128)(2,1)}, bf16[1,128,1280]{2,1,0:T(8,128)(2,1)}, u32[]{:S(2)}, u32[]{:S(2)}) collective-permute-start(bf16[1,128,1280]{2,1,0:T(8,128)(2,1)} %get-tuple-element.42), channel_id=1, source_target_pairs={{0,3},{1,0},{2,1},{3,2},{4,7},{5,4},{6,5},{7,6},{8,11},{9,8},{10,9... | collective-permute-start | bytes 983048 | tf_op jit(solution)/shard_map/ppermute | solution.py:40
  47.2 7.6 %copy-start.22 = (bf16[1024]{0:T(1024)(128)(2,1)S(1)}, bf16[1024]{0:T(1024)(128)(2,1)}, u32[]{:S(2)}) copy-start(bf16[1024]{0:T(1024)(128)(2,1)} %param.13) | copy-start | bytes 6148
  47.2 7.6 %copy-start.24 = (bf16[256]{0:T(256)(128)(2,1)S(1)}, bf16[256]{0:T(256)(128)(2,1)}, u32[]{:S(2)}) copy-start(bf16[256]{0:T(256)(128)(2,1)} %param.15) | copy-start | bytes 1540
  52.6 16.3 %collective-permute-start.11 = (bf16[4,512,256]{2,1,0:T(8,128)(2,1)}, bf16[4,512,256]{2,1,0:T(8,128)(2,1)S(1)}, u32[]{:S(2)}, u32[]{:S(2)}) collective-permute-start(bf16[4,512,256]{2,1,0:T(8,128)(2,1)} %get-tuple-element.46), channel_id=1, source_target_pairs={{0,16},{8,56},{16,32},{24,8},{32,48},{40,24},{48,0},{56,40},{64,80... | collective-permute-start | bytes 3145736 | tf_op jit(solution)/shard_map/ppermute | solution.py:503
  52.6 40.4 %collective-permute-start.12 = (bf16[8,512,256]{2,1,0:T(8,128)(2,1)}, bf16[8,512,256]{2,1,0:T(8,128)(2,1)}, u32[]{:S(2)}, u32[]{:S(2)}) collective-permute-start(bf16[8,512,256]{2,1,0:T(8,128)(2,1)} %get-tuple-element.45.refs_1_), channel_id=1, source_target_pairs={{0,8},{8,0},{16,24},{24,16},{32,40},{40,32},{48,56},{56,48},{64,72... | collective-permute-start | bytes 6291464 | tf_op jit(solution)/shard_map/ppermute | solution.py:44
  55.3 9.9 %collective-permute-start.5 = (bf16[128,1280]{1,0:T(8,128)(2,1)}, bf16[128,1280]{1,0:T(8,128)(2,1)S(1)}, u32[]{:S(2)}, u32[]{:S(2)}) collective-permute-start(bf16[128,1280]{1,0:T(8,128)(2,1)} %get-tuple-element.38), channel_id=1, source_target_pairs={{0,4},{1,5},{2,6},{3,7},{4,0},{5,1},{6,2},{7,3},{8,12},{9,13},{10,... | collective-permute-start | bytes 983048 | tf_op jit(solution)/shard_map/ppermute | solution.py:40
  57.2 1.1 copy-start.15
  59.8 9.0 %copy-start.9 = (bf16[2,128,1280]{2,1,0:T(8,128)(2,1)}, bf16[2,128,1280]{2,1,0:T(8,128)(2,1)S(1)}, u32[]{:S(2)}) copy-start(bf16[2,128,1280]{2,1,0:T(8,128)(2,1)S(1)} %get-tuple-element.43.after_ref) | copy-start | bytes 1966084
  59.8 9.0 %copy-start.16 = (bf16[2,128,1280]{2,1,0:T(8,128)(2,1)}, bf16[2,128,1280]{2,1,0:T(8,128)(2,1)S(1)}, u32[]{:S(2)}) copy-start(bf16[2,128,1280]{2,1,0:T(8,128)(2,1)S(1)} %get-tuple-element.49) | copy-start | bytes 1966084
  65.5 3.3 %copy-start.10 = (bf16[32,32,128]{2,1,0:T(8,128)(2,1)}, bf16[32,32,128]{2,1,0:T(8,128)(2,1)S(1)}, u32[]{:S(2)}) copy-start(bf16[32,32,128]{2,1,0:T(8,128)(2,1)S(1)} %get-tuple-element.44.refs_1_.q_ref) | copy-start | bytes 786436
  68.9 1.0 copy-start.2
  69.9 23.2 %copy-start.23 = (s32[64]{0:T(128)S(1)}, s32[64]{0:T(128)}, u32[]{:S(2)}) copy-start(s32[64]{0:T(128)} %get-tuple-element.67) | copy-start | bytes 772
  69.9 23.2 %copy-start.1 = (bf16[4,512,256]{2,1,0:T(8,128)(2,1)S(1)}, bf16[4,512,256]{2,1,0:T(8,128)(2,1)}, u32[]{:S(2)}) copy-start(bf16[4,512,256]{2,1,0:T(8,128)(2,1)} %copy-done) | copy-start | bytes 3145732
  69.9 23.3 %copy-start.6 = (bf16[4,512,1,256]{3,1,2,0:T(8,128)(2,1)S(1)}, bf16[4,512,1,256]{3,1,2,0:T(8,128)(2,1)}, u32[]{:S(2)}) copy-start(bf16[4,512,1,256]{3,1,2,0:T(8,128)(2,1)} %param.17) | copy-start | bytes 3145732
  69.9 23.3 %copy-start.3 = (bf16[4,512,256]{2,1,0:T(8,128)(2,1)S(1)}, bf16[4,512,256]{2,1,0:T(8,128)(2,1)}, u32[]{:S(2)}) copy-start(bf16[4,512,256]{2,1,0:T(8,128)(2,1)} %hold.1.refs_2_) | copy-start | bytes 3145732
  69.9 23.2 %collective-permute-start.13 = (bf16[4,512,256]{2,1,0:T(8,128)(2,1)}, bf16[4,512,256]{2,1,0:T(8,128)(2,1)S(1)}, u32[]{:S(2)}, u32[]{:S(2)}) collective-permute-start(bf16[4,512,256]{2,1,0:T(8,128)(2,1)} %hold.1.refs_2_), channel_id=1, source_target_pairs={{0,8},{8,0},{16,24},{24,16},{32,40},{40,32},{48,56},{56,48},{64,72... | collective-permute-start | bytes 3145736 | tf_op jit(solution)/shard_map/ppermute | solution.py:44
  70.0 18.6 %collective-permute-start.15 = (bf16[2,128,1280]{2,1,0:T(8,128)(2,1)}, bf16[2,128,1280]{2,1,0:T(8,128)(2,1)S(1)}, u32[]{:S(2)}, u32[]{:S(2)}) collective-permute-start(bf16[2,128,1280]{2,1,0:T(8,128)(2,1)} %copy-done.9), channel_id=1, source_target_pairs={{0,1},{1,2},{2,3},{3,0},{4,5},{5,6},{6,7},{7,4},{8,9},{9,10},{10,1... | collective-permute-start | bytes 1966088 | tf_op jit(solution)/shard_map/ppermute | solution.py:40
  70.5 18.0 %collective-permute-start.16 = (bf16[2,128,1280]{2,1,0:T(8,128)(2,1)}, bf16[2,128,1280]{2,1,0:T(8,128)(2,1)S(1)}, u32[]{:S(2)}, u32[]{:S(2)}) collective-permute-start(bf16[2,128,1280]{2,1,0:T(8,128)(2,1)} %copy-done.16), channel_id=1, source_target_pairs={{0,3},{1,0},{2,1},{3,2},{4,7},{5,4},{6,5},{7,6},{8,11},{9,8},{10,9... | collective-permute-start | bytes 1966088 | tf_op jit(solution)/shard_map/ppermute | solution.py:40
  73.3 19.8 %collective-permute-start.8 = (bf16[32,32,128]{2,1,0:T(8,128)(2,1)}, bf16[32,32,128]{2,1,0:T(8,128)(2,1)S(1)}, u32[]{:S(2)}, u32[]{:S(2)}) collective-permute-start(bf16[32,32,128]{2,1,0:T(8,128)(2,1)} %copy-done.10), channel_id=1, source_target_pairs={{0,64},{8,72},{16,80},{24,88},{32,96},{40,104},{48,112},{56,120},{... | collective-permute-start | bytes 786440 | tf_op jit(solution)/shard_map/ppermute | solution.py:44
  88.5 1.1 copy-start.18
  90.5 0.9 copy-start.12
  91.4 16.8 %collective-permute-start.17 = (bf16[128,1280]{1,0:T(8,128)(2,1)}, bf16[128,1280]{1,0:T(8,128)(2,1)}, u32[]{:S(2)}, u32[]{:S(2)}) collective-permute-start(bf16[128,1280]{1,0:T(8,128)(2,1)} %get-tuple-element.51), channel_id=1, source_target_pairs={{0,4},{1,5},{2,6},{3,7},{4,0},{5,1},{6,2},{7,3},{8,12},{9,13},{10,... | collective-permute-start | bytes 983048 | tf_op jit(solution)/shard_map/ppermute | solution.py:40
  93.1 5.8 %copy-start.19 = (s32[32]{0:T(128)}, s32[32]{0:T(128)S(1)}, u32[]{:S(2)}) copy-start(s32[32]{0:T(128)S(1)} %slice.3.limit_ref) | copy-start | bytes 388
  93.1 5.8 %copy-start.7 = (bf16[4,512,256]{2,1,0:T(8,128)(2,1)}, bf16[4,512,256]{2,1,0:T(8,128)(2,1)S(1)}, u32[]{:S(2)}) copy-start(bf16[4,512,256]{2,1,0:T(8,128)(2,1)S(1)} %collective-permute-done.13.refs_5_) | copy-start | bytes 3145732
  98.9 16.7 %collective-permute-start.14 = (bf16[33,32,128]{2,1,0:T(8,128)(2,1)}, bf16[33,32,128]{2,1,0:T(8,128)(2,1)}, u32[]{:S(2)}, u32[]{:S(2)}) collective-permute-start(bf16[33,32,128]{2,1,0:T(8,128)(2,1)} %attend_prefix.1.after_ref), channel_id=1, source_target_pairs={{0,64},{8,72},{16,80},{24,88},{32,96},{40,104},{48,112},{56,120},{... | collective-permute-start | bytes 811016 | tf_op jit(solution)/shard_map/ppermute | solution.py:44
  101.9 6.3 %copy-start.20 = (s32[32]{0:T(128)S(1)}, s32[32]{0:T(128)}, u32[]{:S(2)}) copy-start(s32[32]{0:T(128)} %copy-done.19) | copy-start | bytes 388
  101.9 1.6 %copy-start.4 = (bf16[64,1,64,1,256]{4,2,3,1,0:T(8,128)(2,1)S(1)}, bf16[64,1,64,1,256]{4,2,3,1,0:T(8,128)(2,1)}, u32[]{:S(2)}) copy-start(bf16[64,1,64,1,256]{4,2,3,1,0:T(8,128)(2,1)} %param.16) | copy-start | bytes 6291460
  103.5 0.9 copy-start.11
  104.5 3.8 %copy-start.5 = (bf16[64,1,64,1,256]{4,2,3,1,0:T(8,128)(2,1)S(1)}, bf16[64,1,64,1,256]{4,2,3,1,0:T(8,128)(2,1)}, u32[]{:S(2)}) copy-start(bf16[64,1,64,1,256]{4,2,3,1,0:T(8,128)(2,1)} %param.16) | copy-start | bytes 6291460
  104.5 3.8 %copy-start.8 = (bf16[4,512,256]{2,1,0:T(8,128)(2,1)S(1)}, bf16[4,512,256]{2,1,0:T(8,128)(2,1)}, u32[]{:S(2)}) copy-start(bf16[4,512,256]{2,1,0:T(8,128)(2,1)} %copy-done.7) | copy-start | bytes 3145732
  108.3 1.1 copy-start.13

commit v8 on v7

--- a/solution.py
+++ b/solution.py
@@ -161,73 +161,42 @@
     )(right, left, up, down, *after)
 
 
-def turn_far(core, below, above, after):
-    count = below.shape[0]
-
-    def kernel(core_ref, below_ref, above_ref, after_ref, o_ref, both_ref, sem):
-        copies = [
-            pltpu.make_async_copy(below_ref, both_ref.at[pl.ds(0, count)], sem.at[0]),
-            pltpu.make_async_copy(above_ref, both_ref.at[pl.ds(count, count)], sem.at[1]),
-        ]
-        for c in copies:
-            c.start()
-        for c in copies:
-            c.wait()
-        o_ref[...] = both_ref[pl.ds(pl.multiple_of(core_ref[0] * count, count), count)]
-
-    return pl.pallas_call(
-        kernel,
-        in_specs=[IN_SMEM, ANY, ANY, ANY],
-        out_specs=[IN_VMEM] * 2,
-        out_shape=[
-            jax.ShapeDtypeStruct(below.shape, BF16),
-            jax.ShapeDtypeStruct((2 * count,) + below.shape[1:], BF16),
-        ],
-        scratch_shapes=[pltpu.SemaphoreType.DMA((2,))],
-        compiler_params=pltpu.CompilerParams(vmem_limit_bytes=VMEM),
-        cost_estimate=SMALL,
-        name="turn_far",
-    )(core, below, above, after)
-
-
-def hold(array, after):
+def hold(arrays, after):
     def kernel(*refs):
         pass
 
-    return pl.pallas_call(
-        kernel,
-        in_specs=[ANY] * 2,
-        out_specs=ANY,
-        out_shape=jax.ShapeDtypeStruct(array.shape, array.dtype),
-        input_output_aliases={0: 0},
+    count = len(arrays)
+    return pl.pallas_call(
+        kernel,
+        in_specs=[ANY] * (count + 1),
+        out_specs=[ANY] * count,
+        out_shape=[jax.ShapeDtypeStruct(a.shape, a.dtype) for a in arrays],
+        input_output_aliases={i: i for i in range(count)},
         cost_estimate=SMALL,
         name="hold",
-    )(array, after)
+    )(*arrays, after)
 
 
 def prefix_copies(refs, buf, sem):
-    sources = []
-    for own, both, far in (refs[:3], refs[3:6]):
-        sources += [own, both.at[pl.ds(0, 4)], both.at[pl.ds(4, 4)], far]
     return [
-        pltpu.make_async_copy(sources[g], buf.at[pl.ds(4 * g, 4), pl.ds(0, 512)], sem.at[g]) for g in range(8)
+        pltpu.make_async_copy(refs[g], buf.at[pl.ds(4 * g, 4), pl.ds(0, 512)], sem.at[g]) for g in range(8)
     ]
 
 
-def sum_x(own, from_left, from_right):
-    def kernel(a, b, c, keep, send):
+def sum_x(own, from_left, from_right, after):
+    def kernel(a, b, c, after_ref, keep, send):
         for i, out in enumerate((keep, send)):
             out[...] = (a[i].astype(F32) + b[i].astype(F32) + c[i].astype(F32)).astype(out.dtype)
 
     return pl.pallas_call(
         kernel,
-        in_specs=[IN_VMEM] * 3,
+        in_specs=[IN_VMEM] * 3 + [ANY],
         out_specs=[IN_VMEM] * 2,
         out_shape=[jax.ShapeDtypeStruct((ROWS, COLS), F32), jax.ShapeDtypeStruct((ROWS, COLS), BF16)],
         compiler_params=pltpu.CompilerParams(vmem_limit_bytes=VMEM),
         cost_estimate=SMALL,
         name="sum_x",
-    )(own, from_left, from_right)
+    )(own, from_left, from_right, after)
 
 
 def rotated(keep_ref, more_ref, bias_ref, cos_ref, sin_ref, first, q_buf):
@@ -287,7 +256,7 @@
     keys = 512 + 64 + 16
 
     def kernel(limit_ref, length_ref, at_ref, keep_ref, more_ref, bias_ref, cos_ref, sin_ref, cache_ref, *refs):
-        o_ref, buf, s_buf, w_buf, top_buf, sum_buf, qbuf, sem, csem = refs[6:]
+        o_ref, buf, s_buf, w_buf, top_buf, sum_buf, qbuf, sem, csem = refs[8:]
         copies = prefix_copies(refs, buf, sem) + [
             pltpu.make_async_copy(cache_ref.at[at_ref[32 + p]], buf.at[p, pl.ds(512, 64)], csem.at[p])
             for p in range(32)
@@ -316,7 +285,7 @@
 
     return pl.pallas_call(
         kernel,
-        in_specs=[IN_SMEM] * 3 + [IN_VMEM] * 5 + [ANY] * 7,
+        in_specs=[IN_SMEM] * 3 + [IN_VMEM] * 5 + [ANY] * 9,
         out_specs=IN_VMEM,
         out_shape=jax.ShapeDtypeStruct((32, 4, COLS), BF16),
         scratch_shapes=buffers(keys)
@@ -344,11 +313,11 @@
     )(keep, more, bias, cosine, sine, after)
 
 
-def attend_prefix(limits, q, kvs):
+def attend_prefix(limits, q, kvs, after):
     keys = 512
 
     def kernel(limit_ref, q_ref, *refs):
-        o_ref, buf, s_buf, w_buf, top_buf, sum_buf, sem = refs[6:]
+        o_ref, buf, s_buf, w_buf, top_buf, sum_buf, sem = refs[9:]
         copies = prefix_copies(refs, buf, sem)
         for c in copies:
             c.start()
@@ -372,14 +341,14 @@
 
     return pl.pallas_call(
         kernel,
-        in_specs=[IN_SMEM, IN_VMEM] + [ANY] * 6,
+        in_specs=[IN_SMEM, IN_VMEM] + [ANY] * 9,
         out_specs=IN_VMEM,
         out_shape=jax.ShapeDtypeStruct((33, 32, HD), BF16),
         scratch_shapes=buffers(keys) + [pltpu.SemaphoreType.DMA((8,))],
         compiler_params=pltpu.CompilerParams(vmem_limit_bytes=VMEM),
         cost_estimate=SMALL,
         name="attend_prefix",
-    )(limits, q, *kvs)
+    )(limits, q, *kvs, after)
 
 
 def attend_near(lengths, order, q, new, cache, after):
@@ -473,6 +442,7 @@
 
     own = prefix_pairs.reshape(-1, 512, 2 * HD)
     below, above, own_c = over_roll(own, 0, 1, 0), over_roll(own, 0, 3, 0), over_roll(own, 0, 0, 1)
+    far = over_roll(below, 0, 1, 0)
 
     x_o, x_m = sort_rows(
         jnp.stack([my_y, my_z, my_c]).astype(jnp.int32),
@@ -492,24 +462,12 @@
     right_m, left_m = add_far(right_m, left_m, over_tp(up_m, 0, 1), over_tp(down_m, 0, 3), (right_o,))
     own_o, own_m = project(heads((0, 0), (1, 0)), [x_o, x_m], *weights, [[0, 1]], after=(right_o, left_o))
 
-    def reduce(right, left, own_part):
-        keep, send = sum_x(own_part, over_tp(right, 0, 1), over_tp(left, 0, 3))
+    def reduce(right, left, own_part, after):
+        keep, send = sum_x(own_part, over_tp(right, 0, 1), over_tp(left, 0, 3), after)
         return keep, over_tp(send, 1, 0)
 
-    full_o = reduce(right_o, left_o, own_o)
-    full_m = reduce(right_m, left_m, own_m)
-
-    far, both = turn_far(jnp.stack([my_c]).astype(jnp.int32), below, above, full_o[0])
-    far = lax.ppermute(
-        far,
-        "roll",
-        [
-            ((y * 4 + z) * 2 + c, (y * 4 + (z + 1 + 2 * c) % 4) * 2 + c)
-            for y in range(2)
-            for z in range(4)
-            for c in range(2)
-        ],
-    )
+    full_o = reduce(right_o, left_o, own_o, right_m)
+    full_m = reduce(right_m, left_m, own_m, full_o[0])
 
     index = jnp.arange(prompts, dtype=jnp.int32)
     half, quarter = jnp.arange(2, dtype=jnp.int32), jnp.arange(4, dtype=jnp.int32)
@@ -535,12 +493,11 @@
     )
     cache = cache_pairs.reshape(prompts, 64, 2 * HD)
 
-    q_o, new_o = make_queries(*full_o, *tables, right_m)
-    far = hold(far, q_o)
-    kvs = [own, both, far, own_c, over_roll(both, 0, 0, 1), over_roll(far, 0, 0, 1)]
-    values = attend_prefix(my_limits, over_roll(q_o, 1, 0, 0), kvs)
-    far = over_roll(values, 1, 0, 0)
-    near = attend_near(lengths, order, q_o, new_o, cache, values)
+    q_o, new_o = make_queries(*full_o, *tables, full_m[0])
+    near = attend_near(lengths, order, q_o, new_o, cache, full_m[1])
+    gathered = hold((below, above, far), q_o)
+    kvs = [own, *gathered, own_c] + [over_roll(a, 0, 0, 1) for a in gathered]
+    far = over_roll(attend_prefix(my_limits, over_roll(q_o, 1, 0, 0), kvs, near), 1, 0, 0)
     done = attend(my_limits, lengths, order, *full_m, *tables, cache, kvs)
     attended, new_pairs = merge_rows(order, far, near, new_o.reshape(32, new, PW), done)
     return (

time: 118 us -> 119 us (level)
  local copies, waits for them, and re-layouts: 10.7 us -> 28.2 us
  waiting for transfers between devices: 32.1 us -> 23.6 us
  starting transfers between devices: 27 us -> 22.4 us
  Pallas kernels: 44 us -> 40.1 us
    unnamed x52 -> x90, local copies, waits for them, and re-layouts: 8.41 us -> 23.8 us
    ppermute x10, waiting for transfers between devices: 28.8 us -> 22.2 us  [over_tp(): return lax.ppermute(a, 'tp', tp_shift(dy, dx))]
    pallas_call x6 -> x5, Pallas kernels: 18.2 us -> 12.6 us  [the longest x1 5.73 us: attend(): pl.pallas_call(kernel, in_specs=[IN_SMEM] * 3 + [IN_VMEM] * 5 + [ANY] * 9...]
    ppermute x1 -> x0, waiting for transfers between devices: 3.33 us -> none  [on_device(): lax.ppermute(far, 'roll', [((y * 4 + z) * 2 + c, (y * 4 + (z + 1 + 2 * c)...]
    ppermute x10, starting transfers between devices: 15 us -> 12.7 us  [over_tp(): return lax.ppermute(a, 'tp', tp_shift(dy, dx))]
    ppermute x7 -> x9, starting transfers between devices: 11.9 us -> 9.75 us  [over_roll(): return lax.ppermute(a, 'roll', roll_shift(dy, dz, dc))]
    ppermute x7 -> x9, waiting for transfers between devices: 0.02 us -> 1.39 us  [over_roll(): return lax.ppermute(a, 'roll', roll_shift(dy, dz, dc))]
  transfers between devices with their start and end apart: 18 -> 19, of which waited for: 5 -> 7; matrix products, arithmetic and copies ran while one was open for 4% -> 6% of each run, Pallas kernels for 36% -> 28%
where the time goes in v8:
time: 119 us; the launch traced here: 118 us
  Pallas kernels  40.1 us (34%)
  local copies, waits for them, and re-layouts  28.2 us (24%)
  waiting for transfers between devices  23.6 us (20%)
  starting transfers between devices  22.4 us (19%)
  other arithmetic  2.16 us (2%)
    unnamed x90, local copies, waits for them, and re-layouts  23.8 us
    ppermute x10, waiting for transfers between devices, over_tp(): return lax.ppermute(a, 'tp', tp_shift(dy, dx))  22.2 us
    pallas_call x3, Pallas kernels, project(): pl.pallas_call(kernel, in_specs=[IN_SMEM] + [IN_VMEM] * len(xs) + [IN_HBM...  16.4 us
    ppermute x10, starting transfers between devices, over_tp(): return lax.ppermute(a, 'tp', tp_shift(dy, dx))  12.7 us
    ppermute x9, starting transfers between devices, over_roll(): return lax.ppermute(a, 'roll', roll_shift(dy, dz, dc))  9.75 us
    pallas_call x1, Pallas kernels, attend(): pl.pallas_call(kernel, in_specs=[IN_SMEM] * 3 + [IN_VMEM] * 5 + [ANY] * 9...  5.73 us
    pallas_call x1, Pallas kernels, attend_prefix(): pl.pallas_call(kernel, in_specs=[IN_SMEM, IN_VMEM] + [ANY] * 9, out_specs...  5.3 us
    pallas_call x2, Pallas kernels, add_far(): pl.pallas_call(kernel, grid=(1,), in_specs=block + [block[0]] * 2 + [ANY]...  4.15 us
  transfers between devices with their start and end apart: 19, of which 7 were waited for; matrix products, arithmetic and copies ran while one was open for 6% of the time, Pallas kernels for 28%

profile of v8, /device:TPU:0, one launch (start us, length us, event | category | flops | bytes accessed | tf_op | source)
XLA Modules:
  0.0 117.7 jit_solution(12651858842534610973)
XLA Ops:
  0.7 2.1 %collective-permute-start.11 = (bf16[4,512,256]{2,1,0:T(8,128)(2,1)}, bf16[4,512,256]{2,1,0:T(8,128)(2,1)S(1)}, u32[]{:S(2)}, u32[]{:S(2)}) collective-permute-start(bf16[4,512,256]{2,1,0:T(8,128)(2,1)} %bitcast.23), channel_id=1, source_target_pairs={{0,16},{8,24},{16,32},{24,40},{32,48},{40,56},{48,0},{56,8},{64,80... | collective-permute-start | bytes 3145736 | tf_op jit(solution)/shard_map/ppermute | solution.py:44
  2.8 2.2 %collective-permute-start.12 = (bf16[4,512,256]{2,1,0:T(8,128)(2,1)}, bf16[4,512,256]{2,1,0:T(8,128)(2,1)S(1)}, u32[]{:S(2)}, u32[]{:S(2)}) collective-permute-start(bf16[4,512,256]{2,1,0:T(8,128)(2,1)} %bitcast.24), channel_id=1, source_target_pairs={{0,48},{8,56},{16,0},{24,8},{32,16},{40,24},{48,32},{56,40},{64,11... | collective-permute-start | bytes 3145736 | tf_op jit(solution)/shard_map/ppermute | solution.py:44
  5.0 2.0 %reshape.175.x_ref = bf16[256,1024]{1,0:T(8,128)(2,1)} reshape(bf16[64,1,4,1024]{3,2,1,0:T(4,128)(2,1)} %param.11) | data formatting | bytes 1048576 | tf_op jit(solution)/shard_map/reshape | solution.py:450
  7.0 0.7 broadcast_in_dim.48
  7.9 1.0 copy-done.27
  9.0 0.9 sort_rows.1
  9.9 5.1 %project.4 = (bf16[1,128,1280]{2,1,0:T(8,128)(2,1)}, bf16[1,128,1280]{2,1,0:T(8,128)(2,1)}, bf16[1,128,1280]{2,1,0:T(8,128)(2,1)S(1)}, bf16[1,128,1280]{2,1,0:T(8,128)(2,1)}) custom-call(s32[2]{0:T(128)S(1)} %pad_add_fusion.3.heads_ref, bf16[128,1024]{1,0:T(8,128)(2,1)S(1)} %get-tuple-element.29.refs_0_, bf16[128,1024]{1,0:T(8,128)(2,1)S(1)} %get-tuple-element.30.refs_1_, ...), custom_call_target="tpu_custom_call" | custom-call | flops 1000000 | bytes 100000 | tf_op jit(solution)/shard_map/project/pallas_call | solution.py:100
  15.0 0.7 copy-done.37
  15.7 1.5 %collective-permute-start.1 = (bf16[1,128,1280]{2,1,0:T(8,128)(2,1)}, bf16[1,128,1280]{2,1,0:T(8,128)(2,1)}, u32[]{:S(2)}, u32[]{:S(2)}) collective-permute-start(bf16[1,128,1280]{2,1,0:T(8,128)(2,1)} %get-tuple-element.33), channel_id=1, source_target_pairs={{0,1},{1,2},{2,3},{3,0},{4,5},{5,6},{6,7},{7,4},{8,9},{9,10},{10,1... | collective-permute-start | bytes 983048 | tf_op jit(solution)/shard_map/ppermute | solution.py:40
  17.2 1.7 %collective-permute-start.2 = (bf16[1,128,1280]{2,1,0:T(8,128)(2,1)}, bf16[1,128,1280]{2,1,0:T(8,128)(2,1)}, u32[]{:S(2)}, u32[]{:S(2)}) collective-permute-start(bf16[1,128,1280]{2,1,0:T(8,128)(2,1)} %get-tuple-element.34), channel_id=1, source_target_pairs={{0,3},{1,0},{2,1},{3,2},{4,7},{5,4},{6,5},{7,6},{8,11},{9,8},{10,9... | collective-permute-start | bytes 983048 | tf_op jit(solution)/shard_map/ppermute | solution.py:40
  20.5 0.9 copy-done.25
  21.5 7.1 %project.3 = (bf16[2,128,1280]{2,1,0:T(8,128)(2,1)}, bf16[2,128,1280]{2,1,0:T(8,128)(2,1)S(1)}, bf16[2,128,1280]{2,1,0:T(8,128)(2,1)}, bf16[2,128,1280]{2,1,0:T(8,128)(2,1)}) custom-call(s32[4]{0:T(128)S(1)} %pad_add_fusion.2.heads_ref, bf16[128,1024]{1,0:T(8,128)(2,1)S(1)} %get-tuple-element.29.refs_0_, bf16[128,1024]{1,0:T(8,128)(2,1)S(1)} %copy-done.25, ...), custom_call_target="tpu_custom_call" | custom-call | flops 1000000 | bytes 100000 | tf_op jit(solution)/shard_map/project/pallas_call | solution.py:100
  28.6 2.3 %collective-permute-start.6 = (bf16[1,128,1280]{2,1,0:T(8,128)(2,1)}, bf16[1,128,1280]{2,1,0:T(8,128)(2,1)}, u32[]{:S(2)}, u32[]{:S(2)}) collective-permute-start(bf16[1,128,1280]{2,1,0:T(8,128)(2,1)} %get-tuple-element.41), channel_id=1, source_target_pairs={{0,3},{1,0},{2,1},{3,2},{4,7},{5,4},{6,5},{7,6},{8,11},{9,8},{10,9... | collective-permute-start | bytes 983048 | tf_op jit(solution)/shard_map/ppermute | solution.py:40
  30.9 2.0 %add_far.2 = (bf16[2,128,1280]{2,1,0:T(8,128)(2,1)}, bf16[2,128,1280]{2,1,0:T(8,128)(2,1)S(1)}) custom-call(bf16[2,128,1280]{2,1,0:T(8,128)(2,1)} %get-tuple-element.31.r, bf16[2,128,1280]{2,1,0:T(8,128)(2,1)S(1)} %get-tuple-element.32.l, bf16[1,128,1280]{2,1,0:T(8,128)(2,1)} %collective-permute-done.1.u, ...), custom_call_target="tpu_custom_call", output_to_operand_aliasing={{0}: (0, {}), {1}: (1, {})} | custom-call | flops 1000000 | bytes 100000 | tf_op jit(solution)/shard_map/add_far/pallas_call | solution.py:151
  34.4 2.8 %collective-permute-start.4 = (bf16[2,128,1280]{2,1,0:T(8,128)(2,1)}, bf16[2,128,1280]{2,1,0:T(8,128)(2,1)}, u32[]{:S(2)}, u32[]{:S(2)}) collective-permute-start(bf16[2,128,1280]{2,1,0:T(8,128)(2,1)} %copy-done.22), channel_id=1, source_target_pairs={{0,3},{1,0},{2,1},{3,2},{4,7},{5,4},{6,5},{7,6},{8,11},{9,8},{10,9... | collective-permute-start | bytes 1966088 | tf_op jit(solution)/shard_map/ppermute | solution.py:40
  37.4 2.2 %collective-permute-done.6.d = bf16[1,128,1280]{2,1,0:T(8,128)(2,1)} collective-permute-done((bf16[1,128,1280]{2,1,0:T(8,128)(2,1)}, bf16[1,128,1280]{2,1,0:T(8,128)(2,1)}, u32[]{:S(2)}, u32[]{:S(2)}) %collective-permute-start.6) | collective-permute-done | bytes 327712 | tf_op jit(solution)/shard_map/ppermute | solution.py:40
  39.6 2.2 %add_far.3 = (bf16[2,128,1280]{2,1,0:T(8,128)(2,1)}, bf16[2,128,1280]{2,1,0:T(8,128)(2,1)}) custom-call(bf16[2,128,1280]{2,1,0:T(8,128)(2,1)} %get-tuple-element.38.r, bf16[2,128,1280]{2,1,0:T(8,128)(2,1)} %get-tuple-element.39.l, bf16[1,128,1280]{2,1,0:T(8,128)(2,1)} %collective-permute-done.5.u, ...), custom_call_target="tpu_custom_call", output_to_operand_aliasing={{0}: (0, {}), {1}: (1, {})} | custom-call | flops 1000000 | bytes 100000 | tf_op jit(solution)/shard_map/add_far/pallas_call | solution.py:151
  41.8 0.8 collective-permute-start.8
  42.6 9.4 %collective-permute-done.3.b = bf16[2,128,1280]{2,1,0:T(8,128)(2,1)S(1)} collective-permute-done((bf16[2,128,1280]{2,1,0:T(8,128)(2,1)}, bf16[2,128,1280]{2,1,0:T(8,128)(2,1)S(1)}, u32[]{:S(2)}, u32[]{:S(2)}) %collective-permute-start.3) | collective-permute-done | bytes 655392 | tf_op jit(solution)/shard_map/ppermute | solution.py:40
  52.6 1.1 copy-done.23
  53.7 4.2 %project.5 = (bf16[2,128,1280]{2,1,0:T(8,128)(2,1)S(1)}, bf16[2,128,1280]{2,1,0:T(8,128)(2,1)S(1)}) custom-call(s32[2]{0:T(128)S(1)} %pad_add_fusion.heads_ref, bf16[128,1024]{1,0:T(8,128)(2,1)S(1)} %get-tuple-element.29.refs_0_, bf16[128,1024]{1,0:T(8,128)(2,1)S(1)} %copy-done.26, bf16[1024,8192]{1,0:T(8,128)(2,1)} %refs_2_.5, bf16[1024,2048]{1,0:T(8,128)(2,1)} %refs_3_.5, ...), custom_call_target="tpu_custom_call" | custom-call | flops 1000000 | bytes 100000 | tf_op jit(solution)/shard_map/project/pallas_call | solution.py:100
  57.9 1.3 %sum_x.2 = (f32[128,1280]{1,0:T(8,128)S(1)}, bf16[128,1280]{1,0:T(8,128)(2,1)S(1)}) custom-call(bf16[2,128,1280]{2,1,0:T(8,128)(2,1)S(1)} %get-tuple-element.37.a, bf16[2,128,1280]{2,1,0:T(8,128)(2,1)S(1)} %collective-permute-done.3.b, bf16[2,128,1280]{2,1,0:T(8,128)(2,1)} %collective-permute-done.4.c, bf16[2,128,1280]{2,1,0:T(8,128)(2,1)} %get-tuple-element.42.after_ref), custom_call_target="tpu_custom_call" | custom-call | flops 1000000 | bytes 100000 | tf_op jit(solution)/shard_map/sum_x/pallas_call | solution.py:191
  59.3 1.7 %collective-permute-start.7 = (bf16[128,1280]{1,0:T(8,128)(2,1)S(1)}, bf16[128,1280]{1,0:T(8,128)(2,1)S(1)}, u32[]{:S(2)}, u32[]{:S(2)}) collective-permute-start(bf16[128,1280]{1,0:T(8,128)(2,1)S(1)} %get-tuple-element.44), channel_id=1, source_target_pairs={{0,4},{1,5},{2,6},{3,7},{4,0},{5,1},{6,2},{7,3},{8,12},{9,13},{10,... | collective-permute-start | bytes 983048 | tf_op jit(solution)/shard_map/ppermute | solution.py:40
  61.1 2.8 %collective-permute-done.8.b = bf16[2,128,1280]{2,1,0:T(8,128)(2,1)S(1)} collective-permute-done((bf16[2,128,1280]{2,1,0:T(8,128)(2,1)}, bf16[2,128,1280]{2,1,0:T(8,128)(2,1)S(1)}, u32[]{:S(2)}, u32[]{:S(2)}) %collective-permute-start.8) | collective-permute-done | bytes 655392 | tf_op jit(solution)/shard_map/ppermute | solution.py:40
  63.9 2.1 %collective-permute-done.9.c = bf16[2,128,1280]{2,1,0:T(8,128)(2,1)S(1)} collective-permute-done((bf16[2,128,1280]{2,1,0:T(8,128)(2,1)}, bf16[2,128,1280]{2,1,0:T(8,128)(2,1)S(1)}, u32[]{:S(2)}, u32[]{:S(2)}) %collective-permute-start.9) | collective-permute-done | bytes 655392 | tf_op jit(solution)/shard_map/ppermute | solution.py:40
  68.9 1.6 %collective-permute-start.17 = (bf16[128,1280]{1,0:T(8,128)(2,1)}, bf16[128,1280]{1,0:T(8,128)(2,1)S(1)}, u32[]{:S(2)}, u32[]{:S(2)}) collective-permute-start(bf16[128,1280]{1,0:T(8,128)(2,1)} %copy-done.38), channel_id=1, source_target_pairs={{0,4},{1,5},{2,6},{3,7},{4,0},{5,1},{6,2},{7,3},{8,12},{9,13},{10,... | collective-permute-start | bytes 983048 | tf_op jit(solution)/shard_map/ppermute | solution.py:40
  70.5 2.9 %collective-permute-start.10 = (bf16[32,32,128]{2,1,0:T(8,128)(2,1)}, bf16[32,32,128]{2,1,0:T(8,128)(2,1)S(1)}, u32[]{:S(2)}, u32[]{:S(2)}) collective-permute-start(bf16[32,32,128]{2,1,0:T(8,128)(2,1)} %copy-done.32), channel_id=1, source_target_pairs={{0,64},{8,72},{16,80},{24,88},{32,96},{40,104},{48,112},{56,120},{... | collective-permute-start | bytes 786440 | tf_op jit(solution)/shard_map/ppermute | solution.py:44
  73.4 0.8 slice.3.limit_ref
  74.2 5.5 %collective-permute-done.17.after_ref.more_ref = bf16[128,1280]{1,0:T(8,128)(2,1)S(1)} collective-permute-done((bf16[128,1280]{1,0:T(8,128)(2,1)}, bf16[128,1280]{1,0:T(8,128)(2,1)S(1)}, u32[]{:S(2)}, u32[]{:S(2)}) %collective-permute-start.17) | collective-permute-done | bytes 327712 | tf_op jit(solution)/shard_map/ppermute | solution.py:40
  79.6 1.6 %copy-done.8 = bf16[64,1,64,1,256]{4,2,3,1,0:T(8,128)(2,1)S(1)} copy-done((bf16[64,1,64,1,256]{4,2,3,1,0:T(8,128)(2,1)S(1)}, bf16[64,1,64,1,256]{4,2,3,1,0:T(8,128)(2,1)}, u32[]{:S(2)}) %copy-start.8) | copy-done | bytes 2097176
  81.2 0.9 copy-done.33
  82.2 3.7 %attend_near.1.refs_8_.near_ref = f32[33,32,128]{2,1,0:T(8,128)S(1)} custom-call(s32[64]{0:T(128)S(1)} %get-tuple-element.62.length_ref, s32[64]{0:T(128)S(1)} %get-tuple-element.64.at_ref.order_ref, bf16[32,32,128]{2,1,0:T(8,128)(2,1)S(1)} %copy-done.33, bf16[128,256]{1,0:T(8,128)(2,1)S(1)} %get-tuple-element.52.new_ref, bf16[64,64,256]{2,1,0:T(8,128)(2,1)S(1)} %bitcast.20, ...), custom_call_target="tpu_custom_call" | custom-call | flops 1000000 | bytes 100000 | tf_op jit(solution)/shard_map/attend_near/pallas_call | solution.py:382
  85.9 1.4 %collective-permute-done.10.q_ref = bf16[32,32,128]{2,1,0:T(8,128)(2,1)S(1)} collective-permute-done((bf16[32,32,128]{2,1,0:T(8,128)(2,1)}, bf16[32,32,128]{2,1,0:T(8,128)(2,1)S(1)}, u32[]{:S(2)}, u32[]{:S(2)}) %collective-permute-start.10) | collective-permute-done | bytes 262176 | tf_op jit(solution)/shard_map/ppermute | solution.py:44
  87.4 2.0 %copy-done.3 = bf16[4,512,256]{2,1,0:T(8,128)(2,1)S(1)} copy-done((bf16[4,512,256]{2,1,0:T(8,128)(2,1)S(1)}, bf16[4,512,256]{2,1,0:T(8,128)(2,1)}, u32[]{:S(2)}) %copy-start.3) | copy-done | bytes 1048600
  89.3 1.2 %copy-done.6 = bf16[4,512,256]{2,1,0:T(8,128)(2,1)S(1)} copy-done((bf16[4,512,256]{2,1,0:T(8,128)(2,1)S(1)}, bf16[4,512,256]{2,1,0:T(8,128)(2,1)}, u32[]{:S(2)}) %copy-start.6) | copy-done | bytes 1048600
  90.6 1.2 %copy-done.12 = bf16[4,512,1,256]{3,1,2,0:T(8,128)(2,1)S(1)} copy-done((bf16[4,512,1,256]{3,1,2,0:T(8,128)(2,1)S(1)}, bf16[4,512,1,256]{3,1,2,0:T(8,128)(2,1)}, u32[]{:S(2)}) %copy-start.12) | copy-done | bytes 1048600
  91.8 5.3 %attend_prefix.1 = bf16[33,32,128]{2,1,0:T(8,128)(2,1)} custom-call(s32[32]{0:T(128)S(1)} %slice.3.limit_ref, bf16[32,32,128]{2,1,0:T(8,128)(2,1)S(1)} %collective-permute-done.10.q_ref, bf16[4,512,256]{2,1,0:T(8,128)(2,1)S(1)} %bitcast.25, bf16[4,512,256]{2,1,0:T(8,128)(2,1)S(1)} %copy-done.3, bf16[4,512,256]{2,1,0:T(8,128)(2,1)S(1)} %copy-done.6, ...), custom_call_target="tpu_custom_call" | custom-call | flops 1000000 | bytes 100000 | tf_op jit(solution)/shard_map/attend_prefix/pallas_call | solution.py:342
  97.1 2.0 %collective-permute-start.18 = (bf16[33,32,128]{2,1,0:T(8,128)(2,1)}, bf16[33,32,128]{2,1,0:T(8,128)(2,1)}, u32[]{:S(2)}, u32[]{:S(2)}) collective-permute-start(bf16[33,32,128]{2,1,0:T(8,128)(2,1)} %attend_prefix.1), channel_id=1, source_target_pairs={{0,64},{8,72},{16,80},{24,88},{32,96},{40,104},{48,112},{56,120},{... | collective-permute-start | bytes 811016 | tf_op jit(solution)/shard_map/ppermute | solution.py:44
  99.8 1.6 %copy-done.9 = bf16[64,1,64,1,256]{4,2,3,1,0:T(8,128)(2,1)S(1)} copy-done((bf16[64,1,64,1,256]{4,2,3,1,0:T(8,128)(2,1)S(1)}, bf16[64,1,64,1,256]{4,2,3,1,0:T(8,128)(2,1)}, u32[]{:S(2)}) %copy-start.9) | copy-done | bytes 2097176
  101.4 1.2 %copy-done.13 = bf16[4,512,1,256]{3,1,2,0:T(8,128)(2,1)S(1)} copy-done((bf16[4,512,1,256]{3,1,2,0:T(8,128)(2,1)S(1)}, bf16[4,512,1,256]{3,1,2,0:T(8,128)(2,1)}, u32[]{:S(2)}) %copy-start.13) | copy-done | bytes 1048600
  102.6 1.2 %copy-done.15 = bf16[4,512,256]{2,1,0:T(8,128)(2,1)S(1)} copy-done((bf16[4,512,256]{2,1,0:T(8,128)(2,1)S(1)}, bf16[4,512,256]{2,1,0:T(8,128)(2,1)}, u32[]{:S(2)}) %copy-start.15) | copy-done | bytes 1048600
  103.8 1.2 %copy-done.17 = bf16[4,512,256]{2,1,0:T(8,128)(2,1)S(1)} copy-done((bf16[4,512,256]{2,1,0:T(8,128)(2,1)S(1)}, bf16[4,512,256]{2,1,0:T(8,128)(2,1)}, u32[]{:S(2)}) %copy-start.17) | copy-done | bytes 1048600
  105.0 1.2 %copy-done.19 = bf16[4,512,256]{2,1,0:T(8,128)(2,1)S(1)} copy-done((bf16[4,512,256]{2,1,0:T(8,128)(2,1)S(1)}, bf16[4,512,256]{2,1,0:T(8,128)(2,1)}, u32[]{:S(2)}) %copy-start.19) | copy-done | bytes 1048600
  106.3 1.1 copy-done.21
  107.3 0.9 copy-done.29
  108.3 0.9 copy-done.31
  109.8 5.7 %attend.1.done_ref = bf16[32,4,1280]{2,1,0:T(4,128)(2,1)S(1)} custom-call(s32[32]{0:T(128)S(1)} %copy-done.36, s32[64]{0:T(128)S(1)} %get-tuple-element.62.length_ref, s32[64]{0:T(128)S(1)} %get-tuple-element.64.at_ref.order_ref, f32[128,1280]{1,0:T(8,128)S(1)} %copy-done.21, bf16[128,1280]{1,0:T(8,128)(2,1)S(1)} %collective-permute-done.17.after_ref.more_ref, ...), custom_call_target="tpu_custom_call" | custom-call | flops 1000000 | bytes 100000 | tf_op jit(solution)/shard_map/attend/pallas_call | solution.py:286
  115.6 2.1 %merge_rows.1 = (bf16[64,4,1024]{2,1,0:T(4,128)(2,1)}, bf16[64,4,256]{2,1,0:T(4,128)(2,1)}) custom-call(s32[64]{0:T(128)S(1)} %get-tuple-element.64.at_ref.order_ref, bf16[33,32,128]{2,1,0:T(8,128)(2,1)} %collective-permute-done.18.far_ref, f32[33,32,128]{2,1,0:T(8,128)S(1)} %copy-done.11, bf16[32,4,256]{2,1,0:T(4,128)(2,1)S(1)} %copy-done.34, ...), custom_call_target="tpu_custom_call" | custom-call | flops 1000000 | bytes 100000 | tf_op jit(solution)/shard_map/merge_rows/pallas_call | solution.py:413
  (120 shorter events, 8.4 us)
Async XLA Ops:
  0.6 18.8 %collective-permute-start = (bf16[4,512,256]{2,1,0:T(8,128)(2,1)}, bf16[4,512,256]{2,1,0:T(8,128)(2,1)S(1)}, u32[]{:S(2)}, u32[]{:S(2)}) collective-permute-start(bf16[4,512,256]{2,1,0:T(8,128)(2,1)} %bitcast.22), channel_id=1, source_target_pairs={{0,8},{8,0},{16,24},{24,16},{32,40},{40,32},{48,56},{56,48},{64,72... | collective-permute-start | bytes 3145736 | tf_op jit(solution)/shard_map/ppermute | solution.py:44
  0.7 32.4 %collective-permute-start.11 = (bf16[4,512,256]{2,1,0:T(8,128)(2,1)}, bf16[4,512,256]{2,1,0:T(8,128)(2,1)S(1)}, u32[]{:S(2)}, u32[]{:S(2)}) collective-permute-start(bf16[4,512,256]{2,1,0:T(8,128)(2,1)} %bitcast.23), channel_id=1, source_target_pairs={{0,16},{8,24},{16,32},{24,40},{32,48},{40,56},{48,0},{56,8},{64,80... | collective-permute-start | bytes 3145736 | tf_op jit(solution)/shard_map/ppermute | solution.py:44
  2.8 64.5 %collective-permute-start.12 = (bf16[4,512,256]{2,1,0:T(8,128)(2,1)}, bf16[4,512,256]{2,1,0:T(8,128)(2,1)S(1)}, u32[]{:S(2)}, u32[]{:S(2)}) collective-permute-start(bf16[4,512,256]{2,1,0:T(8,128)(2,1)} %bitcast.24), channel_id=1, source_target_pairs={{0,48},{8,56},{16,0},{24,8},{32,16},{40,24},{48,32},{56,40},{64,11... | collective-permute-start | bytes 3145736 | tf_op jit(solution)/shard_map/ppermute | solution.py:44
  9.9 5.1 %copy-start.24 = (bf16[128,1024]{1,0:T(8,128)(2,1)}, bf16[128,1024]{1,0:T(8,128)(2,1)S(1)}, u32[]{:S(2)}) copy-start(bf16[128,1024]{1,0:T(8,128)(2,1)S(1)} %get-tuple-element.30.refs_1_) | copy-start | bytes 786436
  9.9 9.1 %copy-start.44 = (s32[4]{0:T(128)S(1)}, s32[4]{0:T(128)}, u32[]{:S(2)}) copy-start(s32[4]{0:T(128)} %constant.143.clone) | copy-start | bytes 52
  15.7 12.8 %collective-permute-start.1 = (bf16[1,128,1280]{2,1,0:T(8,128)(2,1)}, bf16[1,128,1280]{2,1,0:T(8,128)(2,1)}, u32[]{:S(2)}, u32[]{:S(2)}) collective-permute-start(bf16[1,128,1280]{2,1,0:T(8,128)(2,1)} %get-tuple-element.33), channel_id=1, source_target_pairs={{0,1},{1,2},{2,3},{3,0},{4,5},{5,6},{6,7},{7,4},{8,9},{9,10},{10,1... | collective-permute-start | bytes 983048 | tf_op jit(solution)/shard_map/ppermute | solution.py:40
  17.2 13.7 %collective-permute-start.2 = (bf16[1,128,1280]{2,1,0:T(8,128)(2,1)}, bf16[1,128,1280]{2,1,0:T(8,128)(2,1)}, u32[]{:S(2)}, u32[]{:S(2)}) collective-permute-start(bf16[1,128,1280]{2,1,0:T(8,128)(2,1)} %get-tuple-element.34), channel_id=1, source_target_pairs={{0,3},{1,0},{2,1},{3,2},{4,7},{5,4},{6,5},{7,6},{8,11},{9,8},{10,9... | collective-permute-start | bytes 983048 | tf_op jit(solution)/shard_map/ppermute | solution.py:40
  19.5 14.9 %collective-permute-start.5 = (bf16[1,128,1280]{2,1,0:T(8,128)(2,1)}, bf16[1,128,1280]{2,1,0:T(8,128)(2,1)}, u32[]{:S(2)}, u32[]{:S(2)}) collective-permute-start(bf16[1,128,1280]{2,1,0:T(8,128)(2,1)} %copy-done.37), channel_id=1, source_target_pairs={{0,1},{1,2},{2,3},{3,0},{4,5},{5,6},{6,7},{7,4},{8,9},{9,10},{10,1... | collective-permute-start | bytes 983048 | tf_op jit(solution)/shard_map/ppermute | solution.py:40
  21.4 11.4 %copy-start.39 = (s32[64]{0:T(128)S(1)}, s32[64]{0:T(128)}, u32[]{:S(2)}) copy-start(s32[64]{0:T(128)} %param.18) | copy-start | bytes 772
  21.5 11.4 %copy-start.41 = (s32[64,1]{0,1:T(1,128)S(1)}, s32[64,1]{0,1:T(1,128)}, u32[]{:S(2)}) copy-start(s32[64,1]{0,1:T(1,128)} %param.20) | copy-start | bytes 772
  21.5 11.4 %copy-start.42 = (s32[64]{0:T(128)S(1)}, s32[64]{0:T(128)}, u32[]{:S(2)}) copy-start(s32[64]{0:T(128)} %param.19) | copy-start | bytes 772
  21.5 15.9 %copy-start.40 = (bf16[1024]{0:T(1024)(128)(2,1)S(1)}, bf16[1024]{0:T(1024)(128)(2,1)}, u32[]{:S(2)}) copy-start(bf16[1024]{0:T(1024)(128)(2,1)} %param.13) | copy-start | bytes 6148
  21.5 15.9 %copy-start.43 = (bf16[256]{0:T(256)(128)(2,1)S(1)}, bf16[256]{0:T(256)(128)(2,1)}, u32[]{:S(2)}) copy-start(bf16[256]{0:T(256)(128)(2,1)} %param.15) | copy-start | bytes 1540
  28.6 24.0 %copy-start.26 = (bf16[128,1024]{1,0:T(8,128)(2,1)S(1)}, bf16[128,1024]{1,0:T(8,128)(2,1)}, u32[]{:S(2)}) copy-start(bf16[128,1024]{1,0:T(8,128)(2,1)} %copy-done.24) | copy-start | bytes 786436
  28.6 11.0 %collective-permute-start.6 = (bf16[1,128,1280]{2,1,0:T(8,128)(2,1)}, bf16[1,128,1280]{2,1,0:T(8,128)(2,1)}, u32[]{:S(2)}, u32[]{:S(2)}) collective-permute-start(bf16[1,128,1280]{2,1,0:T(8,128)(2,1)} %get-tuple-element.41), channel_id=1, source_target_pairs={{0,3},{1,0},{2,1},{3,2},{4,7},{5,4},{6,5},{7,6},{8,11},{9,8},{10,9... | collective-permute-start | bytes 983048 | tf_op jit(solution)/shard_map/ppermute | solution.py:40
  32.9 19.1 %collective-permute-start.3 = (bf16[2,128,1280]{2,1,0:T(8,128)(2,1)}, bf16[2,128,1280]{2,1,0:T(8,128)(2,1)S(1)}, u32[]{:S(2)}, u32[]{:S(2)}) collective-permute-start(bf16[2,128,1280]{2,1,0:T(8,128)(2,1)} %get-tuple-element.35.refs_4_.refs_0_), channel_id=1, source_target_pairs={{0,1},{1,2},{2,3},{3,0},{4,5},{5,6},{6,7},{7,4},{8,9},{9,10},{10,1... | collective-permute-start | bytes 1966088 | tf_op jit(solution)/shard_map/ppermute | solution.py:40
  33.7 24.2 %copy-start.2 = (bf16[4,512,256]{2,1,0:T(8,128)(2,1)}, bf16[4,512,256]{2,1,0:T(8,128)(2,1)S(1)}, u32[]{:S(2)}) copy-start(bf16[4,512,256]{2,1,0:T(8,128)(2,1)S(1)} %collective-permute-done.11.refs_0_) | copy-start | bytes 3145732
  33.7 33.6 %collective-permute-start.13 = (bf16[4,512,256]{2,1,0:T(8,128)(2,1)S(1)}, bf16[4,512,256]{2,1,0:T(8,128)(2,1)}, u32[]{:S(2)}, u32[]{:S(2)}) collective-permute-start(bf16[4,512,256]{2,1,0:T(8,128)(2,1)S(1)} %collective-permute-done.11.refs_0_), channel_id=1, source_target_pairs={{0,16},{8,24},{16,32},{24,40},{32,48},{40,56},{48,0},{56,8},{64,80... | collective-permute-start | bytes 3145736 | tf_op jit(solution)/shard_map/ppermute | solution.py:44
  34.4 23.6 %collective-permute-start.4 = (bf16[2,128,1280]{2,1,0:T(8,128)(2,1)}, bf16[2,128,1280]{2,1,0:T(8,128)(2,1)}, u32[]{:S(2)}, u32[]{:S(2)}) collective-permute-start(bf16[2,128,1280]{2,1,0:T(8,128)(2,1)} %copy-done.22), channel_id=1, source_target_pairs={{0,3},{1,0},{2,1},{3,2},{4,7},{5,4},{6,5},{7,6},{8,11},{9,8},{10,9... | collective-permute-start | bytes 1966088 | tf_op jit(solution)/shard_map/ppermute | solution.py:40
  41.8 22.1 %collective-permute-start.8 = (bf16[2,128,1280]{2,1,0:T(8,128)(2,1)}, bf16[2,128,1280]{2,1,0:T(8,128)(2,1)S(1)}, u32[]{:S(2)}, u32[]{:S(2)}) collective-permute-start(bf16[2,128,1280]{2,1,0:T(8,128)(2,1)} %get-tuple-element.42.after_ref), channel_id=1, source_target_pairs={{0,1},{1,2},{2,3},{3,0},{4,5},{5,6},{6,7},{7,4},{8,9},{9,10},{10,1... | collective-permute-start | bytes 1966088 | tf_op jit(solution)/shard_map/ppermute | solution.py:40
  52.0 14.1 %collective-permute-start.9 = (bf16[2,128,1280]{2,1,0:T(8,128)(2,1)}, bf16[2,128,1280]{2,1,0:T(8,128)(2,1)S(1)}, u32[]{:S(2)}, u32[]{:S(2)}) collective-permute-start(bf16[2,128,1280]{2,1,0:T(8,128)(2,1)} %get-tuple-element.46), channel_id=1, source_target_pairs={{0,3},{1,0},{2,1},{3,2},{4,7},{5,4},{6,5},{7,6},{8,11},{9,8},{10,9... | collective-permute-start | bytes 1966088 | tf_op jit(solution)/shard_map/ppermute | solution.py:40
  59.3 7.2 %collective-permute-start.7 = (bf16[128,1280]{1,0:T(8,128)(2,1)S(1)}, bf16[128,1280]{1,0:T(8,128)(2,1)S(1)}, u32[]{:S(2)}, u32[]{:S(2)}) collective-permute-start(bf16[128,1280]{1,0:T(8,128)(2,1)S(1)} %get-tuple-element.44), channel_id=1, source_target_pairs={{0,4},{1,5},{2,6},{3,7},{4,0},{5,1},{6,2},{7,3},{8,12},{9,13},{10,... | collective-permute-start | bytes 983048 | tf_op jit(solution)/shard_map/ppermute | solution.py:40
  61.1 6.3 %copy-start.28 = (f32[256,128]{1,0:T(8,128)}, f32[256,128]{1,0:T(8,128)S(1)}, u32[]{:S(2)}) copy-start(f32[256,128]{1,0:T(8,128)S(1)} %get-tuple-element.70.cos_ref) | copy-start | bytes 393220
  61.1 6.3 %copy-start.30 = (f32[256,128]{1,0:T(8,128)}, f32[256,128]{1,0:T(8,128)S(1)}, u32[]{:S(2)}) copy-start(f32[256,128]{1,0:T(8,128)S(1)} %get-tuple-element.71.sin_ref) | copy-start | bytes 393220
  67.0 20.3 %copy-start.1 = (bf16[4,512,256]{2,1,0:T(8,128)(2,1)S(1)}, bf16[4,512,256]{2,1,0:T(8,128)(2,1)}, u32[]{:S(2)}) copy-start(bf16[4,512,256]{2,1,0:T(8,128)(2,1)} %copy-done) | copy-start | bytes 3145732
  68.4 18.9 %collective-permute-start.14 = (bf16[4,512,256]{2,1,0:T(8,128)(2,1)}, bf16[4,512,256]{2,1,0:T(8,128)(2,1)S(1)}, u32[]{:S(2)}, u32[]{:S(2)}) collective-permute-start(bf16[4,512,256]{2,1,0:T(8,128)(2,1)} %get-tuple-element.49.refs_1_), channel_id=1, source_target_pairs={{0,8},{8,0},{16,24},{24,16},{32,40},{40,32},{48,56},{56,48},{64,72... | collective-permute-start | bytes 3145736 | tf_op jit(solution)/shard_map/ppermute | solution.py:44
  68.4 18.9 %collective-permute-start.15 = (bf16[4,512,256]{2,1,0:T(8,128)(2,1)}, bf16[4,512,256]{2,1,0:T(8,128)(2,1)S(1)}, u32[]{:S(2)}, u32[]{:S(2)}) collective-permute-start(bf16[4,512,256]{2,1,0:T(8,128)(2,1)} %get-tuple-element.50.refs_2_), channel_id=1, source_target_pairs={{0,8},{8,0},{16,24},{24,16},{32,40},{40,32},{48,56},{56,48},{64,72... | collective-permute-start | bytes 3145736 | tf_op jit(solution)/shard_map/ppermute | solution.py:44
  68.9 18.4 %collective-permute-start.16 = (bf16[4,512,256]{2,1,0:T(8,128)(2,1)}, bf16[4,512,256]{2,1,0:T(8,128)(2,1)S(1)}, u32[]{:S(2)}, u32[]{:S(2)}) collective-permute-start(bf16[4,512,256]{2,1,0:T(8,128)(2,1)} %get-tuple-element.51.refs_3_), channel_id=1, source_target_pairs={{0,8},{8,0},{16,24},{24,16},{32,40},{40,32},{48,56},{56,48},{64,72... | collective-permute-start | bytes 3145736 | tf_op jit(solution)/shard_map/ppermute | solution.py:44
  68.9 10.7 %collective-permute-start.17 = (bf16[128,1280]{1,0:T(8,128)(2,1)}, bf16[128,1280]{1,0:T(8,128)(2,1)S(1)}, u32[]{:S(2)}, u32[]{:S(2)}) collective-permute-start(bf16[128,1280]{1,0:T(8,128)(2,1)} %copy-done.38), channel_id=1, source_target_pairs={{0,4},{1,5},{2,6},{3,7},{4,0},{5,1},{6,2},{7,3},{8,12},{9,13},{10,... | collective-permute-start | bytes 983048 | tf_op jit(solution)/shard_map/ppermute | solution.py:40
  70.5 16.8 %collective-permute-start.10 = (bf16[32,32,128]{2,1,0:T(8,128)(2,1)}, bf16[32,32,128]{2,1,0:T(8,128)(2,1)S(1)}, u32[]{:S(2)}, u32[]{:S(2)}) collective-permute-start(bf16[32,32,128]{2,1,0:T(8,128)(2,1)} %copy-done.32), channel_id=1, source_target_pairs={{0,64},{8,72},{16,80},{24,88},{32,96},{40,104},{48,112},{56,120},{... | collective-permute-start | bytes 786440 | tf_op jit(solution)/shard_map/ppermute | solution.py:44
  74.1 22.9 %copy-start.35 = (s32[32]{0:T(128)}, s32[32]{0:T(128)S(1)}, u32[]{:S(2)}) copy-start(s32[32]{0:T(128)S(1)} %slice.3.limit_ref) | copy-start | bytes 388
  79.6 1.6 %copy-start.8 = (bf16[64,1,64,1,256]{4,2,3,1,0:T(8,128)(2,1)S(1)}, bf16[64,1,64,1,256]{4,2,3,1,0:T(8,128)(2,1)}, u32[]{:S(2)}) copy-start(bf16[64,1,64,1,256]{4,2,3,1,0:T(8,128)(2,1)} %param.16) | copy-start | bytes 6291460
  82.2 17.6 %copy-start.4 = (bf16[4,512,256]{2,1,0:T(8,128)(2,1)S(1)}, bf16[4,512,256]{2,1,0:T(8,128)(2,1)}, u32[]{:S(2)}) copy-start(bf16[4,512,256]{2,1,0:T(8,128)(2,1)} %get-tuple-element.49.refs_1_) | copy-start | bytes 3145732
  82.2 17.6 %copy-start.7 = (bf16[4,512,256]{2,1,0:T(8,128)(2,1)S(1)}, bf16[4,512,256]{2,1,0:T(8,128)(2,1)}, u32[]{:S(2)}) copy-start(bf16[4,512,256]{2,1,0:T(8,128)(2,1)} %get-tuple-element.50.refs_2_) | copy-start | bytes 3145732
  85.9 11.2 %copy-start.10 = (f32[33,32,128]{2,1,0:T(8,128)}, f32[33,32,128]{2,1,0:T(8,128)S(1)}, u32[]{:S(2)}) copy-start(f32[33,32,128]{2,1,0:T(8,128)S(1)} %attend_near.1.refs_8_.near_ref) | copy-start | bytes 1622020
  87.3 9.8 %copy-start.14 = (bf16[4,512,256]{2,1,0:T(8,128)(2,1)}, bf16[4,512,256]{2,1,0:T(8,128)(2,1)S(1)}, u32[]{:S(2)}) copy-start(bf16[4,512,256]{2,1,0:T(8,128)(2,1)S(1)} %collective-permute-done.14.refs_5_) | copy-start | bytes 3145732
  87.3 9.8 %copy-start.16 = (bf16[4,512,256]{2,1,0:T(8,128)(2,1)}, bf16[4,512,256]{2,1,0:T(8,128)(2,1)S(1)}, u32[]{:S(2)}) copy-start(bf16[4,512,256]{2,1,0:T(8,128)(2,1)S(1)} %collective-permute-done.15.refs_6_) | copy-start | bytes 3145732
  87.4 2.0 %copy-start.3 = (bf16[4,512,256]{2,1,0:T(8,128)(2,1)S(1)}, bf16[4,512,256]{2,1,0:T(8,128)(2,1)}, u32[]{:S(2)}) copy-start(bf16[4,512,256]{2,1,0:T(8,128)(2,1)} %get-tuple-element.49.refs_1_) | copy-start | bytes 3145732
  89.3 1.2 %copy-start.6 = (bf16[4,512,256]{2,1,0:T(8,128)(2,1)S(1)}, bf16[4,512,256]{2,1,0:T(8,128)(2,1)}, u32[]{:S(2)}) copy-start(bf16[4,512,256]{2,1,0:T(8,128)(2,1)} %get-tuple-element.50.refs_2_) | copy-start | bytes 3145732
  90.5 1.2 %copy-start.12 = (bf16[4,512,1,256]{3,1,2,0:T(8,128)(2,1)S(1)}, bf16[4,512,1,256]{3,1,2,0:T(8,128)(2,1)}, u32[]{:S(2)}) copy-start(bf16[4,512,1,256]{3,1,2,0:T(8,128)(2,1)} %param.17) | copy-start | bytes 3145732
  91.8 5.4 %copy-start.18 = (bf16[4,512,256]{2,1,0:T(8,128)(2,1)}, bf16[4,512,256]{2,1,0:T(8,128)(2,1)S(1)}, u32[]{:S(2)}) copy-start(bf16[4,512,256]{2,1,0:T(8,128)(2,1)S(1)} %collective-permute-done.16.refs_7_) | copy-start | bytes 3145732
  97.1 18.4 %collective-permute-start.18 = (bf16[33,32,128]{2,1,0:T(8,128)(2,1)}, bf16[33,32,128]{2,1,0:T(8,128)(2,1)}, u32[]{:S(2)}, u32[]{:S(2)}) collective-permute-start(bf16[33,32,128]{2,1,0:T(8,128)(2,1)} %attend_prefix.1), channel_id=1, source_target_pairs={{0,64},{8,72},{16,80},{24,88},{32,96},{40,104},{48,112},{56,120},{... | collective-permute-start | bytes 811016 | tf_op jit(solution)/shard_map/ppermute | solution.py:44
  99.8 1.6 %copy-start.9 = (bf16[64,1,64,1,256]{4,2,3,1,0:T(8,128)(2,1)S(1)}, bf16[64,1,64,1,256]{4,2,3,1,0:T(8,128)(2,1)}, u32[]{:S(2)}) copy-start(bf16[64,1,64,1,256]{4,2,3,1,0:T(8,128)(2,1)} %param.16) | copy-start | bytes 6291460
  102.6 1.2 %copy-start.15 = (bf16[4,512,256]{2,1,0:T(8,128)(2,1)S(1)}, bf16[4,512,256]{2,1,0:T(8,128)(2,1)}, u32[]{:S(2)}) copy-start(bf16[4,512,256]{2,1,0:T(8,128)(2,1)} %copy-done.14) | copy-start | bytes 3145732
  103.8 1.2 %copy-start.17 = (bf16[4,512,256]{2,1,0:T(8,128)(2,1)S(1)}, bf16[4,512,256]{2,1,0:T(8,128)(2,1)}, u32[]{:S(2)}) copy-start(bf16[4,512,256]{2,1,0:T(8,128)(2,1)} %copy-done.16) | copy-start | bytes 3145732
  105.0 1.2 %copy-start.19 = (bf16[4,512,256]{2,1,0:T(8,128)(2,1)S(1)}, bf16[4,512,256]{2,1,0:T(8,128)(2,1)}, u32[]{:S(2)}) copy-start(bf16[4,512,256]{2,1,0:T(8,128)(2,1)} %copy-done.18) | copy-start | bytes 3145732
  109.8 5.8 %copy-start.11 = (f32[33,32,128]{2,1,0:T(8,128)S(1)}, f32[33,32,128]{2,1,0:T(8,128)}, u32[]{:S(2)}) copy-start(f32[33,32,128]{2,1,0:T(8,128)} %copy-done.10) | copy-start | bytes 1622020
  109.8 5.8 %copy-start.34 = (bf16[32,4,256]{2,1,0:T(4,128)(2,1)S(1)}, bf16[32,4,256]{2,1,0:T(4,128)(2,1)}, u32[]{:S(2)}) copy-start(bf16[32,4,256]{2,1,0:T(4,128)(2,1)} %reshape.178.new_ref) | copy-start | bytes 196612
  (16 other events, 15.0 us)

commit v9 on v8

--- a/solution.py
+++ b/solution.py
@@ -20,7 +20,7 @@
 F32 = jnp.float32
 BF16 = jnp.bfloat16
 VMEM = 20 * 1024 * 1024
-VMEM_PROJECT = 50 * 1024 * 1024
+VMEM_PROJECT = 28 * 1024 * 1024
 
 
 def tp_shift(dy, dx):
@@ -59,6 +59,10 @@
 
 SMALL = cost(0.04)
 IN_SMEM = pl.BlockSpec(memory_space=pltpu.SMEM)
+
+
+def in_hbm(*arrays):
+    return [pltpu.with_memory_space_constraint(a, pltpu.HBM) for a in arrays]
 
 
 def project(heads, xs, wq, wp, groups, after=()):
@@ -111,7 +115,7 @@
         compiler_params=pltpu.CompilerParams(vmem_limit_bytes=VMEM_PROJECT),
         cost_estimate=SMALL,
         name="project",
-    )(heads, *xs, wq, wp, *after)
+    )(heads, *xs, *in_hbm(wq, wp), *after)
 
 
 def sort_rows(place, owner, tokens):
@@ -138,7 +142,7 @@
         compiler_params=pltpu.CompilerParams(vmem_limit_bytes=VMEM),
         cost_estimate=SMALL,
         name="sort_rows",
-    )(place, owner, tokens)
+    )(place, owner, *in_hbm(tokens))
 
 
 def add_far(right, left, up, down, after):
@@ -170,8 +174,9 @@
         kernel,
         in_specs=[ANY] * (count + 1),
         out_specs=[ANY] * count,
-        out_shape=[jax.ShapeDtypeStruct(a.shape, a.dtype) for a in arrays],
+        out_shape=[pltpu.HBM(a.shape, a.dtype) for a in arrays],
         input_output_aliases={i: i for i in range(count)},
+        compiler_params=pltpu.CompilerParams(vmem_limit_bytes=1024 * 1024),
         cost_estimate=SMALL,
         name="hold",
     )(*arrays, after)
@@ -293,7 +298,7 @@
         compiler_params=pltpu.CompilerParams(vmem_limit_bytes=VMEM),
         cost_estimate=SMALL,
         name="attend",
-    )(limits, lengths, order, keep, more, bias, cosine, sine, cache, *kvs)
+    )(limits, lengths, order, keep, more, bias, cosine, sine, *in_hbm(cache, *kvs))
 
 
 def make_queries(keep, more, bias, cosine, sine, after):
@@ -348,7 +353,7 @@
         compiler_params=pltpu.CompilerParams(vmem_limit_bytes=VMEM),
         cost_estimate=SMALL,
         name="attend_prefix",
-    )(limits, q, *kvs, after)
+    )(limits, q, *in_hbm(*kvs, after))
 
 
 def attend_near(lengths, order, q, new, cache, after):
@@ -383,12 +388,12 @@
         kernel,
         in_specs=[IN_SMEM] * 2 + [IN_VMEM] * 2 + [ANY] * 2,
         out_specs=IN_VMEM,
-        out_shape=jax.ShapeDtypeStruct((33, 32, HD), F32),
+        out_shape=pltpu.HBM((33, 32, HD), F32),
         scratch_shapes=buffers(keys) + [pltpu.SemaphoreType.DMA((32,))],
         compiler_params=pltpu.CompilerParams(vmem_limit_bytes=VMEM),
         cost_estimate=SMALL,
         name="attend_near",
-    )(lengths, order, q, new, cache, after)
+    )(lengths, order, q, new, *in_hbm(cache, after))
 
 
 def merge_rows(order, far, near, new, done):
@@ -418,7 +423,7 @@
         compiler_params=pltpu.CompilerParams(vmem_limit_bytes=VMEM),
         cost_estimate=SMALL,
         name="merge_rows",
-    )(order, far, near, new, done)
+    )(order, far, *in_hbm(near), new, done)
 
 
 def on_device(
@@ -494,9 +499,9 @@
     cache = cache_pairs.reshape(prompts, 64, 2 * HD)
 
     q_o, new_o = make_queries(*full_o, *tables, full_m[0])
-    near = attend_near(lengths, order, q_o, new_o, cache, full_m[1])
     gathered = hold((below, above, far), q_o)
     kvs = [own, *gathered, own_c] + [over_roll(a, 0, 0, 1) for a in gathered]
+    near = attend_near(lengths, order, q_o, new_o, cache, kvs[-1])
     far = over_roll(attend_prefix(my_limits, over_roll(q_o, 1, 0, 0), kvs, near), 1, 0, 0)
     done = attend(my_limits, lengths, order, *full_m, *tables, cache, kvs)
     attended, new_pairs = merge_rows(order, far, near, new_o.reshape(32, new, PW), done)

time: 119 us -> 96.6 us (0.81)
  local copies, waits for them, and re-layouts: 28.2 us -> 6.12 us
  waiting for transfers between devices: 23.6 us -> 21.3 us
  Pallas kernels: 40.1 us -> 42 us
    unnamed x90 -> x22, local copies, waits for them, and re-layouts: 23.8 us -> 3.03 us
    ppermute x10, waiting for transfers between devices: 22.2 us -> 19.9 us  [over_tp(): return lax.ppermute(a, 'tp', tp_shift(dy, dx))]
    ppermute x9, starting transfers between devices: 9.75 us -> 11.6 us  [over_roll(): return lax.ppermute(a, 'roll', roll_shift(dy, dz, dc))]
    ppermute x10, starting transfers between devices: 12.7 us -> 11.4 us  [over_tp(): return lax.ppermute(a, 'tp', tp_shift(dy, dx))]
    pallas_call x1, Pallas kernels: 5.73 us -> 6.97 us  [attend(): pl.pallas_call(kernel, in_specs=[IN_SMEM] * 3 + [IN_VMEM] * 5 + [ANY] * 9...]
  transfers between devices with their start and end apart: 19 -> 19, of which waited for: 7 -> 7; matrix products, arithmetic and copies ran while one was open for 6% -> 5% of each run, Pallas kernels for 28% -> 42%
where the time goes in v9:
time: 96.6 us; the launch traced here: 95.4 us
  Pallas kernels  42 us (43%)
  starting transfers between devices  23 us (24%)
  waiting for transfers between devices  21.3 us (22%)
  local copies, waits for them, and re-layouts  6.12 us (6%)
  other arithmetic  2.05 us (2%)
  between operations  1 us (1%)
    ppermute x10, waiting for transfers between devices, over_tp(): return lax.ppermute(a, 'tp', tp_shift(dy, dx))  19.9 us
    pallas_call x3, Pallas kernels, project(): pl.pallas_call(kernel, in_specs=[IN_SMEM] + [IN_VMEM] * len(xs) + [IN_HBM...  16.5 us
    ppermute x9, starting transfers between devices, over_roll(): return lax.ppermute(a, 'roll', roll_shift(dy, dz, dc))  11.6 us
    ppermute x10, starting transfers between devices, over_tp(): return lax.ppermute(a, 'tp', tp_shift(dy, dx))  11.4 us
    pallas_call x1, Pallas kernels, attend(): pl.pallas_call(kernel, in_specs=[IN_SMEM] * 3 + [IN_VMEM] * 5 + [ANY] * 9...  6.97 us
    pallas_call x1, Pallas kernels, attend_prefix(): pl.pallas_call(kernel, in_specs=[IN_SMEM, IN_VMEM] + [ANY] * 9, out_specs...  5.42 us
    pallas_call x1, Pallas kernels, attend_near(): pl.pallas_call(kernel, in_specs=[IN_SMEM] * 2 + [IN_VMEM] * 2 + [ANY] * 2...  4.25 us
    pallas_call x2, Pallas kernels, add_far(): pl.pallas_call(kernel, grid=(1,), in_specs=block + [block[0]] * 2 + [ANY]...  3.43 us
  transfers between devices with their start and end apart: 19, of which 7 were waited for; matrix products, arithmetic and copies ran while one was open for 5% of the time, Pallas kernels for 42%

profile of v9, /device:TPU:0, one launch (start us, length us, event | category | flops | bytes accessed | tf_op | source)
XLA Modules:
  0.0 95.4 jit_solution(3695199226755504170)
XLA Ops:
  0.6 0.1 collective-permute-start
  0.7 2.1 %collective-permute-start.11 = (bf16[4,512,256]{2,1,0:T(8,128)(2,1)}, bf16[4,512,256]{2,1,0:T(8,128)(2,1)}, u32[]{:S(2)}, u32[]{:S(2)}) collective-permute-start(bf16[4,512,256]{2,1,0:T(8,128)(2,1)} %bitcast.23), channel_id=1, source_target_pairs={{0,16},{8,24},{16,32},{24,40},{32,48},{40,56},{48,0},{56,8},{64,80... | collective-permute-start | bytes 3145736 | tf_op jit(solution)/shard_map/ppermute | solution.py:44
  2.8 2.2 %collective-permute-start.12 = (bf16[4,512,256]{2,1,0:T(8,128)(2,1)}, bf16[4,512,256]{2,1,0:T(8,128)(2,1)}, u32[]{:S(2)}, u32[]{:S(2)}) collective-permute-start(bf16[4,512,256]{2,1,0:T(8,128)(2,1)} %bitcast.24), channel_id=1, source_target_pairs={{0,48},{8,56},{16,0},{24,8},{32,16},{40,24},{48,32},{56,40},{64,11... | collective-permute-start | bytes 3145736 | tf_op jit(solution)/shard_map/ppermute | solution.py:44
  5.0 2.0 %reshape.175.x_ref = bf16[256,1024]{1,0:T(8,128)(2,1)} reshape(bf16[64,1,4,1024]{3,2,1,0:T(4,128)(2,1)} %param.11) | data formatting | bytes 1048576 | tf_op jit(solution)/shard_map/reshape | solution.py:455
  7.0 0.7 broadcast_in_dim.48
  7.7 0.1 reshape.174.owner_ref
  7.9 1.4 %sort_rows.1 = (bf16[128,1024]{1,0:T(8,128)(2,1)S(1)}, bf16[128,1024]{1,0:T(8,128)(2,1)S(1)}) custom-call(s32[3]{0:T(128)S(1)} %pad_add_fusion.1.place_ref, s32[1,256]{1,0:T(1,128)S(1)} %reshape.174.owner_ref, bf16[256,1024]{1,0:T(8,128)(2,1)} %reshape.175.x_ref), custom_call_target="tpu_custom_call" | custom-call | flops 1000000 | bytes 100000 | tf_op jit(solution)/shard_map/sort_rows/pallas_call | solution.py:137
  9.4 5.2 %project.4 = (bf16[1,128,1280]{2,1,0:T(8,128)(2,1)}, bf16[1,128,1280]{2,1,0:T(8,128)(2,1)}, bf16[1,128,1280]{2,1,0:T(8,128)(2,1)}, bf16[1,128,1280]{2,1,0:T(8,128)(2,1)}) custom-call(s32[2]{0:T(128)S(1)} %pad_add_fusion.3.heads_ref, bf16[128,1024]{1,0:T(8,128)(2,1)S(1)} %get-tuple-element.29.refs_0_, bf16[128,1024]{1,0:T(8,128)(2,1)S(1)} %get-tuple-element.30.refs_1_, ...), custom_call_target="tpu_custom_call" | custom-call | flops 1000000 | bytes 100000 | tf_op jit(solution)/shard_map/project/pallas_call | solution.py:104
  14.6 1.6 %collective-permute-start.1 = (bf16[1,128,1280]{2,1,0:T(8,128)(2,1)}, bf16[1,128,1280]{2,1,0:T(8,128)(2,1)}, u32[]{:S(2)}, u32[]{:S(2)}) collective-permute-start(bf16[1,128,1280]{2,1,0:T(8,128)(2,1)} %get-tuple-element.33), channel_id=1, source_target_pairs={{0,1},{1,2},{2,3},{3,0},{4,5},{5,6},{6,7},{7,4},{8,9},{9,10},{10,1... | collective-permute-start | bytes 983048 | tf_op jit(solution)/shard_map/ppermute | solution.py:40
  16.1 1.7 %collective-permute-start.2 = (bf16[1,128,1280]{2,1,0:T(8,128)(2,1)}, bf16[1,128,1280]{2,1,0:T(8,128)(2,1)}, u32[]{:S(2)}, u32[]{:S(2)}) collective-permute-start(bf16[1,128,1280]{2,1,0:T(8,128)(2,1)} %get-tuple-element.34), channel_id=1, source_target_pairs={{0,3},{1,0},{2,1},{3,2},{4,7},{5,4},{6,5},{7,6},{8,11},{9,8},{10,9... | collective-permute-start | bytes 983048 | tf_op jit(solution)/shard_map/ppermute | solution.py:40
  18.2 0.1 add.236
  18.4 0.3 collective-permute-start.5
  18.8 7.1 %project.3 = (bf16[2,128,1280]{2,1,0:T(8,128)(2,1)S(1)}, bf16[2,128,1280]{2,1,0:T(8,128)(2,1)S(1)}, bf16[2,128,1280]{2,1,0:T(8,128)(2,1)S(1)}, bf16[2,128,1280]{2,1,0:T(8,128)(2,1)}) custom-call(s32[4]{0:T(128)S(1)} %pad_add_fusion.2.heads_ref, bf16[128,1024]{1,0:T(8,128)(2,1)S(1)} %get-tuple-element.29.refs_0_, ...), custom_call_target="tpu_custom_call" | custom-call | flops 1000000 | bytes 100000 | tf_op jit(solution)/shard_map/project/pallas_call | solution.py:104
  25.9 0.9 collective-permute-done.1.u
  26.7 2.2 %collective-permute-start.6 = (bf16[1,128,1280]{2,1,0:T(8,128)(2,1)}, bf16[1,128,1280]{2,1,0:T(8,128)(2,1)S(1)}, u32[]{:S(2)}, u32[]{:S(2)}) collective-permute-start(bf16[1,128,1280]{2,1,0:T(8,128)(2,1)} %get-tuple-element.41), channel_id=1, source_target_pairs={{0,3},{1,0},{2,1},{3,2},{4,7},{5,4},{6,5},{7,6},{8,11},{9,8},{10,9... | collective-permute-start | bytes 983048 | tf_op jit(solution)/shard_map/ppermute | solution.py:40
  28.9 1.6 %add_far.2 = (bf16[2,128,1280]{2,1,0:T(8,128)(2,1)S(1)}, bf16[2,128,1280]{2,1,0:T(8,128)(2,1)S(1)}) custom-call(bf16[2,128,1280]{2,1,0:T(8,128)(2,1)S(1)} %get-tuple-element.31.r, bf16[2,128,1280]{2,1,0:T(8,128)(2,1)S(1)} %get-tuple-element.32.l, bf16[1,128,1280]{2,1,0:T(8,128)(2,1)} %collective-permute-done.1.u, ...), custom_call_target="tpu_custom_call", output_to_operand_aliasing={{0}: (0, {}), {1}: (1, {})} | custom-call | flops 1000000 | bytes 100000 | tf_op jit(solution)/shard_map/add_far/pallas_call | solution.py:155
  30.6 0.2 fusion.3
  30.9 0.5 fusion.8
  31.4 1.5 %collective-permute-done.5.u = bf16[1,128,1280]{2,1,0:T(8,128)(2,1)} collective-permute-done((bf16[1,128,1280]{2,1,0:T(8,128)(2,1)}, bf16[1,128,1280]{2,1,0:T(8,128)(2,1)}, u32[]{:S(2)}, u32[]{:S(2)}) %collective-permute-start.5) | collective-permute-done | bytes 327712 | tf_op jit(solution)/shard_map/ppermute | solution.py:40
  32.9 2.4 %collective-permute-start.4 = (bf16[2,128,1280]{2,1,0:T(8,128)(2,1)S(1)}, bf16[2,128,1280]{2,1,0:T(8,128)(2,1)}, u32[]{:S(2)}, u32[]{:S(2)}) collective-permute-start(bf16[2,128,1280]{2,1,0:T(8,128)(2,1)S(1)} %get-tuple-element.36.refs_5_), channel_id=1, source_target_pairs={{0,3},{1,0},{2,1},{3,2},{4,7},{5,4},{6,5},{7,6},{8,11},{9,8},{10,9... | collective-permute-start | bytes 1966088 | tf_op jit(solution)/shard_map/ppermute | solution.py:40
  35.4 0.1 convert_element_type.22
  35.5 1.7 %collective-permute-done.6.d = bf16[1,128,1280]{2,1,0:T(8,128)(2,1)S(1)} collective-permute-done((bf16[1,128,1280]{2,1,0:T(8,128)(2,1)}, bf16[1,128,1280]{2,1,0:T(8,128)(2,1)S(1)}, u32[]{:S(2)}, u32[]{:S(2)}) %collective-permute-start.6) | collective-permute-done | bytes 327712 | tf_op jit(solution)/shard_map/ppermute | solution.py:40
  37.2 1.9 %add_far.3 = (bf16[2,128,1280]{2,1,0:T(8,128)(2,1)S(1)}, bf16[2,128,1280]{2,1,0:T(8,128)(2,1)}) custom-call(bf16[2,128,1280]{2,1,0:T(8,128)(2,1)S(1)} %get-tuple-element.38.r, bf16[2,128,1280]{2,1,0:T(8,128)(2,1)} %get-tuple-element.39.l, bf16[1,128,1280]{2,1,0:T(8,128)(2,1)} %collective-permute-done.5.u, ...), custom_call_target="tpu_custom_call", output_to_operand_aliasing={{0}: (0, {}), {1}: (1, {})} | custom-call | flops 1000000 | bytes 100000 | tf_op jit(solution)/shard_map/add_far/pallas_call | solution.py:155
  39.1 0.7 collective-permute-start.8
  39.8 9.6 %collective-permute-done.3.b = bf16[2,128,1280]{2,1,0:T(8,128)(2,1)S(1)} collective-permute-done((bf16[2,128,1280]{2,1,0:T(8,128)(2,1)S(1)}, bf16[2,128,1280]{2,1,0:T(8,128)(2,1)S(1)}, u32[]{:S(2)}, u32[]{:S(2)}) %collective-permute-start.3) | collective-permute-done | bytes 655392 | tf_op jit(solution)/shard_map/ppermute | solution.py:40
  49.5 0.5 fusion
  50.0 4.2 %project.5 = (bf16[2,128,1280]{2,1,0:T(8,128)(2,1)S(1)}, bf16[2,128,1280]{2,1,0:T(8,128)(2,1)S(1)}) custom-call(s32[2]{0:T(128)S(1)} %pad_add_fusion.heads_ref, bf16[128,1024]{1,0:T(8,128)(2,1)S(1)} %get-tuple-element.29.refs_0_, bf16[128,1024]{1,0:T(8,128)(2,1)S(1)} %get-tuple-element.30.refs_1_, bf16[1024,8192]{1,0:T(8,128)(2,1)} %refs_2_.5, ...), custom_call_target="tpu_custom_call" | custom-call | flops 1000000 | bytes 100000 | tf_op jit(solution)/shard_map/project/pallas_call | solution.py:104
  54.3 1.3 %sum_x.2 = (f32[128,1280]{1,0:T(8,128)S(1)}, bf16[128,1280]{1,0:T(8,128)(2,1)S(1)}) custom-call(bf16[2,128,1280]{2,1,0:T(8,128)(2,1)S(1)} %get-tuple-element.37.a, bf16[2,128,1280]{2,1,0:T(8,128)(2,1)S(1)} %collective-permute-done.3.b, bf16[2,128,1280]{2,1,0:T(8,128)(2,1)} %collective-permute-done.4.c, bf16[2,128,1280]{2,1,0:T(8,128)(2,1)S(1)} %get-tuple-element.42.after_ref), custom_call_target="tpu_custom_call" | custom-call | flops 1000000 | bytes 100000 | tf_op jit(solution)/shard_map/sum_x/pallas_call | solution.py:196
  55.6 1.7 %collective-permute-start.7 = (bf16[128,1280]{1,0:T(8,128)(2,1)S(1)}, bf16[128,1280]{1,0:T(8,128)(2,1)S(1)}, u32[]{:S(2)}, u32[]{:S(2)}) collective-permute-start(bf16[128,1280]{1,0:T(8,128)(2,1)S(1)} %get-tuple-element.44), channel_id=1, source_target_pairs={{0,4},{1,5},{2,6},{3,7},{4,0},{5,1},{6,2},{7,3},{8,12},{9,13},{10,... | collective-permute-start | bytes 983048 | tf_op jit(solution)/shard_map/ppermute | solution.py:40
  57.3 0.1 pad_maximum_fusion
  57.4 3.9 %collective-permute-done.8.b = bf16[2,128,1280]{2,1,0:T(8,128)(2,1)S(1)} collective-permute-done((bf16[2,128,1280]{2,1,0:T(8,128)(2,1)S(1)}, bf16[2,128,1280]{2,1,0:T(8,128)(2,1)S(1)}, u32[]{:S(2)}, u32[]{:S(2)}) %collective-permute-start.8) | collective-permute-done | bytes 655392 | tf_op jit(solution)/shard_map/ppermute | solution.py:40
  61.4 2.3 %collective-permute-done.9.c = bf16[2,128,1280]{2,1,0:T(8,128)(2,1)S(1)} collective-permute-done((bf16[2,128,1280]{2,1,0:T(8,128)(2,1)}, bf16[2,128,1280]{2,1,0:T(8,128)(2,1)S(1)}, u32[]{:S(2)}, u32[]{:S(2)}) %collective-permute-start.9) | collective-permute-done | bytes 655392 | tf_op jit(solution)/shard_map/ppermute | solution.py:40
  63.7 0.2 sum_x.3
  63.9 0.3 make_queries.1
  64.2 0.1 collective-permute-start.16
  64.3 0.5 collective-permute-start.14
  64.8 0.1 collective-permute-start.15
  64.9 3.2 %collective-permute-start.10 = (bf16[32,32,128]{2,1,0:T(8,128)(2,1)S(1)}, bf16[32,32,128]{2,1,0:T(8,128)(2,1)S(1)}, u32[]{:S(2)}, u32[]{:S(2)}) collective-permute-start(bf16[32,32,128]{2,1,0:T(8,128)(2,1)S(1)} %get-tuple-element.48.refs_3_.q_ref), channel_id=1, source_target_pairs={{0,64},{8,72},{16,80},{24,88},{32,96},{40,104},{48,112},{56,120},{... | collective-permute-start | bytes 786440 | tf_op jit(solution)/shard_map/ppermute | solution.py:44
  68.1 0.7 collective-permute-start.18
  68.8 1.0 %copy-done.1 = bf16[4,512,256]{2,1,0:T(8,128)(2,1)} copy-done((bf16[4,512,256]{2,1,0:T(8,128)(2,1)}, bf16[4,512,256]{2,1,0:T(8,128)(2,1)S(1)}, u32[]{:S(2)}) %copy-start.1) | copy-done | bytes 1048600
  69.9 4.3 %attend_near.1.refs_8_.near_ref = f32[33,32,128]{2,1,0:T(8,128)} custom-call(s32[64]{0:T(128)S(1)} %get-tuple-element.62.length_ref, s32[64]{0:T(128)S(1)} %get-tuple-element.64.at_ref.order_ref, bf16[32,32,128]{2,1,0:T(8,128)(2,1)S(1)} %get-tuple-element.48.refs_3_.q_ref, bf16[128,256]{1,0:T(8,128)(2,1)S(1)} %get-tuple-element.52.new_ref, ...), custom_call_target="tpu_custom_call" | custom-call | flops 1000000 | bytes 100000 | tf_op jit(solution)/shard_map/attend_near/pallas_call | solution.py:387
  74.1 1.4 %collective-permute-done.10.q_ref = bf16[32,32,128]{2,1,0:T(8,128)(2,1)S(1)} collective-permute-done((bf16[32,32,128]{2,1,0:T(8,128)(2,1)S(1)}, bf16[32,32,128]{2,1,0:T(8,128)(2,1)S(1)}, u32[]{:S(2)}, u32[]{:S(2)}) %collective-permute-start.10) | collective-permute-done | bytes 262176 | tf_op jit(solution)/shard_map/ppermute | solution.py:44
  75.5 1.0 %copy-done.2 = bf16[4,512,256]{2,1,0:T(8,128)(2,1)} copy-done((bf16[4,512,256]{2,1,0:T(8,128)(2,1)}, bf16[4,512,256]{2,1,0:T(8,128)(2,1)S(1)}, u32[]{:S(2)}) %copy-start.2) | copy-done | bytes 1048600
  76.5 1.0 %copy-done.3 = bf16[4,512,256]{2,1,0:T(8,128)(2,1)} copy-done((bf16[4,512,256]{2,1,0:T(8,128)(2,1)}, bf16[4,512,256]{2,1,0:T(8,128)(2,1)S(1)}, u32[]{:S(2)}) %copy-start.3) | copy-done | bytes 1048600
  77.5 5.4 %attend_prefix.1 = bf16[33,32,128]{2,1,0:T(8,128)(2,1)S(1)} custom-call(s32[32]{0:T(128)S(1)} %slice.3.limit_ref, bf16[32,32,128]{2,1,0:T(8,128)(2,1)S(1)} %collective-permute-done.10.q_ref, bf16[4,512,256]{2,1,0:T(8,128)(2,1)} %bitcast.25, bf16[4,512,256]{2,1,0:T(8,128)(2,1)} %get-tuple-element.49.refs_1_, bf16[4,512,256]{2,1,0:T(8,128)(2,1)} %get-tuple-element.50.refs_2_, ...), custom_call_target="tpu_custom_call" | custom-call | flops 1000000 | bytes 100000 | tf_op jit(solution)/shard_map/attend_prefix/pallas_call | solution.py:347
  82.9 3.3 %collective-permute-start.17 = (bf16[33,32,128]{2,1,0:T(8,128)(2,1)S(1)}, bf16[33,32,128]{2,1,0:T(8,128)(2,1)S(1)}, u32[]{:S(2)}, u32[]{:S(2)}) collective-permute-start(bf16[33,32,128]{2,1,0:T(8,128)(2,1)S(1)} %attend_prefix.1), channel_id=1, source_target_pairs={{0,64},{8,72},{16,80},{24,88},{32,96},{40,104},{48,112},{56,120},{... | collective-permute-start | bytes 811016 | tf_op jit(solution)/shard_map/ppermute | solution.py:44
  86.2 7.0 %attend.1.done_ref = bf16[32,4,1280]{2,1,0:T(4,128)(2,1)S(1)} custom-call(s32[32]{0:T(128)S(1)} %slice.3.limit_ref, s32[64]{0:T(128)S(1)} %get-tuple-element.62.length_ref, s32[64]{0:T(128)S(1)} %get-tuple-element.64.at_ref.order_ref, f32[128,1280]{1,0:T(8,128)S(1)} %get-tuple-element.47.after_ref.keep_ref, ...), custom_call_target="tpu_custom_call" | custom-call | flops 1000000 | bytes 100000 | tf_op jit(solution)/shard_map/attend/pallas_call | solution.py:291
  93.2 2.2 %merge_rows.1 = (bf16[64,4,1024]{2,1,0:T(4,128)(2,1)}, bf16[64,4,256]{2,1,0:T(4,128)(2,1)}) custom-call(s32[64]{0:T(128)S(1)} %get-tuple-element.64.at_ref.order_ref, bf16[33,32,128]{2,1,0:T(8,128)(2,1)S(1)} %collective-permute-done.17.far_ref, f32[33,32,128]{2,1,0:T(8,128)} %attend_near.1.refs_8_.near_ref, bf16[32,4,256]{2,1,0:T(4,128)(2,1)S(1)} %reshape.178.new_ref, ...), custom_call_target="tpu_custom_call" | custom-call | flops 1000000 | bytes 100000 | tf_op jit(solution)/shard_map/merge_rows/pallas_call | solution.py:418
  (52 shorter events, 1.0 us)
Async XLA Ops:
  0.6 17.7 %collective-permute-start = (bf16[4,512,256]{2,1,0:T(8,128)(2,1)}, bf16[4,512,256]{2,1,0:T(8,128)(2,1)S(1)}, u32[]{:S(2)}, u32[]{:S(2)}) collective-permute-start(bf16[4,512,256]{2,1,0:T(8,128)(2,1)} %bitcast.22), channel_id=1, source_target_pairs={{0,8},{8,0},{16,24},{24,16},{32,40},{40,32},{48,56},{56,48},{64,72... | collective-permute-start | bytes 3145736 | tf_op jit(solution)/shard_map/ppermute | solution.py:44
  0.7 30.1 %collective-permute-start.11 = (bf16[4,512,256]{2,1,0:T(8,128)(2,1)}, bf16[4,512,256]{2,1,0:T(8,128)(2,1)}, u32[]{:S(2)}, u32[]{:S(2)}) collective-permute-start(bf16[4,512,256]{2,1,0:T(8,128)(2,1)} %bitcast.23), channel_id=1, source_target_pairs={{0,16},{8,24},{16,32},{24,40},{32,48},{40,56},{48,0},{56,8},{64,80... | collective-permute-start | bytes 3145736 | tf_op jit(solution)/shard_map/ppermute | solution.py:44
  2.8 61.4 %collective-permute-start.12 = (bf16[4,512,256]{2,1,0:T(8,128)(2,1)}, bf16[4,512,256]{2,1,0:T(8,128)(2,1)}, u32[]{:S(2)}, u32[]{:S(2)}) collective-permute-start(bf16[4,512,256]{2,1,0:T(8,128)(2,1)} %bitcast.24), channel_id=1, source_target_pairs={{0,48},{8,56},{16,0},{24,8},{32,16},{40,24},{48,32},{56,40},{64,11... | collective-permute-start | bytes 3145736 | tf_op jit(solution)/shard_map/ppermute | solution.py:44
  9.4 8.5 %copy-start.10 = (s32[4]{0:T(128)S(1)}, s32[4]{0:T(128)}, u32[]{:S(2)}) copy-start(s32[4]{0:T(128)} %constant.143.clone) | copy-start | bytes 52
  14.6 12.2 %collective-permute-start.1 = (bf16[1,128,1280]{2,1,0:T(8,128)(2,1)}, bf16[1,128,1280]{2,1,0:T(8,128)(2,1)}, u32[]{:S(2)}, u32[]{:S(2)}) collective-permute-start(bf16[1,128,1280]{2,1,0:T(8,128)(2,1)} %get-tuple-element.33), channel_id=1, source_target_pairs={{0,1},{1,2},{2,3},{3,0},{4,5},{5,6},{6,7},{7,4},{8,9},{9,10},{10,1... | collective-permute-start | bytes 983048 | tf_op jit(solution)/shard_map/ppermute | solution.py:40
  16.1 12.8 %collective-permute-start.2 = (bf16[1,128,1280]{2,1,0:T(8,128)(2,1)}, bf16[1,128,1280]{2,1,0:T(8,128)(2,1)}, u32[]{:S(2)}, u32[]{:S(2)}) collective-permute-start(bf16[1,128,1280]{2,1,0:T(8,128)(2,1)} %get-tuple-element.34), channel_id=1, source_target_pairs={{0,3},{1,0},{2,1},{3,2},{4,7},{5,4},{6,5},{7,6},{8,11},{9,8},{10,9... | collective-permute-start | bytes 983048 | tf_op jit(solution)/shard_map/ppermute | solution.py:40
  18.4 7.5 %copy-start = (bf16[4,512,256]{2,1,0:T(8,128)(2,1)}, bf16[4,512,256]{2,1,0:T(8,128)(2,1)S(1)}, u32[]{:S(2)}) copy-start(bf16[4,512,256]{2,1,0:T(8,128)(2,1)S(1)} %collective-permute-done.refs_4_) | copy-start | bytes 3145732
  18.4 12.2 %copy-start.4 = (s32[64]{0:T(128)S(1)}, s32[64]{0:T(128)}, u32[]{:S(2)}) copy-start(s32[64]{0:T(128)} %param.18) | copy-start | bytes 772
  18.4 12.2 %copy-start.6 = (s32[64,1]{0,1:T(1,128)S(1)}, s32[64,1]{0,1:T(1,128)}, u32[]{:S(2)}) copy-start(s32[64,1]{0,1:T(1,128)} %param.20) | copy-start | bytes 772
  18.4 12.2 %copy-start.7 = (s32[64]{0:T(128)S(1)}, s32[64]{0:T(128)}, u32[]{:S(2)}) copy-start(s32[64]{0:T(128)} %param.19) | copy-start | bytes 772
  18.4 17.1 %copy-start.5 = (bf16[1024]{0:T(1024)(128)(2,1)S(1)}, bf16[1024]{0:T(1024)(128)(2,1)}, u32[]{:S(2)}) copy-start(bf16[1024]{0:T(1024)(128)(2,1)} %param.13) | copy-start | bytes 6148
  18.4 17.1 %copy-start.9 = (bf16[256]{0:T(256)(128)(2,1)S(1)}, bf16[256]{0:T(256)(128)(2,1)}, u32[]{:S(2)}) copy-start(bf16[256]{0:T(256)(128)(2,1)} %param.15) | copy-start | bytes 1540
  18.4 14.5 %collective-permute-start.5 = (bf16[1,128,1280]{2,1,0:T(8,128)(2,1)}, bf16[1,128,1280]{2,1,0:T(8,128)(2,1)}, u32[]{:S(2)}, u32[]{:S(2)}) collective-permute-start(bf16[1,128,1280]{2,1,0:T(8,128)(2,1)} %get-tuple-element.40), channel_id=1, source_target_pairs={{0,1},{1,2},{2,3},{3,0},{4,5},{5,6},{6,7},{7,4},{8,9},{9,10},{10,1... | collective-permute-start | bytes 983048 | tf_op jit(solution)/shard_map/ppermute | solution.py:40
  26.7 10.5 %collective-permute-start.6 = (bf16[1,128,1280]{2,1,0:T(8,128)(2,1)}, bf16[1,128,1280]{2,1,0:T(8,128)(2,1)S(1)}, u32[]{:S(2)}, u32[]{:S(2)}) collective-permute-start(bf16[1,128,1280]{2,1,0:T(8,128)(2,1)} %get-tuple-element.41), channel_id=1, source_target_pairs={{0,3},{1,0},{2,1},{3,2},{4,7},{5,4},{6,5},{7,6},{8,11},{9,8},{10,9... | collective-permute-start | bytes 983048 | tf_op jit(solution)/shard_map/ppermute | solution.py:40
  30.5 18.9 %collective-permute-start.3 = (bf16[2,128,1280]{2,1,0:T(8,128)(2,1)S(1)}, bf16[2,128,1280]{2,1,0:T(8,128)(2,1)S(1)}, u32[]{:S(2)}, u32[]{:S(2)}) collective-permute-start(bf16[2,128,1280]{2,1,0:T(8,128)(2,1)S(1)} %get-tuple-element.35.refs_4_.refs_0_), channel_id=1, source_target_pairs={{0,1},{1,2},{2,3},{3,0},{4,5},{5,6},{6,7},{7,4},{8,9},{9,10},{10,1... | collective-permute-start | bytes 1966088 | tf_op jit(solution)/shard_map/ppermute | solution.py:40
  30.8 33.4 %collective-permute-start.13 = (bf16[4,512,256]{2,1,0:T(8,128)(2,1)}, bf16[4,512,256]{2,1,0:T(8,128)(2,1)}, u32[]{:S(2)}, u32[]{:S(2)}) collective-permute-start(bf16[4,512,256]{2,1,0:T(8,128)(2,1)} %collective-permute-done.11.refs_0_), channel_id=1, source_target_pairs={{0,16},{8,24},{16,32},{24,40},{32,48},{40,56},{48,0},{56,8},{64,80... | collective-permute-start | bytes 3145736 | tf_op jit(solution)/shard_map/ppermute | solution.py:44
  32.9 21.4 %collective-permute-start.4 = (bf16[2,128,1280]{2,1,0:T(8,128)(2,1)S(1)}, bf16[2,128,1280]{2,1,0:T(8,128)(2,1)}, u32[]{:S(2)}, u32[]{:S(2)}) collective-permute-start(bf16[2,128,1280]{2,1,0:T(8,128)(2,1)S(1)} %get-tuple-element.36.refs_5_), channel_id=1, source_target_pairs={{0,3},{1,0},{2,1},{3,2},{4,7},{5,4},{6,5},{7,6},{8,11},{9,8},{10,9... | collective-permute-start | bytes 1966088 | tf_op jit(solution)/shard_map/ppermute | solution.py:40
  39.1 22.3 %collective-permute-start.8 = (bf16[2,128,1280]{2,1,0:T(8,128)(2,1)S(1)}, bf16[2,128,1280]{2,1,0:T(8,128)(2,1)S(1)}, u32[]{:S(2)}, u32[]{:S(2)}) collective-permute-start(bf16[2,128,1280]{2,1,0:T(8,128)(2,1)S(1)} %get-tuple-element.42.after_ref), channel_id=1, source_target_pairs={{0,1},{1,2},{2,3},{3,0},{4,5},{5,6},{6,7},{7,4},{8,9},{9,10},{10,1... | collective-permute-start | bytes 1966088 | tf_op jit(solution)/shard_map/ppermute | solution.py:40
  49.4 14.2 %collective-permute-start.9 = (bf16[2,128,1280]{2,1,0:T(8,128)(2,1)}, bf16[2,128,1280]{2,1,0:T(8,128)(2,1)S(1)}, u32[]{:S(2)}, u32[]{:S(2)}) collective-permute-start(bf16[2,128,1280]{2,1,0:T(8,128)(2,1)} %get-tuple-element.46), channel_id=1, source_target_pairs={{0,3},{1,0},{2,1},{3,2},{4,7},{5,4},{6,5},{7,6},{8,11},{9,8},{10,9... | collective-permute-start | bytes 1966088 | tf_op jit(solution)/shard_map/ppermute | solution.py:40
  55.6 8.3 %collective-permute-start.7 = (bf16[128,1280]{1,0:T(8,128)(2,1)S(1)}, bf16[128,1280]{1,0:T(8,128)(2,1)S(1)}, u32[]{:S(2)}, u32[]{:S(2)}) collective-permute-start(bf16[128,1280]{1,0:T(8,128)(2,1)S(1)} %get-tuple-element.44), channel_id=1, source_target_pairs={{0,4},{1,5},{2,6},{3,7},{4,0},{5,1},{6,2},{7,3},{8,12},{9,13},{10,... | collective-permute-start | bytes 983048 | tf_op jit(solution)/shard_map/ppermute | solution.py:40
  57.3 11.5 %copy-start.8 = (s32[64]{0:T(128)S(1)}, s32[64]{0:T(128)}, u32[]{:S(2)}) copy-start(s32[64]{0:T(128)} %get-tuple-element.69) | copy-start | bytes 772
  64.2 4.6 %collective-permute-start.16 = (bf16[4,512,256]{2,1,0:T(8,128)(2,1)}, bf16[4,512,256]{2,1,0:T(8,128)(2,1)S(1)}, u32[]{:S(2)}, u32[]{:S(2)}) collective-permute-start(bf16[4,512,256]{2,1,0:T(8,128)(2,1)} %get-tuple-element.51.refs_3_), channel_id=1, source_target_pairs={{0,8},{8,0},{16,24},{24,16},{32,40},{40,32},{48,56},{56,48},{64,72... | collective-permute-start | bytes 3145736 | tf_op jit(solution)/shard_map/ppermute | solution.py:44
  64.3 11.2 %collective-permute-start.14 = (bf16[4,512,256]{2,1,0:T(8,128)(2,1)}, bf16[4,512,256]{2,1,0:T(8,128)(2,1)S(1)}, u32[]{:S(2)}, u32[]{:S(2)}) collective-permute-start(bf16[4,512,256]{2,1,0:T(8,128)(2,1)} %get-tuple-element.49.refs_1_), channel_id=1, source_target_pairs={{0,8},{8,0},{16,24},{24,16},{32,40},{40,32},{48,56},{56,48},{64,72... | collective-permute-start | bytes 3145736 | tf_op jit(solution)/shard_map/ppermute | solution.py:44
  64.8 10.7 %collective-permute-start.15 = (bf16[4,512,256]{2,1,0:T(8,128)(2,1)}, bf16[4,512,256]{2,1,0:T(8,128)(2,1)S(1)}, u32[]{:S(2)}, u32[]{:S(2)}) collective-permute-start(bf16[4,512,256]{2,1,0:T(8,128)(2,1)} %get-tuple-element.50.refs_2_), channel_id=1, source_target_pairs={{0,8},{8,0},{16,24},{24,16},{32,40},{40,32},{48,56},{56,48},{64,72... | collective-permute-start | bytes 3145736 | tf_op jit(solution)/shard_map/ppermute | solution.py:44
  64.9 10.6 %collective-permute-start.10 = (bf16[32,32,128]{2,1,0:T(8,128)(2,1)S(1)}, bf16[32,32,128]{2,1,0:T(8,128)(2,1)S(1)}, u32[]{:S(2)}, u32[]{:S(2)}) collective-permute-start(bf16[32,32,128]{2,1,0:T(8,128)(2,1)S(1)} %get-tuple-element.48.refs_3_.q_ref), channel_id=1, source_target_pairs={{0,64},{8,72},{16,80},{24,88},{32,96},{40,104},{48,112},{56,120},{... | collective-permute-start | bytes 786440 | tf_op jit(solution)/shard_map/ppermute | solution.py:44
  68.1 18.1 %collective-permute-start.18 = (bf16[128,1280]{1,0:T(8,128)(2,1)S(1)}, bf16[128,1280]{1,0:T(8,128)(2,1)S(1)}, u32[]{:S(2)}, u32[]{:S(2)}) collective-permute-start(bf16[128,1280]{1,0:T(8,128)(2,1)S(1)} %get-tuple-element.53), channel_id=1, source_target_pairs={{0,4},{1,5},{2,6},{3,7},{4,0},{5,1},{6,2},{7,3},{8,12},{9,13},{10,... | collective-permute-start | bytes 983048 | tf_op jit(solution)/shard_map/ppermute | solution.py:40
  68.8 1.0 %copy-start.1 = (bf16[4,512,256]{2,1,0:T(8,128)(2,1)}, bf16[4,512,256]{2,1,0:T(8,128)(2,1)S(1)}, u32[]{:S(2)}) copy-start(bf16[4,512,256]{2,1,0:T(8,128)(2,1)S(1)} %collective-permute-done.16.after_ref.refs_7_) | copy-start | bytes 3145732
  75.5 1.0 %copy-start.2 = (bf16[4,512,256]{2,1,0:T(8,128)(2,1)}, bf16[4,512,256]{2,1,0:T(8,128)(2,1)S(1)}, u32[]{:S(2)}) copy-start(bf16[4,512,256]{2,1,0:T(8,128)(2,1)S(1)} %collective-permute-done.14.refs_5_) | copy-start | bytes 3145732
  76.5 1.0 %copy-start.3 = (bf16[4,512,256]{2,1,0:T(8,128)(2,1)}, bf16[4,512,256]{2,1,0:T(8,128)(2,1)S(1)}, u32[]{:S(2)}) copy-start(bf16[4,512,256]{2,1,0:T(8,128)(2,1)S(1)} %collective-permute-done.15.refs_6_) | copy-start | bytes 3145732
  82.9 10.3 %collective-permute-start.17 = (bf16[33,32,128]{2,1,0:T(8,128)(2,1)S(1)}, bf16[33,32,128]{2,1,0:T(8,128)(2,1)S(1)}, u32[]{:S(2)}, u32[]{:S(2)}) collective-permute-start(bf16[33,32,128]{2,1,0:T(8,128)(2,1)S(1)} %attend_prefix.1), channel_id=1, source_target_pairs={{0,64},{8,72},{16,80},{24,88},{32,96},{40,104},{48,112},{56,120},{... | collective-permute-start | bytes 811016 | tf_op jit(solution)/shard_map/ppermute | solution.py:44

commit v10 on v9

--- a/solution.py
+++ b/solution.py
@@ -19,8 +19,8 @@
 LOG2_SCALE = HD ** -0.5 / math.log(2.0)
 F32 = jnp.float32
 BF16 = jnp.bfloat16
-VMEM = 20 * 1024 * 1024
-VMEM_PROJECT = 28 * 1024 * 1024
+VMEM = 18 * 1024 * 1024
+VMEM_PROJECT = 18 * 1024 * 1024
 
 
 def tp_shift(dy, dx):
@@ -118,12 +118,29 @@
     )(heads, *xs, *in_hbm(wq, wp), *after)
 
 
-def sort_rows(place, owner, tokens):
-    rows, width = tokens.shape
-
-    def kernel(place_ref, owner_ref, x_ref, *outs):
-        x = x_ref[...]
-        for b, out in enumerate(outs):
+def project_far(heads, place, owner, tokens, wq, wp):
+    rows, depth = tokens.shape
+
+    def kernel(heads_ref, place_ref, owner_ref, t_ref, wq_ref, wp_ref, *refs):
+        xs, outs, (q_buf, p_buf, q_sem, p_sem) = refs[:2], refs[2:6], refs[6:]
+        copies = []
+        for d in range(2):
+            k = heads_ref[d]
+            copies.append(
+                (
+                    pltpu.make_async_copy(
+                        wq_ref.at[:, pl.ds(pl.multiple_of(k * QW, QW), QW)], q_buf.at[d], q_sem.at[d]
+                    ),
+                    pltpu.make_async_copy(
+                        wp_ref.at[:, pl.ds(pl.multiple_of(k * PW, PW), PW)], p_buf.at[d], p_sem.at[d]
+                    ),
+                )
+            )
+        for pair in copies:
+            for c in pair:
+                c.start()
+        t = t_ref[...]
+        for b, out in enumerate(xs):
             row = lax.broadcasted_iota(jnp.int32, (ROWS, rows), 0)
             col = lax.broadcasted_iota(jnp.int32, (ROWS, rows), 1)
             i = row // 4
@@ -132,17 +149,32 @@
             z = (jnp.where(step == 1, 3, jnp.where(step == 0, 0, step - 1)) + place_ref[1]) % 4
             slot = ((y * 4 + z) * 2 + c) * 4 + j
             hit = (owner_ref[...] == slot) & (col % 4 == row % 4)
-            out[...] = dot(jnp.where(hit, 1.0, 0.0).astype(BF16), x).astype(BF16)
-
-    return pl.pallas_call(
-        kernel,
-        in_specs=[IN_SMEM, IN_VMEM, IN_VMEM],
-        out_specs=[IN_VMEM] * 2,
-        out_shape=[jax.ShapeDtypeStruct((ROWS, width), BF16)] * 2,
-        compiler_params=pltpu.CompilerParams(vmem_limit_bytes=VMEM),
-        cost_estimate=SMALL,
-        name="sort_rows",
-    )(place, owner, *in_hbm(tokens))
+            out[...] = dot(jnp.where(hit, 1.0, 0.0).astype(BF16), t).astype(BF16)
+        x = jnp.concatenate([r[...] for r in xs], 0)
+        for d in range(2):
+            for c in copies[d]:
+                c.wait()
+            for buf, low, high in ((q_buf, 0, QW), (p_buf, QW, COLS)):
+                y = dot(x, buf[d]).astype(BF16)
+                for b in range(2):
+                    outs[2 * b + d][0, :, low:high] = y[b * ROWS : (b + 1) * ROWS]
+
+    return pl.pallas_call(
+        kernel,
+        in_specs=[IN_SMEM, IN_SMEM, IN_VMEM, IN_VMEM, IN_HBM, IN_HBM],
+        out_specs=[IN_VMEM] * 6,
+        out_shape=[jax.ShapeDtypeStruct((ROWS, depth), BF16)] * 2
+        + [jax.ShapeDtypeStruct((1, ROWS, COLS), BF16)] * 4,
+        scratch_shapes=[
+            pltpu.VMEM((2, depth, QW), BF16),
+            pltpu.VMEM((2, depth, PW), BF16),
+            pltpu.SemaphoreType.DMA((2,)),
+            pltpu.SemaphoreType.DMA((2,)),
+        ],
+        compiler_params=pltpu.CompilerParams(vmem_limit_bytes=VMEM_PROJECT),
+        cost_estimate=SMALL,
+        name="project_far",
+    )(heads, place, owner, *in_hbm(tokens, wq, wp))
 
 
 def add_far(right, left, up, down, after):
@@ -449,23 +481,23 @@
     below, above, own_c = over_roll(own, 0, 1, 0), over_roll(own, 0, 3, 0), over_roll(own, 0, 0, 1)
     far = over_roll(below, 0, 1, 0)
 
-    x_o, x_m = sort_rows(
+    def heads(*pairs):
+        return jnp.stack([(tp_y + dy) % 2 * 4 + (tp_x + dx) % 4 for dy, dx in pairs]).astype(jnp.int32)
+
+    weights = (query_weight, pair_weight)
+    x_o, x_m, up_o, down_o, up_m, down_m = project_far(
+        heads((0, 2), (1, 2)),
         jnp.stack([my_y, my_z, my_c]).astype(jnp.int32),
         jnp.broadcast_to(owner_slot[:, None], (prompts, new)).reshape(1, prompts * new),
         tokens.reshape(prompts * new, width),
+        *weights,
     )
-
-    def heads(*pairs):
-        return jnp.stack([(tp_y + dy) % 2 * 4 + (tp_x + dx) % 4 for dy, dx in pairs]).astype(jnp.int32)
-
-    weights = (query_weight, pair_weight)
-    up_o, down_o, up_m, down_m = project(heads((0, 2), (1, 2)), [x_o, x_m], *weights, [[0], [1]])
     right_o, left_o, right_m, left_m = project(
         heads((0, 1), (1, 1), (0, 3), (1, 3)), [x_o, x_m], *weights, [[0, 1], [2, 3]], after=(own_c,)
     )
     right_o, left_o = add_far(right_o, left_o, over_tp(up_o, 0, 1), over_tp(down_o, 0, 3), ())
-    right_m, left_m = add_far(right_m, left_m, over_tp(up_m, 0, 1), over_tp(down_m, 0, 3), (right_o,))
     own_o, own_m = project(heads((0, 0), (1, 0)), [x_o, x_m], *weights, [[0, 1]], after=(right_o, left_o))
+    right_m, left_m = add_far(right_m, left_m, over_tp(up_m, 0, 1), over_tp(down_m, 0, 3), (right_o, own_m))
 
     def reduce(right, left, own_part, after):
         keep, send = sum_x(own_part, over_tp(right, 0, 1), over_tp(left, 0, 3), after)

time: 96.6 us -> 95.6 us (0.990)
  waiting for transfers between devices: 21.3 us -> 23 us
  Pallas kernels: 42 us -> 40.7 us
    pallas_call x3 -> x2, Pallas kernels: 16.5 us -> 10.5 us  [project(): pl.pallas_call(kernel, in_specs=[IN_SMEM] + [IN_VMEM] * len(xs) + [IN_HBM...]
    pallas_call x1, Pallas kernels: 1.41 us -> 6.51 us  [project_far(): pl.pallas_call(kernel, in_specs=[IN_SMEM, IN_SMEM, IN_VMEM, IN_VMEM, IN_H...]
    ppermute x10, waiting for transfers between devices: 19.9 us -> 21.6 us  [over_tp(): return lax.ppermute(a, 'tp', tp_shift(dy, dx))]
    unnamed x22 -> x24, local copies, waits for them, and re-layouts: 3.03 us -> 3.02 us
  transfers between devices with their start and end apart: 19 -> 19, of which waited for: 7 -> 7; matrix products, arithmetic and copies ran while one was open for 5% -> 5% of each run, Pallas kernels for 42% -> 41%
where the time goes in v10:
time: 95.6 us; the launch traced here: 94.6 us
  Pallas kernels  40.7 us (43%)
  waiting for transfers between devices  23 us (24%)
  starting transfers between devices  22.3 us (23%)
  local copies, waits for them, and re-layouts  6.12 us (6%)
  other arithmetic  1.55 us (2%)
  between operations  0.98 us (1%)
    ppermute x10, waiting for transfers between devices, over_tp(): return lax.ppermute(a, 'tp', tp_shift(dy, dx))  21.6 us
    ppermute x9, starting transfers between devices, over_roll(): return lax.ppermute(a, 'roll', roll_shift(dy, dz, dc))  11.6 us
    ppermute x10, starting transfers between devices, over_tp(): return lax.ppermute(a, 'tp', tp_shift(dy, dx))  10.7 us
    pallas_call x2, Pallas kernels, project(): pl.pallas_call(kernel, in_specs=[IN_SMEM] + [IN_VMEM] * len(xs) + [IN_HBM...  10.5 us
    pallas_call x1, Pallas kernels, attend(): pl.pallas_call(kernel, in_specs=[IN_SMEM] * 3 + [IN_VMEM] * 5 + [ANY] * 9...  6.98 us
    pallas_call x1, Pallas kernels, project_far(): pl.pallas_call(kernel, in_specs=[IN_SMEM, IN_SMEM, IN_VMEM, IN_VMEM, IN_H...  6.51 us
    pallas_call x1, Pallas kernels, attend_prefix(): pl.pallas_call(kernel, in_specs=[IN_SMEM, IN_VMEM] + [ANY] * 9, out_specs...  5.42 us
    pallas_call x1, Pallas kernels, attend_near(): pl.pallas_call(kernel, in_specs=[IN_SMEM] * 2 + [IN_VMEM] * 2 + [ANY] * 2...  4.25 us
  transfers between devices with their start and end apart: 19, of which 7 were waited for; matrix products, arithmetic and copies ran while one was open for 5% of the time, Pallas kernels for 41%

profile of v10, /device:TPU:0, one launch (start us, length us, event | category | flops | bytes accessed | tf_op | source)
XLA Modules:
  0.0 94.6 jit_solution(12551582803365651809)
XLA Ops:
  0.6 0.1 collective-permute-start
  0.7 2.1 %collective-permute-start.11 = (bf16[4,512,256]{2,1,0:T(8,128)(2,1)}, bf16[4,512,256]{2,1,0:T(8,128)(2,1)}, u32[]{:S(2)}, u32[]{:S(2)}) collective-permute-start(bf16[4,512,256]{2,1,0:T(8,128)(2,1)} %bitcast.23), channel_id=1, source_target_pairs={{0,16},{8,24},{16,32},{24,40},{32,48},{40,56},{48,0},{56,8},{64,80... | collective-permute-start | bytes 3145736 | tf_op jit(solution)/shard_map/ppermute | solution.py:44
  2.8 2.2 %collective-permute-start.12 = (bf16[4,512,256]{2,1,0:T(8,128)(2,1)}, bf16[4,512,256]{2,1,0:T(8,128)(2,1)}, u32[]{:S(2)}, u32[]{:S(2)}) collective-permute-start(bf16[4,512,256]{2,1,0:T(8,128)(2,1)} %bitcast.24), channel_id=1, source_target_pairs={{0,48},{8,56},{16,0},{24,8},{32,16},{40,24},{48,32},{56,40},{64,11... | collective-permute-start | bytes 3145736 | tf_op jit(solution)/shard_map/ppermute | solution.py:44
  5.0 2.0 %reshape.175.t_ref = bf16[256,1024]{1,0:T(8,128)(2,1)} reshape(bf16[64,1,4,1024]{3,2,1,0:T(4,128)(2,1)} %param.11) | data formatting | bytes 1048576 | tf_op jit(solution)/shard_map/reshape | solution.py:492
  7.0 0.7 broadcast_in_dim.48
  7.7 0.1 reshape.174.owner_ref
  7.9 6.5 %project_far.1 = (bf16[128,1024]{1,0:T(8,128)(2,1)S(1)}, bf16[128,1024]{1,0:T(8,128)(2,1)S(1)}, bf16[1,128,1280]{2,1,0:T(8,128)(2,1)}, bf16[1,128,1280]{2,1,0:T(...) custom-call(s32[2]{0:T(128)S(1)} %pad_add_fusion.1.heads_ref, s32[3]{0:T(128)S(1)} %pad_add_fusion.2.place_ref, ...), custom_call_target="tpu_custom_call" | custom-call | flops 1000000 | bytes 100000 | tf_op jit(solution)/shard_map/project_far/pallas_call | solution.py:162
  14.5 1.6 %collective-permute-start.1 = (bf16[1,128,1280]{2,1,0:T(8,128)(2,1)}, bf16[1,128,1280]{2,1,0:T(8,128)(2,1)}, u32[]{:S(2)}, u32[]{:S(2)}) collective-permute-start(bf16[1,128,1280]{2,1,0:T(8,128)(2,1)} %get-tuple-element.33), channel_id=1, source_target_pairs={{0,1},{1,2},{2,3},{3,0},{4,5},{5,6},{6,7},{7,4},{8,9},{9,10},{10,1... | collective-permute-start | bytes 983048 | tf_op jit(solution)/shard_map/ppermute | solution.py:40
  16.0 1.7 %collective-permute-start.2 = (bf16[1,128,1280]{2,1,0:T(8,128)(2,1)}, bf16[1,128,1280]{2,1,0:T(8,128)(2,1)}, u32[]{:S(2)}, u32[]{:S(2)}) collective-permute-start(bf16[1,128,1280]{2,1,0:T(8,128)(2,1)} %get-tuple-element.34), channel_id=1, source_target_pairs={{0,3},{1,0},{2,1},{3,2},{4,7},{5,4},{6,5},{7,6},{8,11},{9,8},{10,9... | collective-permute-start | bytes 983048 | tf_op jit(solution)/shard_map/ppermute | solution.py:40
  18.1 0.1 add.236
  18.2 0.1 pad_add_fusion.3.heads_ref
  18.3 0.3 collective-permute-start.5
  18.6 6.2 %project.2 = (bf16[2,128,1280]{2,1,0:T(8,128)(2,1)S(1)}, bf16[2,128,1280]{2,1,0:T(8,128)(2,1)S(1)}, bf16[2,128,1280]{2,1,0:T(8,128)(2,1)S(1)}, bf16[2,128,1280]{2,1,0:T(8,128)(2,1)S(1)}) custom-call(s32[4]{0:T(128)S(1)} %pad_add_fusion.3.heads_ref, bf16[128,1024]{1,0:T(8,128)(2,1)S(1)} %get-tuple-element.29.refs_0_, ...), custom_call_target="tpu_custom_call" | custom-call | flops 1000000 | bytes 100000 | tf_op jit(solution)/shard_map/project/pallas_call | solution.py:104
  24.9 1.8 %collective-permute-done.1.u = bf16[1,128,1280]{2,1,0:T(8,128)(2,1)} collective-permute-done((bf16[1,128,1280]{2,1,0:T(8,128)(2,1)}, bf16[1,128,1280]{2,1,0:T(8,128)(2,1)}, u32[]{:S(2)}, u32[]{:S(2)}) %collective-permute-start.1) | collective-permute-done | bytes 327712 | tf_op jit(solution)/shard_map/ppermute | solution.py:40
  26.6 1.5 %collective-permute-start.6 = (bf16[1,128,1280]{2,1,0:T(8,128)(2,1)}, bf16[1,128,1280]{2,1,0:T(8,128)(2,1)S(1)}, u32[]{:S(2)}, u32[]{:S(2)}) collective-permute-start(bf16[1,128,1280]{2,1,0:T(8,128)(2,1)} %get-tuple-element.41), channel_id=1, source_target_pairs={{0,3},{1,0},{2,1},{3,2},{4,7},{5,4},{6,5},{7,6},{8,11},{9,8},{10,9... | collective-permute-start | bytes 983048 | tf_op jit(solution)/shard_map/ppermute | solution.py:40
  28.2 1.6 %add_far.2 = (bf16[2,128,1280]{2,1,0:T(8,128)(2,1)S(1)}, bf16[2,128,1280]{2,1,0:T(8,128)(2,1)S(1)}) custom-call(bf16[2,128,1280]{2,1,0:T(8,128)(2,1)S(1)} %get-tuple-element.31.r, bf16[2,128,1280]{2,1,0:T(8,128)(2,1)S(1)} %get-tuple-element.32.l, bf16[1,128,1280]{2,1,0:T(8,128)(2,1)} %collective-permute-done.1.u, ...), custom_call_target="tpu_custom_call", output_to_operand_aliasing={{0}: (0, {}), {1}: (1, {})} | custom-call | flops 1000000 | bytes 100000 | tf_op jit(solution)/shard_map/add_far/pallas_call | solution.py:187
  29.8 0.6 collective-permute-start.3
  30.3 0.2 fusion.3
  30.6 2.4 %collective-permute-done.5.u = bf16[1,128,1280]{2,1,0:T(8,128)(2,1)} collective-permute-done((bf16[1,128,1280]{2,1,0:T(8,128)(2,1)}, bf16[1,128,1280]{2,1,0:T(8,128)(2,1)}, u32[]{:S(2)}, u32[]{:S(2)}) %collective-permute-start.5) | collective-permute-done | bytes 327712 | tf_op jit(solution)/shard_map/ppermute | solution.py:40
  33.1 2.1 %collective-permute-start.4 = (bf16[2,128,1280]{2,1,0:T(8,128)(2,1)S(1)}, bf16[2,128,1280]{2,1,0:T(8,128)(2,1)}, u32[]{:S(2)}, u32[]{:S(2)}) collective-permute-start(bf16[2,128,1280]{2,1,0:T(8,128)(2,1)S(1)} %get-tuple-element.36.refs_5_), channel_id=1, source_target_pairs={{0,3},{1,0},{2,1},{3,2},{4,7},{5,4},{6,5},{7,6},{8,11},{9,8},{10,9... | collective-permute-start | bytes 1966088 | tf_op jit(solution)/shard_map/ppermute | solution.py:40
  35.3 0.1 convert_element_type.22
  35.5 4.2 %project.3 = (bf16[2,128,1280]{2,1,0:T(8,128)(2,1)S(1)}, bf16[2,128,1280]{2,1,0:T(8,128)(2,1)S(1)}) custom-call(s32[2]{0:T(128)S(1)} %pad_add_fusion.heads_ref, bf16[128,1024]{1,0:T(8,128)(2,1)S(1)} %get-tuple-element.29.refs_0_, bf16[128,1024]{1,0:T(8,128)(2,1)S(1)} %get-tuple-element.30.refs_1_, bf16[1024,8192]{1,0:T(8,128)(2,1)} %refs_2_.3, ...), custom_call_target="tpu_custom_call" | custom-call | flops 1000000 | bytes 100000 | tf_op jit(solution)/shard_map/project/pallas_call | solution.py:104
  39.8 1.5 %add_far.3 = (bf16[2,128,1280]{2,1,0:T(8,128)(2,1)S(1)}, bf16[2,128,1280]{2,1,0:T(8,128)(2,1)S(1)}) custom-call(bf16[2,128,1280]{2,1,0:T(8,128)(2,1)S(1)} %get-tuple-element.38.r, bf16[2,128,1280]{2,1,0:T(8,128)(2,1)S(1)} %copy-done.2, bf16[1,128,1280]{2,1,0:T(8,128)(2,1)} %collective-permute-done.5.u, ...), custom_call_target="tpu_custom_call", output_to_operand_aliasing={{0}: (0, {}), {1}: (1, {})} | custom-call | flops 1000000 | bytes 100000 | tf_op jit(solution)/shard_map/add_far/pallas_call | solution.py:187
  41.3 7.4 %collective-permute-done.3.b = bf16[2,128,1280]{2,1,0:T(8,128)(2,1)S(1)} collective-permute-done((bf16[2,128,1280]{2,1,0:T(8,128)(2,1)S(1)}, bf16[2,128,1280]{2,1,0:T(8,128)(2,1)S(1)}, u32[]{:S(2)}, u32[]{:S(2)}) %collective-permute-start.3) | collective-permute-done | bytes 655392 | tf_op jit(solution)/shard_map/ppermute | solution.py:40
  48.7 0.4 collective-permute-start.9
  49.1 0.5 fusion
  49.7 0.5 collective-permute-done.4.c
  50.2 1.3 %sum_x.2 = (f32[128,1280]{1,0:T(8,128)S(1)}, bf16[128,1280]{1,0:T(8,128)(2,1)S(1)}) custom-call(bf16[2,128,1280]{2,1,0:T(8,128)(2,1)S(1)} %get-tuple-element.37.a, bf16[2,128,1280]{2,1,0:T(8,128)(2,1)S(1)} %collective-permute-done.3.b, bf16[2,128,1280]{2,1,0:T(8,128)(2,1)} %collective-permute-done.4.c, bf16[2,128,1280]{2,1,0:T(8,128)(2,1)S(1)} %get-tuple-element.43.after_ref), custom_call_target="tpu_custom_call" | custom-call | flops 1000000 | bytes 100000 | tf_op jit(solution)/shard_map/sum_x/pallas_call | solution.py:228
  51.5 1.7 %collective-permute-start.7 = (bf16[128,1280]{1,0:T(8,128)(2,1)S(1)}, bf16[128,1280]{1,0:T(8,128)(2,1)S(1)}, u32[]{:S(2)}, u32[]{:S(2)}) collective-permute-start(bf16[128,1280]{1,0:T(8,128)(2,1)S(1)} %get-tuple-element.45), channel_id=1, source_target_pairs={{0,4},{1,5},{2,6},{3,7},{4,0},{5,1},{6,2},{7,3},{8,12},{9,13},{10,... | collective-permute-start | bytes 983048 | tf_op jit(solution)/shard_map/ppermute | solution.py:40
  53.2 0.1 pad_maximum_fusion
  53.3 7.4 %collective-permute-done.8.b = bf16[2,128,1280]{2,1,0:T(8,128)(2,1)S(1)} collective-permute-done((bf16[2,128,1280]{2,1,0:T(8,128)(2,1)S(1)}, bf16[2,128,1280]{2,1,0:T(8,128)(2,1)S(1)}, u32[]{:S(2)}, u32[]{:S(2)}) %collective-permute-start.8) | collective-permute-done | bytes 655392 | tf_op jit(solution)/shard_map/ppermute | solution.py:40
  60.7 2.1 %collective-permute-done.9.c = bf16[2,128,1280]{2,1,0:T(8,128)(2,1)S(1)} collective-permute-done((bf16[2,128,1280]{2,1,0:T(8,128)(2,1)S(1)}, bf16[2,128,1280]{2,1,0:T(8,128)(2,1)S(1)}, u32[]{:S(2)}, u32[]{:S(2)}) %collective-permute-start.9) | collective-permute-done | bytes 655392 | tf_op jit(solution)/shard_map/ppermute | solution.py:40
  62.9 0.2 sum_x.3
  63.1 0.3 make_queries.1
  63.4 0.1 collective-permute-start.16
  63.5 0.5 collective-permute-start.14
  64.0 0.1 collective-permute-start.15
  64.1 3.2 %collective-permute-start.10 = (bf16[32,32,128]{2,1,0:T(8,128)(2,1)S(1)}, bf16[32,32,128]{2,1,0:T(8,128)(2,1)S(1)}, u32[]{:S(2)}, u32[]{:S(2)}) collective-permute-start(bf16[32,32,128]{2,1,0:T(8,128)(2,1)S(1)} %get-tuple-element.48.refs_3_.q_ref), channel_id=1, source_target_pairs={{0,64},{8,72},{16,80},{24,88},{32,96},{40,104},{48,112},{56,120},{... | collective-permute-start | bytes 786440 | tf_op jit(solution)/shard_map/ppermute | solution.py:44
  67.3 0.7 collective-permute-start.18
  68.1 1.0 %copy-done.3 = bf16[4,512,256]{2,1,0:T(8,128)(2,1)} copy-done((bf16[4,512,256]{2,1,0:T(8,128)(2,1)}, bf16[4,512,256]{2,1,0:T(8,128)(2,1)S(1)}, u32[]{:S(2)}) %copy-start.3) | copy-done | bytes 1048600
  69.1 4.3 %attend_near.1.refs_8_.near_ref = f32[33,32,128]{2,1,0:T(8,128)} custom-call(s32[64]{0:T(128)S(1)} %get-tuple-element.62.length_ref, s32[64]{0:T(128)S(1)} %get-tuple-element.64.at_ref.order_ref, bf16[32,32,128]{2,1,0:T(8,128)(2,1)S(1)} %get-tuple-element.48.refs_3_.q_ref, bf16[128,256]{1,0:T(8,128)(2,1)S(1)} %get-tuple-element.52.new_ref, ...), custom_call_target="tpu_custom_call" | custom-call | flops 1000000 | bytes 100000 | tf_op jit(solution)/shard_map/attend_near/pallas_call | solution.py:419
  73.3 1.4 %collective-permute-done.10.q_ref = bf16[32,32,128]{2,1,0:T(8,128)(2,1)S(1)} collective-permute-done((bf16[32,32,128]{2,1,0:T(8,128)(2,1)S(1)}, bf16[32,32,128]{2,1,0:T(8,128)(2,1)S(1)}, u32[]{:S(2)}, u32[]{:S(2)}) %collective-permute-start.10) | collective-permute-done | bytes 262176 | tf_op jit(solution)/shard_map/ppermute | solution.py:44
  74.7 1.0 %copy-done.4 = bf16[4,512,256]{2,1,0:T(8,128)(2,1)} copy-done((bf16[4,512,256]{2,1,0:T(8,128)(2,1)}, bf16[4,512,256]{2,1,0:T(8,128)(2,1)S(1)}, u32[]{:S(2)}) %copy-start.4) | copy-done | bytes 1048600
  75.7 1.0 %copy-done.5 = bf16[4,512,256]{2,1,0:T(8,128)(2,1)} copy-done((bf16[4,512,256]{2,1,0:T(8,128)(2,1)}, bf16[4,512,256]{2,1,0:T(8,128)(2,1)S(1)}, u32[]{:S(2)}) %copy-start.5) | copy-done | bytes 1048600
  76.7 5.4 %attend_prefix.1 = bf16[33,32,128]{2,1,0:T(8,128)(2,1)S(1)} custom-call(s32[32]{0:T(128)S(1)} %slice.3.limit_ref, bf16[32,32,128]{2,1,0:T(8,128)(2,1)S(1)} %collective-permute-done.10.q_ref, bf16[4,512,256]{2,1,0:T(8,128)(2,1)} %bitcast.25, bf16[4,512,256]{2,1,0:T(8,128)(2,1)} %get-tuple-element.49.refs_1_, bf16[4,512,256]{2,1,0:T(8,128)(2,1)} %get-tuple-element.50.refs_2_, ...), custom_call_target="tpu_custom_call" | custom-call | flops 1000000 | bytes 100000 | tf_op jit(solution)/shard_map/attend_prefix/pallas_call | solution.py:379
  82.1 3.3 %collective-permute-start.17 = (bf16[33,32,128]{2,1,0:T(8,128)(2,1)S(1)}, bf16[33,32,128]{2,1,0:T(8,128)(2,1)S(1)}, u32[]{:S(2)}, u32[]{:S(2)}) collective-permute-start(bf16[33,32,128]{2,1,0:T(8,128)(2,1)S(1)} %attend_prefix.1), channel_id=1, source_target_pairs={{0,64},{8,72},{16,80},{24,88},{32,96},{40,104},{48,112},{56,120},{... | collective-permute-start | bytes 811016 | tf_op jit(solution)/shard_map/ppermute | solution.py:44
  85.4 7.0 %attend.1.done_ref = bf16[32,4,1280]{2,1,0:T(4,128)(2,1)S(1)} custom-call(s32[32]{0:T(128)S(1)} %slice.3.limit_ref, s32[64]{0:T(128)S(1)} %get-tuple-element.62.length_ref, s32[64]{0:T(128)S(1)} %get-tuple-element.64.at_ref.order_ref, f32[128,1280]{1,0:T(8,128)S(1)} %get-tuple-element.47.after_ref.keep_ref, ...), custom_call_target="tpu_custom_call" | custom-call | flops 1000000 | bytes 100000 | tf_op jit(solution)/shard_map/attend/pallas_call | solution.py:323
  92.4 2.2 %merge_rows.1 = (bf16[64,4,1024]{2,1,0:T(4,128)(2,1)}, bf16[64,4,256]{2,1,0:T(4,128)(2,1)}) custom-call(s32[64]{0:T(128)S(1)} %get-tuple-element.64.at_ref.order_ref, bf16[33,32,128]{2,1,0:T(8,128)(2,1)S(1)} %collective-permute-done.17.far_ref, f32[33,32,128]{2,1,0:T(8,128)} %attend_near.1.refs_8_.near_ref, bf16[32,4,256]{2,1,0:T(4,128)(2,1)S(1)} %reshape.178.new_ref, ...), custom_call_target="tpu_custom_call" | custom-call | flops 1000000 | bytes 100000 | tf_op jit(solution)/shard_map/merge_rows/pallas_call | solution.py:450
  (53 shorter events, 0.9 us)
Async XLA Ops:
  0.6 17.6 %collective-permute-start = (bf16[4,512,256]{2,1,0:T(8,128)(2,1)}, bf16[4,512,256]{2,1,0:T(8,128)(2,1)S(1)}, u32[]{:S(2)}, u32[]{:S(2)}) collective-permute-start(bf16[4,512,256]{2,1,0:T(8,128)(2,1)} %bitcast.22), channel_id=1, source_target_pairs={{0,8},{8,0},{16,24},{24,16},{32,40},{40,32},{48,56},{56,48},{64,72... | collective-permute-start | bytes 3145736 | tf_op jit(solution)/shard_map/ppermute | solution.py:44
  0.7 29.8 %collective-permute-start.11 = (bf16[4,512,256]{2,1,0:T(8,128)(2,1)}, bf16[4,512,256]{2,1,0:T(8,128)(2,1)}, u32[]{:S(2)}, u32[]{:S(2)}) collective-permute-start(bf16[4,512,256]{2,1,0:T(8,128)(2,1)} %bitcast.23), channel_id=1, source_target_pairs={{0,16},{8,24},{16,32},{24,40},{32,48},{40,56},{48,0},{56,8},{64,80... | collective-permute-start | bytes 3145736 | tf_op jit(solution)/shard_map/ppermute | solution.py:44
  2.8 60.6 %collective-permute-start.12 = (bf16[4,512,256]{2,1,0:T(8,128)(2,1)}, bf16[4,512,256]{2,1,0:T(8,128)(2,1)}, u32[]{:S(2)}, u32[]{:S(2)}) collective-permute-start(bf16[4,512,256]{2,1,0:T(8,128)(2,1)} %bitcast.24), channel_id=1, source_target_pairs={{0,48},{8,56},{16,0},{24,8},{32,16},{40,24},{48,32},{56,40},{64,11... | collective-permute-start | bytes 3145736 | tf_op jit(solution)/shard_map/ppermute | solution.py:44
  7.9 9.8 %copy-start.11 = (s32[4]{0:T(128)S(1)}, s32[4]{0:T(128)}, u32[]{:S(2)}) copy-start(s32[4]{0:T(128)} %constant.143.clone) | copy-start | bytes 52
  14.5 12.2 %collective-permute-start.1 = (bf16[1,128,1280]{2,1,0:T(8,128)(2,1)}, bf16[1,128,1280]{2,1,0:T(8,128)(2,1)}, u32[]{:S(2)}, u32[]{:S(2)}) collective-permute-start(bf16[1,128,1280]{2,1,0:T(8,128)(2,1)} %get-tuple-element.33), channel_id=1, source_target_pairs={{0,1},{1,2},{2,3},{3,0},{4,5},{5,6},{6,7},{7,4},{8,9},{9,10},{10,1... | collective-permute-start | bytes 983048 | tf_op jit(solution)/shard_map/ppermute | solution.py:40
  16.0 12.2 %collective-permute-start.2 = (bf16[1,128,1280]{2,1,0:T(8,128)(2,1)}, bf16[1,128,1280]{2,1,0:T(8,128)(2,1)}, u32[]{:S(2)}, u32[]{:S(2)}) collective-permute-start(bf16[1,128,1280]{2,1,0:T(8,128)(2,1)} %get-tuple-element.34), channel_id=1, source_target_pairs={{0,3},{1,0},{2,1},{3,2},{4,7},{5,4},{6,5},{7,6},{8,11},{9,8},{10,9... | collective-permute-start | bytes 983048 | tf_op jit(solution)/shard_map/ppermute | solution.py:40
  18.2 6.6 %copy-start = (bf16[4,512,256]{2,1,0:T(8,128)(2,1)}, bf16[4,512,256]{2,1,0:T(8,128)(2,1)S(1)}, u32[]{:S(2)}) copy-start(bf16[4,512,256]{2,1,0:T(8,128)(2,1)S(1)} %collective-permute-done.refs_4_) | copy-start | bytes 3145732
  18.3 14.8 %collective-permute-start.5 = (bf16[1,128,1280]{2,1,0:T(8,128)(2,1)}, bf16[1,128,1280]{2,1,0:T(8,128)(2,1)}, u32[]{:S(2)}, u32[]{:S(2)}) collective-permute-start(bf16[1,128,1280]{2,1,0:T(8,128)(2,1)} %get-tuple-element.40), channel_id=1, source_target_pairs={{0,1},{1,2},{2,3},{3,0},{4,5},{5,6},{6,7},{7,4},{8,9},{9,10},{10,1... | collective-permute-start | bytes 983048 | tf_op jit(solution)/shard_map/ppermute | solution.py:40
  18.6 11.7 %copy-start.6 = (s32[64]{0:T(128)S(1)}, s32[64]{0:T(128)}, u32[]{:S(2)}) copy-start(s32[64]{0:T(128)} %param.18) | copy-start | bytes 772
  18.6 11.7 %copy-start.8 = (s32[64,1]{0,1:T(1,128)S(1)}, s32[64,1]{0,1:T(1,128)}, u32[]{:S(2)}) copy-start(s32[64,1]{0,1:T(1,128)} %param.20) | copy-start | bytes 772
  18.6 11.7 %copy-start.9 = (s32[64]{0:T(128)S(1)}, s32[64]{0:T(128)}, u32[]{:S(2)}) copy-start(s32[64]{0:T(128)} %param.19) | copy-start | bytes 772
  18.6 16.8 %copy-start.7 = (bf16[1024]{0:T(1024)(128)(2,1)S(1)}, bf16[1024]{0:T(1024)(128)(2,1)}, u32[]{:S(2)}) copy-start(bf16[1024]{0:T(1024)(128)(2,1)} %param.13) | copy-start | bytes 6148
  18.6 16.8 %copy-start.10 = (bf16[256]{0:T(256)(128)(2,1)S(1)}, bf16[256]{0:T(256)(128)(2,1)}, u32[]{:S(2)}) copy-start(bf16[256]{0:T(256)(128)(2,1)} %param.15) | copy-start | bytes 1540
  24.9 4.9 %copy-start.1 = (bf16[2,128,1280]{2,1,0:T(8,128)(2,1)}, bf16[2,128,1280]{2,1,0:T(8,128)(2,1)S(1)}, u32[]{:S(2)}) copy-start(bf16[2,128,1280]{2,1,0:T(8,128)(2,1)S(1)} %get-tuple-element.39.l) | copy-start | bytes 1966084
  26.6 13.1 %collective-permute-start.6 = (bf16[1,128,1280]{2,1,0:T(8,128)(2,1)}, bf16[1,128,1280]{2,1,0:T(8,128)(2,1)S(1)}, u32[]{:S(2)}, u32[]{:S(2)}) collective-permute-start(bf16[1,128,1280]{2,1,0:T(8,128)(2,1)} %get-tuple-element.41), channel_id=1, source_target_pairs={{0,3},{1,0},{2,1},{3,2},{4,7},{5,4},{6,5},{7,6},{8,11},{9,8},{10,9... | collective-permute-start | bytes 983048 | tf_op jit(solution)/shard_map/ppermute | solution.py:40
  29.8 19.0 %collective-permute-start.3 = (bf16[2,128,1280]{2,1,0:T(8,128)(2,1)S(1)}, bf16[2,128,1280]{2,1,0:T(8,128)(2,1)S(1)}, u32[]{:S(2)}, u32[]{:S(2)}) collective-permute-start(bf16[2,128,1280]{2,1,0:T(8,128)(2,1)S(1)} %get-tuple-element.35.refs_4_.refs_0_), channel_id=1, source_target_pairs={{0,1},{1,2},{2,3},{3,0},{4,5},{5,6},{6,7},{7,4},{8,9},{9,10},{10,1... | collective-permute-start | bytes 1966088 | tf_op jit(solution)/shard_map/ppermute | solution.py:40
  30.5 32.9 %collective-permute-start.13 = (bf16[4,512,256]{2,1,0:T(8,128)(2,1)}, bf16[4,512,256]{2,1,0:T(8,128)(2,1)}, u32[]{:S(2)}, u32[]{:S(2)}) collective-permute-start(bf16[4,512,256]{2,1,0:T(8,128)(2,1)} %collective-permute-done.11.refs_0_), channel_id=1, source_target_pairs={{0,16},{8,24},{16,32},{24,40},{32,48},{40,56},{48,0},{56,8},{64,80... | collective-permute-start | bytes 3145736 | tf_op jit(solution)/shard_map/ppermute | solution.py:44
  33.1 17.1 %collective-permute-start.4 = (bf16[2,128,1280]{2,1,0:T(8,128)(2,1)S(1)}, bf16[2,128,1280]{2,1,0:T(8,128)(2,1)}, u32[]{:S(2)}, u32[]{:S(2)}) collective-permute-start(bf16[2,128,1280]{2,1,0:T(8,128)(2,1)S(1)} %get-tuple-element.36.refs_5_), channel_id=1, source_target_pairs={{0,3},{1,0},{2,1},{3,2},{4,7},{5,4},{6,5},{7,6},{8,11},{9,8},{10,9... | collective-permute-start | bytes 1966088 | tf_op jit(solution)/shard_map/ppermute | solution.py:40
  35.5 4.3 %copy-start.2 = (bf16[2,128,1280]{2,1,0:T(8,128)(2,1)S(1)}, bf16[2,128,1280]{2,1,0:T(8,128)(2,1)}, u32[]{:S(2)}) copy-start(bf16[2,128,1280]{2,1,0:T(8,128)(2,1)} %copy-done.1) | copy-start | bytes 1966084
  41.2 19.5 %collective-permute-start.8 = (bf16[2,128,1280]{2,1,0:T(8,128)(2,1)S(1)}, bf16[2,128,1280]{2,1,0:T(8,128)(2,1)S(1)}, u32[]{:S(2)}, u32[]{:S(2)}) collective-permute-start(bf16[2,128,1280]{2,1,0:T(8,128)(2,1)S(1)} %get-tuple-element.43.after_ref), channel_id=1, source_target_pairs={{0,1},{1,2},{2,3},{3,0},{4,5},{5,6},{6,7},{7,4},{8,9},{9,10},{10,1... | collective-permute-start | bytes 1966088 | tf_op jit(solution)/shard_map/ppermute | solution.py:40
  48.7 14.2 %collective-permute-start.9 = (bf16[2,128,1280]{2,1,0:T(8,128)(2,1)S(1)}, bf16[2,128,1280]{2,1,0:T(8,128)(2,1)S(1)}, u32[]{:S(2)}, u32[]{:S(2)}) collective-permute-start(bf16[2,128,1280]{2,1,0:T(8,128)(2,1)S(1)} %get-tuple-element.46), channel_id=1, source_target_pairs={{0,3},{1,0},{2,1},{3,2},{4,7},{5,4},{6,5},{7,6},{8,11},{9,8},{10,9... | collective-permute-start | bytes 1966088 | tf_op jit(solution)/shard_map/ppermute | solution.py:40
  51.5 11.6 %collective-permute-start.7 = (bf16[128,1280]{1,0:T(8,128)(2,1)S(1)}, bf16[128,1280]{1,0:T(8,128)(2,1)S(1)}, u32[]{:S(2)}, u32[]{:S(2)}) collective-permute-start(bf16[128,1280]{1,0:T(8,128)(2,1)S(1)} %get-tuple-element.45), channel_id=1, source_target_pairs={{0,4},{1,5},{2,6},{3,7},{4,0},{5,1},{6,2},{7,3},{8,12},{9,13},{10,... | collective-permute-start | bytes 983048 | tf_op jit(solution)/shard_map/ppermute | solution.py:40
  63.4 4.6 %collective-permute-start.16 = (bf16[4,512,256]{2,1,0:T(8,128)(2,1)}, bf16[4,512,256]{2,1,0:T(8,128)(2,1)S(1)}, u32[]{:S(2)}, u32[]{:S(2)}) collective-permute-start(bf16[4,512,256]{2,1,0:T(8,128)(2,1)} %get-tuple-element.51.refs_3_), channel_id=1, source_target_pairs={{0,8},{8,0},{16,24},{24,16},{32,40},{40,32},{48,56},{56,48},{64,72... | collective-permute-start | bytes 3145736 | tf_op jit(solution)/shard_map/ppermute | solution.py:44
  63.5 11.2 %collective-permute-start.14 = (bf16[4,512,256]{2,1,0:T(8,128)(2,1)}, bf16[4,512,256]{2,1,0:T(8,128)(2,1)S(1)}, u32[]{:S(2)}, u32[]{:S(2)}) collective-permute-start(bf16[4,512,256]{2,1,0:T(8,128)(2,1)} %get-tuple-element.49.refs_1_), channel_id=1, source_target_pairs={{0,8},{8,0},{16,24},{24,16},{32,40},{40,32},{48,56},{56,48},{64,72... | collective-permute-start | bytes 3145736 | tf_op jit(solution)/shard_map/ppermute | solution.py:44
  64.0 10.7 %collective-permute-start.15 = (bf16[4,512,256]{2,1,0:T(8,128)(2,1)}, bf16[4,512,256]{2,1,0:T(8,128)(2,1)S(1)}, u32[]{:S(2)}, u32[]{:S(2)}) collective-permute-start(bf16[4,512,256]{2,1,0:T(8,128)(2,1)} %get-tuple-element.50.refs_2_), channel_id=1, source_target_pairs={{0,8},{8,0},{16,24},{24,16},{32,40},{40,32},{48,56},{56,48},{64,72... | collective-permute-start | bytes 3145736 | tf_op jit(solution)/shard_map/ppermute | solution.py:44
  64.1 10.6 %collective-permute-start.10 = (bf16[32,32,128]{2,1,0:T(8,128)(2,1)S(1)}, bf16[32,32,128]{2,1,0:T(8,128)(2,1)S(1)}, u32[]{:S(2)}, u32[]{:S(2)}) collective-permute-start(bf16[32,32,128]{2,1,0:T(8,128)(2,1)S(1)} %get-tuple-element.48.refs_3_.q_ref), channel_id=1, source_target_pairs={{0,64},{8,72},{16,80},{24,88},{32,96},{40,104},{48,112},{56,120},{... | collective-permute-start | bytes 786440 | tf_op jit(solution)/shard_map/ppermute | solution.py:44
  67.3 18.1 %collective-permute-start.18 = (bf16[128,1280]{1,0:T(8,128)(2,1)S(1)}, bf16[128,1280]{1,0:T(8,128)(2,1)S(1)}, u32[]{:S(2)}, u32[]{:S(2)}) collective-permute-start(bf16[128,1280]{1,0:T(8,128)(2,1)S(1)} %get-tuple-element.53), channel_id=1, source_target_pairs={{0,4},{1,5},{2,6},{3,7},{4,0},{5,1},{6,2},{7,3},{8,12},{9,13},{10,... | collective-permute-start | bytes 983048 | tf_op jit(solution)/shard_map/ppermute | solution.py:40
  68.1 1.0 %copy-start.3 = (bf16[4,512,256]{2,1,0:T(8,128)(2,1)}, bf16[4,512,256]{2,1,0:T(8,128)(2,1)S(1)}, u32[]{:S(2)}) copy-start(bf16[4,512,256]{2,1,0:T(8,128)(2,1)S(1)} %collective-permute-done.16.after_ref.refs_7_) | copy-start | bytes 3145732
  74.7 1.0 %copy-start.4 = (bf16[4,512,256]{2,1,0:T(8,128)(2,1)}, bf16[4,512,256]{2,1,0:T(8,128)(2,1)S(1)}, u32[]{:S(2)}) copy-start(bf16[4,512,256]{2,1,0:T(8,128)(2,1)S(1)} %collective-permute-done.14.refs_5_) | copy-start | bytes 3145732
  75.7 1.0 %copy-start.5 = (bf16[4,512,256]{2,1,0:T(8,128)(2,1)}, bf16[4,512,256]{2,1,0:T(8,128)(2,1)S(1)}, u32[]{:S(2)}) copy-start(bf16[4,512,256]{2,1,0:T(8,128)(2,1)S(1)} %collective-permute-done.15.refs_6_) | copy-start | bytes 3145732
  82.1 10.3 %collective-permute-start.17 = (bf16[33,32,128]{2,1,0:T(8,128)(2,1)S(1)}, bf16[33,32,128]{2,1,0:T(8,128)(2,1)S(1)}, u32[]{:S(2)}, u32[]{:S(2)}) collective-permute-start(bf16[33,32,128]{2,1,0:T(8,128)(2,1)S(1)} %attend_prefix.1), channel_id=1, source_target_pairs={{0,64},{8,72},{16,80},{24,88},{32,96},{40,104},{48,112},{56,120},{... | collective-permute-start | bytes 811016 | tf_op jit(solution)/shard_map/ppermute | solution.py:44

commit v11 on v10

--- a/solution.py
+++ b/solution.py
@@ -298,8 +298,9 @@
             pltpu.make_async_copy(cache_ref.at[at_ref[32 + p]], buf.at[p, pl.ds(512, 64)], csem.at[p])
             for p in range(32)
         ]
-        for c in copies:
-            c.start()
+        for g in range(8):
+            for c in [copies[g]] + copies[8 + 4 * g : 12 + 4 * g]:
+                c.start()
         new_all = rotated(keep_ref, more_ref, bias_ref, cos_ref, sin_ref, ROWS, qbuf)
         for p in range(32):
             o_ref[p, :, QW:] = new_all[4 * p : 4 * p + 4].astype(BF16)
@@ -307,9 +308,10 @@
         row = lax.broadcasted_iota(jnp.int32, (32, keys), 0)
         col = lax.broadcasted_iota(jnp.int32, (32, keys), 1)
         fresh = (col >= 576) & (col - 576 <= row & 3)
-        for c in copies:
-            c.wait()
-        for p in range(32):
+        for p in range(32):
+            if p % 4 == 0:
+                for c in [copies[p // 4]] + copies[8 + p : 12 + p]:
+                    c.wait()
             valid = (col < limit_ref[p]) | ((col >= 512) & (col < 512 + length_ref[32 + p])) | fresh
             rows = slice(32 * p, 32 * p + 32)
             s_buf[rows, :] = masked_scores(qbuf[rows, :].astype(BF16), buf[p, :, :HD], valid)

time: 95.6 us -> 94.6 us (0.990)
  Pallas kernels: 40.7 us -> 39.6 us
    pallas_call x1, Pallas kernels: 6.98 us -> 5.92 us  [attend(): pl.pallas_call(kernel, in_specs=[IN_SMEM] * 3 + [IN_VMEM] * 5 + [ANY] * 9...]
  transfers between devices with their start and end apart: 19 -> 19, of which waited for: 7 -> 7; matrix products, arithmetic and copies ran while one was open for 5% -> 5% of each run, Pallas kernels for 41% -> 40%
where the time goes in v11:
time: 94.6 us; the launch traced here: 93.6 us
  Pallas kernels  39.6 us (42%)
  waiting for transfers between devices  23 us (24%)
  starting transfers between devices  22.3 us (24%)
  local copies, waits for them, and re-layouts  6.12 us (6%)
  other arithmetic  1.55 us (2%)
  between operations  0.98 us (1%)
    ppermute x10, waiting for transfers between devices, over_tp(): return lax.ppermute(a, 'tp', tp_shift(dy, dx))  21.6 us
    ppermute x9, starting transfers between devices, over_roll(): return lax.ppermute(a, 'roll', roll_shift(dy, dz, dc))  11.6 us
    ppermute x10, starting transfers between devices, over_tp(): return lax.ppermute(a, 'tp', tp_shift(dy, dx))  10.7 us
    pallas_call x2, Pallas kernels, project(): pl.pallas_call(kernel, in_specs=[IN_SMEM] + [IN_VMEM] * len(xs) + [IN_HBM...  10.5 us
    pallas_call x1, Pallas kernels, project_far(): pl.pallas_call(kernel, in_specs=[IN_SMEM, IN_SMEM, IN_VMEM, IN_VMEM, IN_H...  6.51 us
    pallas_call x1, Pallas kernels, attend(): pl.pallas_call(kernel, in_specs=[IN_SMEM] * 3 + [IN_VMEM] * 5 + [ANY] * 9...  5.92 us
    pallas_call x1, Pallas kernels, attend_prefix(): pl.pallas_call(kernel, in_specs=[IN_SMEM, IN_VMEM] + [ANY] * 9, out_specs...  5.42 us
    pallas_call x1, Pallas kernels, attend_near(): pl.pallas_call(kernel, in_specs=[IN_SMEM] * 2 + [IN_VMEM] * 2 + [ANY] * 2...  4.25 us
  transfers between devices with their start and end apart: 19, of which 7 were waited for; matrix products, arithmetic and copies ran while one was open for 5% of the time, Pallas kernels for 40%

profile of v11, /device:TPU:0, one launch (start us, length us, event | category | flops | bytes accessed | tf_op | source)
XLA Modules:
  0.0 93.6 jit_solution(10431929030817409866)
XLA Ops:
  0.6 0.1 collective-permute-start
  0.7 2.1 %collective-permute-start.11 = (bf16[4,512,256]{2,1,0:T(8,128)(2,1)}, bf16[4,512,256]{2,1,0:T(8,128)(2,1)}, u32[]{:S(2)}, u32[]{:S(2)}) collective-permute-start(bf16[4,512,256]{2,1,0:T(8,128)(2,1)} %bitcast.23), channel_id=1, source_target_pairs={{0,16},{8,24},{16,32},{24,40},{32,48},{40,56},{48,0},{56,8},{64,80... | collective-permute-start | bytes 3145736 | tf_op jit(solution)/shard_map/ppermute | solution.py:44
  2.8 2.2 %collective-permute-start.12 = (bf16[4,512,256]{2,1,0:T(8,128)(2,1)}, bf16[4,512,256]{2,1,0:T(8,128)(2,1)}, u32[]{:S(2)}, u32[]{:S(2)}) collective-permute-start(bf16[4,512,256]{2,1,0:T(8,128)(2,1)} %bitcast.24), channel_id=1, source_target_pairs={{0,48},{8,56},{16,0},{24,8},{32,16},{40,24},{48,32},{56,40},{64,11... | collective-permute-start | bytes 3145736 | tf_op jit(solution)/shard_map/ppermute | solution.py:44
  5.0 2.0 %reshape.175.t_ref = bf16[256,1024]{1,0:T(8,128)(2,1)} reshape(bf16[64,1,4,1024]{3,2,1,0:T(4,128)(2,1)} %param.11) | data formatting | bytes 1048576 | tf_op jit(solution)/shard_map/reshape | solution.py:494
  7.0 0.7 broadcast_in_dim.48
  7.7 0.1 reshape.174.owner_ref
  7.9 6.5 %project_far.1 = (bf16[128,1024]{1,0:T(8,128)(2,1)S(1)}, bf16[128,1024]{1,0:T(8,128)(2,1)S(1)}, bf16[1,128,1280]{2,1,0:T(8,128)(2,1)}, bf16[1,128,1280]{2,1,0:T(...) custom-call(s32[2]{0:T(128)S(1)} %pad_add_fusion.1.heads_ref, s32[3]{0:T(128)S(1)} %pad_add_fusion.2.place_ref, ...), custom_call_target="tpu_custom_call" | custom-call | flops 1000000 | bytes 100000 | tf_op jit(solution)/shard_map/project_far/pallas_call | solution.py:162
  14.5 1.6 %collective-permute-start.1 = (bf16[1,128,1280]{2,1,0:T(8,128)(2,1)}, bf16[1,128,1280]{2,1,0:T(8,128)(2,1)}, u32[]{:S(2)}, u32[]{:S(2)}) collective-permute-start(bf16[1,128,1280]{2,1,0:T(8,128)(2,1)} %get-tuple-element.33), channel_id=1, source_target_pairs={{0,1},{1,2},{2,3},{3,0},{4,5},{5,6},{6,7},{7,4},{8,9},{9,10},{10,1... | collective-permute-start | bytes 983048 | tf_op jit(solution)/shard_map/ppermute | solution.py:40
  16.0 1.7 %collective-permute-start.2 = (bf16[1,128,1280]{2,1,0:T(8,128)(2,1)}, bf16[1,128,1280]{2,1,0:T(8,128)(2,1)}, u32[]{:S(2)}, u32[]{:S(2)}) collective-permute-start(bf16[1,128,1280]{2,1,0:T(8,128)(2,1)} %get-tuple-element.34), channel_id=1, source_target_pairs={{0,3},{1,0},{2,1},{3,2},{4,7},{5,4},{6,5},{7,6},{8,11},{9,8},{10,9... | collective-permute-start | bytes 983048 | tf_op jit(solution)/shard_map/ppermute | solution.py:40
  18.1 0.1 add.236
  18.2 0.1 pad_add_fusion.3.heads_ref
  18.3 0.3 collective-permute-start.5
  18.6 6.2 %project.2 = (bf16[2,128,1280]{2,1,0:T(8,128)(2,1)S(1)}, bf16[2,128,1280]{2,1,0:T(8,128)(2,1)S(1)}, bf16[2,128,1280]{2,1,0:T(8,128)(2,1)S(1)}, bf16[2,128,1280]{2,1,0:T(8,128)(2,1)S(1)}) custom-call(s32[4]{0:T(128)S(1)} %pad_add_fusion.3.heads_ref, bf16[128,1024]{1,0:T(8,128)(2,1)S(1)} %get-tuple-element.29.refs_0_, ...), custom_call_target="tpu_custom_call" | custom-call | flops 1000000 | bytes 100000 | tf_op jit(solution)/shard_map/project/pallas_call | solution.py:104
  24.9 1.8 %collective-permute-done.1.u = bf16[1,128,1280]{2,1,0:T(8,128)(2,1)} collective-permute-done((bf16[1,128,1280]{2,1,0:T(8,128)(2,1)}, bf16[1,128,1280]{2,1,0:T(8,128)(2,1)}, u32[]{:S(2)}, u32[]{:S(2)}) %collective-permute-start.1) | collective-permute-done | bytes 327712 | tf_op jit(solution)/shard_map/ppermute | solution.py:40
  26.6 1.5 %collective-permute-start.6 = (bf16[1,128,1280]{2,1,0:T(8,128)(2,1)}, bf16[1,128,1280]{2,1,0:T(8,128)(2,1)S(1)}, u32[]{:S(2)}, u32[]{:S(2)}) collective-permute-start(bf16[1,128,1280]{2,1,0:T(8,128)(2,1)} %get-tuple-element.41), channel_id=1, source_target_pairs={{0,3},{1,0},{2,1},{3,2},{4,7},{5,4},{6,5},{7,6},{8,11},{9,8},{10,9... | collective-permute-start | bytes 983048 | tf_op jit(solution)/shard_map/ppermute | solution.py:40
  28.2 1.6 %add_far.2 = (bf16[2,128,1280]{2,1,0:T(8,128)(2,1)S(1)}, bf16[2,128,1280]{2,1,0:T(8,128)(2,1)S(1)}) custom-call(bf16[2,128,1280]{2,1,0:T(8,128)(2,1)S(1)} %get-tuple-element.31.r, bf16[2,128,1280]{2,1,0:T(8,128)(2,1)S(1)} %get-tuple-element.32.l, bf16[1,128,1280]{2,1,0:T(8,128)(2,1)} %collective-permute-done.1.u, ...), custom_call_target="tpu_custom_call", output_to_operand_aliasing={{0}: (0, {}), {1}: (1, {})} | custom-call | flops 1000000 | bytes 100000 | tf_op jit(solution)/shard_map/add_far/pallas_call | solution.py:187
  29.8 0.6 collective-permute-start.3
  30.3 0.2 fusion.3
  30.6 2.4 %collective-permute-done.5.u = bf16[1,128,1280]{2,1,0:T(8,128)(2,1)} collective-permute-done((bf16[1,128,1280]{2,1,0:T(8,128)(2,1)}, bf16[1,128,1280]{2,1,0:T(8,128)(2,1)}, u32[]{:S(2)}, u32[]{:S(2)}) %collective-permute-start.5) | collective-permute-done | bytes 327712 | tf_op jit(solution)/shard_map/ppermute | solution.py:40
  33.1 2.1 %collective-permute-start.4 = (bf16[2,128,1280]{2,1,0:T(8,128)(2,1)S(1)}, bf16[2,128,1280]{2,1,0:T(8,128)(2,1)}, u32[]{:S(2)}, u32[]{:S(2)}) collective-permute-start(bf16[2,128,1280]{2,1,0:T(8,128)(2,1)S(1)} %get-tuple-element.36.refs_5_), channel_id=1, source_target_pairs={{0,3},{1,0},{2,1},{3,2},{4,7},{5,4},{6,5},{7,6},{8,11},{9,8},{10,9... | collective-permute-start | bytes 1966088 | tf_op jit(solution)/shard_map/ppermute | solution.py:40
  35.3 0.1 convert_element_type.22
  35.5 4.2 %project.3 = (bf16[2,128,1280]{2,1,0:T(8,128)(2,1)S(1)}, bf16[2,128,1280]{2,1,0:T(8,128)(2,1)S(1)}) custom-call(s32[2]{0:T(128)S(1)} %pad_add_fusion.heads_ref, bf16[128,1024]{1,0:T(8,128)(2,1)S(1)} %get-tuple-element.29.refs_0_, bf16[128,1024]{1,0:T(8,128)(2,1)S(1)} %get-tuple-element.30.refs_1_, bf16[1024,8192]{1,0:T(8,128)(2,1)} %refs_2_.3, ...), custom_call_target="tpu_custom_call" | custom-call | flops 1000000 | bytes 100000 | tf_op jit(solution)/shard_map/project/pallas_call | solution.py:104
  39.8 1.5 %add_far.3 = (bf16[2,128,1280]{2,1,0:T(8,128)(2,1)S(1)}, bf16[2,128,1280]{2,1,0:T(8,128)(2,1)S(1)}) custom-call(bf16[2,128,1280]{2,1,0:T(8,128)(2,1)S(1)} %get-tuple-element.38.r, bf16[2,128,1280]{2,1,0:T(8,128)(2,1)S(1)} %copy-done.2, bf16[1,128,1280]{2,1,0:T(8,128)(2,1)} %collective-permute-done.5.u, ...), custom_call_target="tpu_custom_call", output_to_operand_aliasing={{0}: (0, {}), {1}: (1, {})} | custom-call | flops 1000000 | bytes 100000 | tf_op jit(solution)/shard_map/add_far/pallas_call | solution.py:187
  41.3 7.4 %collective-permute-done.3.b = bf16[2,128,1280]{2,1,0:T(8,128)(2,1)S(1)} collective-permute-done((bf16[2,128,1280]{2,1,0:T(8,128)(2,1)S(1)}, bf16[2,128,1280]{2,1,0:T(8,128)(2,1)S(1)}, u32[]{:S(2)}, u32[]{:S(2)}) %collective-permute-start.3) | collective-permute-done | bytes 655392 | tf_op jit(solution)/shard_map/ppermute | solution.py:40
  48.7 0.4 collective-permute-start.9
  49.1 0.5 fusion
  49.7 0.5 collective-permute-done.4.c
  50.2 1.3 %sum_x.2 = (f32[128,1280]{1,0:T(8,128)S(1)}, bf16[128,1280]{1,0:T(8,128)(2,1)S(1)}) custom-call(bf16[2,128,1280]{2,1,0:T(8,128)(2,1)S(1)} %get-tuple-element.37.a, bf16[2,128,1280]{2,1,0:T(8,128)(2,1)S(1)} %collective-permute-done.3.b, bf16[2,128,1280]{2,1,0:T(8,128)(2,1)} %collective-permute-done.4.c, bf16[2,128,1280]{2,1,0:T(8,128)(2,1)S(1)} %get-tuple-element.43.after_ref), custom_call_target="tpu_custom_call" | custom-call | flops 1000000 | bytes 100000 | tf_op jit(solution)/shard_map/sum_x/pallas_call | solution.py:228
  51.5 1.7 %collective-permute-start.7 = (bf16[128,1280]{1,0:T(8,128)(2,1)S(1)}, bf16[128,1280]{1,0:T(8,128)(2,1)S(1)}, u32[]{:S(2)}, u32[]{:S(2)}) collective-permute-start(bf16[128,1280]{1,0:T(8,128)(2,1)S(1)} %get-tuple-element.45), channel_id=1, source_target_pairs={{0,4},{1,5},{2,6},{3,7},{4,0},{5,1},{6,2},{7,3},{8,12},{9,13},{10,... | collective-permute-start | bytes 983048 | tf_op jit(solution)/shard_map/ppermute | solution.py:40
  53.2 0.1 pad_maximum_fusion
  53.3 7.4 %collective-permute-done.8.b = bf16[2,128,1280]{2,1,0:T(8,128)(2,1)S(1)} collective-permute-done((bf16[2,128,1280]{2,1,0:T(8,128)(2,1)S(1)}, bf16[2,128,1280]{2,1,0:T(8,128)(2,1)S(1)}, u32[]{:S(2)}, u32[]{:S(2)}) %collective-permute-start.8) | collective-permute-done | bytes 655392 | tf_op jit(solution)/shard_map/ppermute | solution.py:40
  60.7 2.1 %collective-permute-done.9.c = bf16[2,128,1280]{2,1,0:T(8,128)(2,1)S(1)} collective-permute-done((bf16[2,128,1280]{2,1,0:T(8,128)(2,1)S(1)}, bf16[2,128,1280]{2,1,0:T(8,128)(2,1)S(1)}, u32[]{:S(2)}, u32[]{:S(2)}) %collective-permute-start.9) | collective-permute-done | bytes 655392 | tf_op jit(solution)/shard_map/ppermute | solution.py:40
  62.9 0.2 sum_x.3
  63.1 0.3 make_queries.1
  63.4 0.1 collective-permute-start.16
  63.5 0.5 collective-permute-start.14
  64.0 0.1 collective-permute-start.15
  64.1 3.2 %collective-permute-start.10 = (bf16[32,32,128]{2,1,0:T(8,128)(2,1)S(1)}, bf16[32,32,128]{2,1,0:T(8,128)(2,1)S(1)}, u32[]{:S(2)}, u32[]{:S(2)}) collective-permute-start(bf16[32,32,128]{2,1,0:T(8,128)(2,1)S(1)} %get-tuple-element.48.refs_3_.q_ref), channel_id=1, source_target_pairs={{0,64},{8,72},{16,80},{24,88},{32,96},{40,104},{48,112},{56,120},{... | collective-permute-start | bytes 786440 | tf_op jit(solution)/shard_map/ppermute | solution.py:44
  67.3 0.7 collective-permute-start.18
  68.1 1.0 %copy-done.3 = bf16[4,512,256]{2,1,0:T(8,128)(2,1)} copy-done((bf16[4,512,256]{2,1,0:T(8,128)(2,1)}, bf16[4,512,256]{2,1,0:T(8,128)(2,1)S(1)}, u32[]{:S(2)}) %copy-start.3) | copy-done | bytes 1048600
  69.1 4.3 %attend_near.1.refs_8_.near_ref = f32[33,32,128]{2,1,0:T(8,128)} custom-call(s32[64]{0:T(128)S(1)} %get-tuple-element.62.length_ref, s32[64]{0:T(128)S(1)} %get-tuple-element.64.at_ref.order_ref, bf16[32,32,128]{2,1,0:T(8,128)(2,1)S(1)} %get-tuple-element.48.refs_3_.q_ref, bf16[128,256]{1,0:T(8,128)(2,1)S(1)} %get-tuple-element.52.new_ref, ...), custom_call_target="tpu_custom_call" | custom-call | flops 1000000 | bytes 100000 | tf_op jit(solution)/shard_map/attend_near/pallas_call | solution.py:421
  73.3 1.4 %collective-permute-done.10.q_ref = bf16[32,32,128]{2,1,0:T(8,128)(2,1)S(1)} collective-permute-done((bf16[32,32,128]{2,1,0:T(8,128)(2,1)S(1)}, bf16[32,32,128]{2,1,0:T(8,128)(2,1)S(1)}, u32[]{:S(2)}, u32[]{:S(2)}) %collective-permute-start.10) | collective-permute-done | bytes 262176 | tf_op jit(solution)/shard_map/ppermute | solution.py:44
  74.7 1.0 %copy-done.4 = bf16[4,512,256]{2,1,0:T(8,128)(2,1)} copy-done((bf16[4,512,256]{2,1,0:T(8,128)(2,1)}, bf16[4,512,256]{2,1,0:T(8,128)(2,1)S(1)}, u32[]{:S(2)}) %copy-start.4) | copy-done | bytes 1048600
  75.7 1.0 %copy-done.5 = bf16[4,512,256]{2,1,0:T(8,128)(2,1)} copy-done((bf16[4,512,256]{2,1,0:T(8,128)(2,1)}, bf16[4,512,256]{2,1,0:T(8,128)(2,1)S(1)}, u32[]{:S(2)}) %copy-start.5) | copy-done | bytes 1048600
  76.7 5.4 %attend_prefix.1 = bf16[33,32,128]{2,1,0:T(8,128)(2,1)S(1)} custom-call(s32[32]{0:T(128)S(1)} %slice.3.limit_ref, bf16[32,32,128]{2,1,0:T(8,128)(2,1)S(1)} %collective-permute-done.10.q_ref, bf16[4,512,256]{2,1,0:T(8,128)(2,1)} %bitcast.25, bf16[4,512,256]{2,1,0:T(8,128)(2,1)} %get-tuple-element.49.refs_1_, bf16[4,512,256]{2,1,0:T(8,128)(2,1)} %get-tuple-element.50.refs_2_, ...), custom_call_target="tpu_custom_call" | custom-call | flops 1000000 | bytes 100000 | tf_op jit(solution)/shard_map/attend_prefix/pallas_call | solution.py:381
  82.1 3.3 %collective-permute-start.17 = (bf16[33,32,128]{2,1,0:T(8,128)(2,1)S(1)}, bf16[33,32,128]{2,1,0:T(8,128)(2,1)S(1)}, u32[]{:S(2)}, u32[]{:S(2)}) collective-permute-start(bf16[33,32,128]{2,1,0:T(8,128)(2,1)S(1)} %attend_prefix.1), channel_id=1, source_target_pairs={{0,64},{8,72},{16,80},{24,88},{32,96},{40,104},{48,112},{56,120},{... | collective-permute-start | bytes 811016 | tf_op jit(solution)/shard_map/ppermute | solution.py:44
  85.4 5.9 %attend.1.done_ref = bf16[32,4,1280]{2,1,0:T(4,128)(2,1)S(1)} custom-call(s32[32]{0:T(128)S(1)} %slice.3.limit_ref, s32[64]{0:T(128)S(1)} %get-tuple-element.62.length_ref, s32[64]{0:T(128)S(1)} %get-tuple-element.64.at_ref.order_ref, f32[128,1280]{1,0:T(8,128)S(1)} %get-tuple-element.47.after_ref.keep_ref, ...), custom_call_target="tpu_custom_call" | custom-call | flops 1000000 | bytes 100000 | tf_op jit(solution)/shard_map/attend/pallas_call | solution.py:325
  91.4 2.2 %merge_rows.1 = (bf16[64,4,1024]{2,1,0:T(4,128)(2,1)}, bf16[64,4,256]{2,1,0:T(4,128)(2,1)}) custom-call(s32[64]{0:T(128)S(1)} %get-tuple-element.64.at_ref.order_ref, bf16[33,32,128]{2,1,0:T(8,128)(2,1)S(1)} %collective-permute-done.17.far_ref, f32[33,32,128]{2,1,0:T(8,128)} %attend_near.1.refs_8_.near_ref, bf16[32,4,256]{2,1,0:T(4,128)(2,1)S(1)} %reshape.178.new_ref, ...), custom_call_target="tpu_custom_call" | custom-call | flops 1000000 | bytes 100000 | tf_op jit(solution)/shard_map/merge_rows/pallas_call | solution.py:452
  (53 shorter events, 0.9 us)
Async XLA Ops:
  0.6 17.6 %collective-permute-start = (bf16[4,512,256]{2,1,0:T(8,128)(2,1)}, bf16[4,512,256]{2,1,0:T(8,128)(2,1)S(1)}, u32[]{:S(2)}, u32[]{:S(2)}) collective-permute-start(bf16[4,512,256]{2,1,0:T(8,128)(2,1)} %bitcast.22), channel_id=1, source_target_pairs={{0,8},{8,0},{16,24},{24,16},{32,40},{40,32},{48,56},{56,48},{64,72... | collective-permute-start | bytes 3145736 | tf_op jit(solution)/shard_map/ppermute | solution.py:44
  0.7 29.8 %collective-permute-start.11 = (bf16[4,512,256]{2,1,0:T(8,128)(2,1)}, bf16[4,512,256]{2,1,0:T(8,128)(2,1)}, u32[]{:S(2)}, u32[]{:S(2)}) collective-permute-start(bf16[4,512,256]{2,1,0:T(8,128)(2,1)} %bitcast.23), channel_id=1, source_target_pairs={{0,16},{8,24},{16,32},{24,40},{32,48},{40,56},{48,0},{56,8},{64,80... | collective-permute-start | bytes 3145736 | tf_op jit(solution)/shard_map/ppermute | solution.py:44
  2.8 60.6 %collective-permute-start.12 = (bf16[4,512,256]{2,1,0:T(8,128)(2,1)}, bf16[4,512,256]{2,1,0:T(8,128)(2,1)}, u32[]{:S(2)}, u32[]{:S(2)}) collective-permute-start(bf16[4,512,256]{2,1,0:T(8,128)(2,1)} %bitcast.24), channel_id=1, source_target_pairs={{0,48},{8,56},{16,0},{24,8},{32,16},{40,24},{48,32},{56,40},{64,11... | collective-permute-start | bytes 3145736 | tf_op jit(solution)/shard_map/ppermute | solution.py:44
  7.9 9.8 %copy-start.11 = (s32[4]{0:T(128)S(1)}, s32[4]{0:T(128)}, u32[]{:S(2)}) copy-start(s32[4]{0:T(128)} %constant.143.clone) | copy-start | bytes 52
  14.5 12.2 %collective-permute-start.1 = (bf16[1,128,1280]{2,1,0:T(8,128)(2,1)}, bf16[1,128,1280]{2,1,0:T(8,128)(2,1)}, u32[]{:S(2)}, u32[]{:S(2)}) collective-permute-start(bf16[1,128,1280]{2,1,0:T(8,128)(2,1)} %get-tuple-element.33), channel_id=1, source_target_pairs={{0,1},{1,2},{2,3},{3,0},{4,5},{5,6},{6,7},{7,4},{8,9},{9,10},{10,1... | collective-permute-start | bytes 983048 | tf_op jit(solution)/shard_map/ppermute | solution.py:40
  16.0 12.2 %collective-permute-start.2 = (bf16[1,128,1280]{2,1,0:T(8,128)(2,1)}, bf16[1,128,1280]{2,1,0:T(8,128)(2,1)}, u32[]{:S(2)}, u32[]{:S(2)}) collective-permute-start(bf16[1,128,1280]{2,1,0:T(8,128)(2,1)} %get-tuple-element.34), channel_id=1, source_target_pairs={{0,3},{1,0},{2,1},{3,2},{4,7},{5,4},{6,5},{7,6},{8,11},{9,8},{10,9... | collective-permute-start | bytes 983048 | tf_op jit(solution)/shard_map/ppermute | solution.py:40
  18.2 6.6 %copy-start = (bf16[4,512,256]{2,1,0:T(8,128)(2,1)}, bf16[4,512,256]{2,1,0:T(8,128)(2,1)S(1)}, u32[]{:S(2)}) copy-start(bf16[4,512,256]{2,1,0:T(8,128)(2,1)S(1)} %collective-permute-done.refs_4_) | copy-start | bytes 3145732
  18.3 14.8 %collective-permute-start.5 = (bf16[1,128,1280]{2,1,0:T(8,128)(2,1)}, bf16[1,128,1280]{2,1,0:T(8,128)(2,1)}, u32[]{:S(2)}, u32[]{:S(2)}) collective-permute-start(bf16[1,128,1280]{2,1,0:T(8,128)(2,1)} %get-tuple-element.40), channel_id=1, source_target_pairs={{0,1},{1,2},{2,3},{3,0},{4,5},{5,6},{6,7},{7,4},{8,9},{9,10},{10,1... | collective-permute-start | bytes 983048 | tf_op jit(solution)/shard_map/ppermute | solution.py:40
  18.6 11.7 %copy-start.6 = (s32[64]{0:T(128)S(1)}, s32[64]{0:T(128)}, u32[]{:S(2)}) copy-start(s32[64]{0:T(128)} %param.18) | copy-start | bytes 772
  18.6 11.7 %copy-start.8 = (s32[64,1]{0,1:T(1,128)S(1)}, s32[64,1]{0,1:T(1,128)}, u32[]{:S(2)}) copy-start(s32[64,1]{0,1:T(1,128)} %param.20) | copy-start | bytes 772
  18.6 11.7 %copy-start.9 = (s32[64]{0:T(128)S(1)}, s32[64]{0:T(128)}, u32[]{:S(2)}) copy-start(s32[64]{0:T(128)} %param.19) | copy-start | bytes 772
  18.6 16.8 %copy-start.7 = (bf16[1024]{0:T(1024)(128)(2,1)S(1)}, bf16[1024]{0:T(1024)(128)(2,1)}, u32[]{:S(2)}) copy-start(bf16[1024]{0:T(1024)(128)(2,1)} %param.13) | copy-start | bytes 6148
  18.6 16.8 %copy-start.10 = (bf16[256]{0:T(256)(128)(2,1)S(1)}, bf16[256]{0:T(256)(128)(2,1)}, u32[]{:S(2)}) copy-start(bf16[256]{0:T(256)(128)(2,1)} %param.15) | copy-start | bytes 1540
  24.9 4.9 %copy-start.1 = (bf16[2,128,1280]{2,1,0:T(8,128)(2,1)}, bf16[2,128,1280]{2,1,0:T(8,128)(2,1)S(1)}, u32[]{:S(2)}) copy-start(bf16[2,128,1280]{2,1,0:T(8,128)(2,1)S(1)} %get-tuple-element.39.l) | copy-start | bytes 1966084
  26.6 13.1 %collective-permute-start.6 = (bf16[1,128,1280]{2,1,0:T(8,128)(2,1)}, bf16[1,128,1280]{2,1,0:T(8,128)(2,1)S(1)}, u32[]{:S(2)}, u32[]{:S(2)}) collective-permute-start(bf16[1,128,1280]{2,1,0:T(8,128)(2,1)} %get-tuple-element.41), channel_id=1, source_target_pairs={{0,3},{1,0},{2,1},{3,2},{4,7},{5,4},{6,5},{7,6},{8,11},{9,8},{10,9... | collective-permute-start | bytes 983048 | tf_op jit(solution)/shard_map/ppermute | solution.py:40
  29.8 19.0 %collective-permute-start.3 = (bf16[2,128,1280]{2,1,0:T(8,128)(2,1)S(1)}, bf16[2,128,1280]{2,1,0:T(8,128)(2,1)S(1)}, u32[]{:S(2)}, u32[]{:S(2)}) collective-permute-start(bf16[2,128,1280]{2,1,0:T(8,128)(2,1)S(1)} %get-tuple-element.35.refs_4_.refs_0_), channel_id=1, source_target_pairs={{0,1},{1,2},{2,3},{3,0},{4,5},{5,6},{6,7},{7,4},{8,9},{9,10},{10,1... | collective-permute-start | bytes 1966088 | tf_op jit(solution)/shard_map/ppermute | solution.py:40
  30.5 32.9 %collective-permute-start.13 = (bf16[4,512,256]{2,1,0:T(8,128)(2,1)}, bf16[4,512,256]{2,1,0:T(8,128)(2,1)}, u32[]{:S(2)}, u32[]{:S(2)}) collective-permute-start(bf16[4,512,256]{2,1,0:T(8,128)(2,1)} %collective-permute-done.11.refs_0_), channel_id=1, source_target_pairs={{0,16},{8,24},{16,32},{24,40},{32,48},{40,56},{48,0},{56,8},{64,80... | collective-permute-start | bytes 3145736 | tf_op jit(solution)/shard_map/ppermute | solution.py:44
  33.1 17.1 %collective-permute-start.4 = (bf16[2,128,1280]{2,1,0:T(8,128)(2,1)S(1)}, bf16[2,128,1280]{2,1,0:T(8,128)(2,1)}, u32[]{:S(2)}, u32[]{:S(2)}) collective-permute-start(bf16[2,128,1280]{2,1,0:T(8,128)(2,1)S(1)} %get-tuple-element.36.refs_5_), channel_id=1, source_target_pairs={{0,3},{1,0},{2,1},{3,2},{4,7},{5,4},{6,5},{7,6},{8,11},{9,8},{10,9... | collective-permute-start | bytes 1966088 | tf_op jit(solution)/shard_map/ppermute | solution.py:40
  35.5 4.3 %copy-start.2 = (bf16[2,128,1280]{2,1,0:T(8,128)(2,1)S(1)}, bf16[2,128,1280]{2,1,0:T(8,128)(2,1)}, u32[]{:S(2)}) copy-start(bf16[2,128,1280]{2,1,0:T(8,128)(2,1)} %copy-done.1) | copy-start | bytes 1966084
  41.2 19.5 %collective-permute-start.8 = (bf16[2,128,1280]{2,1,0:T(8,128)(2,1)S(1)}, bf16[2,128,1280]{2,1,0:T(8,128)(2,1)S(1)}, u32[]{:S(2)}, u32[]{:S(2)}) collective-permute-start(bf16[2,128,1280]{2,1,0:T(8,128)(2,1)S(1)} %get-tuple-element.43.after_ref), channel_id=1, source_target_pairs={{0,1},{1,2},{2,3},{3,0},{4,5},{5,6},{6,7},{7,4},{8,9},{9,10},{10,1... | collective-permute-start | bytes 1966088 | tf_op jit(solution)/shard_map/ppermute | solution.py:40
  48.7 14.2 %collective-permute-start.9 = (bf16[2,128,1280]{2,1,0:T(8,128)(2,1)S(1)}, bf16[2,128,1280]{2,1,0:T(8,128)(2,1)S(1)}, u32[]{:S(2)}, u32[]{:S(2)}) collective-permute-start(bf16[2,128,1280]{2,1,0:T(8,128)(2,1)S(1)} %get-tuple-element.46), channel_id=1, source_target_pairs={{0,3},{1,0},{2,1},{3,2},{4,7},{5,4},{6,5},{7,6},{8,11},{9,8},{10,9... | collective-permute-start | bytes 1966088 | tf_op jit(solution)/shard_map/ppermute | solution.py:40
  51.5 11.6 %collective-permute-start.7 = (bf16[128,1280]{1,0:T(8,128)(2,1)S(1)}, bf16[128,1280]{1,0:T(8,128)(2,1)S(1)}, u32[]{:S(2)}, u32[]{:S(2)}) collective-permute-start(bf16[128,1280]{1,0:T(8,128)(2,1)S(1)} %get-tuple-element.45), channel_id=1, source_target_pairs={{0,4},{1,5},{2,6},{3,7},{4,0},{5,1},{6,2},{7,3},{8,12},{9,13},{10,... | collective-permute-start | bytes 983048 | tf_op jit(solution)/shard_map/ppermute | solution.py:40
  63.4 4.6 %collective-permute-start.16 = (bf16[4,512,256]{2,1,0:T(8,128)(2,1)}, bf16[4,512,256]{2,1,0:T(8,128)(2,1)S(1)}, u32[]{:S(2)}, u32[]{:S(2)}) collective-permute-start(bf16[4,512,256]{2,1,0:T(8,128)(2,1)} %get-tuple-element.51.refs_3_), channel_id=1, source_target_pairs={{0,8},{8,0},{16,24},{24,16},{32,40},{40,32},{48,56},{56,48},{64,72... | collective-permute-start | bytes 3145736 | tf_op jit(solution)/shard_map/ppermute | solution.py:44
  63.5 11.2 %collective-permute-start.14 = (bf16[4,512,256]{2,1,0:T(8,128)(2,1)}, bf16[4,512,256]{2,1,0:T(8,128)(2,1)S(1)}, u32[]{:S(2)}, u32[]{:S(2)}) collective-permute-start(bf16[4,512,256]{2,1,0:T(8,128)(2,1)} %get-tuple-element.49.refs_1_), channel_id=1, source_target_pairs={{0,8},{8,0},{16,24},{24,16},{32,40},{40,32},{48,56},{56,48},{64,72... | collective-permute-start | bytes 3145736 | tf_op jit(solution)/shard_map/ppermute | solution.py:44
  64.0 10.7 %collective-permute-start.15 = (bf16[4,512,256]{2,1,0:T(8,128)(2,1)}, bf16[4,512,256]{2,1,0:T(8,128)(2,1)S(1)}, u32[]{:S(2)}, u32[]{:S(2)}) collective-permute-start(bf16[4,512,256]{2,1,0:T(8,128)(2,1)} %get-tuple-element.50.refs_2_), channel_id=1, source_target_pairs={{0,8},{8,0},{16,24},{24,16},{32,40},{40,32},{48,56},{56,48},{64,72... | collective-permute-start | bytes 3145736 | tf_op jit(solution)/shard_map/ppermute | solution.py:44
  64.1 10.6 %collective-permute-start.10 = (bf16[32,32,128]{2,1,0:T(8,128)(2,1)S(1)}, bf16[32,32,128]{2,1,0:T(8,128)(2,1)S(1)}, u32[]{:S(2)}, u32[]{:S(2)}) collective-permute-start(bf16[32,32,128]{2,1,0:T(8,128)(2,1)S(1)} %get-tuple-element.48.refs_3_.q_ref), channel_id=1, source_target_pairs={{0,64},{8,72},{16,80},{24,88},{32,96},{40,104},{48,112},{56,120},{... | collective-permute-start | bytes 786440 | tf_op jit(solution)/shard_map/ppermute | solution.py:44
  67.3 18.1 %collective-permute-start.18 = (bf16[128,1280]{1,0:T(8,128)(2,1)S(1)}, bf16[128,1280]{1,0:T(8,128)(2,1)S(1)}, u32[]{:S(2)}, u32[]{:S(2)}) collective-permute-start(bf16[128,1280]{1,0:T(8,128)(2,1)S(1)} %get-tuple-element.53), channel_id=1, source_target_pairs={{0,4},{1,5},{2,6},{3,7},{4,0},{5,1},{6,2},{7,3},{8,12},{9,13},{10,... | collective-permute-start | bytes 983048 | tf_op jit(solution)/shard_map/ppermute | solution.py:40
  68.1 1.0 %copy-start.3 = (bf16[4,512,256]{2,1,0:T(8,128)(2,1)}, bf16[4,512,256]{2,1,0:T(8,128)(2,1)S(1)}, u32[]{:S(2)}) copy-start(bf16[4,512,256]{2,1,0:T(8,128)(2,1)S(1)} %collective-permute-done.16.after_ref.refs_7_) | copy-start | bytes 3145732
  74.7 1.0 %copy-start.4 = (bf16[4,512,256]{2,1,0:T(8,128)(2,1)}, bf16[4,512,256]{2,1,0:T(8,128)(2,1)S(1)}, u32[]{:S(2)}) copy-start(bf16[4,512,256]{2,1,0:T(8,128)(2,1)S(1)} %collective-permute-done.14.refs_5_) | copy-start | bytes 3145732
  75.7 1.0 %copy-start.5 = (bf16[4,512,256]{2,1,0:T(8,128)(2,1)}, bf16[4,512,256]{2,1,0:T(8,128)(2,1)S(1)}, u32[]{:S(2)}) copy-start(bf16[4,512,256]{2,1,0:T(8,128)(2,1)S(1)} %collective-permute-done.15.refs_6_) | copy-start | bytes 3145732
  82.1 9.2 %collective-permute-start.17 = (bf16[33,32,128]{2,1,0:T(8,128)(2,1)S(1)}, bf16[33,32,128]{2,1,0:T(8,128)(2,1)S(1)}, u32[]{:S(2)}, u32[]{:S(2)}) collective-permute-start(bf16[33,32,128]{2,1,0:T(8,128)(2,1)S(1)} %attend_prefix.1), channel_id=1, source_target_pairs={{0,64},{8,72},{16,80},{24,88},{32,96},{40,104},{48,112},{56,120},{... | collective-permute-start | bytes 811016 | tf_op jit(solution)/shard_map/ppermute | solution.py:44
